TPU v7x, 128 devices: a whole 4x4x4 slice. The times are simulated.
128 devices in a mesh: dp: 16 (over y, x), tensor: 8 (over z, core).
Axes of the slice: x: 4, y: 4, z: 4, core: 2. Of those that a mesh axis runs over, the one named last changes fastest.
Arguments:
- queries: bfloat16 [6144, 8192], P('dp', 'tensor'), may hold values from -16 to 16
- fresh_kv: bfloat16 [6144, 2048], P('dp', 'tensor'), may hold values from -17 to 17
- kv_pool: bfloat16 [720, 64, 2048], P('dp', None, 'tensor'), may hold values from -9 to 9
- page_table: int32 [384, 16], replicated, may hold values from 0 to 719, as said below
- path_len: int32 [384], replicated, may hold values from 769 to 1024, as said below
- parent: int32 [384], replicated, may hold values from -1 to 383, as said below
- w_out: bfloat16 [8192, 8192], P('tensor'), may hold values from -4 to 4
- residual: bfloat16 [6144, 8192], P('dp'), may hold values from -6 to 6
- gain: bfloat16 [8192], replicated, may hold values from 0.5 to 1.5
Outputs:
- mixed: bfloat16 [6144, 8192], P('dp', 'tensor')
- normed: bfloat16 [6144, 8192], P('dp', 'tensor')
Inputs may be any that keep to these rules, and one draw needn't show every extreme that they name: `page_table`: page p is held by dp rank p // 45. Each rank's nodes form aligned families of 4 consecutive nodes sharing their first 8 pages; all other entries among one rank's nodes are distinct pages. For every pair of ranks, the nodes of the first reference exactly 24 page slots and exactly 15 distinct pages held by the second. `path_len`: some node's path is full. `parent`: the first 12 nodes of each rank have -1; every other node names one of those nodes, on any rank.
All inputs are finite; a program needn't handle non-finite values.
Results may differ from a plain program's by a relative error of at most 0.019.
Values may be sent and summed in bfloat16 or wider, within the bound.
No kernel may reach another device: no remote copies, remote signals or barrier semaphores. Data moves between devices by JAX's collectives and lax.ppermute only.
A program may use at most 192 MiB of HBM per device.

v0:
```python
import jax
import jax.numpy as jnp
from jax import lax
from jax.sharding import PartitionSpec as P

D = 8192
HD = 128
NEW = 16
PAGE = 64
PATH_PAGES = 16


def send_lists(dest_table, rank, pages_dev, flags, capacity):
    owner = dest_table // pages_dev
    local = dest_table % pages_dev
    mine = (owner == rank) & flags
    count = mine.astype(jnp.int32)
    before = jnp.cumsum(count, axis=1) - count
    chosen = mine[:, None, :] & (
        before[:, None, :] == jnp.arange(capacity, dtype=jnp.int32)[None, :, None]
    )
    return jnp.sum(jnp.where(chosen, local[:, None, :], 0), axis=2)


def recv_positions(own_table, pages_dev, flags, groups):
    owner = own_table // pages_dev
    match = owner[:, None] == jnp.arange(groups, dtype=jnp.int32)[None, :]
    hits = (match & flags[:, None]).astype(jnp.int32)
    before = jnp.cumsum(hits, axis=0) - hits
    return (owner, jnp.sum(before * match.astype(jnp.int32), axis=1))


def body(queries, fresh_kv, kv_pool, page_table, path_len, parent, w_out, residual, gain):
    ranks = lax.axis_size("dp")
    rank = lax.axis_index("dp")
    rows = queries.shape[0]
    nodes = rows // NEW
    slots = nodes * PATH_PAGES
    pages_dev = kv_pool.shape[0]
    width = kv_pool.shape[2]
    kv_dev = width // (2 * HD)
    group = queries.shape[1] // (kv_dev * HD)
    span = PATH_PAGES * PAGE
    scale = HD ** (-0.5)
    dest_table = page_table.reshape(ranks, slots)
    own_table = lax.dynamic_index_in_dim(dest_table, rank, 0, keepdims=False)
    flags_all = jnp.ones((ranks, slots), dtype=bool)
    wanted = send_lists(dest_table, rank, pages_dev, flags_all, slots // ranks)
    received = lax.all_to_all(
        jnp.take(kv_pool, wanted, axis=0), "dp", split_axis=0, concat_axis=0, tiled=True
    )
    owner, place = recv_positions(own_table, pages_dev, jnp.ones((slots,), dtype=bool), ranks)
    path = received[owner, place].reshape(nodes, span, kv_dev, 2, HD)
    lengths = lax.dynamic_slice_in_dim(path_len, rank * nodes, nodes)
    parents = lax.dynamic_slice_in_dim(parent, rank * nodes, nodes)
    query = queries.reshape(nodes, NEW, kv_dev, group, HD)
    fresh = fresh_kv.reshape(nodes, NEW, kv_dev, 2, HD)
    path_scores = (
        jnp.einsum("ntkgd,nskd->nktgs", query, path[:, :, :, 0], preferred_element_type=jnp.float32)
        * scale
    )
    valid = jnp.arange(span, dtype=jnp.int32)[None, :] < lengths[:, None]
    path_scores = jnp.where(valid[:, None, None, None, :], path_scores, -jnp.inf)
    own_scores = (
        jnp.einsum(
            "ntkgd,nskd->nktgs", query, fresh[:, :, :, 0], preferred_element_type=jnp.float32
        )
        * scale
    )
    causal = jnp.arange(NEW)[None, :] <= jnp.arange(NEW)[:, None]
    own_scores = jnp.where(causal[None, None, :, None, :], own_scores, -jnp.inf)
    top = jnp.maximum(jnp.max(path_scores, axis=-1), jnp.max(own_scores, axis=-1))
    path_weight = jnp.exp(path_scores - top[..., None])
    own_weight = jnp.exp(own_scores - top[..., None])
    total = jnp.sum(path_weight, axis=-1) + jnp.sum(own_weight, axis=-1)
    accum = jnp.einsum(
        "nktgs,nskd->nktgd",
        path_weight.astype(jnp.bfloat16),
        path[:, :, :, 1],
        preferred_element_type=jnp.float32,
    )
    accum = accum + jnp.einsum(
        "nktgs,nskd->nktgd",
        own_weight.astype(jnp.bfloat16),
        fresh[:, :, :, 1],
        preferred_element_type=jnp.float32,
    )
    piece = lax.all_gather(fresh_kv, "dp", axis=0, tiled=True)
    weight_sum = total
    values_sum = accum
    count = piece.shape[0] // NEW
    inside = (parents >= 0) & (parents < count)
    picked = jnp.take(
        piece.reshape(count, NEW, kv_dev, 2, HD), jnp.clip(parents, 0, count - 1), axis=0
    )
    scores = (
        jnp.einsum(
            "ntkgd,nskd->nktgs", query, picked[:, :, :, 0], preferred_element_type=jnp.float32
        )
        * scale
    )
    scores = jnp.where(inside[:, None, None, None, None], scores, -jnp.inf)
    new_best = jnp.maximum(top, jnp.max(scores, axis=-1))
    fade = jnp.exp(top - new_best)
    weight = jnp.exp(scores - new_best[..., None])
    values_sum = values_sum * fade[..., None] + jnp.einsum(
        "nktgs,nskd->nktgd",
        weight.astype(jnp.bfloat16),
        picked[:, :, :, 1],
        preferred_element_type=jnp.float32,
    )
    total = weight_sum * fade + jnp.sum(weight, axis=-1)
    attn = (
        (values_sum / total[..., None])
        .transpose(0, 2, 1, 3, 4)
        .reshape(rows, kv_dev * group * HD)
        .astype(jnp.bfloat16)
    )
    partial_out = jnp.dot(attn, w_out, preferred_element_type=jnp.float32)
    tensor_rank = lax.axis_index("tensor")
    cols = D // lax.axis_size("tensor")
    summed = lax.psum(partial_out.astype(jnp.bfloat16), "tensor").astype(jnp.float32)
    mixed_full = residual.astype(jnp.float32) + summed
    power = jnp.mean(mixed_full * mixed_full, axis=1, keepdims=True)
    normed_full = mixed_full * lax.rsqrt(power + 1e-05) * gain.astype(jnp.float32)
    mixed = lax.dynamic_slice_in_dim(mixed_full, tensor_rank * cols, cols, 1)
    normed = lax.dynamic_slice_in_dim(normed_full, tensor_rank * cols, cols, 1)
    return (mixed.astype(jnp.bfloat16), normed.astype(jnp.bfloat16))


def solution(mesh):
    return jax.shard_map(
        body,
        mesh=mesh,
        in_specs=(
            P("dp", "tensor"),
            P("dp", "tensor"),
            P("dp", None, "tensor"),
            P(),
            P(),
            P(),
            P("tensor", None),
            P("dp", None),
            P(),
        ),
        out_specs=(P("dp", "tensor"), P("dp", "tensor")),
        check_vma=False,
    )
```

profile of v0, /device:TPU:2, one launch (start us, length us, event | category | flops | bytes accessed | tf_op | source)
XLA Modules:
  0.0 471.0 jit_solution(13372365678998038267)
XLA Ops:
  7.2 0.9 broadcast_divide_fusion
  8.1 0.8 fusion.30
  8.8 0.9 copy.137
  9.7 0.1 copy.139
  9.8 0.1 div.62
  9.9 0.2 copy.138
  10.1 0.1 and.77
  10.3 0.9 reduce-window.14
  11.2 0.2 slice_reduce_fusion.1
  11.4 0.1 reshape.426
  11.6 0.4 select_reduce_fusion
  12.1 11.3 %gather_fusion = bf16[384,64,256]{2,1,0:T(8,128)(2,1)} fusion(bf16[45,64,256]{2,1,0:T(8,128)(2,1)S(1)} %copy-done, s32[1024]{0:T(1024)S(1)} %pad_clamp_fusion.1), kind=kCustom, calls=%fused_computation | custom fusion | bytes 25167360 | tf_op jit(solution)/shard_map/jit(_take)/gather | solution.py:50
  23.4 10.7 %broadcast_select_fusion = bf16[16,24,64,256]{3,2,1,0:T(8,128)(2,1)} fusion(bf16[16,24,64,256]{3,2,1,0:T(8,128)(2,1)} %bitcast.130, pred[16,24]{1,0:T(8,128)(4,1)S(1)} %compare_and_fusion), kind=kLoop, calls=%fused_computation.9 | loop fusion | flops 6291456 | bytes 25166208 | tf_op jit(solution)/shard_map/jit(_take)/select_n | solution.py:50
  34.2 7.6 %all-to-all-start = ((bf16[16,24,64,256]{3,2,1,0:T(8,128)(2,1)}), bf16[16,24,64,256]{3,2,1,0:T(8,128)(2,1)}, u32[]{:S(2)}, u32[]{:S(2)}) async-start(bf16[16,24,64,256]{3,2,1,0:T(8,128)(2,1)} %broadcast_select_fusion), calls=%async_computation | async-start | bytes 25165824 | tf_op jit(solution)/shard_map/all_to_all | solution.py:49
  41.8 0.7 all-gather.2.cloned.1.call-update
  42.5 0.2 all-reduce.2.cloned.1.call-start
  42.9 0.9 reduce-window.16
  43.8 0.2 slice_reduce_fusion
  44.0 0.2 copy.176
  44.2 0.3 fusion.45
  44.5 0.7 fusion.46
  45.3 0.8 dynamic_slice.16
  46.1 0.8 compare_and_fusion.2
  46.9 0.1 fusion.28
  47.1 179.9 %all-gather.2.cloned.1.call-done = bf16[6144,256]{1,0:T(8,128)(2,1)} async-done(((bf16[384,256]{1,0:T(8,128)(2,1)}), bf16[6144,256]{1,0:T(8,128)(2,1)}) %all-gather.2.cloned.1.call-update) | async-done | bytes 3145744 | tf_op jit(solution)/shard_map/all_gather | solution.py:88
  227.0 5.5 %reshape.453 = bf16[384,16,2,128]{3,2,1,0:T(2,128)(2,1)} reshape(bf16[6144,256]{1,0:T(8,128)(2,1)} %all-gather.2.cloned.1.call-done) | data formatting | bytes 6291456 | tf_op jit(solution)/shard_map/reshape | solution.py:94
  232.5 4.0 copy.153
  236.5 2.5 gather_fusion.2
  239.0 0.1 bitcast_select_fusion
  239.1 3.1 bitcast_reduce_fusion.1
  242.2 21.0 %gather_fusion.1 = bf16[384,64,256]{2,1,0:T(8,128)(2,1)} fusion(bf16[16,24,64,256]{3,2,1,0:T(8,128)(2,1)} %all-to-all-done, s32[384]{0:T(512)S(1)} %fusion.36), kind=kCustom, calls=%fused_computation.1 | custom fusion | bytes 25168896 | tf_op jit(solution)/shard_map/gather | solution.py:53
  263.2 18.1 %reshape.429 = bf16[24,1024,1,2,128]{4,3,1,0,2:T(2,128)(2,1)} reshape(bf16[384,64,256]{2,1,0:T(8,128)(2,1)} %gather_fusion.1) | data formatting | bytes 25165824 | tf_op jit(solution)/shard_map/reshape | solution.py:53
  281.4 24.6 %fusion.44 = (bf16[24,1024,1,1,128]{4,3,1,0,2:T(2,128)(2,1)}, bf16[24,1024,1,1,128]{4,3,1,0,2:T(2,128)(2,1)}) fusion(bf16[24,1024,1,2,128]{4,3,1,0,2:T(2,128)(2,1)} %reshape.429), kind=kLoop, calls=%fused_computation.104 | loop fusion | bytes 25165824 | tf_op jit(solution)/shard_map/slice | solution.py:79
  306.0 11.4 %bitcast_reduce_fusion = (f32[24,16,8]{1,2,0:T(8,128)S(1)}, f32[24,1024,16,8]{1,2,3,0:T(8,128)}) fusion(pred[24,1024]{1,0:T(8,128)(4,1)S(1)} %iota_compare_fusion.1, bf16[24,16,8,128]{3,2,1,0:T(8,128)(2,1)S(1)} %bitcast.133, bf16[24,1024,1,1,128]{4,3,1,0,2:T(2,128)(2,1)} %get-tuple-element.17), kind=kOutput, calls=%fused_computation.4 | convolution fusion | flops 814740480 | bytes 19697664 | tf_op jit(solution)/shard_map/ntkgd,nskd->nktgs/dot_general | solution.py:59
  317.4 0.1 copy.150
  317.5 6.7 %fusion.1 = f32[24,16,8]{1,2,0:T(8,128)S(1)} fusion(f32[24,1024,16,8]{1,2,3,0:T(8,128)} %get-tuple-element.27, f32[24,16,8]{1,2,0:T(8,128)S(1)} %get-tuple-element.5, pred[24,1024]{1,0:T(8,128)(4,1)S(1)} %iota_compare_fusion.1), kind=kLoop, calls=%fused_computation.11 | loop fusion | flops 12579840 | bytes 12632064 | tf_op jit(solution)/shard_map/reduce_sum | solution.py:75
  324.3 0.9 fusion.11
  325.3 13.1 %fusion.3 = f32[24,16,8,128]{3,1,2,0:T(8,128)} fusion(f32[24,1024,16,8]{1,2,3,0:T(8,128)} %get-tuple-element.27, bf16[24,1024,1,1,128]{4,3,1,0,2:T(2,128)(2,1)} %get-tuple-element.16, f32[24,16,8]{1,2,0:T(8,128)S(1)} %get-tuple-element.5, pred[24,1024]{1,0:T(8,128)(4,1)S(1)} %iota_compare_fusion.1), kind=kOutput, calls=%fused_computation.13 | convolution fusion | flops 817889280 | bytes 20484096 | tf_op jit(solution)/shard_map/nktgs,nskd->nktgd/dot_general | solution.py:76
  338.4 0.5 fusion.13
  338.9 0.3 fusion.18
  339.3 3.0 divide_convert_fusion
  342.3 0.2 copy.159
  342.6 14.4 %convolution_convert_fusion = bf16[384,8192]{1,0:T(8,128)(2,1)} fusion(bf16[1024,8192]{1,0:T(8,128)(2,1)} %param.15, bf16[48,8,8,128]{3,2,1,0:T(8,128)(2,1)S(1)} %bitcast.135), kind=kOutput, calls=%fused_computation.10 | convolution fusion | flops 6445596672 | bytes 23855104 | tf_op jit(solution)/shard_map/dot_general | solution.py:119
  357.0 0.7 dynamic-slice
  357.6 90.3 %all-reduce.2.cloned.1.call-done = bf16[384,8192]{1,0:T(8,128)(2,1)} async-done(((bf16[384,8192]{1,0:T(8,128)(2,1)}), bf16[384,8192]{1,0:T(8,128)(2,1)}) %all-reduce.2.cloned.1.call-update) | async-done | bytes 6291472 | tf_op jit(solution)/shard_map/psum | solution.py:122
  447.9 11.3 %multiply_reduce_fusion = (f32[384]{0:T(512)S(1)}, f32[384,8192]{1,0:T(8,128)}) fusion(bf16[384,8192]{1,0:T(8,128)(2,1)} %all-reduce.2.cloned.1.call-done, bf16[384,8192]{1,0:T(8,128)(2,1)} %param.16), kind=kLoop, calls=%fused_computation.6 | loop fusion | flops 15728256 | bytes 25167360 | tf_op jit(solution)/shard_map/reduce_sum | solution.py:124
  459.2 2.4 dynamic-slice_convert_fusion
  461.6 2.5 multiply_convert_fusion
  (36 shorter events, 0.9 us)
Async XLA Ops:
  7.2 4.9 %copy-start = (bf16[45,64,256]{2,1,0:T(8,128)(2,1)S(1)}, bf16[45,64,256]{2,1,0:T(8,128)(2,1)}, u32[]{:S(2)}) copy-start(bf16[45,64,256]{2,1,0:T(8,128)(2,1)} %param.11) | copy-start | bytes 4423684
  34.2 8.6 %copy-start.4 = (bf16[384,256]{1,0:T(8,128)(2,1)S(1)}, bf16[384,256]{1,0:T(8,128)(2,1)}, u32[]{:S(2)}) copy-start(bf16[384,256]{1,0:T(8,128)(2,1)} %param.10) | copy-start | bytes 589828
  34.2 9.9 %copy-start.3 = (bf16[384,1024]{1,0:T(8,128)(2,1)S(1)}, bf16[384,1024]{1,0:T(8,128)(2,1)}, u32[]{:S(2)}) copy-start(bf16[384,1024]{1,0:T(8,128)(2,1)} %param.9) | copy-start | bytes 2359300
  34.2 208.1 %all-to-all-start = ((bf16[16,24,64,256]{3,2,1,0:T(8,128)(2,1)}), bf16[16,24,64,256]{3,2,1,0:T(8,128)(2,1)}, u32[]{:S(2)}, u32[]{:S(2)}) async-start(bf16[16,24,64,256]{3,2,1,0:T(8,128)(2,1)} %broadcast_select_fusion), calls=%async_computation | async-start | bytes 25165824 | tf_op jit(solution)/shard_map/all_to_all | solution.py:49
  41.8 185.2 %all-gather.2.cloned.1.call-start = ((), (), s32[]{:S(2)}) async-start(), calls=%async_computation.1 | async-start | bytes 3342336 | tf_op jit(solution)/shard_map/all_gather | solution.py:88
  42.5 405.4 %all-reduce.2.cloned.1.call-start = ((), (), s32[]{:S(2)}) async-start(), calls=%async_computation.2 | async-start | bytes 12582912 | tf_op jit(solution)/shard_map/psum | solution.py:122
  325.3 13.1 %copy-start.2 = (f32[24,16,16,8]{2,1,3,0:T(8,128)S(1)}, f32[24,16,16,8]{2,1,3,0:T(8,128)}, u32[]{:S(2)}) copy-start(f32[24,16,16,8]{2,1,3,0:T(8,128)} %get-tuple-element.25) | copy-start | bytes 589828
  447.9 16.2 %copy-start.1 = (bf16[45,64,256]{2,1,0:T(8,128)(2,1)S(1)}, bf16[45,64,256]{2,1,0:T(8,128)(2,1)}, u32[]{:S(2)}) copy-start(bf16[45,64,256]{2,1,0:T(8,128)(2,1)} %param.11) | copy-start | bytes 4423684
Sparse Core Ops, SparseCore 0:
  44.7 182.1 all-gather.1
  357.1 90.7 all-reduce.1
where the time goes:
time: 473 us; the launch traced here: 471 us
  waiting for transfers between devices  271 us (57%)
  local copies, waits for them, and re-layouts  94.1 us (20%)
  matrix products  46.1 us (10%)
  other arithmetic  37.8 us (8%)
  between operations  14.3 us (3%)
  starting transfers between devices  7.86 us (2%)
    all_gather x1, waiting for transfers between devices, body(): piece = lax.all_gather(fresh_kv, 'dp', axis=0, tiled=True)  180 us
    psum x1, waiting for transfers between devices, body(): lax.psum(partial_out.astype(jnp.bfloat16), 'tensor').astype(jnp.float32)  90.3 us
    slice x1, local copies, waits for them, and re-layouts, body(): path[:, :, :, 1]  24.6 us
    gather x1, local copies, waits for them, and re-layouts, body(): path = received[owner, place].reshape(nodes, span, kv_dev, 2, HD)  21 us
    reshape x1, local copies, waits for them, and re-layouts, body(): path = received[owner, place].reshape(nodes, span, kv_dev, 2, HD)  18.1 us
    dot_general x1, matrix products, body(): partial_out = jnp.dot(attn, w_out, preferred_element_type=jnp.float32)  14.4 us
    dot_general x1, matrix products, body(): jnp.einsum('nktgs,nskd->nktgd', path_weight.astype(jnp.bfloat16), path[:,...  13.1 us
    dot_general x1, matrix products, body(): jnp.einsum('ntkgd,nskd->nktgs', query, path[:, :, :, 0], preferred_elemen...  11.4 us
  transfers between devices with their start and end apart: 3, of which 2 were waited for; matrix products, arithmetic and copies ran while one was open for 4% of the time, Pallas kernels for 0%

commit v1 on v0

v1 whole, which is shorter than its diff:
```python
import functools

import jax
import jax.numpy as jnp
from jax import lax
from jax.experimental import pallas as pl
from jax.experimental.pallas import tpu as pltpu
from jax.sharding import PartitionSpec as P

D = 8192
HD = 128
NEW = 16
PAGE = 64
PATH_PAGES = 16
SHARED = 8
FAM = 4
RANKS = 16
PAIR = 15
ROOTS = 12
LOG2E = 1.4426950408889634
MIB = 1024 * 1024


def pack_kernel(pages_dev, rank_ref, table_ref, pool_ref, send_ref, wanted_ref, wanted_smem, sem, sems):
    base = rank_ref[0] * pages_dev
    table = table_ref[...]
    lane = lax.broadcasted_iota(jnp.int32, (RANKS, 128), 1)
    present = jnp.zeros((RANKS, 128), jnp.float32)
    for page in range(pages_dev):
        hit = jnp.max((table == base + page).astype(jnp.float32), axis=1, keepdims=True)
        present = jnp.where(lane == page, hit, present)
    row = lax.broadcasted_iota(jnp.int32, (128, 128), 0)
    col = lax.broadcasted_iota(jnp.int32, (128, 128), 1)
    before = jnp.dot(
        present.astype(jnp.bfloat16),
        (row < col).astype(jnp.bfloat16),
        preferred_element_type=jnp.float32,
    )
    place = jnp.where(present > 0, before, -1.0)
    wanted = jnp.zeros((RANKS, 128), jnp.float32)
    lane_f = lane.astype(jnp.float32)
    for slot in range(PAIR):
        page = jnp.sum(jnp.where(place == slot, lane_f, 0.0), axis=1, keepdims=True)
        wanted = jnp.where(lane == slot, page, wanted)
    wanted_ref[...] = wanted.astype(jnp.int32)
    copy = pltpu.make_async_copy(wanted_ref, wanted_smem, sem)
    copy.start()
    copy.wait()

    @pl.loop(0, RANKS)
    def _(dest):
        for slot in range(PAIR):
            page = jnp.clip(wanted_smem[dest, slot], 0, pages_dev - 1)
            pltpu.make_async_copy(pool_ref.at[page], send_ref.at[dest, slot], sems).start()

    pltpu.make_async_copy(send_ref, send_ref, sems).wait()


def pack(rank, table, pool):
    pages_dev = pool.shape[0]
    return pl.pallas_call(
        functools.partial(pack_kernel, pages_dev),
        out_shape=jax.ShapeDtypeStruct((RANKS, PAIR) + pool.shape[1:], pool.dtype),
        in_specs=[
            pl.BlockSpec(memory_space=pltpu.SMEM),
            pl.BlockSpec(memory_space=pltpu.VMEM),
            pl.BlockSpec(memory_space=pltpu.VMEM),
        ],
        out_specs=pl.BlockSpec(memory_space=pl.ANY),
        scratch_shapes=[
            pltpu.VMEM((RANKS, 128), jnp.int32),
            pltpu.SMEM((RANKS, 128), jnp.int32),
            pltpu.SemaphoreType.DMA,
            pltpu.SemaphoreType.DMA,
        ],
        name="pack_pages",
    )(rank, table, pool)


def attend_kernel(idx_ref, len_ref, parent_ref, q_ref, fresh_ref, roots_ref, recv_ref, out_ref):
    family = pl.program_id(0)
    scale = HD ** (-0.5) * LOG2E
    nt = (((1,), (1,)), ((), ()))

    def pages(node, first):
        blocks = [recv_ref[idx_ref[node * PATH_PAGES + first + s]] for s in range(SHARED)]
        return jnp.concatenate(blocks, axis=0)

    shared = pages(family * FAM, 0)
    q_nodes = []
    for i in range(FAM):
        rows = q_ref[i * NEW : (i + 1) * NEW, :]
        heads = rows.shape[1] // HD
        q_nodes.append(jnp.concatenate([rows[:, h * HD : (h + 1) * HD] for h in range(heads)], axis=0))
    query = jnp.concatenate(q_nodes, axis=0)
    span = q_nodes[0].shape[0]
    s_shared = lax.dot_general(query, shared[:, :HD], nt, preferred_element_type=jnp.float32)
    top_shared = jnp.max(s_shared, axis=1, keepdims=True)
    tops, totals, accums = [], [], []
    for i in range(FAM):
        node = family * FAM + i
        above = parent_ref[node]
        own = pages(node, SHARED)
        start = pl.multiple_of(jnp.maximum(above, 0) * NEW, NEW)
        near = jnp.concatenate(
            [fresh_ref[i * NEW : (i + 1) * NEW, :], roots_ref[pl.ds(start, NEW), :]], axis=0
        )
        s_own = lax.dot_general(q_nodes[i], own[:, :HD], nt, preferred_element_type=jnp.float32)
        s_near = lax.dot_general(q_nodes[i], near[:, :HD], nt, preferred_element_type=jnp.float32)
        spot = lax.broadcasted_iota(jnp.int32, s_own.shape, 1) + SHARED * PAGE
        s_own = jnp.where(spot < len_ref[node], s_own, -jnp.inf)
        token = lax.broadcasted_iota(jnp.int32, s_near.shape, 0) % NEW
        key = lax.broadcasted_iota(jnp.int32, s_near.shape, 1)
        allowed = (key <= token) | ((key >= NEW) & (above >= 0))
        s_near = jnp.where(allowed, s_near, -jnp.inf)
        top = jnp.maximum(
            jnp.maximum(top_shared[i * span : (i + 1) * span], jnp.max(s_own, axis=1, keepdims=True)),
            jnp.max(s_near, axis=1, keepdims=True),
        )
        w_own = jnp.exp2((s_own - top) * scale)
        w_near = jnp.exp2((s_near - top) * scale)
        totals.append(jnp.sum(w_own, axis=1, keepdims=True) + jnp.sum(w_near, axis=1, keepdims=True))
        accums.append(
            jnp.dot(w_own.astype(jnp.bfloat16), own[:, HD:], preferred_element_type=jnp.float32)
            + jnp.dot(w_near.astype(jnp.bfloat16), near[:, HD:], preferred_element_type=jnp.float32)
        )
        tops.append(top)
    top = jnp.concatenate(tops, axis=0)
    w_shared = jnp.exp2((s_shared - top) * scale)
    total = jnp.concatenate(totals, axis=0) + jnp.sum(w_shared, axis=1, keepdims=True)
    accum = jnp.concatenate(accums, axis=0) + jnp.dot(
        w_shared.astype(jnp.bfloat16), shared[:, HD:], preferred_element_type=jnp.float32
    )
    attn = (accum / total).astype(jnp.bfloat16)
    for i in range(FAM):
        for h in range(span // NEW):
            block = attn[i * span + h * NEW : i * span + (h + 1) * NEW, :]
            out_ref[i * NEW : (i + 1) * NEW, h * HD : (h + 1) * HD] = block


def attend(idx, lengths, above, queries, fresh, roots, received):
    rows, width = queries.shape
    step = FAM * NEW
    pages = received.shape[0]
    return pl.pallas_call(
        attend_kernel,
        out_shape=jax.ShapeDtypeStruct((rows, width), jnp.bfloat16),
        grid_spec=pltpu.PrefetchScalarGridSpec(
            num_scalar_prefetch=3,
            grid=(rows // step,),
            in_specs=[
                pl.BlockSpec((step, width), lambda f, *_: (f, 0)),
                pl.BlockSpec((step, fresh.shape[1]), lambda f, *_: (f, 0)),
                pl.BlockSpec(memory_space=pltpu.VMEM),
                pl.BlockSpec(memory_space=pltpu.VMEM),
            ],
            out_specs=pl.BlockSpec((step, width), lambda f, *_: (f, 0)),
        ),
        compiler_params=pltpu.CompilerParams(vmem_limit_bytes=40 * MIB),
        cost_estimate=pl.CostEstimate(
            flops=4 * rows * width * 1056, bytes_accessed=pages * PAGE * 512 + 4 * rows * width, transcendentals=rows * 8 * 1056
        ),
        name="attend",
    )(idx, lengths, above, queries, fresh, roots, received)


def project_kernel(attn_ref, w_ref, out_ref):
    out_ref[0] = jnp.dot(attn_ref[...], w_ref[...], preferred_element_type=jnp.float32).astype(jnp.bfloat16)


def project(attn, w_out, parts):
    rows, depth = attn.shape
    cols = w_out.shape[1] // parts
    half = cols // 2
    return pl.pallas_call(
        project_kernel,
        out_shape=jax.ShapeDtypeStruct((parts, rows, cols), jnp.bfloat16),
        grid=(parts, 2),
        in_specs=[
            pl.BlockSpec((rows, depth), lambda p, c: (0, 0)),
            pl.BlockSpec((depth, half), lambda p, c: (0, p * 2 + c)),
        ],
        out_specs=pl.BlockSpec((1, rows, half), lambda p, c: (p, 0, c)),
        compiler_params=pltpu.CompilerParams(vmem_limit_bytes=40 * MIB),
        cost_estimate=pl.CostEstimate(
            flops=2 * rows * depth * w_out.shape[1], bytes_accessed=w_out.size * 2 + rows * w_out.shape[1] * 2, transcendentals=0
        ),
        name="project",
    )(attn, w_out)


def share_roots(fresh):
    def along(dy, dx):
        return [(s, (s // 4 + dy) % 4 * 4 + (s % 4 + dx) % 4) for s in range(RANKS)]

    mine = fresh[: ROOTS * NEW]
    row = jnp.concatenate([mine] + [lax.ppermute(mine, "dp", along(0, d)) for d in (1, 2, 3)], axis=0)
    return jnp.concatenate([row] + [lax.ppermute(row, "dp", along(d, 0)) for d in (1, 2, 3)], axis=0)


def slots_of(table, ranks, pages_dev):
    owner = table // pages_dev
    page = jnp.arange(ranks * pages_dev, dtype=jnp.int32)
    present = jnp.any(table[None, :] == page[:, None], axis=1)
    place = jnp.sum(
        (present[None, :] & (page[None, :] // pages_dev == owner[:, None]) & (page[None, :] < table[:, None])).astype(jnp.int32),
        axis=1,
    )
    return owner * PAIR + place


def body(queries, fresh_kv, kv_pool, page_table, path_len, parent, w_out, residual, gain):
    rank = lax.axis_index("dp")
    tensor_rank = lax.axis_index("tensor")
    tensors = lax.axis_size("tensor")
    rows = queries.shape[0]
    nodes = rows // NEW
    pages_dev = kv_pool.shape[0]
    dest_table = page_table.reshape(RANKS, nodes * PATH_PAGES)
    send = pack(rank.reshape(1), dest_table, kv_pool)
    received = lax.all_to_all(send, "dp", split_axis=0, concat_axis=0, tiled=True)
    received = received.reshape(RANKS * PAIR, PAGE, kv_pool.shape[2])
    roots = share_roots(fresh_kv)

    own_table = lax.dynamic_index_in_dim(dest_table, rank, 0, keepdims=False)
    idx = slots_of(own_table, RANKS, pages_dev)
    lengths = lax.dynamic_slice_in_dim(path_len, rank * nodes, nodes)
    above = lax.dynamic_slice_in_dim(parent, rank * nodes, nodes)
    up_rank, up_node = above // nodes, above % nodes
    away_y = (rank // 4 - up_rank // 4) % 4
    away_x = (rank % 4 - up_rank % 4) % 4
    above = jnp.where(above >= 0, (away_y * 4 + away_x) * ROOTS + up_node, -1)

    attn = attend(idx, lengths, above, queries, fresh_kv, roots, received)
    parts = project(attn, w_out, tensors)
    summed = lax.psum_scatter(parts, "tensor", scatter_dimension=0, tiled=True)[0]
    cols = summed.shape[1]
    kept = lax.dynamic_slice_in_dim(residual, tensor_rank * cols, cols, 1)
    mixed = kept.astype(jnp.float32) + summed.astype(jnp.float32)
    power = jnp.sum(mixed * mixed, axis=1).reshape(rows // 128, 128)
    total = power
    for d in range(1, tensors):
        total = total + lax.ppermute(power, "tensor", [(t, (t + d) % tensors) for t in range(tensors)])
    norm = lax.rsqrt(total.reshape(rows, 1) / D + 1e-05)
    own_gain = lax.dynamic_slice_in_dim(gain, tensor_rank * cols, cols)
    normed = mixed * norm * own_gain.astype(jnp.float32)
    return (mixed.astype(jnp.bfloat16), normed.astype(jnp.bfloat16))


def solution(mesh):
    return jax.shard_map(
        body,
        mesh=mesh,
        in_specs=(
            P("dp", "tensor"),
            P("dp", "tensor"),
            P("dp", None, "tensor"),
            P(),
            P(),
            P(),
            P("tensor", None),
            P("dp", None),
            P(),
        ),
        out_specs=(P("dp", "tensor"), P("dp", "tensor")),
        check_vma=False,
    )
```

time: 473 us -> 262 us (0.55)
  waiting for transfers between devices: 271 us -> 172 us
  local copies, waits for them, and re-layouts: 94.1 us -> 5.86 us
  matrix products: 46.1 us -> 0 us
  Pallas kernels: 0 us -> 36.9 us
  other arithmetic: 37.8 us -> 6.48 us
  starting transfers between devices: 7.86 us -> 25.6 us
    all_gather x1 -> x0, waiting for transfers between devices: 180 us -> none  [body(): piece = lax.all_gather(fresh_kv, 'dp', axis=0, tiled=True)]
    ppermute x0 -> x13, waiting for transfers between devices: none -> 127 us  [the longest x3 111 us: share_roots(): lax.ppermute(mine, 'dp', along(0, d))]
    psum x1 -> x0, waiting for transfers between devices: 90.3 us -> none  [body(): lax.psum(partial_out.astype(jnp.bfloat16), 'tensor').astype(jnp.float32)]
    dot_general x7 -> x0, matrix products: 46.1 us -> none  [the longest x1 14.4 us: body(): partial_out = jnp.dot(attn, w_out, preferred_element_type=jnp.float32)]
    reduce_scatter x0 -> x1, waiting for transfers between devices: none -> 44.6 us  [body(): lax.psum_scatter(parts, 'tensor', scatter_dimension=0, tiled=True)[0]]
    pallas_call x0 -> x3, Pallas kernels: none -> 36.9 us  [the longest x1 15.8 us: project(): pl.pallas_call(project_kernel, out_shape=jax.ShapeDtypeStruct((parts, row...]
    gather x3 -> x0, local copies, waits for them, and re-layouts: 34.8 us -> none  [the longest x1 21 us: body(): path = received[owner, place].reshape(nodes, span, kv_dev, 2, HD)]
    reshape x5 -> x1, local copies, waits for them, and re-layouts: 27.8 us -> 0.73 us  [body(): dest_table = page_table.reshape(RANKS, nodes * PATH_PAGES)]
  transfers between devices with their start and end apart: 3 -> 15, of which waited for: 2 -> 9; matrix products, arithmetic and copies ran while one was open for 4% -> 1% of each run, Pallas kernels for 0% -> 0%
where the time goes in v1:
time: 262 us; the launch traced here: 261 us
  waiting for transfers between devices  172 us (66%)
  Pallas kernels  36.9 us (14%)
  starting transfers between devices  25.6 us (10%)
  between operations  14.2 us (5%)
  other arithmetic  6.48 us (2%)
  local copies, waits for them, and re-layouts  5.86 us (2%)
    ppermute x3, waiting for transfers between devices, share_roots(): lax.ppermute(mine, 'dp', along(0, d))  111 us
    reduce_scatter x1, waiting for transfers between devices, body(): lax.psum_scatter(parts, 'tensor', scatter_dimension=0, tiled=True)[0]  44.6 us
    pallas_call x1, Pallas kernels, project(): pl.pallas_call(project_kernel, out_shape=jax.ShapeDtypeStruct((parts, row...  15.8 us
    pallas_call x1, Pallas kernels, attend(): pl.pallas_call(attend_kernel, out_shape=jax.ShapeDtypeStruct((rows, width...  15.5 us
    ppermute x3, waiting for transfers between devices, share_roots(): lax.ppermute(row, 'dp', along(d, 0))  14.2 us
    all_to_all x1, starting transfers between devices, body(): lax.all_to_all(send, 'dp', split_axis=0, concat_axis=0, tiled=True)  7.62 us
    ppermute x7, starting transfers between devices, body(): lax.ppermute(power, 'tensor', [(t, (t + d) % tensors) for t in range(tens...  7.53 us
    ppermute x3, starting transfers between devices, share_roots(): lax.ppermute(row, 'dp', along(d, 0))  5.65 us
  transfers between devices with their start and end apart: 15, of which 9 were waited for; matrix products, arithmetic and copies ran while one was open for 1% of the time, Pallas kernels for 0%

profile of v1, /device:TPU:2, one launch (start us, length us, event | category | flops | bytes accessed | tf_op | source)
XLA Modules:
  0.0 260.9 jit_solution(7140933169342309308)
XLA Ops:
  7.2 0.9 copy.13
  8.0 0.7 reshape.80.table_ref
  8.8 5.6 %pack_pages.1 = bf16[16,15,64,256]{3,2,1,0:T(8,128)(2,1)} custom-call(s32[1]{0:T(128)} %bitcast.rank_ref, s32[16,384]{1,0:T(8,128)} %reshape.80.table_ref, bf16[45,64,256]{2,1,0:T(8,128)(2,1)} %pool_ref.1), custom_call_target="tpu_custom_call" | custom-call | tf_op jit(solution)/shard_map/pack_pages/pallas_call | solution.py:61
  14.4 0.0 copy-start.2
  14.4 7.6 %all-to-all-start = ((bf16[16,15,64,256]{3,2,1,0:T(8,128)(2,1)}), bf16[16,15,64,256]{3,2,1,0:T(8,128)(2,1)}, u32[]{:S(2)}, u32[]{:S(2)}) async-start(bf16[16,15,64,256]{3,2,1,0:T(8,128)(2,1)} %pack_pages.1), calls=%async_computation | async-start | bytes 15728640 | tf_op jit(solution)/shard_map/all_to_all | solution.py:221
  22.0 0.0 reduce-scatter.2.cloned.1.call-start
  22.1 0.0 copy-done.2
  22.1 1.5 collective-permute-start
  23.6 0.8 collective-permute-start.1
  24.4 2.5 collective-permute-start.2
  26.9 0.7 dynamic-slice_reduce_fusion
  27.6 0.2 fusion.1
  27.8 0.3 convert_reduce_fusion
  28.2 102.4 %collective-permute-done = bf16[192,256]{1,0:T(8,128)(2,1)S(1)} collective-permute-done((bf16[192,256]{1,0:T(8,128)(2,1)S(1)}, bf16[192,256]{1,0:T(8,128)(2,1)S(1)}, u32[]{:S(2)}, u32[]{:S(2)}) %collective-permute-start) | collective-permute-done | bytes 98336 | tf_op jit(solution)/shard_map/ppermute | solution.py:197
  130.6 7.6 %collective-permute-done.1 = bf16[192,256]{1,0:T(8,128)(2,1)S(1)} collective-permute-done((bf16[192,256]{1,0:T(8,128)(2,1)S(1)}, bf16[192,256]{1,0:T(8,128)(2,1)S(1)}, u32[]{:S(2)}, u32[]{:S(2)}) %collective-permute-start.1) | collective-permute-done | bytes 98336 | tf_op jit(solution)/shard_map/ppermute | solution.py:197
  138.2 1.1 collective-permute-done.2
  139.3 0.0 copy-start.1
  139.3 0.1 collective-permute-start.3
  139.4 0.8 compare_select_fusion.4.parent_ref
  140.2 0.8 dynamic_slice.18.len_ref
  141.0 3.0 %collective-permute-start.4 = (bf16[768,256]{1,0:T(8,128)(2,1)S(1)}, bf16[768,256]{1,0:T(8,128)(2,1)S(1)}, u32[]{:S(2)}, u32[]{:S(2)}) collective-permute-start(bf16[768,256]{1,0:T(8,128)(2,1)S(1)} %pad_maximum_fusion), channel_id=1, source_target_pairs={{0,64},{8,72},{16,80},{24,88},{32,96},{40,104},{48,112},{56,120},{... | collective-permute-start | bytes 1179656 | tf_op jit(solution)/shard_map/ppermute | solution.py:198
  144.0 2.6 collective-permute-start.5
  146.6 5.7 %collective-permute-done.3 = bf16[768,256]{1,0:T(8,128)(2,1)S(1)} collective-permute-done((bf16[768,256]{1,0:T(8,128)(2,1)S(1)}, bf16[768,256]{1,0:T(8,128)(2,1)S(1)}, u32[]{:S(2)}, u32[]{:S(2)}) %collective-permute-start.3) | collective-permute-done | bytes 393248 | tf_op jit(solution)/shard_map/ppermute | solution.py:198
  152.3 6.5 %collective-permute-done.4 = bf16[768,256]{1,0:T(8,128)(2,1)S(1)} collective-permute-done((bf16[768,256]{1,0:T(8,128)(2,1)S(1)}, bf16[768,256]{1,0:T(8,128)(2,1)S(1)}, u32[]{:S(2)}, u32[]{:S(2)}) %collective-permute-start.4) | collective-permute-done | bytes 393248 | tf_op jit(solution)/shard_map/ppermute | solution.py:198
  158.8 2.1 collective-permute-done.5
  160.9 0.0 all-to-all-done
  160.9 15.5 %attend.1.attn_ref = bf16[384,1024]{1,0:T(8,128)(2,1)S(1)} custom-call(s32[384]{0:T(512)S(1)} %multiply_add_fusion.idx_ref, s32[24]{0:T(128)S(1)} %dynamic_slice.18.len_ref, s32[24]{0:T(128)S(1)} %compare_select_fusion.4.parent_ref, bf16[384,1024]{1,0:T(8,128)(2,1)S(1)} %copy-done.1, bf16[384,256]{1,0:T(8,128)(2,1)S(1)} %copy-done.2, ...), custom_call_target="tpu_custom_call" | custom-call | flops 1660944384 | bytes 9437184 | tf_op jit(solution)/shard_map/attend/pallas_call | solution.py:145
  176.4 15.8 %project.1 = bf16[8,384,1024]{2,1,0:T(8,128)(2,1)S(1)} custom-call(bf16[384,1024]{1,0:T(8,128)(2,1)S(1)} %attend.1.attn_ref, bf16[1024,8192]{1,0:T(8,128)(2,1)} %w_ref.1), custom_call_target="tpu_custom_call" | custom-call | flops 6442450944 | bytes 23068672 | tf_op jit(solution)/shard_map/project/pallas_call | solution.py:175
  192.2 2.7 %copy-done = bf16[8,384,1024]{2,1,0:T(8,128)(2,1)} copy-done((bf16[8,384,1024]{2,1,0:T(8,128)(2,1)}, bf16[8,384,1024]{2,1,0:T(8,128)(2,1)S(1)}, u32[]{:S(2)}) %copy-start) | copy-done | bytes 6291480
  194.9 0.0 reduce-scatter.2.cloned.1.call-update
  194.9 44.6 %reduce-scatter.2.cloned.1.call-done = bf16[1,384,1024]{2,1,0:T(8,128)(2,1)} async-done(((bf16[8,384,1024]{2,1,0:T(8,128)(2,1)}), bf16[1,384,1024]{2,1,0:T(8,128)(2,1)}) %reduce-scatter.2.cloned.1.call-update) | async-done | bytes 786448 | tf_op jit(solution)/shard_map/reduce_scatter | solution.py:236
  239.5 1.8 multiply_reduce_fusion
  241.3 1.4 collective-permute-start.10
  242.7 1.4 collective-permute-start.11
  244.0 0.0 collective-permute-start.12
  244.0 0.5 collective-permute-start.6
  244.6 0.6 collective-permute-start.7
  245.2 0.0 collective-permute-done.10
  245.2 1.1 collective-permute-start.8
  246.3 0.0 collective-permute-done.11
  246.3 2.5 collective-permute-start.9
  248.8 0.7 dynamic-slice_convert_fusion
  249.5 0.0 collective-permute-done.12
  249.5 0.0 collective-permute-done.6
  249.5 0.0 collective-permute-done.7
  249.5 0.2 collective-permute-done.8
  249.7 1.7 collective-permute-done.9
  251.4 2.6 multiply_convert_fusion
  (16 shorter events, 0.2 us)
Async XLA Ops:
  14.4 7.7 %copy-start.2 = (bf16[384,256]{1,0:T(8,128)(2,1)S(1)}, bf16[384,256]{1,0:T(8,128)(2,1)}, u32[]{:S(2)}) copy-start(bf16[384,256]{1,0:T(8,128)(2,1)} %fresh_ref.1) | copy-start | bytes 589828
  14.4 146.5 %all-to-all-start = ((bf16[16,15,64,256]{3,2,1,0:T(8,128)(2,1)}), bf16[16,15,64,256]{3,2,1,0:T(8,128)(2,1)}, u32[]{:S(2)}, u32[]{:S(2)}) async-start(bf16[16,15,64,256]{3,2,1,0:T(8,128)(2,1)} %pack_pages.1), calls=%async_computation | async-start | bytes 15728640 | tf_op jit(solution)/shard_map/all_to_all | solution.py:221
  22.0 217.5 %reduce-scatter.2.cloned.1.call-start = ((), (), s32[]{:S(2)}) async-start(), calls=%async_computation.2 | async-start | bytes 7077888 | tf_op jit(solution)/shard_map/reduce_scatter | solution.py:236
  22.1 108.5 %collective-permute-start = (bf16[192,256]{1,0:T(8,128)(2,1)S(1)}, bf16[192,256]{1,0:T(8,128)(2,1)S(1)}, u32[]{:S(2)}, u32[]{:S(2)}) collective-permute-start(bf16[192,256]{1,0:T(8,128)(2,1)S(1)} %get-tuple-element.4), channel_id=1, source_target_pairs={{0,8},{8,16},{16,24},{24,0},{32,40},{40,48},{48,56},{56,32},{64,72... | collective-permute-start | bytes 294920 | tf_op jit(solution)/shard_map/ppermute | solution.py:197
  23.6 114.6 %collective-permute-start.1 = (bf16[192,256]{1,0:T(8,128)(2,1)S(1)}, bf16[192,256]{1,0:T(8,128)(2,1)S(1)}, u32[]{:S(2)}, u32[]{:S(2)}) collective-permute-start(bf16[192,256]{1,0:T(8,128)(2,1)S(1)} %get-tuple-element.4), channel_id=1, source_target_pairs={{0,16},{8,24},{16,0},{24,8},{32,48},{40,56},{48,32},{56,40},{64,80... | collective-permute-start | bytes 294920 | tf_op jit(solution)/shard_map/ppermute | solution.py:197
  24.4 114.9 %collective-permute-start.2 = (bf16[192,256]{1,0:T(8,128)(2,1)S(1)}, bf16[192,256]{1,0:T(8,128)(2,1)S(1)}, u32[]{:S(2)}, u32[]{:S(2)}) collective-permute-start(bf16[192,256]{1,0:T(8,128)(2,1)S(1)} %get-tuple-element.4), channel_id=1, source_target_pairs={{0,24},{8,0},{16,8},{24,16},{32,56},{40,32},{48,40},{56,48},{64,88... | collective-permute-start | bytes 294920 | tf_op jit(solution)/shard_map/ppermute | solution.py:197
  139.3 21.6 %copy-start.1 = (bf16[384,1024]{1,0:T(8,128)(2,1)S(1)}, bf16[384,1024]{1,0:T(8,128)(2,1)}, u32[]{:S(2)}) copy-start(bf16[384,1024]{1,0:T(8,128)(2,1)} %q_ref.1) | copy-start | bytes 2359300
  139.3 13.0 %collective-permute-start.3 = (bf16[768,256]{1,0:T(8,128)(2,1)S(1)}, bf16[768,256]{1,0:T(8,128)(2,1)S(1)}, u32[]{:S(2)}, u32[]{:S(2)}) collective-permute-start(bf16[768,256]{1,0:T(8,128)(2,1)S(1)} %pad_maximum_fusion), channel_id=1, source_target_pairs={{0,32},{8,40},{16,48},{24,56},{32,64},{40,72},{48,80},{56,88},{64,... | collective-permute-start | bytes 1179656 | tf_op jit(solution)/shard_map/ppermute | solution.py:198
  141.0 17.8 %collective-permute-start.4 = (bf16[768,256]{1,0:T(8,128)(2,1)S(1)}, bf16[768,256]{1,0:T(8,128)(2,1)S(1)}, u32[]{:S(2)}, u32[]{:S(2)}) collective-permute-start(bf16[768,256]{1,0:T(8,128)(2,1)S(1)} %pad_maximum_fusion), channel_id=1, source_target_pairs={{0,64},{8,72},{16,80},{24,88},{32,96},{40,104},{48,112},{56,120},{... | collective-permute-start | bytes 1179656 | tf_op jit(solution)/shard_map/ppermute | solution.py:198
  144.0 16.9 %collective-permute-start.5 = (bf16[768,256]{1,0:T(8,128)(2,1)S(1)}, bf16[768,256]{1,0:T(8,128)(2,1)S(1)}, u32[]{:S(2)}, u32[]{:S(2)}) collective-permute-start(bf16[768,256]{1,0:T(8,128)(2,1)S(1)} %pad_maximum_fusion), channel_id=1, source_target_pairs={{0,96},{8,104},{16,112},{24,120},{32,0},{40,8},{48,16},{56,24},{64... | collective-permute-start | bytes 1179656 | tf_op jit(solution)/shard_map/ppermute | solution.py:198
  192.2 2.7 %copy-start = (bf16[8,384,1024]{2,1,0:T(8,128)(2,1)}, bf16[8,384,1024]{2,1,0:T(8,128)(2,1)S(1)}, u32[]{:S(2)}) copy-start(bf16[8,384,1024]{2,1,0:T(8,128)(2,1)S(1)} %project.1) | copy-start | bytes 18874372
  239.5 11.9 %copy-start.3 = (bf16[1,384,1024]{2,1,0:T(8,128)(2,1)S(1)}, bf16[1,384,1024]{2,1,0:T(8,128)(2,1)}, u32[]{:S(2)}) copy-start(bf16[1,384,1024]{2,1,0:T(8,128)(2,1)} %reduce-scatter.2.cloned.1.call-done) | copy-start | bytes 2359300
  241.3 3.9 %collective-permute-start.10 = (f32[3,128]{1,0:T(4,128)S(1)}, f32[3,128]{1,0:T(4,128)S(1)}, u32[]{:S(2)}, u32[]{:S(2)}) collective-permute-start(f32[3,128]{1,0:T(4,128)S(1)} %bitcast.11), channel_id=1, source_target_pairs={{0,5},{1,6},{2,7},{3,0},{4,1},{5,2},{6,3},{7,4},{8,13},{9,14},{10,... | collective-permute-start | bytes 4616 | tf_op jit(solution)/shard_map/ppermute | solution.py:243
  242.7 3.7 %collective-permute-start.11 = (f32[3,128]{1,0:T(4,128)S(1)}, f32[3,128]{1,0:T(4,128)S(1)}, u32[]{:S(2)}, u32[]{:S(2)}) collective-permute-start(f32[3,128]{1,0:T(4,128)S(1)} %bitcast.12), channel_id=1, source_target_pairs={{0,6},{1,7},{2,0},{3,1},{4,2},{5,3},{6,4},{7,5},{8,14},{9,15},{10,... | collective-permute-start | bytes 4616 | tf_op jit(solution)/shard_map/ppermute | solution.py:243
  244.0 5.5 %collective-permute-start.12 = (f32[3,128]{1,0:T(4,128)S(1)}, f32[3,128]{1,0:T(4,128)S(1)}, u32[]{:S(2)}, u32[]{:S(2)}) collective-permute-start(f32[3,128]{1,0:T(4,128)S(1)} %bitcast.13), channel_id=1, source_target_pairs={{0,7},{1,0},{2,1},{3,2},{4,3},{5,4},{6,5},{7,6},{8,15},{9,8},{10,9... | collective-permute-start | bytes 4616 | tf_op jit(solution)/shard_map/ppermute | solution.py:243
  244.0 5.5 %collective-permute-start.6 = (f32[3,128]{1,0:T(4,128)S(1)}, f32[3,128]{1,0:T(4,128)S(1)}, u32[]{:S(2)}, u32[]{:S(2)}) collective-permute-start(f32[3,128]{1,0:T(4,128)S(1)} %bitcast.14), channel_id=1, source_target_pairs={{0,1},{1,2},{2,3},{3,4},{4,5},{5,6},{6,7},{7,0},{8,9},{9,10},{10,1... | collective-permute-start | bytes 4616 | tf_op jit(solution)/shard_map/ppermute | solution.py:243
  244.6 5.0 %collective-permute-start.7 = (f32[3,128]{1,0:T(4,128)S(1)}, f32[3,128]{1,0:T(4,128)S(1)}, u32[]{:S(2)}, u32[]{:S(2)}) collective-permute-start(f32[3,128]{1,0:T(4,128)S(1)} %bitcast.15), channel_id=1, source_target_pairs={{0,2},{1,3},{2,4},{3,5},{4,6},{5,7},{6,0},{7,1},{8,10},{9,11},{10,... | collective-permute-start | bytes 4616 | tf_op jit(solution)/shard_map/ppermute | solution.py:243
  245.2 4.5 %collective-permute-start.8 = (f32[3,128]{1,0:T(4,128)S(1)}, f32[3,128]{1,0:T(4,128)S(1)}, u32[]{:S(2)}, u32[]{:S(2)}) collective-permute-start(f32[3,128]{1,0:T(4,128)S(1)} %bitcast.16), channel_id=1, source_target_pairs={{0,3},{1,4},{2,5},{3,6},{4,7},{5,0},{6,1},{7,2},{8,11},{9,12},{10,... | collective-permute-start | bytes 4616 | tf_op jit(solution)/shard_map/ppermute | solution.py:243
  246.3 5.1 %collective-permute-start.9 = (f32[3,128]{1,0:T(4,128)S(1)}, f32[3,128]{1,0:T(4,128)S(1)}, u32[]{:S(2)}, u32[]{:S(2)}) collective-permute-start(f32[3,128]{1,0:T(4,128)S(1)} %bitcast.17), channel_id=1, source_target_pairs={{0,4},{1,5},{2,6},{3,7},{4,0},{5,1},{6,2},{7,3},{8,12},{9,13},{10,... | collective-permute-start | bytes 4616 | tf_op jit(solution)/shard_map/ppermute | solution.py:243
Sparse Core Ops, SparseCore 0:
  195.0 44.4 reduce-scatter.1

commit v2 on v1

v2 whole, which is shorter than its diff:
```python
import functools

import jax
import jax.numpy as jnp
from jax import lax
from jax.experimental import pallas as pl
from jax.experimental.pallas import tpu as pltpu
from jax.sharding import PartitionSpec as P

D = 8192
HD = 128
NEW = 16
PAGE = 64
PATH_PAGES = 16
SHARED = 8
FAM = 4
RANKS = 16
PAIR = 15
ROOTS = 12
FIRST = 3
LOG2E = 1.4426950408889634
MIB = 1024 * 1024


def pack_kernel(rank_ref, table_ref, pool_ref, send_ref, wanted_ref, wanted_smem, sem, send_sem):
    pages_dev = pool_ref.shape[0]
    slots, nodes = table_ref.shape
    base = rank_ref[0] * pages_dev
    table = table_ref[...]
    height = -(-pages_dev // 16) * 16
    row = lax.broadcasted_iota(jnp.int32, (height, nodes), 0)
    hits = jnp.zeros((height, nodes), jnp.float32)
    for page in range(pages_dev):
        hit = jnp.max((table == base + page).astype(jnp.float32), axis=0, keepdims=True)
        hits = jnp.where(row == page, hit, hits)
    node = lax.broadcasted_iota(jnp.int32, (nodes, 128), 0)
    begin = lax.broadcasted_iota(jnp.int32, (nodes, 128), 1) * (nodes // RANKS)
    belongs = ((node >= begin) & (node < begin + nodes // RANKS)).astype(jnp.bfloat16)
    present = jnp.dot(hits.astype(jnp.bfloat16), belongs, preferred_element_type=jnp.float32) > 0
    low = lax.broadcasted_iota(jnp.int32, (height, height), 0)
    high = lax.broadcasted_iota(jnp.int32, (height, height), 1)
    before = jnp.dot(
        (high < low).astype(jnp.bfloat16), present.astype(jnp.bfloat16), preferred_element_type=jnp.float32
    )
    place = jnp.where(present, before, -1.0)
    page_id = lax.broadcasted_iota(jnp.int32, (height, 128), 0).astype(jnp.float32)
    line = lax.broadcasted_iota(jnp.int32, (16, 128), 0)
    wanted = jnp.zeros((16, 128), jnp.float32)
    for slot in range(PAIR):
        page = jnp.sum(jnp.where(place == slot, page_id, 0.0), axis=0, keepdims=True)
        wanted = jnp.where(line == slot, page, wanted)
    wanted_ref[...] = wanted.astype(jnp.int32)
    copy = pltpu.make_async_copy(wanted_ref, wanted_smem, sem)
    copy.start()
    copy.wait()

    @pl.loop(0, RANKS)
    def _(dest):
        for slot in range(PAIR):
            page = jnp.clip(wanted_smem[slot, dest], 0, pages_dev - 1)
            pltpu.make_async_copy(pool_ref.at[page], send_ref.at[dest, slot], send_sem).start()

    pltpu.make_async_copy(send_ref, send_ref, send_sem).wait()


def pack(rank, table, pool):
    return pl.pallas_call(
        pack_kernel,
        out_shape=jax.ShapeDtypeStruct((RANKS, PAIR) + pool.shape[1:], pool.dtype),
        in_specs=[
            pl.BlockSpec(memory_space=pltpu.SMEM),
            pl.BlockSpec(memory_space=pltpu.VMEM),
            pl.BlockSpec(memory_space=pltpu.VMEM),
        ],
        out_specs=pl.BlockSpec(memory_space=pltpu.HBM),
        scratch_shapes=[
            pltpu.VMEM((16, 128), jnp.int32),
            pltpu.SMEM((16, 128), jnp.int32),
            pltpu.SemaphoreType.DMA,
            pltpu.SemaphoreType.DMA,
        ],
        name="pack_pages",
    )(rank, table, pool)


def attend_family(first, node, idx_ref, len_ref, above_ref, q_ref, fresh_ref, roots_ref, pages_ref, attn_ref):
    scale = HD ** (-0.5) * LOG2E
    nt = (((1,), (1,)), ((), ()))

    def pages(n, slot):
        return jnp.concatenate([pages_ref[idx_ref[n * PATH_PAGES + slot + s]] for s in range(SHARED)], axis=0)

    heads = q_ref.shape[1] // HD
    span = heads * NEW
    shared = pages(node, 0)
    queries = []
    for i in range(FAM):
        rows = q_ref[first + i * NEW : first + (i + 1) * NEW, :]
        queries.append(jnp.concatenate([rows[:, h * HD : (h + 1) * HD] for h in range(heads)], axis=0))
    s_shared = lax.dot_general(
        jnp.concatenate(queries, axis=0), shared[:, :HD], nt, preferred_element_type=jnp.float32
    )
    half = SHARED * PAGE // 2
    own, s_own = [], []
    for i in range(FAM):
        above = above_ref[node + i]
        start = pl.multiple_of(jnp.maximum(above, 0) * NEW, NEW)
        fresh = fresh_ref[first + i * NEW : first + (i + 1) * NEW, :]
        kv = jnp.concatenate([pages(node + i, SHARED), fresh, roots_ref[pl.ds(start, NEW), :]], axis=0)
        s = lax.dot_general(queries[i], kv[:, :HD], nt, preferred_element_type=jnp.float32)
        late = s[:, half:]
        spot = lax.broadcasted_iota(jnp.int32, late.shape, 1) + SHARED * PAGE + half
        token = lax.broadcasted_iota(jnp.int32, late.shape, 0) % NEW
        key = spot - PATH_PAGES * PAGE
        limit = jnp.where(above >= 0, 2 * NEW, NEW)
        allowed = (spot < len_ref[node + i]) | ((key >= 0) & (key <= token)) | ((key >= NEW) & (key < limit))
        own.append(kv)
        s_own.append(jnp.concatenate([s[:, :half], jnp.where(allowed, late, -jnp.inf)], axis=1))
    tops = [
        jnp.maximum(
            jnp.max(s_shared[i * span : (i + 1) * span], axis=1, keepdims=True),
            jnp.max(s_own[i], axis=1, keepdims=True),
        )
        for i in range(FAM)
    ]
    w_own = [jnp.exp2((s_own[i] - tops[i]) * scale).astype(jnp.bfloat16) for i in range(FAM)]
    w_shared = jnp.exp2((s_shared - jnp.concatenate(tops, axis=0)) * scale).astype(jnp.bfloat16)
    ones = jnp.ones((own[0].shape[0], HD), jnp.bfloat16)
    accum = [
        jnp.dot(w_own[i], jnp.concatenate([own[i][:, HD:], ones], axis=1), preferred_element_type=jnp.float32)
        for i in range(FAM)
    ]
    accum = jnp.concatenate(accum, axis=0) + jnp.dot(
        w_shared, jnp.concatenate([shared[:, HD:], ones[: SHARED * PAGE]], axis=1), preferred_element_type=jnp.float32
    )
    attn = (accum[:, :HD] / accum[:, HD:]).astype(jnp.bfloat16)
    for i in range(FAM):
        for h in range(heads):
            block = attn[i * span + h * NEW : i * span + (h + 1) * NEW, :]
            attn_ref[first + i * NEW : first + (i + 1) * NEW, h * HD : (h + 1) * HD] = block


def rollout_kernel(
    node0, families, counts, idx_ref, len_ref, above_ref, order_ref, q_ref, fresh_ref, roots_ref, pages_ref, w_ref, *refs
):
    outs, (attn_ref, stage, out_sem) = refs[: len(counts)], refs[len(counts) :]
    blocks, _, cols = stage.shape
    for f in range(families):
        attend_family(
            f * FAM * NEW, node0 + f * FAM, idx_ref, len_ref, above_ref, q_ref, fresh_ref, roots_ref, pages_ref, attn_ref
        )
    base = 0
    for out, count in zip(outs, counts):

        @pl.loop(0, count)
        def _(b):
            slot = base + b
            start = pl.multiple_of(order_ref[slot] * cols, cols)
            w = w_ref[:, pl.ds(start, cols)]
            stage[slot] = jnp.dot(attn_ref[...], w, preferred_element_type=jnp.float32).astype(jnp.bfloat16)
            pltpu.make_async_copy(stage.at[slot], out.at[b], out_sem).start()

        base += count
    base = 0
    for out, count in zip(outs, counts):
        pltpu.make_async_copy(stage.at[pl.ds(base, count)], out, out_sem).wait()
        base += count


def rollout(node0, families, counts, idx, lengths, above, order, queries, fresh, roots, received, w_out):
    width = queries.shape[1]
    rows = families * FAM * NEW
    first = node0 * NEW
    blocks = sum(counts)
    cols = w_out.shape[1] // blocks
    smem = pl.BlockSpec(memory_space=pltpu.SMEM)
    vmem = pl.BlockSpec(memory_space=pltpu.VMEM)
    hbm = pl.BlockSpec(memory_space=pltpu.HBM)
    return pl.pallas_call(
        functools.partial(rollout_kernel, node0, families, counts),
        out_shape=[jax.ShapeDtypeStruct((count, rows, cols), jnp.bfloat16) for count in counts],
        in_specs=[smem, smem, smem, smem, vmem, vmem, vmem, vmem, vmem],
        out_specs=[hbm] * len(counts),
        scratch_shapes=[
            pltpu.VMEM((rows, width), jnp.bfloat16),
            pltpu.VMEM((blocks, rows, cols), jnp.bfloat16),
            pltpu.SemaphoreType.DMA,
        ],
        compiler_params=pltpu.CompilerParams(vmem_limit_bytes=24 * MIB),
        cost_estimate=pl.CostEstimate(
            flops=4 * rows * width * 1056 + 2 * rows * width * w_out.shape[1],
            bytes_accessed=received.size * 2 + w_out.size * 2 + rows * w_out.shape[1] * 2,
            transcendentals=rows * 8 * 1056,
        ),
        name="rollout",
    )(idx, lengths, above, order, queries[first : first + rows], fresh[first : first + rows], roots, received, w_out)


def shift(dy, dx):
    return [(s, (s // 4 + dy) % 4 * 4 + (s % 4 + dx) % 4) for s in range(RANKS)]


def turn(d):
    return [(t, (t + 2 * d) % 8) for t in range(8)]


def gather_row(fresh):
    mine = fresh[: ROOTS * NEW]
    return jnp.concatenate([mine] + [lax.ppermute(mine, "dp", shift(0, d)) for d in (1, 2, 3)], axis=0)


def deliver_parents(row, rank, parent, nodes):
    y, x = rank // 4, rank % 4
    column = lax.dynamic_index_in_dim(parent.reshape(4, 4, nodes), x, 1, keepdims=False)
    column = lax.dynamic_slice_in_dim(jnp.concatenate([column, column], axis=0), y, 4)
    named = jnp.maximum(column[:, ROOTS:], 0)
    away = (x - named // nodes % 4) % 4
    places = jnp.clip(away * ROOTS + named % nodes, 0, 4 * ROOTS - 1).reshape(-1)
    picked = jnp.take(row.reshape(4 * ROOTS, NEW, row.shape[1]), places, axis=0, mode="clip")
    picked = picked.reshape(4, (nodes - ROOTS) * NEW, row.shape[1])
    got = [picked[0]] + [lax.ppermute(picked[d], "dp", shift(d, 0)) for d in (1, 2, 3)]
    own = column[0]
    child = jnp.arange(nodes, dtype=jnp.int32) - ROOTS
    up = (y - jnp.maximum(own, 0) // nodes // 4) % 4 * (nodes - ROOTS) + child
    return jnp.concatenate(got, axis=0), jnp.where((own >= 0) & (child >= 0), up, -1)


def slots_of(table, ranks, pages_dev):
    owner = table // pages_dev
    page = jnp.arange(ranks * pages_dev, dtype=jnp.int32)
    present = jnp.any(table[None, :] == page[:, None], axis=1)
    place = jnp.sum(
        (present[None, :] & (page[None, :] // pages_dev == owner[:, None]) & (page[None, :] < table[:, None])).astype(jnp.int32),
        axis=1,
    )
    return owner * PAIR + place


def body(queries, fresh_kv, kv_pool, page_table, path_len, parent, w_out, residual, gain):
    rank = lax.axis_index("dp")
    tensor_rank = lax.axis_index("tensor")
    tensors = lax.axis_size("tensor")
    rows = queries.shape[0]
    nodes = rows // NEW
    pages_dev = kv_pool.shape[0]
    row = gather_row(fresh_kv)
    send = pack(rank.reshape(1), page_table.T, kv_pool)
    send, row, page_table, path_len, parent = lax.optimization_barrier((send, row, page_table, path_len, parent))
    received = lax.all_to_all(send, "dp", split_axis=0, concat_axis=0, tiled=True)
    received = received.reshape(RANKS * PAIR, PAGE, kv_pool.shape[2])
    roots, above = deliver_parents(row, rank, parent, nodes)

    own_table = lax.dynamic_slice_in_dim(page_table, rank * nodes, nodes).reshape(-1)
    idx = slots_of(own_table, RANKS, pages_dev)
    lengths = lax.dynamic_slice_in_dim(path_len, rank * nodes, nodes)

    z, core = tensor_rank // 2, tensor_rank % 2
    around = (z + jnp.arange(4, dtype=jnp.int32)) % 4 * 2
    order = jnp.concatenate([around + 1 - core, around + core])
    plain = jnp.arange(tensors, dtype=jnp.int32)
    args = (queries, fresh_kv, roots, received, w_out)
    early = FIRST * FAM
    (parts,) = rollout(0, FIRST, (tensors,), idx, lengths, above, plain, *args)
    parts, order = lax.optimization_barrier((parts, order))
    summed_a = lax.psum_scatter(parts, "tensor", scatter_dimension=0, tiled=True)[0].astype(jnp.float32)

    away, kept = rollout(early, nodes // FAM - FIRST, (4, 4), idx, lengths, above, order, *args)
    back = lax.ppermute(away, "tensor", [(t, t ^ 1) for t in range(tensors)])

    def pair(i):
        return kept[i].astype(jnp.float32) + back[i].astype(jnp.float32)

    half = kept.shape[1] // 2
    far = pair(2).astype(jnp.bfloat16)
    from_low = lax.ppermute(far[:half], "tensor", turn(1)).astype(jnp.float32)
    from_high = lax.ppermute(far[half:], "tensor", turn(-1)).astype(jnp.float32)
    up, down = pair(1), pair(3)
    up = jnp.concatenate([up[:half] + from_low, up[half:]], axis=0).astype(jnp.bfloat16)
    down = jnp.concatenate([down[:half], down[half:] + from_high], axis=0).astype(jnp.bfloat16)
    summed_b = (
        pair(0)
        + lax.ppermute(up, "tensor", turn(1)).astype(jnp.float32)
        + lax.ppermute(down, "tensor", turn(-1)).astype(jnp.float32)
    )

    cols = summed_a.shape[1]
    mine = lax.dynamic_slice_in_dim(residual, tensor_rank * cols, cols, 1)
    mixed = mine.astype(jnp.float32) + jnp.concatenate([summed_a, summed_b], axis=0)
    power = jnp.sum(mixed * mixed, axis=1).reshape(rows // 128, 128)
    power = power + lax.ppermute(power, "tensor", [(t, t ^ 1) for t in range(tensors)])
    total = power
    for d in (1, 2, 3):
        total = total + lax.ppermute(power, "tensor", turn(d))
    norm = lax.rsqrt(total.reshape(rows, 1) / D + 1e-05)
    own_gain = lax.dynamic_slice_in_dim(gain, tensor_rank * cols, cols)
    normed = mixed * norm * own_gain.astype(jnp.float32)
    return (mixed.astype(jnp.bfloat16), normed.astype(jnp.bfloat16))


def solution(mesh):
    return jax.shard_map(
        body,
        mesh=mesh,
        in_specs=(
            P("dp", "tensor"),
            P("dp", "tensor"),
            P("dp", None, "tensor"),
            P(),
            P(),
            P(),
            P("tensor", None),
            P("dp", None),
            P(),
        ),
        out_specs=(P("dp", "tensor"), P("dp", "tensor")),
        check_vma=False,
    )
```

time: 262 us -> 228 us (0.87); the launches traced: 261 us -> 224 us
  waiting for transfers between devices: 172 us -> 126 us
  local copies, waits for them, and re-layouts: 5.86 us -> 16.3 us
  Pallas kernels: 36.9 us -> 30.3 us
  starting transfers between devices: 25.6 us -> 28.6 us
    reduce_scatter x1, waiting for transfers between devices: 44.6 us -> 0.02 us  [body(): lax.psum_scatter(parts, 'tensor', scatter_dimension=0, tiled=True)[0]]
    ppermute x13 -> x15, waiting for transfers between devices: 127 us -> 108 us  [the longest x3 83.4 us: deliver_parents(): lax.ppermute(picked[d], 'dp', shift(d, 0))]
    all_to_all x1, waiting for transfers between devices: 0.01 us -> 18.3 us  [body(): lax.all_to_all(send, 'dp', split_axis=0, concat_axis=0, tiled=True)]
    unnamed x14 -> x10, local copies, waits for them, and re-layouts: 3.61 us -> 12.7 us
    pallas_call x3, Pallas kernels: 36.9 us -> 30.3 us  [the longest x2 24.5 us: rollout(): pl.pallas_call(functools.partial(rollout_kernel, node0, families, counts)...]
    ppermute x13 -> x15, starting transfers between devices: 17.9 us -> 22.4 us  [the longest x3 5.67 us: deliver_parents(): lax.ppermute(picked[d], 'dp', shift(d, 0))]
  transfers between devices with their start and end apart: 15 -> 17, of which waited for: 9 -> 11; matrix products, arithmetic and copies ran while one was open for 1% -> 3% of each run, Pallas kernels for 0% -> 8%
where the time goes in v2:
time: 228 us; the launch traced here: 224 us
  waiting for transfers between devices  126 us (55%)
  Pallas kernels  30.3 us (13%)
  starting transfers between devices  28.6 us (13%)
  local copies, waits for them, and re-layouts  16.3 us (7%)
  between operations  14.3 us (6%)
  other arithmetic  8.44 us (4%)
    ppermute x3, waiting for transfers between devices, deliver_parents(): lax.ppermute(picked[d], 'dp', shift(d, 0))  83.4 us
    pallas_call x2, Pallas kernels, rollout(): pl.pallas_call(functools.partial(rollout_kernel, node0, families, counts)...  24.5 us
    all_to_all x1, waiting for transfers between devices, body(): lax.all_to_all(send, 'dp', split_axis=0, concat_axis=0, tiled=True)  18.3 us
    unnamed x10, local copies, waits for them, and re-layouts  12.7 us
    ppermute x1, waiting for transfers between devices, body(): lax.ppermute(up, 'tensor', turn(1)).astype(jnp.float32)  10.2 us
    ppermute x1, waiting for transfers between devices, body(): from_low = lax.ppermute(far[:half], 'tensor', turn(1)).astype(jnp.float32)  6.9 us
    all_to_all x1, starting transfers between devices, body(): lax.all_to_all(send, 'dp', split_axis=0, concat_axis=0, tiled=True)  6.09 us
    pallas_call x1, Pallas kernels, pack(): pl.pallas_call(pack_kernel, out_shape=jax.ShapeDtypeStruct((RANKS, PAIR)...  5.79 us
  transfers between devices with their start and end apart: 17, of which 11 were waited for; matrix products, arithmetic and copies ran while one was open for 3% of the time, Pallas kernels for 8%

profile of v2, /device:TPU:2, one launch (start us, length us, event | category | flops | bytes accessed | tf_op | source)
XLA Modules:
  0.0 224.2 jit_solution(17714004480417521435)
XLA Ops:
  7.2 1.0 fusion.29
  8.1 1.6 collective-permute-start
  9.7 1.0 collective-permute-start.1
  10.7 2.2 collective-permute-start.2
  12.9 5.8 %pack_pages.1 = bf16[16,15,64,256]{3,2,1,0:T(8,128)(2,1)} custom-call(s32[1]{0:T(128)} %bitcast.rank_ref, s32[16,384]{1,0:T(8,128)} %bitcast.59, bf16[45,64,256]{2,1,0:T(8,128)(2,1)} %pool_ref.1), custom_call_target="tpu_custom_call" | custom-call | tf_op jit(solution)/shard_map/pack_pages/pallas_call | solution.py:67
  18.8 6.1 %all-to-all-start = ((bf16[16,15,64,256]{3,2,1,0:T(8,128)(2,1)}), bf16[16,15,64,256]{3,2,1,0:T(8,128)(2,1)}, u32[]{:S(2)}, u32[]{:S(2)}) async-start(bf16[16,15,64,256]{3,2,1,0:T(8,128)(2,1)} %pack_pages.1), calls=%async_computation | async-start | bytes 15728640 | tf_op jit(solution)/shard_map/all_to_all | solution.py:249
  25.0 0.1 pad_add_fusion.1.order_ref
  25.2 0.4 copy-done.4
  25.6 0.1 reshape.134
  25.7 0.1 fusion.17
  25.8 0.1 reshape.141
  25.9 0.6 gather_fusion
  26.6 1.5 collective-permute-start.3
  28.1 2.7 %collective-permute-start.4 = (bf16[192,256]{1,0:T(8,128)(2,1)S(1)}, bf16[192,256]{1,0:T(8,128)(2,1)S(1)}, u32[]{:S(2)}, u32[]{:S(2)}) collective-permute-start(bf16[192,256]{1,0:T(8,128)(2,1)S(1)} %bitcast.57), channel_id=1, source_target_pairs={{0,64},{8,72},{16,80},{24,88},{32,96},{40,104},{48,112},{56,120},{... | collective-permute-start | bytes 294920 | tf_op jit(solution)/shard_map/ppermute | solution.py:221
  30.8 1.4 collective-permute-start.5
  32.2 0.8 constant_dynamic-slice_fusion.2
  33.1 0.1 reshape.133
  33.2 0.2 fusion
  33.4 0.3 convert_reduce_fusion
  33.8 0.8 dynamic_slice.21.len_ref
  34.5 66.9 %collective-permute-done.3 = bf16[192,256]{1,0:T(8,128)(2,1)S(1)} collective-permute-done((bf16[192,256]{1,0:T(8,128)(2,1)S(1)}, bf16[192,256]{1,0:T(8,128)(2,1)S(1)}, u32[]{:S(2)}, u32[]{:S(2)}) %collective-permute-start.3) | collective-permute-done | bytes 98336 | tf_op jit(solution)/shard_map/ppermute | solution.py:221
  101.4 7.7 %collective-permute-done.4 = bf16[192,256]{1,0:T(8,128)(2,1)S(1)} collective-permute-done((bf16[192,256]{1,0:T(8,128)(2,1)S(1)}, bf16[192,256]{1,0:T(8,128)(2,1)S(1)}, u32[]{:S(2)}, u32[]{:S(2)}) %collective-permute-start.4) | collective-permute-done | bytes 98336 | tf_op jit(solution)/shard_map/ppermute | solution.py:221
  109.1 8.7 %collective-permute-done.5 = bf16[192,256]{1,0:T(8,128)(2,1)S(1)} collective-permute-done((bf16[192,256]{1,0:T(8,128)(2,1)S(1)}, bf16[192,256]{1,0:T(8,128)(2,1)S(1)}, u32[]{:S(2)}, u32[]{:S(2)}) %collective-permute-start.5) | collective-permute-done | bytes 98336 | tf_op jit(solution)/shard_map/ppermute | solution.py:221
  117.9 18.3 %all-to-all-done = bf16[16,15,64,256]{3,2,1,0:T(8,128)(2,1)} async-done(((bf16[16,15,64,256]{3,2,1,0:T(8,128)(2,1)}), bf16[16,15,64,256]{3,2,1,0:T(8,128)(2,1)}, u32[]{:S(2)}, u32[]{:S(2)}) %all-to-all-start) | async-done | bytes 7864352 | tf_op jit(solution)/shard_map/all_to_all | solution.py:249
  136.2 5.8 %copy-done = bf16[1024,8192]{1,0:T(8,128)(2,1)S(1)} copy-done((bf16[1024,8192]{1,0:T(8,128)(2,1)S(1)}, bf16[1024,8192]{1,0:T(8,128)(2,1)}, u32[]{:S(2)}) %copy-start) | copy-done | bytes 16777240
  142.0 11.9 %rollout.2 = bf16[8,192,1024]{2,1,0:T(8,128)(2,1)} custom-call(s32[384]{0:T(512)S(1)} %multiply_add_fusion.idx_ref, s32[24]{0:T(128)S(1)} %dynamic_slice.21.len_ref, s32[24]{0:T(128)S(1)} %fusion.20.above_ref, s32[8]{0:T(128)S(1)} %iota.23.order_ref, bf16[192,1024]{1,0:T(8,128)(2,1)S(1)} %get-tuple-element.26.q_ref, ...), custom_call_target="tpu_custom_call" | custom-call | flops 4051697664 | bytes 27787264 | tf_op jit(solution)/shard_map/rollout/pallas_call | solution.py:179
  153.9 5.8 %copy-done.1 = bf16[1024,8192]{1,0:T(8,128)(2,1)S(1)} copy-done((bf16[1024,8192]{1,0:T(8,128)(2,1)S(1)}, bf16[1024,8192]{1,0:T(8,128)(2,1)}, u32[]{:S(2)}) %copy-start.1) | copy-done | bytes 16777240
  159.7 12.6 %rollout.3 = (bf16[4,192,1024]{2,1,0:T(8,128)(2,1)S(1)}, bf16[4,192,1024]{2,1,0:T(8,128)(2,1)S(1)}) custom-call(s32[384]{0:T(512)S(1)} %multiply_add_fusion.idx_ref, s32[24]{0:T(128)S(1)} %dynamic_slice.21.len_ref, s32[24]{0:T(128)S(1)} %fusion.20.above_ref, s32[8]{0:T(128)S(1)} %pad_add_fusion.1.order_ref, bf16[192,1024]{1,0:T(8,128)(2,1)S(1)} %get-tuple-element.25.q_ref, ...), custom_call_target="tpu_custom_call" | custom-call | flops 4051697664 | bytes 27787264 | tf_op jit(solution)/shard_map/rollout/pallas_call | solution.py:179
  172.3 0.1 collective-permute-start.6
  172.4 3.4 %collective-permute-done.6 = bf16[4,192,1024]{2,1,0:T(8,128)(2,1)S(1)} collective-permute-done((bf16[4,192,1024]{2,1,0:T(8,128)(2,1)S(1)}, bf16[4,192,1024]{2,1,0:T(8,128)(2,1)S(1)}, u32[]{:S(2)}, u32[]{:S(2)}) %collective-permute-start.6) | collective-permute-done | bytes 1572896 | tf_op jit(solution)/shard_map/ppermute | solution.py:268
  175.8 0.4 convert_add_fusion.1
  176.3 0.7 copy-done.2
  177.0 2.2 collective-permute-start.7
  179.2 2.2 collective-permute-start.9
  181.4 6.9 %collective-permute-done.7 = bf16[96,1024]{1,0:T(8,128)(2,1)S(1)} collective-permute-done((bf16[96,1024]{1,0:T(8,128)(2,1)S(1)}, bf16[96,1024]{1,0:T(8,128)(2,1)S(1)}, u32[]{:S(2)}, u32[]{:S(2)}) %collective-permute-start.7) | collective-permute-done | bytes 196640 | tf_op jit(solution)/shard_map/ppermute | solution.py:275
  188.4 0.3 collective-permute-start.8
  188.9 3.0 %collective-permute-start.10 = (bf16[192,1024]{1,0:T(8,128)(2,1)S(1)}, bf16[192,1024]{1,0:T(8,128)(2,1)S(1)}, u32[]{:S(2)}, u32[]{:S(2)}) collective-permute-start(bf16[192,1024]{1,0:T(8,128)(2,1)S(1)} %pad_maximum_fusion.3), channel_id=1, source_target_pairs={{0,6},{1,7},{2,0},{3,1},{4,2},{5,3},{6,4},{7,5},{8,14},{9,15},{10,... | collective-permute-start | bytes 1179656 | tf_op jit(solution)/shard_map/ppermute | solution.py:283
  191.9 10.2 %collective-permute-done.8 = bf16[192,1024]{1,0:T(8,128)(2,1)S(1)} collective-permute-done((bf16[192,1024]{1,0:T(8,128)(2,1)S(1)}, bf16[192,1024]{1,0:T(8,128)(2,1)S(1)}, u32[]{:S(2)}, u32[]{:S(2)}) %collective-permute-start.8) | collective-permute-done | bytes 393248 | tf_op jit(solution)/shard_map/ppermute | solution.py:282
  202.1 1.2 fusion.2
  203.4 1.1 bitcast_convert_fusion
  204.4 1.4 multiply_reduce_fusion
  205.9 0.1 collective-permute-start.11
  206.0 1.1 collective-permute-done.11
  207.1 4.1 %collective-permute-start.13 = (f32[3,128]{1,0:T(4,128)S(1)}, f32[3,128]{1,0:T(4,128)S(1)}, u32[]{:S(2)}, u32[]{:S(2)}) collective-permute-start(f32[3,128]{1,0:T(4,128)S(1)} %bitcast_add_fusion.1), channel_id=1, source_target_pairs={{0,4},{1,5},{2,6},{3,7},{4,0},{5,1},{6,2},{7,3},{8,12},{9,13},{10,... | collective-permute-start | bytes 4616 | tf_op jit(solution)/shard_map/ppermute | solution.py:293
  211.2 0.7 dynamic-slice_convert_fusion
  211.9 0.8 collective-permute-done.13
  212.7 2.0 collective-permute-done.14
  214.8 2.6 %multiply_convert_fusion = (bf16[384,1024]{1,0:T(8,128)(2,1)}, bf16[384,1024]{1,0:T(8,128)(2,1)}) fusion(f32[1024]{0:T(1024)S(1)} %dynamic-slice_convert_fusion, f32[384]{0:T(512)S(1)} %rsqrt_bitcast_fusion, f32[192,1024]{1,0:T(8,128)S(1)} %fusion.2, f32[192,1024]{1,0:T(8,128)S(1)} %bitcast_convert_fusion, bf16[384,8192]{1,0:T(8,128)(2,1)} %param.16, ...), kind=kLoop, calls=%fused_computation.2 | loop fusion | flops 2752512 | bytes 3937796 | tf_op jit(solution)/shard_map/convert_element_type | solution.py:297
  (41 shorter events, 0.7 us)
Async XLA Ops:
  8.1 10.6 %collective-permute-start = (bf16[192,256]{1,0:T(8,128)(2,1)S(1)}, bf16[192,256]{1,0:T(8,128)(2,1)S(1)}, u32[]{:S(2)}, u32[]{:S(2)}) collective-permute-start(bf16[192,256]{1,0:T(8,128)(2,1)S(1)} %get-tuple-element.34.fresh_ref), channel_id=1, source_target_pairs={{0,8},{8,16},{16,24},{24,0},{32,40},{40,48},{48,56},{56,32},{64,72... | collective-permute-start | bytes 294920 | tf_op jit(solution)/shard_map/ppermute | solution.py:209
  9.7 9.1 %collective-permute-start.1 = (bf16[192,256]{1,0:T(8,128)(2,1)S(1)}, bf16[192,256]{1,0:T(8,128)(2,1)S(1)}, u32[]{:S(2)}, u32[]{:S(2)}) collective-permute-start(bf16[192,256]{1,0:T(8,128)(2,1)S(1)} %get-tuple-element.34.fresh_ref), channel_id=1, source_target_pairs={{0,16},{8,24},{16,0},{24,8},{32,48},{40,56},{48,32},{56,40},{64,80... | collective-permute-start | bytes 294920 | tf_op jit(solution)/shard_map/ppermute | solution.py:209
  10.7 8.1 %collective-permute-start.2 = (bf16[192,256]{1,0:T(8,128)(2,1)S(1)}, bf16[192,256]{1,0:T(8,128)(2,1)S(1)}, u32[]{:S(2)}, u32[]{:S(2)}) collective-permute-start(bf16[192,256]{1,0:T(8,128)(2,1)S(1)} %get-tuple-element.34.fresh_ref), channel_id=1, source_target_pairs={{0,24},{8,0},{16,8},{24,16},{32,56},{40,32},{48,40},{56,48},{64,88... | collective-permute-start | bytes 294920 | tf_op jit(solution)/shard_map/ppermute | solution.py:209
  18.8 6.3 %copy-start.3 = (bf16[384,1024]{1,0:T(8,128)(2,1)S(1)}, bf16[384,1024]{1,0:T(8,128)(2,1)}, u32[]{:S(2)}) copy-start(bf16[384,1024]{1,0:T(8,128)(2,1)} %param.9) | copy-start | bytes 2359300
  18.8 117.4 %all-to-all-start = ((bf16[16,15,64,256]{3,2,1,0:T(8,128)(2,1)}), bf16[16,15,64,256]{3,2,1,0:T(8,128)(2,1)}, u32[]{:S(2)}, u32[]{:S(2)}) async-start(bf16[16,15,64,256]{3,2,1,0:T(8,128)(2,1)} %pack_pages.1), calls=%async_computation | async-start | bytes 15728640 | tf_op jit(solution)/shard_map/all_to_all | solution.py:249
  24.9 0.7 copy-start.4
  24.9 178.4 %reduce-scatter.2.cloned.1.call-start = ((), (), s32[]{:S(2)}) async-start(), calls=%async_computation.2 | async-start | bytes 3538944 | tf_op jit(solution)/shard_map/reduce_scatter | solution.py:265
  26.6 74.8 %collective-permute-start.3 = (bf16[192,256]{1,0:T(8,128)(2,1)S(1)}, bf16[192,256]{1,0:T(8,128)(2,1)S(1)}, u32[]{:S(2)}, u32[]{:S(2)}) collective-permute-start(bf16[192,256]{1,0:T(8,128)(2,1)S(1)} %bitcast.58), channel_id=1, source_target_pairs={{0,32},{8,40},{16,48},{24,56},{32,64},{40,72},{48,80},{56,88},{64,... | collective-permute-start | bytes 294920 | tf_op jit(solution)/shard_map/ppermute | solution.py:221
  28.1 81.0 %collective-permute-start.4 = (bf16[192,256]{1,0:T(8,128)(2,1)S(1)}, bf16[192,256]{1,0:T(8,128)(2,1)S(1)}, u32[]{:S(2)}, u32[]{:S(2)}) collective-permute-start(bf16[192,256]{1,0:T(8,128)(2,1)S(1)} %bitcast.57), channel_id=1, source_target_pairs={{0,64},{8,72},{16,80},{24,88},{32,96},{40,104},{48,112},{56,120},{... | collective-permute-start | bytes 294920 | tf_op jit(solution)/shard_map/ppermute | solution.py:221
  30.8 87.1 %collective-permute-start.5 = (bf16[192,256]{1,0:T(8,128)(2,1)S(1)}, bf16[192,256]{1,0:T(8,128)(2,1)S(1)}, u32[]{:S(2)}, u32[]{:S(2)}) collective-permute-start(bf16[192,256]{1,0:T(8,128)(2,1)S(1)} %bitcast.56), channel_id=1, source_target_pairs={{0,96},{8,104},{16,112},{24,120},{32,0},{40,8},{48,16},{56,24},{64... | collective-permute-start | bytes 294920 | tf_op jit(solution)/shard_map/ppermute | solution.py:221
  136.2 5.8 %copy-start = (bf16[1024,8192]{1,0:T(8,128)(2,1)S(1)}, bf16[1024,8192]{1,0:T(8,128)(2,1)}, u32[]{:S(2)}) copy-start(bf16[1024,8192]{1,0:T(8,128)(2,1)} %w_ref.3) | copy-start | bytes 50331652
  153.9 5.8 %copy-start.1 = (bf16[1024,8192]{1,0:T(8,128)(2,1)S(1)}, bf16[1024,8192]{1,0:T(8,128)(2,1)}, u32[]{:S(2)}) copy-start(bf16[1024,8192]{1,0:T(8,128)(2,1)} %w_ref.3) | copy-start | bytes 50331652
  172.3 3.5 %collective-permute-start.6 = (bf16[4,192,1024]{2,1,0:T(8,128)(2,1)S(1)}, bf16[4,192,1024]{2,1,0:T(8,128)(2,1)S(1)}, u32[]{:S(2)}, u32[]{:S(2)}) collective-permute-start(bf16[4,192,1024]{2,1,0:T(8,128)(2,1)S(1)} %get-tuple-element.19), channel_id=1, source_target_pairs={{0,1},{1,0},{2,3},{3,2},{4,5},{5,4},{6,7},{7,6},{8,9},{9,8},{10,11... | collective-permute-start | bytes 4718600 | tf_op jit(solution)/shard_map/ppermute | solution.py:268
  175.8 1.2 copy-start.2
  177.0 11.3 %collective-permute-start.7 = (bf16[96,1024]{1,0:T(8,128)(2,1)S(1)}, bf16[96,1024]{1,0:T(8,128)(2,1)S(1)}, u32[]{:S(2)}, u32[]{:S(2)}) collective-permute-start(bf16[96,1024]{1,0:T(8,128)(2,1)S(1)} %get-tuple-element.27), channel_id=1, source_target_pairs={{0,2},{1,3},{2,4},{3,5},{4,6},{5,7},{6,0},{7,1},{8,10},{9,11},{10,... | collective-permute-start | bytes 589832 | tf_op jit(solution)/shard_map/ppermute | solution.py:275
  179.2 9.5 %collective-permute-start.9 = (bf16[96,1024]{1,0:T(8,128)(2,1)S(1)}, bf16[96,1024]{1,0:T(8,128)(2,1)S(1)}, u32[]{:S(2)}, u32[]{:S(2)}) collective-permute-start(bf16[96,1024]{1,0:T(8,128)(2,1)S(1)} %get-tuple-element.28), channel_id=1, source_target_pairs={{0,6},{1,7},{2,0},{3,1},{4,2},{5,3},{6,4},{7,5},{8,14},{9,15},{10,... | collective-permute-start | bytes 589832 | tf_op jit(solution)/shard_map/ppermute | solution.py:276
  188.4 13.7 %collective-permute-start.8 = (bf16[192,1024]{1,0:T(8,128)(2,1)S(1)}, bf16[192,1024]{1,0:T(8,128)(2,1)S(1)}, u32[]{:S(2)}, u32[]{:S(2)}) collective-permute-start(bf16[192,1024]{1,0:T(8,128)(2,1)S(1)} %pad_maximum_fusion.2), channel_id=1, source_target_pairs={{0,2},{1,3},{2,4},{3,5},{4,6},{5,7},{6,0},{7,1},{8,10},{9,11},{10,... | collective-permute-start | bytes 1179656 | tf_op jit(solution)/shard_map/ppermute | solution.py:282
  188.9 13.2 %collective-permute-start.10 = (bf16[192,1024]{1,0:T(8,128)(2,1)S(1)}, bf16[192,1024]{1,0:T(8,128)(2,1)S(1)}, u32[]{:S(2)}, u32[]{:S(2)}) collective-permute-start(bf16[192,1024]{1,0:T(8,128)(2,1)S(1)} %pad_maximum_fusion.3), channel_id=1, source_target_pairs={{0,6},{1,7},{2,0},{3,1},{4,2},{5,3},{6,4},{7,5},{8,14},{9,15},{10,... | collective-permute-start | bytes 1179656 | tf_op jit(solution)/shard_map/ppermute | solution.py:283
  205.9 1.2 collective-permute-start.11
  207.1 4.8 %collective-permute-start.12 = (f32[3,128]{1,0:T(4,128)S(1)}, f32[3,128]{1,0:T(4,128)S(1)}, u32[]{:S(2)}, u32[]{:S(2)}) collective-permute-start(f32[3,128]{1,0:T(4,128)S(1)} %bitcast_add_fusion.1), channel_id=1, source_target_pairs={{0,2},{1,3},{2,4},{3,5},{4,6},{5,7},{6,0},{7,1},{8,10},{9,11},{10,... | collective-permute-start | bytes 4616 | tf_op jit(solution)/shard_map/ppermute | solution.py:293
  207.1 5.6 %collective-permute-start.13 = (f32[3,128]{1,0:T(4,128)S(1)}, f32[3,128]{1,0:T(4,128)S(1)}, u32[]{:S(2)}, u32[]{:S(2)}) collective-permute-start(f32[3,128]{1,0:T(4,128)S(1)} %bitcast_add_fusion.1), channel_id=1, source_target_pairs={{0,4},{1,5},{2,6},{3,7},{4,0},{5,1},{6,2},{7,3},{8,12},{9,13},{10,... | collective-permute-start | bytes 4616 | tf_op jit(solution)/shard_map/ppermute | solution.py:293
  211.2 3.6 %collective-permute-start.14 = (f32[3,128]{1,0:T(4,128)S(1)}, f32[3,128]{1,0:T(4,128)S(1)}, u32[]{:S(2)}, u32[]{:S(2)}) collective-permute-start(f32[3,128]{1,0:T(4,128)S(1)} %bitcast_add_fusion.1), channel_id=1, source_target_pairs={{0,6},{1,7},{2,0},{3,1},{4,2},{5,3},{6,4},{7,5},{8,14},{9,15},{10,... | collective-permute-start | bytes 4616 | tf_op jit(solution)/shard_map/ppermute | solution.py:293
Sparse Core Ops, SparseCore 0:
  154.0 44.5 reduce-scatter.1

commit v3 on v2

v3 whole, which is shorter than its diff:
```python
import functools

import jax
import jax.numpy as jnp
from jax import lax
from jax.experimental import pallas as pl
from jax.experimental.pallas import tpu as pltpu
from jax.sharding import PartitionSpec as P

D = 8192
HD = 128
NEW = 16
PAGE = 64
PATH_PAGES = 16
SHARED = 8
FAM = 4
RANKS = 16
PAIR = 15
ROOTS = 12
SHARE = 3
GROUPS = (3, 3)
LOG2E = 1.4426950408889634
MIB = 1024 * 1024


def pack_kernel(rank_ref, table_ref, pool_ref, send_ref, wanted_ref, wanted_smem, sem, send_sem):
    pages_dev = pool_ref.shape[0]
    slots, nodes = table_ref.shape
    base = rank_ref[0] * pages_dev
    table = table_ref[...]
    height = -(-pages_dev // 16) * 16
    row = lax.broadcasted_iota(jnp.int32, (height, nodes), 0)
    hits = jnp.zeros((height, nodes), jnp.float32)
    for page in range(pages_dev):
        hit = jnp.max((table == base + page).astype(jnp.float32), axis=0, keepdims=True)
        hits = jnp.where(row == page, hit, hits)
    node = lax.broadcasted_iota(jnp.int32, (nodes, 128), 0)
    begin = lax.broadcasted_iota(jnp.int32, (nodes, 128), 1) * (nodes // RANKS)
    belongs = ((node >= begin) & (node < begin + nodes // RANKS)).astype(jnp.bfloat16)
    present = jnp.dot(hits.astype(jnp.bfloat16), belongs, preferred_element_type=jnp.float32) > 0
    low = lax.broadcasted_iota(jnp.int32, (height, height), 0)
    high = lax.broadcasted_iota(jnp.int32, (height, height), 1)
    before = jnp.dot(
        (high < low).astype(jnp.bfloat16), present.astype(jnp.bfloat16), preferred_element_type=jnp.float32
    )
    place = jnp.where(present, before, -1.0)
    page_id = lax.broadcasted_iota(jnp.int32, (height, 128), 0).astype(jnp.float32)
    line = lax.broadcasted_iota(jnp.int32, (16, 128), 0)
    wanted = jnp.zeros((16, 128), jnp.float32)
    for slot in range(PAIR):
        page = jnp.sum(jnp.where(place == slot, page_id, 0.0), axis=0, keepdims=True)
        wanted = jnp.where(line == slot, page, wanted)
    wanted_ref[...] = wanted.astype(jnp.int32)
    copy = pltpu.make_async_copy(wanted_ref, wanted_smem, sem)
    copy.start()
    copy.wait()

    @pl.loop(0, RANKS)
    def _(dest):
        for slot in range(PAIR):
            page = jnp.clip(wanted_smem[slot, dest], 0, pages_dev - 1)
            pltpu.make_async_copy(pool_ref.at[page], send_ref.at[dest, slot], send_sem).start()

    filled = send_ref.at[:, pl.ds(0, PAIR)]
    pltpu.make_async_copy(filled, filled, send_sem).wait()


def pack(rank, table, pool):
    return pl.pallas_call(
        pack_kernel,
        out_shape=jax.ShapeDtypeStruct((RANKS, PAIR + 1) + pool.shape[1:], pool.dtype),
        in_specs=[
            pl.BlockSpec(memory_space=pltpu.SMEM),
            pl.BlockSpec(memory_space=pltpu.VMEM),
            pl.BlockSpec(memory_space=pltpu.VMEM),
        ],
        out_specs=pl.BlockSpec(memory_space=pltpu.HBM),
        scratch_shapes=[
            pltpu.VMEM((16, 128), jnp.int32),
            pltpu.SMEM((16, 128), jnp.int32),
            pltpu.SemaphoreType.DMA,
            pltpu.SemaphoreType.DMA,
        ],
        name="pack_pages",
    )(rank, table, pool)


def pack_parents_kernel(rank_ref, parent_ref, row_ref, _, send_ref, sem):
    y, x = rank_ref[0] // 4, rank_ref[0] % 4
    nodes = parent_ref.shape[0] // RANKS

    def copy(dest, i, place):
        source = row_ref.at[pl.ds(pl.multiple_of(place * NEW, NEW), NEW)]
        return pltpu.make_async_copy(source, send_ref.at[dest, PAIR, pl.ds(i * NEW, NEW)], sem)

    @pl.loop(0, RANKS)
    def _(dest):
        for i in range(SHARE):
            named = jnp.maximum(parent_ref[dest * nodes + ROOTS + x * SHARE + i], 0)
            away = (x + 4 - named // nodes % 4) % 4
            copy(dest, i, jnp.minimum(away * ROOTS + named % nodes, 4 * ROOTS - 1)).start()

    filled = send_ref.at[:, PAIR, pl.ds(0, SHARE * NEW)]
    pltpu.make_async_copy(filled, filled, sem).wait()


def pack_parents(rank, parent, row, send):
    smem = pl.BlockSpec(memory_space=pltpu.SMEM)
    hbm = pl.BlockSpec(memory_space=pltpu.HBM)
    return pl.pallas_call(
        pack_parents_kernel,
        out_shape=jax.ShapeDtypeStruct(send.shape, send.dtype),
        in_specs=[smem, smem, pl.BlockSpec(memory_space=pltpu.VMEM), hbm],
        out_specs=hbm,
        scratch_shapes=[pltpu.SemaphoreType.DMA],
        input_output_aliases={3: 0},
        name="pack_parents",
    )(rank, parent, row, send)


def attend_family(first, node, idx_ref, len_ref, above_ref, q_ref, fresh_ref, pages_ref, attn_ref):
    scale = HD ** (-0.5) * LOG2E
    nt = (((1,), (1,)), ((), ()))

    def pages(n, slot):
        return jnp.concatenate([pages_ref[idx_ref[n * PATH_PAGES + slot + s]] for s in range(SHARED)], axis=0)

    heads = q_ref.shape[1] // HD
    span = heads * NEW
    shared = pages(node, 0)
    queries = []
    for i in range(FAM):
        rows = q_ref[first + i * NEW : first + (i + 1) * NEW, :]
        queries.append(jnp.concatenate([rows[:, h * HD : (h + 1) * HD] for h in range(heads)], axis=0))
    s_shared = lax.dot_general(
        jnp.concatenate(queries, axis=0), shared[:, :HD], nt, preferred_element_type=jnp.float32
    )
    half = SHARED * PAGE // 2
    own, s_own = [], []
    for i in range(FAM):
        above = above_ref[node + i]
        spot = jnp.maximum(above, 0)
        upper = pages_ref[spot // PAGE, pl.ds(pl.multiple_of(spot % PAGE, NEW), NEW), :]
        fresh = fresh_ref[first + i * NEW : first + (i + 1) * NEW, :]
        kv = jnp.concatenate([pages(node + i, SHARED), fresh, upper], axis=0)
        s = lax.dot_general(queries[i], kv[:, :HD], nt, preferred_element_type=jnp.float32)
        late = s[:, half:]
        spot = lax.broadcasted_iota(jnp.int32, late.shape, 1) + SHARED * PAGE + half
        token = lax.broadcasted_iota(jnp.int32, late.shape, 0) % NEW
        key = spot - PATH_PAGES * PAGE
        limit = jnp.where(above >= 0, 2 * NEW, NEW)
        allowed = (spot < len_ref[node + i]) | ((key >= 0) & (key <= token)) | ((key >= NEW) & (key < limit))
        own.append(kv)
        s_own.append(jnp.concatenate([s[:, :half], jnp.where(allowed, late, -jnp.inf)], axis=1))
    tops = [
        jnp.maximum(
            jnp.max(s_shared[i * span : (i + 1) * span], axis=1, keepdims=True),
            jnp.max(s_own[i], axis=1, keepdims=True),
        )
        for i in range(FAM)
    ]
    w_own = [jnp.exp2((s_own[i] - tops[i]) * scale).astype(jnp.bfloat16) for i in range(FAM)]
    w_shared = jnp.exp2((s_shared - jnp.concatenate(tops, axis=0)) * scale).astype(jnp.bfloat16)
    ones = jnp.ones((own[0].shape[0], HD), jnp.bfloat16)
    accum = [
        jnp.dot(w_own[i], jnp.concatenate([own[i][:, HD:], ones], axis=1), preferred_element_type=jnp.float32)
        for i in range(FAM)
    ]
    accum = jnp.concatenate(accum, axis=0) + jnp.dot(
        w_shared, jnp.concatenate([shared[:, HD:], ones[: SHARED * PAGE]], axis=1), preferred_element_type=jnp.float32
    )
    attn = (accum[:, :HD] / accum[:, HD:]).astype(jnp.bfloat16)
    for i in range(FAM):
        for h in range(heads):
            block = attn[i * span + h * NEW : i * span + (h + 1) * NEW, :]
            attn_ref[first + i * NEW : first + (i + 1) * NEW, h * HD : (h + 1) * HD] = block


def attend_kernel(idx_ref, len_ref, above_ref, q_ref, fresh_ref, recv_ref, attn_ref, pages_ref, sem):
    ranks = RANKS * (PAIR + 1)
    for r in range(RANKS):
        part = pl.ds(r * (ranks // RANKS), ranks // RANKS)
        pltpu.make_async_copy(recv_ref.at[part], pages_ref.at[part], sem).start()
    pltpu.make_async_copy(recv_ref, pages_ref, sem).wait()
    for f in range(q_ref.shape[0] // (FAM * NEW)):
        attend_family(f * FAM * NEW, f * FAM, idx_ref, len_ref, above_ref, q_ref, fresh_ref, pages_ref, attn_ref)


def attend(idx, lengths, above, queries, fresh, received):
    rows, width = queries.shape
    smem = pl.BlockSpec(memory_space=pltpu.SMEM)
    vmem = pl.BlockSpec(memory_space=pltpu.VMEM)
    return pl.pallas_call(
        attend_kernel,
        out_shape=jax.ShapeDtypeStruct((rows, width), jnp.bfloat16),
        in_specs=[smem, smem, smem, vmem, vmem, pl.BlockSpec(memory_space=pltpu.HBM)],
        out_specs=vmem,
        scratch_shapes=[pltpu.VMEM(received.shape, jnp.bfloat16), pltpu.SemaphoreType.DMA],
        compiler_params=pltpu.CompilerParams(vmem_limit_bytes=24 * MIB),
        cost_estimate=pl.CostEstimate(
            flops=4 * rows * width * 1056 * 4, bytes_accessed=received.size * 2 + 4 * rows * width, transcendentals=rows * 8 * 1056
        ),
        name="attend",
    )(idx, lengths, above, queries, fresh, received)


def project_kernel(first, order_ref, attn_ref, w_ref, out_ref):
    count, rows, cols = out_ref.shape

    @pl.loop(0, count)
    def _(b):
        w = w_ref[:, pl.ds(pl.multiple_of(order_ref[b] * cols, cols), cols)]
        attn = attn_ref[first : first + rows, :]
        out_ref[b] = jnp.dot(attn, w, preferred_element_type=jnp.float32).astype(jnp.bfloat16)


def project(first, rows, order, attn, w_out):
    depth, width = w_out.shape
    cols = width // 8
    count = order.shape[0]
    smem = pl.BlockSpec(memory_space=pltpu.SMEM)
    vmem = pl.BlockSpec(memory_space=pltpu.VMEM)
    return pl.pallas_call(
        functools.partial(project_kernel, first),
        out_shape=jax.ShapeDtypeStruct((count, rows, cols), jnp.bfloat16),
        in_specs=[smem, vmem, vmem],
        out_specs=vmem,
        compiler_params=pltpu.CompilerParams(vmem_limit_bytes=24 * MIB),
        cost_estimate=pl.CostEstimate(
            flops=2 * rows * depth * cols * count, bytes_accessed=rows * cols * count * 2, transcendentals=0
        ),
        name="project",
    )(order, attn, w_out)


def shift(dy, dx):
    return [(s, (s // 4 + dy) % 4 * 4 + (s % 4 + dx) % 4) for s in range(RANKS)]


def turn(d):
    return [(t, (t + 2 * d) % 8) for t in range(8)]


def gather_row(fresh):
    mine = fresh[: ROOTS * NEW]
    return jnp.concatenate([mine] + [lax.ppermute(mine, "dp", shift(0, d)) for d in (1, 2, 3)], axis=0)


def above_of(parent, rank, nodes):
    own = lax.dynamic_slice_in_dim(parent, rank * nodes, nodes)
    child = jnp.arange(nodes, dtype=jnp.int32) - ROOTS
    source = jnp.maximum(own, 0) // nodes // 4 * 4 + child // SHARE
    row = (source * (PAIR + 1) + PAIR) * PAGE + child % SHARE * NEW
    return jnp.where((own >= 0) & (child >= 0), row, -1)


def slots_of(table, ranks, pages_dev):
    owner = table // pages_dev
    page = jnp.arange(ranks * pages_dev, dtype=jnp.int32)
    present = jnp.any(table[None, :] == page[:, None], axis=1)
    place = jnp.sum(
        (present[None, :] & (page[None, :] // pages_dev == owner[:, None]) & (page[None, :] < table[:, None])).astype(jnp.int32),
        axis=1,
    )
    return owner * (PAIR + 1) + place


def sum_over_tensor(kept, back):
    def pair(i):
        return kept[i].astype(jnp.float32) + back[i].astype(jnp.float32)

    half = kept.shape[1] // 2
    far = pair(2).astype(jnp.bfloat16)
    from_low = lax.ppermute(far[:half], "tensor", turn(1)).astype(jnp.float32)
    from_high = lax.ppermute(far[half:], "tensor", turn(-1)).astype(jnp.float32)
    up, down = pair(1), pair(3)
    up = jnp.concatenate([up[:half] + from_low, up[half:]], axis=0).astype(jnp.bfloat16)
    down = jnp.concatenate([down[:half], down[half:] + from_high], axis=0).astype(jnp.bfloat16)
    return (
        pair(0)
        + lax.ppermute(up, "tensor", turn(1)).astype(jnp.float32)
        + lax.ppermute(down, "tensor", turn(-1)).astype(jnp.float32)
    )


def body(queries, fresh_kv, kv_pool, page_table, path_len, parent, w_out, residual, gain):
    rank = lax.axis_index("dp")
    tensor_rank = lax.axis_index("tensor")
    tensors = lax.axis_size("tensor")
    rows = queries.shape[0]
    nodes = rows // NEW
    pages_dev = kv_pool.shape[0]
    row = gather_row(fresh_kv)
    send = pack(rank.reshape(1), page_table.T, kv_pool)
    send = pack_parents(rank.reshape(1), parent, row, send)

    own_table = lax.dynamic_slice_in_dim(page_table, rank * nodes, nodes).reshape(-1)
    idx = slots_of(own_table, RANKS, pages_dev)
    lengths = lax.dynamic_slice_in_dim(path_len, rank * nodes, nodes)
    above = above_of(parent, rank, nodes)
    z, core = tensor_rank // 2, tensor_rank % 2
    around = (z + jnp.arange(4, dtype=jnp.int32)) % 4 * 2
    other, same = around + 1 - core, around + core

    send, idx, lengths, above, other, same = lax.optimization_barrier((send, idx, lengths, above, other, same))
    received = lax.all_to_all(send, "dp", split_axis=0, concat_axis=0, tiled=True)
    received, queries, fresh_kv, w_out, residual, gain = lax.optimization_barrier(
        (received, queries, fresh_kv, w_out, residual, gain)
    )
    received = received.reshape(RANKS * (PAIR + 1), PAGE, kv_pool.shape[2])
    attn = attend(idx, lengths, above, queries, fresh_kv, received)
    swap = [(t, t ^ 1) for t in range(tensors)]
    summed, first = [], 0
    for families in GROUPS:
        count = families * FAM * NEW
        away = project(first, count, other, attn, w_out)
        away, attn = lax.optimization_barrier((away, attn))
        back = lax.ppermute(away, "tensor", swap)
        kept = project(first, count, same, attn, w_out)
        kept, attn = lax.optimization_barrier((kept, attn))
        summed.append(sum_over_tensor(kept, back))
        first += count

    cols = summed[0].shape[1]
    mine = lax.dynamic_slice_in_dim(residual, tensor_rank * cols, cols, 1)
    mixed = mine.astype(jnp.float32) + jnp.concatenate(summed, axis=0)
    power = jnp.sum(mixed * mixed, axis=1).reshape(rows // 128, 128)
    power = power + lax.ppermute(power, "tensor", swap)
    total = power
    for d in (1, 2, 3):
        total = total + lax.ppermute(power, "tensor", turn(d))
    norm = lax.rsqrt(total.reshape(rows, 1) / D + 1e-05)
    own_gain = lax.dynamic_slice_in_dim(gain, tensor_rank * cols, cols)
    normed = mixed * norm * own_gain.astype(jnp.float32)
    return (mixed.astype(jnp.bfloat16), normed.astype(jnp.bfloat16))


def solution(mesh):
    return jax.shard_map(
        body,
        mesh=mesh,
        in_specs=(
            P("dp", "tensor"),
            P("dp", "tensor"),
            P("dp", None, "tensor"),
            P(),
            P(),
            P(),
            P("tensor", None),
            P("dp", None),
            P(),
        ),
        out_specs=(P("dp", "tensor"), P("dp", "tensor")),
        check_vma=False,
    )
```

time: 228 us -> 188 us (0.82); the launches traced: 224 us -> 187 us
  waiting for transfers between devices: 126 us -> 18.3 us
  blocking collectives: 0 us -> 101 us
  between operations: 14.3 us -> 0.98 us
  local copies, waits for them, and re-layouts: 16.3 us -> 4.21 us
  starting transfers between devices: 28.6 us -> 21.7 us
  other arithmetic: 8.44 us -> 13.8 us
  Pallas kernels: 30.3 us -> 26.7 us
    all_to_all x0 -> x1, blocking collectives: none -> 101 us  [body(): lax.all_to_all(send, 'dp', split_axis=0, concat_axis=0, tiled=True)]
    ppermute x9 -> x11, waiting for transfers between devices: 105 us -> 14.7 us  [the longest x2 8.64 us: sum_over_tensor(): lax.ppermute(up, 'tensor', turn(1)).astype(jnp.float32)]
    all_to_all x1 -> x0, waiting for transfers between devices: 18.3 us -> none  [body(): lax.all_to_all(send, 'dp', split_axis=0, concat_axis=0, tiled=True)]
    unnamed x10 -> x16, local copies, waits for them, and re-layouts: 12.7 us -> 1.45 us
    all_to_all x1 -> x0, starting transfers between devices: 6.09 us -> none  [body(): lax.all_to_all(send, 'dp', split_axis=0, concat_axis=0, tiled=True)]
    pallas_call x3 -> x7, Pallas kernels: 30.3 us -> 26.7 us  [the longest x4 11.7 us: project(): pl.pallas_call(functools.partial(project_kernel, first), out_shape=jax.Sh...]
    concatenate x5 -> x4, other arithmetic: 0.17 us -> 3.12 us  [the longest x2 1.56 us: sum_over_tensor(): jnp.concatenate([up[:half] + from_low, up[half:]], axis=0)]
    ppermute x9 -> x11, starting transfers between devices: 13.6 us -> 14.9 us  [the longest x2 7.41 us: sum_over_tensor(): from_high = lax.ppermute(far[half:], 'tensor', turn(-1)).astype(jnp.float32)]
  transfers between devices with their start and end apart: 17 -> 17, of which waited for: 11 -> 8; matrix products, arithmetic and copies ran while one was open for 3% -> 5% of each run, Pallas kernels for 8% -> 5%
where the time goes in v3:
time: 188 us; the launch traced here: 187 us
  blocking collectives  101 us (54%)
  Pallas kernels  26.7 us (14%)
  starting transfers between devices  21.7 us (12%)
  waiting for transfers between devices  18.3 us (10%)
  other arithmetic  13.8 us (7%)
  local copies, waits for them, and re-layouts  4.21 us (2%)
    all_to_all x1, blocking collectives, body(): lax.all_to_all(send, 'dp', split_axis=0, concat_axis=0, tiled=True)  101 us
    pallas_call x4, Pallas kernels, project(): pl.pallas_call(functools.partial(project_kernel, first), out_shape=jax.Sh...  11.7 us
    ppermute x2, waiting for transfers between devices, sum_over_tensor(): lax.ppermute(up, 'tensor', turn(1)).astype(jnp.float32)  8.64 us
    ppermute x2, starting transfers between devices, sum_over_tensor(): from_high = lax.ppermute(far[half:], 'tensor', turn(-1)).astype(jnp.float32)  7.41 us
    pallas_call x1, Pallas kernels, attend(): pl.pallas_call(attend_kernel, out_shape=jax.ShapeDtypeStruct((rows, width...  6.95 us
    ppermute x2, starting transfers between devices, sum_over_tensor(): lax.ppermute(down, 'tensor', turn(-1)).astype(jnp.float32)  6.73 us
    pallas_call x1, Pallas kernels, pack(): pl.pallas_call(pack_kernel, out_shape=jax.ShapeDtypeStruct((RANKS, PAIR +...  5.75 us
    ppermute x2, waiting for transfers between devices, sum_over_tensor(): lax.ppermute(down, 'tensor', turn(-1)).astype(jnp.float32)  4.94 us
  transfers between devices with their start and end apart: 17, of which 8 were waited for; matrix products, arithmetic and copies ran while one was open for 5% of the time, Pallas kernels for 5%

profile of v3, /device:TPU:2, one launch (start us, length us, event | category | flops | bytes accessed | tf_op | source)
XLA Modules:
  0.0 186.7 jit_solution(7079654994339818114)
XLA Ops:
  0.6 0.9 slice.127
  1.5 0.5 collective-permute-start.2
  2.0 2.5 %collective-permute-start.1 = (bf16[192,256]{1,0:T(8,128)(2,1)S(1)}, bf16[192,256]{1,0:T(8,128)(2,1)S(1)}, u32[]{:S(2)}, u32[]{:S(2)}) collective-permute-start(bf16[192,256]{1,0:T(8,128)(2,1)S(1)} %slice.127), channel_id=1, source_target_pairs={{0,16},{8,24},{16,0},{24,8},{32,48},{40,56},{48,32},{56,40},{64,80... | collective-permute-start | bytes 294920 | tf_op jit(solution)/shard_map/ppermute | solution.py:246
  4.5 1.8 collective-permute-start
  6.3 0.8 constant_dynamic-slice_fusion
  7.2 0.1 reshape.122
  7.3 0.2 fusion
  7.5 0.3 convert_reduce_fusion
  7.8 0.8 dynamic_slice.16.len_ref
  8.6 5.7 %pack_pages.1._ = bf16[16,16,64,256]{3,2,1,0:T(8,128)(2,1)} custom-call(s32[1]{0:T(128)} %bitcast.rank_ref, s32[16,384]{1,0:T(8,128)} %bitcast.60, bf16[45,64,256]{2,1,0:T(8,128)(2,1)} %pool_ref.1), custom_call_target="tpu_custom_call" | custom-call | tf_op jit(solution)/shard_map/pack_pages/pallas_call | solution.py:69
  14.3 0.8 and_select_fusion.5.above_ref
  15.2 0.8 pad_maximum_fusion.row_ref
  15.9 2.3 %pack_parents.1 = bf16[16,16,64,256]{3,2,1,0:T(8,128)(2,1)} custom-call(s32[1]{0:T(128)} %bitcast.rank_ref, s32[384]{0:T(512)} %parent_ref.1, bf16[768,256]{1,0:T(8,128)(2,1)} %pad_maximum_fusion.row_ref, bf16[16,16,64,256]{3,2,1,0:T(8,128)(2,1)} %pack_pages.1._), custom_call_target="tpu_custom_call", output_to_operand_aliasing={{}: (3, {})} | custom-call | tf_op jit(solution)/shard_map/pack_parents/pallas_call | solution.py:110
  18.3 101.0 %all_to_all.5 = bf16[16,16,64,256]{3,2,1,0:T(8,128)(2,1)S(1)} all-to-all(bf16[16,16,64,256]{3,2,1,0:T(8,128)(2,1)} %pack_parents.1), channel_id=1, replica_groups=mesh['dp'=16,'tensor'=8] {'dp'}, dimensions={0} | all-to-all | bytes 16777216 | tf_op jit(solution)/shard_map/all_to_all | solution.py:306
  119.4 7.0 %attend.1.attn_ref = bf16[384,1024]{1,0:T(8,128)(2,1)S(1)} custom-call(s32[384]{0:T(512)S(1)} %multiply_add_fusion.idx_ref, s32[24]{0:T(128)S(1)} %dynamic_slice.16.len_ref, s32[24]{0:T(128)S(1)} %and_select_fusion.5.above_ref, bf16[384,1024]{1,0:T(8,128)(2,1)S(1)} %copy-done.1, bf16[384,256]{1,0:T(8,128)(2,1)S(1)} %copy-done, bf16[256,64,256]{2,1,0:T(8,128)(2,1)S(1)} %bitcast.59), custom_call_target="tpu_custom_call" | custom-call | flops 6643777536 | bytes 9961472 | tf_op jit(solution)/shard_map/attend/pallas_call | solution.py:193
  126.4 2.9 %project.4 = bf16[4,192,1024]{2,1,0:T(8,128)(2,1)S(1)} custom-call(s32[4]{0:T(128)S(1)} %get-tuple-element.24.order_ref, bf16[384,1024]{1,0:T(8,128)(2,1)S(1)} %attend.1.attn_ref, bf16[1024,8192]{1,0:T(8,128)(2,1)S(1)} %bitcast.58), custom_call_target="tpu_custom_call" | custom-call | flops 1610612736 | bytes 1572864 | tf_op jit(solution)/shard_map/project/pallas_call | solution.py:223
  129.3 2.9 %project.5 = bf16[4,192,1024]{2,1,0:T(8,128)(2,1)S(1)} custom-call(s32[4]{0:T(128)S(1)} %get-tuple-element.23.order_ref, bf16[384,1024]{1,0:T(8,128)(2,1)S(1)} %attend.1.attn_ref, bf16[1024,8192]{1,0:T(8,128)(2,1)S(1)} %bitcast.58), custom_call_target="tpu_custom_call" | custom-call | flops 1610612736 | bytes 1572864 | tf_op jit(solution)/shard_map/project/pallas_call | solution.py:223
  132.2 2.9 %project.6 = bf16[4,192,1024]{2,1,0:T(8,128)(2,1)S(1)} custom-call(s32[4]{0:T(128)S(1)} %get-tuple-element.24.order_ref, bf16[384,1024]{1,0:T(8,128)(2,1)S(1)} %attend.1.attn_ref, bf16[1024,8192]{1,0:T(8,128)(2,1)S(1)} %bitcast.58), custom_call_target="tpu_custom_call" | custom-call | flops 1610612736 | bytes 1572864 | tf_op jit(solution)/shard_map/project/pallas_call | solution.py:223
  135.2 0.1 collective-permute-start.8
  135.3 0.5 collective-permute-start.3
  135.8 2.9 %project.7 = bf16[4,192,1024]{2,1,0:T(8,128)(2,1)S(1)} custom-call(s32[4]{0:T(128)S(1)} %get-tuple-element.23.order_ref, bf16[384,1024]{1,0:T(8,128)(2,1)S(1)} %attend.1.attn_ref, bf16[1024,8192]{1,0:T(8,128)(2,1)S(1)} %bitcast.58), custom_call_target="tpu_custom_call" | custom-call | flops 1610612736 | bytes 1572864 | tf_op jit(solution)/shard_map/project/pallas_call | solution.py:223
  138.7 0.4 convert_add_fusion.1
  139.1 0.7 copy-done.3
  139.8 4.1 %collective-permute-start.11 = (bf16[96,1024]{1,0:T(8,128)(2,1)S(1)}, bf16[96,1024]{1,0:T(8,128)(2,1)S(1)}, u32[]{:S(2)}, u32[]{:S(2)}) collective-permute-start(bf16[96,1024]{1,0:T(8,128)(2,1)S(1)} %get-tuple-element.51), channel_id=1, source_target_pairs={{0,6},{1,7},{2,0},{3,1},{4,2},{5,3},{6,4},{7,5},{8,14},{9,15},{10,... | collective-permute-start | bytes 589832 | tf_op jit(solution)/shard_map/ppermute | solution.py:275
  144.0 0.4 convert_add_fusion.3
  144.5 0.7 copy-done.2
  145.2 3.3 %collective-permute-start.6 = (bf16[96,1024]{1,0:T(8,128)(2,1)S(1)}, bf16[96,1024]{1,0:T(8,128)(2,1)S(1)}, u32[]{:S(2)}, u32[]{:S(2)}) collective-permute-start(bf16[96,1024]{1,0:T(8,128)(2,1)S(1)} %get-tuple-element.49), channel_id=1, source_target_pairs={{0,6},{1,7},{2,0},{3,1},{4,2},{5,3},{6,4},{7,5},{8,14},{9,15},{10,... | collective-permute-start | bytes 589832 | tf_op jit(solution)/shard_map/ppermute | solution.py:275
  148.7 0.8 pad_maximum_fusion.4
  149.5 3.5 %collective-permute-start.12 = (bf16[192,1024]{1,0:T(8,128)(2,1)}, bf16[192,1024]{1,0:T(8,128)(2,1)S(1)}, u32[]{:S(2)}, u32[]{:S(2)}) collective-permute-start(bf16[192,1024]{1,0:T(8,128)(2,1)} %pad_maximum_fusion.4), channel_id=1, source_target_pairs={{0,6},{1,7},{2,0},{3,1},{4,2},{5,3},{6,4},{7,5},{8,14},{9,15},{10,... | collective-permute-start | bytes 1179656 | tf_op jit(solution)/shard_map/ppermute | solution.py:282
  153.1 0.8 pad_maximum_fusion.3
  153.9 0.8 pad_maximum_fusion.2
  154.7 3.2 %collective-permute-start.7 = (bf16[192,1024]{1,0:T(8,128)(2,1)}, bf16[192,1024]{1,0:T(8,128)(2,1)}, u32[]{:S(2)}, u32[]{:S(2)}) collective-permute-start(bf16[192,1024]{1,0:T(8,128)(2,1)} %pad_maximum_fusion.2), channel_id=1, source_target_pairs={{0,6},{1,7},{2,0},{3,1},{4,2},{5,3},{6,4},{7,5},{8,14},{9,15},{10,... | collective-permute-start | bytes 1179656 | tf_op jit(solution)/shard_map/ppermute | solution.py:282
  157.9 0.8 pad_maximum_fusion.1
  158.7 4.2 %collective-permute-done.12 = bf16[192,1024]{1,0:T(8,128)(2,1)S(1)} collective-permute-done((bf16[192,1024]{1,0:T(8,128)(2,1)}, bf16[192,1024]{1,0:T(8,128)(2,1)S(1)}, u32[]{:S(2)}, u32[]{:S(2)}) %collective-permute-start.12) | collective-permute-done | bytes 393248 | tf_op jit(solution)/shard_map/ppermute | solution.py:282
  162.9 4.5 %collective-permute-done.10 = bf16[192,1024]{1,0:T(8,128)(2,1)} collective-permute-done((bf16[192,1024]{1,0:T(8,128)(2,1)}, bf16[192,1024]{1,0:T(8,128)(2,1)}, u32[]{:S(2)}, u32[]{:S(2)}) %collective-permute-start.10) | collective-permute-done | bytes 393248 | tf_op jit(solution)/shard_map/ppermute | solution.py:281
  167.4 1.4 fusion.2
  168.8 0.8 collective-permute-done.7
  169.6 4.1 %collective-permute-done.5 = bf16[192,1024]{1,0:T(8,128)(2,1)} collective-permute-done((bf16[192,1024]{1,0:T(8,128)(2,1)}, bf16[192,1024]{1,0:T(8,128)(2,1)}, u32[]{:S(2)}, u32[]{:S(2)}) %collective-permute-start.5) | collective-permute-done | bytes 393248 | tf_op jit(solution)/shard_map/ppermute | solution.py:281
  173.7 1.5 fusion.3
  175.2 1.5 multiply_reduce_fusion
  176.7 1.1 collective-permute-done.13
  177.9 1.1 collective-permute-start.15
  179.0 0.9 collective-permute-start.14
  179.9 0.7 dynamic-slice_convert_fusion
  180.6 0.9 collective-permute-done.16
  181.4 1.5 collective-permute-done.15
  182.9 1.2 collective-permute-done.14
  184.1 2.6 %multiply_convert_fusion = (bf16[384,1024]{1,0:T(8,128)(2,1)}, bf16[384,1024]{1,0:T(8,128)(2,1)}) fusion(f32[1024]{0:T(1024)S(1)} %dynamic-slice_convert_fusion, f32[384]{0:T(512)S(1)} %rsqrt_bitcast_fusion, f32[192,1024]{1,0:T(8,128)S(1)} %fusion.2, f32[192,1024]{1,0:T(8,128)S(1)} %fusion.3, bf16[384,8192]{1,0:T(8,128)(2,1)} %param.16, s32[]{:T(128)S(6)} %select_n.77), kind=kLoop, calls=%fused_computation.1 | loop fusion | flops 2752512 | bytes 3937796 | tf_op jit(solution)/shard_map/convert_element_type | solution.py:335
  (47 shorter events, 0.7 us)
Async XLA Ops:
  1.5 13.6 %collective-permute-start.2 = (bf16[192,256]{1,0:T(8,128)(2,1)S(1)}, bf16[192,256]{1,0:T(8,128)(2,1)S(1)}, u32[]{:S(2)}, u32[]{:S(2)}) collective-permute-start(bf16[192,256]{1,0:T(8,128)(2,1)S(1)} %slice.127), channel_id=1, source_target_pairs={{0,24},{8,0},{16,8},{24,16},{32,56},{40,32},{48,40},{56,48},{64,88... | collective-permute-start | bytes 294920 | tf_op jit(solution)/shard_map/ppermute | solution.py:246
  2.0 13.2 %collective-permute-start.1 = (bf16[192,256]{1,0:T(8,128)(2,1)S(1)}, bf16[192,256]{1,0:T(8,128)(2,1)S(1)}, u32[]{:S(2)}, u32[]{:S(2)}) collective-permute-start(bf16[192,256]{1,0:T(8,128)(2,1)S(1)} %slice.127), channel_id=1, source_target_pairs={{0,16},{8,24},{16,0},{24,8},{32,48},{40,56},{48,32},{56,40},{64,80... | collective-permute-start | bytes 294920 | tf_op jit(solution)/shard_map/ppermute | solution.py:246
  4.5 10.7 %collective-permute-start = (bf16[192,256]{1,0:T(8,128)(2,1)S(1)}, bf16[192,256]{1,0:T(8,128)(2,1)S(1)}, u32[]{:S(2)}, u32[]{:S(2)}) collective-permute-start(bf16[192,256]{1,0:T(8,128)(2,1)S(1)} %slice.127), channel_id=1, source_target_pairs={{0,8},{8,16},{16,24},{24,0},{32,40},{40,48},{48,56},{56,32},{64,72... | collective-permute-start | bytes 294920 | tf_op jit(solution)/shard_map/ppermute | solution.py:246
  18.3 101.1 %copy-start = (bf16[384,256]{1,0:T(8,128)(2,1)S(1)}, bf16[384,256]{1,0:T(8,128)(2,1)}, u32[]{:S(2)}) copy-start(bf16[384,256]{1,0:T(8,128)(2,1)} %fresh_ref) | copy-start | bytes 589828
  18.3 101.1 %copy-start.1 = (bf16[384,1024]{1,0:T(8,128)(2,1)S(1)}, bf16[384,1024]{1,0:T(8,128)(2,1)}, u32[]{:S(2)}) copy-start(bf16[384,1024]{1,0:T(8,128)(2,1)} %q_ref) | copy-start | bytes 2359300
  18.3 108.0 %slice-start = ((s8[16777216]{0:T(1024)(128)(4,1)}), s8[4194304]{0:T(1024)(128)(4,1)S(1)}, s32[]{:S(2)}) async-start(s8[16777216]{0:T(1024)(128)(4,1)} %bitcast.57), calls=%async_computation.1 | async-start | bytes 8388608
  18.3 108.0 %slice-start.1 = ((s8[16777216]{0:T(1024)(128)(4,1)}), s8[4194304]{0:T(1024)(128)(4,1)S(1)}, s32[]{:S(2)}) async-start(s8[16777216]{0:T(1024)(128)(4,1)} %bitcast.57), calls=%async_computation.2 | async-start | bytes 8388608
  119.4 7.0 %slice-start.2 = ((s8[16777216]{0:T(1024)(128)(4,1)}), s8[4194304]{0:T(1024)(128)(4,1)S(1)}, s32[]{:S(2)}) async-start(s8[16777216]{0:T(1024)(128)(4,1)} %bitcast.57), calls=%async_computation.3 | async-start | bytes 8388608
  119.4 7.0 %slice-start.3 = ((s8[16777216]{0:T(1024)(128)(4,1)}), s8[4194304]{0:T(1024)(128)(4,1)S(1)}, s32[]{:S(2)}) async-start(s8[16777216]{0:T(1024)(128)(4,1)} %bitcast.57), calls=%async_computation.4 | async-start | bytes 8388608
  135.2 3.5 %collective-permute-start.8 = (bf16[4,192,1024]{2,1,0:T(8,128)(2,1)S(1)}, bf16[4,192,1024]{2,1,0:T(8,128)(2,1)S(1)}, u32[]{:S(2)}, u32[]{:S(2)}) collective-permute-start(bf16[4,192,1024]{2,1,0:T(8,128)(2,1)S(1)} %project.6), channel_id=1, source_target_pairs={{0,1},{1,0},{2,3},{3,2},{4,5},{5,4},{6,7},{7,6},{8,9},{9,8},{10,11... | collective-permute-start | bytes 4718600 | tf_op jit(solution)/shard_map/ppermute | solution.py:318
  135.3 8.8 %collective-permute-start.3 = (bf16[4,192,1024]{2,1,0:T(8,128)(2,1)S(1)}, bf16[4,192,1024]{2,1,0:T(8,128)(2,1)S(1)}, u32[]{:S(2)}, u32[]{:S(2)}) collective-permute-start(bf16[4,192,1024]{2,1,0:T(8,128)(2,1)S(1)} %project.4), channel_id=1, source_target_pairs={{0,1},{1,0},{2,3},{3,2},{4,5},{5,4},{6,7},{7,6},{8,9},{9,8},{10,11... | collective-permute-start | bytes 4718600 | tf_op jit(solution)/shard_map/ppermute | solution.py:318
  138.7 1.1 copy-start.3
  139.8 8.8 %collective-permute-start.11 = (bf16[96,1024]{1,0:T(8,128)(2,1)S(1)}, bf16[96,1024]{1,0:T(8,128)(2,1)S(1)}, u32[]{:S(2)}, u32[]{:S(2)}) collective-permute-start(bf16[96,1024]{1,0:T(8,128)(2,1)S(1)} %get-tuple-element.51), channel_id=1, source_target_pairs={{0,6},{1,7},{2,0},{3,1},{4,2},{5,3},{6,4},{7,5},{8,14},{9,15},{10,... | collective-permute-start | bytes 589832 | tf_op jit(solution)/shard_map/ppermute | solution.py:275
  143.9 9.1 %collective-permute-start.9 = (bf16[96,1024]{1,0:T(8,128)(2,1)S(1)}, bf16[96,1024]{1,0:T(8,128)(2,1)S(1)}, u32[]{:S(2)}, u32[]{:S(2)}) collective-permute-start(bf16[96,1024]{1,0:T(8,128)(2,1)S(1)} %get-tuple-element.50), channel_id=1, source_target_pairs={{0,2},{1,3},{2,4},{3,5},{4,6},{5,7},{6,0},{7,1},{8,10},{9,11},{10,... | collective-permute-start | bytes 589832 | tf_op jit(solution)/shard_map/ppermute | solution.py:274
  144.0 1.2 copy-start.2
  145.2 8.6 %collective-permute-start.6 = (bf16[96,1024]{1,0:T(8,128)(2,1)S(1)}, bf16[96,1024]{1,0:T(8,128)(2,1)S(1)}, u32[]{:S(2)}, u32[]{:S(2)}) collective-permute-start(bf16[96,1024]{1,0:T(8,128)(2,1)S(1)} %get-tuple-element.49), channel_id=1, source_target_pairs={{0,6},{1,7},{2,0},{3,1},{4,2},{5,3},{6,4},{7,5},{8,14},{9,15},{10,... | collective-permute-start | bytes 589832 | tf_op jit(solution)/shard_map/ppermute | solution.py:275
  148.6 9.3 %collective-permute-start.4 = (bf16[96,1024]{1,0:T(8,128)(2,1)S(1)}, bf16[96,1024]{1,0:T(8,128)(2,1)S(1)}, u32[]{:S(2)}, u32[]{:S(2)}) collective-permute-start(bf16[96,1024]{1,0:T(8,128)(2,1)S(1)} %get-tuple-element.48), channel_id=1, source_target_pairs={{0,2},{1,3},{2,4},{3,5},{4,6},{5,7},{6,0},{7,1},{8,10},{9,11},{10,... | collective-permute-start | bytes 589832 | tf_op jit(solution)/shard_map/ppermute | solution.py:274
  149.5 13.4 %collective-permute-start.12 = (bf16[192,1024]{1,0:T(8,128)(2,1)}, bf16[192,1024]{1,0:T(8,128)(2,1)S(1)}, u32[]{:S(2)}, u32[]{:S(2)}) collective-permute-start(bf16[192,1024]{1,0:T(8,128)(2,1)} %pad_maximum_fusion.4), channel_id=1, source_target_pairs={{0,6},{1,7},{2,0},{3,1},{4,2},{5,3},{6,4},{7,5},{8,14},{9,15},{10,... | collective-permute-start | bytes 1179656 | tf_op jit(solution)/shard_map/ppermute | solution.py:282
  153.8 13.6 %collective-permute-start.10 = (bf16[192,1024]{1,0:T(8,128)(2,1)}, bf16[192,1024]{1,0:T(8,128)(2,1)}, u32[]{:S(2)}, u32[]{:S(2)}) collective-permute-start(bf16[192,1024]{1,0:T(8,128)(2,1)} %pad_maximum_fusion.3), channel_id=1, source_target_pairs={{0,2},{1,3},{2,4},{3,5},{4,6},{5,7},{6,0},{7,1},{8,10},{9,11},{10,... | collective-permute-start | bytes 1179656 | tf_op jit(solution)/shard_map/ppermute | solution.py:281
  154.7 14.9 %collective-permute-start.7 = (bf16[192,1024]{1,0:T(8,128)(2,1)}, bf16[192,1024]{1,0:T(8,128)(2,1)}, u32[]{:S(2)}, u32[]{:S(2)}) collective-permute-start(bf16[192,1024]{1,0:T(8,128)(2,1)} %pad_maximum_fusion.2), channel_id=1, source_target_pairs={{0,6},{1,7},{2,0},{3,1},{4,2},{5,3},{6,4},{7,5},{8,14},{9,15},{10,... | collective-permute-start | bytes 1179656 | tf_op jit(solution)/shard_map/ppermute | solution.py:282
  158.7 15.0 %collective-permute-start.5 = (bf16[192,1024]{1,0:T(8,128)(2,1)}, bf16[192,1024]{1,0:T(8,128)(2,1)}, u32[]{:S(2)}, u32[]{:S(2)}) collective-permute-start(bf16[192,1024]{1,0:T(8,128)(2,1)} %pad_maximum_fusion.1), channel_id=1, source_target_pairs={{0,2},{1,3},{2,4},{3,5},{4,6},{5,7},{6,0},{7,1},{8,10},{9,11},{10,... | collective-permute-start | bytes 1179656 | tf_op jit(solution)/shard_map/ppermute | solution.py:281
  176.6 1.2 collective-permute-start.13
  177.9 3.6 %collective-permute-start.16 = (f32[3,128]{1,0:T(4,128)S(1)}, f32[3,128]{1,0:T(4,128)S(1)}, u32[]{:S(2)}, u32[]{:S(2)}) collective-permute-start(f32[3,128]{1,0:T(4,128)S(1)} %bitcast_add_fusion.2), channel_id=1, source_target_pairs={{0,6},{1,7},{2,0},{3,1},{4,2},{5,3},{6,4},{7,5},{8,14},{9,15},{10,... | collective-permute-start | bytes 4616 | tf_op jit(solution)/shard_map/ppermute | solution.py:331
  177.9 5.1 %collective-permute-start.15 = (f32[3,128]{1,0:T(4,128)S(1)}, f32[3,128]{1,0:T(4,128)S(1)}, u32[]{:S(2)}, u32[]{:S(2)}) collective-permute-start(f32[3,128]{1,0:T(4,128)S(1)} %bitcast_add_fusion.2), channel_id=1, source_target_pairs={{0,4},{1,5},{2,6},{3,7},{4,0},{5,1},{6,2},{7,3},{8,12},{9,13},{10,... | collective-permute-start | bytes 4616 | tf_op jit(solution)/shard_map/ppermute | solution.py:331
  179.0 5.1 %collective-permute-start.14 = (f32[3,128]{1,0:T(4,128)S(1)}, f32[3,128]{1,0:T(4,128)S(1)}, u32[]{:S(2)}, u32[]{:S(2)}) collective-permute-start(f32[3,128]{1,0:T(4,128)S(1)} %bitcast_add_fusion.2), channel_id=1, source_target_pairs={{0,2},{1,3},{2,4},{3,5},{4,6},{5,7},{6,0},{7,1},{8,10},{9,11},{10,... | collective-permute-start | bytes 4616 | tf_op jit(solution)/shard_map/ppermute | solution.py:331

commit v4 on v3

v4 whole, which is shorter than its diff:
```python
import functools

import jax
import jax.numpy as jnp
from jax import lax
from jax.experimental import pallas as pl
from jax.experimental.pallas import tpu as pltpu
from jax.sharding import PartitionSpec as P

D = 8192
HD = 128
NEW = 16
PAGE = 64
PATH_PAGES = 16
SHARED = 8
FAM = 4
RANKS = 16
PAIR = 15
ROOTS = 12
SHARE = 3
GROUPS = 2
LOG2E = 1.4426950408889634
MIB = 1024 * 1024


def pack_kernel(
    rank_ref,
    parent_hbm,
    table_hbm,
    pool_hbm,
    near0_ref,
    near1_ref,
    near2_ref,
    near3_ref,
    send_ref,
    parent_ref,
    table_ref,
    pool_ref,
    wanted_ref,
    wanted_smem,
    sems,
):
    pages_dev = pool_ref.shape[0]
    slots, nodes = table_ref.shape
    base = rank_ref[0] * pages_dev
    table_copy = pltpu.make_async_copy(table_hbm, table_ref, sems.at[0])
    parent_copy = pltpu.make_async_copy(parent_hbm, parent_ref, sems.at[1])
    pool_copy = pltpu.make_async_copy(pool_hbm, pool_ref, sems.at[2])
    table_copy.start()
    parent_copy.start()
    pool_copy.start()
    table_copy.wait()
    table = table_ref[...]
    height = -(-pages_dev // 16) * 16
    row = lax.broadcasted_iota(jnp.int32, (height, nodes), 0)
    hits = jnp.zeros((height, nodes), jnp.float32)
    for page in range(pages_dev):
        hit = jnp.max((table == base + page).astype(jnp.float32), axis=0, keepdims=True)
        hits = jnp.where(row == page, hit, hits)
    node = lax.broadcasted_iota(jnp.int32, (nodes, 128), 0)
    begin = lax.broadcasted_iota(jnp.int32, (nodes, 128), 1) * (nodes // RANKS)
    belongs = ((node >= begin) & (node < begin + nodes // RANKS)).astype(jnp.bfloat16)
    present = jnp.dot(hits.astype(jnp.bfloat16), belongs, preferred_element_type=jnp.float32) > 0
    low = lax.broadcasted_iota(jnp.int32, (height, height), 0)
    high = lax.broadcasted_iota(jnp.int32, (height, height), 1)
    before = jnp.dot(
        (high < low).astype(jnp.bfloat16), present.astype(jnp.bfloat16), preferred_element_type=jnp.float32
    )
    place = jnp.where(present, before, -1.0)
    page_id = lax.broadcasted_iota(jnp.int32, (height, 128), 0).astype(jnp.float32)
    line = lax.broadcasted_iota(jnp.int32, (16, 128), 0)
    wanted = jnp.zeros((16, 128), jnp.float32)
    for slot in range(PAIR):
        page = jnp.sum(jnp.where(place == slot, page_id, 0.0), axis=0, keepdims=True)
        wanted = jnp.where(line == slot, page, wanted)
    wanted_ref[...] = wanted.astype(jnp.int32)
    copy = pltpu.make_async_copy(wanted_ref, wanted_smem, sems.at[3])
    copy.start()
    parent_copy.wait()
    x = rank_ref[0] % 4
    per_rank = nodes // RANKS

    @pl.loop(0, RANKS)
    def _(dest):
        for i in range(SHARE):
            named = jnp.maximum(parent_ref[dest * per_rank + ROOTS + x * SHARE + i], 0)
            away = (x + 4 - named // per_rank % 4) % 4
            rows = pl.ds(pl.multiple_of(named % per_rank * NEW, NEW), NEW)
            picked = near0_ref[rows, :]
            for d, ref in ((1, near1_ref), (2, near2_ref), (3, near3_ref)):
                picked = jnp.where(away == d, ref[rows, :], picked)
            send_ref[dest, PAIR, i * NEW : (i + 1) * NEW, :] = picked

    copy.wait()
    pool_copy.wait()

    @pl.loop(0, RANKS)
    def _(dest):
        for slot in range(PAIR):
            page = jnp.clip(wanted_smem[slot, dest], 0, pages_dev - 1)
            send_ref[dest, slot] = pool_ref[page]


def pack(rank, parent, table, pool, near):
    smem = pl.BlockSpec(memory_space=pltpu.SMEM)
    vmem = pl.BlockSpec(memory_space=pltpu.VMEM)
    return pl.pallas_call(
        pack_kernel,
        out_shape=pltpu.VMEM((RANKS, PAIR + 1) + pool.shape[1:], pool.dtype),
        in_specs=[smem] + [pl.BlockSpec(memory_space=pltpu.HBM)] * 3 + [vmem] * 4,
        out_specs=vmem,
        scratch_shapes=[
            pltpu.SMEM(parent.shape, jnp.int32),
            pltpu.VMEM(table.shape, jnp.int32),
            pltpu.VMEM(pool.shape, pool.dtype),
            pltpu.VMEM((16, 128), jnp.int32),
            pltpu.SMEM((16, 128), jnp.int32),
            pltpu.SemaphoreType.DMA((4,)),
        ],
        compiler_params=pltpu.CompilerParams(vmem_limit_bytes=55 * MIB),
        name="pack",
    )(rank, parent, table, pool, *near)


def attend_family(first, node, idx_ref, len_ref, above_ref, q_ref, fresh_ref, pages_ref, attn_ref):
    scale = HD ** (-0.5) * LOG2E
    nt = (((1,), (1,)), ((), ()))

    def pages(n, slot):
        return jnp.concatenate([pages_ref[idx_ref[n * PATH_PAGES + slot + s]] for s in range(SHARED)], axis=0)

    heads = q_ref.shape[1] // HD
    span = heads * NEW
    shared = pages(node, 0)
    queries = []
    for i in range(FAM):
        rows = q_ref[first + i * NEW : first + (i + 1) * NEW, :]
        queries.append(jnp.concatenate([rows[:, h * HD : (h + 1) * HD] for h in range(heads)], axis=0))
    s_shared = lax.dot_general(
        jnp.concatenate(queries, axis=0), shared[:, :HD], nt, preferred_element_type=jnp.float32
    )
    half = SHARED * PAGE // 2
    own, s_own = [], []
    for i in range(FAM):
        above = above_ref[node + i]
        spot = jnp.maximum(above, 0)
        upper = pages_ref[spot // PAGE, pl.ds(pl.multiple_of(spot % PAGE, NEW), NEW), :]
        fresh = fresh_ref[first + i * NEW : first + (i + 1) * NEW, :]
        kv = jnp.concatenate([pages(node + i, SHARED), fresh, upper], axis=0)
        s = lax.dot_general(queries[i], kv[:, :HD], nt, preferred_element_type=jnp.float32)
        late = s[:, half:]
        spot = lax.broadcasted_iota(jnp.int32, late.shape, 1) + SHARED * PAGE + half
        token = lax.broadcasted_iota(jnp.int32, late.shape, 0) % NEW
        key = spot - PATH_PAGES * PAGE
        limit = jnp.where(above >= 0, 2 * NEW, NEW)
        allowed = (spot < len_ref[node + i]) | ((key >= 0) & (key <= token)) | ((key >= NEW) & (key < limit))
        own.append(kv)
        s_own.append(jnp.concatenate([s[:, :half], jnp.where(allowed, late, -jnp.inf)], axis=1))
    tops = [
        jnp.maximum(
            jnp.max(s_shared[i * span : (i + 1) * span], axis=1, keepdims=True),
            jnp.max(s_own[i], axis=1, keepdims=True),
        )
        for i in range(FAM)
    ]
    w_own = [jnp.exp2((s_own[i] - tops[i]) * scale).astype(jnp.bfloat16) for i in range(FAM)]
    w_shared = jnp.exp2((s_shared - jnp.concatenate(tops, axis=0)) * scale).astype(jnp.bfloat16)
    ones = jnp.ones((own[0].shape[0], HD), jnp.bfloat16)
    accum = [
        jnp.dot(w_own[i], jnp.concatenate([own[i][:, HD:], ones], axis=1), preferred_element_type=jnp.float32)
        for i in range(FAM)
    ]
    accum = jnp.concatenate(accum, axis=0) + jnp.dot(
        w_shared, jnp.concatenate([shared[:, HD:], ones[: SHARED * PAGE]], axis=1), preferred_element_type=jnp.float32
    )
    attn = (accum[:, :HD] / accum[:, HD:]).astype(jnp.bfloat16)
    for i in range(FAM):
        for h in range(heads):
            block = attn[i * span + h * NEW : i * span + (h + 1) * NEW, :]
            attn_ref[first + i * NEW : first + (i + 1) * NEW, h * HD : (h + 1) * HD] = block


def attend_kernel(idx_ref, len_ref, above_ref, q_ref, fresh_ref, pages_ref, attn_ref):
    for f in range(q_ref.shape[0] // (FAM * NEW)):
        attend_family(f * FAM * NEW, f * FAM, idx_ref, len_ref, above_ref, q_ref, fresh_ref, pages_ref, attn_ref)


def attend(idx, lengths, above, queries, fresh, received):
    rows, width = queries.shape
    smem = pl.BlockSpec(memory_space=pltpu.SMEM)
    vmem = pl.BlockSpec(memory_space=pltpu.VMEM)
    return pl.pallas_call(
        attend_kernel,
        out_shape=jax.ShapeDtypeStruct((rows, width), jnp.bfloat16),
        in_specs=[smem, smem, smem, vmem, vmem, vmem],
        out_specs=vmem,
        compiler_params=pltpu.CompilerParams(vmem_limit_bytes=24 * MIB),
        cost_estimate=pl.CostEstimate(
            flops=4 * rows * width * 1056 * 4, bytes_accessed=received.size * 2 + 4 * rows * width, transcendentals=rows * 8 * 1056
        ),
        name="attend",
    )(idx, lengths, above, queries, fresh, received)


def project_kernel(order_ref, attn_ref, w_ref, out_ref):
    count, rows, cols = out_ref.shape

    @pl.loop(0, count)
    def _(b):
        w = w_ref[:, pl.ds(pl.multiple_of(order_ref[b] * cols, cols), cols)]
        out_ref[b] = jnp.dot(attn_ref[...], w, preferred_element_type=jnp.float32).astype(jnp.bfloat16)


def project(order, attn, w_out):
    rows, depth = attn.shape
    cols = w_out.shape[1] // 8
    count = order.shape[0]
    smem = pl.BlockSpec(memory_space=pltpu.SMEM)
    vmem = pl.BlockSpec(memory_space=pltpu.VMEM)
    return pl.pallas_call(
        project_kernel,
        out_shape=jax.ShapeDtypeStruct((count, rows, cols), jnp.bfloat16),
        in_specs=[smem, vmem, vmem],
        out_specs=vmem,
        compiler_params=pltpu.CompilerParams(vmem_limit_bytes=12 * MIB),
        cost_estimate=pl.CostEstimate(
            flops=2 * rows * depth * cols * count, bytes_accessed=rows * cols * count * 2, transcendentals=0
        ),
        name="project",
    )(order, attn, w_out)


def shift(dy, dx):
    return [(s, (s // 4 + dy) % 4 * 4 + (s % 4 + dx) % 4) for s in range(RANKS)]


def turn(d):
    return [(t, (t + 2 * d) % 8) for t in range(8)]


def above_of(parent, rank, nodes):
    own = lax.dynamic_slice_in_dim(parent, rank * nodes, nodes)
    child = jnp.arange(nodes, dtype=jnp.int32) - ROOTS
    source = jnp.maximum(own, 0) // nodes // 4 * 4 + child // SHARE
    row = (source * (PAIR + 1) + PAIR) * PAGE + child % SHARE * NEW
    return jnp.where((own >= 0) & (child >= 0), row, -1)


def slots_of(table, ranks, pages_dev):
    owner = table // pages_dev
    page = jnp.arange(ranks * pages_dev, dtype=jnp.int32)
    present = jnp.any(table[None, :] == page[:, None], axis=1)
    place = jnp.sum(
        (present[None, :] & (page[None, :] // pages_dev == owner[:, None]) & (page[None, :] < table[:, None])).astype(jnp.int32),
        axis=1,
    )
    return owner * (PAIR + 1) + place


def far_kernel(kept_ref, back_ref, *out_refs):
    rows = out_refs[0].shape[0]
    for i, ref in enumerate(out_refs):
        part = pl.ds(i * rows, rows)
        ref[...] = (kept_ref[1, part].astype(jnp.float32) + back_ref[part].astype(jnp.float32)).astype(jnp.bfloat16)


def near_kernel(first, kept_ref, back_ref, from_low_ref, from_high_ref, up_ref, down_ref):
    half = from_low_ref.shape[0]
    low, high = pl.ds(0, half), pl.ds(half, half)

    def pair(i, start):
        part = pl.ds(first + start, half)
        return kept_ref[i, part].astype(jnp.float32) + back_ref[i, part].astype(jnp.float32)

    up_ref[low] = (pair(0, 0) + from_low_ref[...].astype(jnp.float32)).astype(jnp.bfloat16)
    up_ref[high] = pair(0, half).astype(jnp.bfloat16)
    down_ref[low] = pair(1, 0).astype(jnp.bfloat16)
    down_ref[high] = (pair(1, half) + from_high_ref[...].astype(jnp.float32)).astype(jnp.bfloat16)


def last_kernel(first, kept_ref, back_ref, up_ref, down_ref, residual_ref, mixed_ref, power_ref):
    part = pl.ds(first, up_ref.shape[0])
    mixed = residual_ref[part].astype(jnp.float32)
    for term in (kept_ref[2, part], back_ref[2, part], up_ref[...], down_ref[...]):
        mixed = mixed + term.astype(jnp.float32)
    mixed_ref[...] = mixed
    power_ref[...] = lax.dot_general(
        jnp.ones((8, mixed.shape[1]), jnp.float32),
        mixed * mixed,
        (((1,), (1,)), ((), ())),
        precision=lax.Precision.HIGHEST,
        preferred_element_type=jnp.float32,
    )


def local(kernel, name, outs, *args):
    vmem = pl.BlockSpec(memory_space=pltpu.VMEM)
    return pl.pallas_call(
        kernel,
        out_shape=[jax.ShapeDtypeStruct(shape, dtype) for shape, dtype in outs],
        in_specs=[vmem] * len(args),
        out_specs=[vmem] * len(outs),
        compiler_params=pltpu.CompilerParams(vmem_limit_bytes=12 * MIB),
        name=name,
    )(*args)


def body(queries, fresh_kv, kv_pool, page_table, path_len, parent, w_out, residual, gain):
    rank = lax.axis_index("dp")
    tensor_rank = lax.axis_index("tensor")
    tensors = lax.axis_size("tensor")
    rows = queries.shape[0]
    nodes = rows // NEW
    pages_dev = kv_pool.shape[0]
    roots = fresh_kv[: ROOTS * NEW]
    near = [roots] + [lax.ppermute(roots, "dp", shift(0, d)) for d in (1, 2, 3)]
    send = pack(rank.reshape(1), parent, page_table.T, kv_pool, near)

    own_table = lax.dynamic_slice_in_dim(page_table, rank * nodes, nodes).reshape(-1)
    idx = slots_of(own_table, RANKS, pages_dev)
    lengths = lax.dynamic_slice_in_dim(path_len, rank * nodes, nodes)
    above = above_of(parent, rank, nodes)
    z, core = tensor_rank // 2, tensor_rank % 2
    far, rest = (z + 2) % 4 * 2, (z + jnp.array([1, 3, 0], jnp.int32)) % 4 * 2
    far = jnp.stack([far + 1 - core, far + core])
    other, same = rest + 1 - core, rest + core

    send, idx, lengths, above, far, other, same = lax.optimization_barrier((send, idx, lengths, above, far, other, same))
    received = lax.all_to_all(send, "dp", split_axis=0, concat_axis=0, tiled=True)
    received, queries, fresh_kv, w_out, residual, gain = lax.optimization_barrier(
        (received, queries, fresh_kv, w_out, residual, gain)
    )
    received = received.reshape(RANKS * (PAIR + 1), PAGE, kv_pool.shape[2])
    attn = attend(idx, lengths, above, queries, fresh_kv, received)

    swap = [(t, t ^ 1) for t in range(tensors)]
    cols = D // tensors
    mine = lax.dynamic_slice_in_dim(residual, tensor_rank * cols, cols, 1)
    group = rows // GROUPS
    both = project(far, attn, w_out)
    both, attn = lax.optimization_barrier((both, attn))
    far_back = lax.ppermute(both[0], "tensor", swap)
    away = project(other, attn, w_out)
    far_back, away, attn = lax.optimization_barrier((far_back, away, attn))
    back = lax.ppermute(away, "tensor", swap)
    halves = [((group // 2, cols), jnp.bfloat16)] * (2 * GROUPS)
    sent = local(far_kernel, "far", halves, both, far_back)
    *sent, attn = lax.optimization_barrier((*sent, attn))
    low = [lax.ppermute(sent[2 * g], "tensor", turn(1)) for g in range(GROUPS)]
    high = [lax.ppermute(sent[2 * g + 1], "tensor", turn(-1)) for g in range(GROUPS)]
    kept = project(same, attn, w_out)
    whole = ((group, cols), jnp.bfloat16)
    ups, downs = [], []
    for g in range(GROUPS):
        up, down = local(
            functools.partial(near_kernel, g * group), "near", [whole, whole], kept, back, low[g], high[g]
        )
        ups.append(lax.ppermute(up, "tensor", turn(1)))
        downs.append(lax.ppermute(down, "tensor", turn(-1)))
    outs = [((group, cols), jnp.float32), ((8, group), jnp.float32)]
    done = [
        local(functools.partial(last_kernel, g * group), "last", outs, kept, back, ups[g], downs[g], mine)
        for g in range(GROUPS)
    ]

    mixed = jnp.concatenate([m for m, _ in done], axis=0)
    power = jnp.concatenate([p for _, p in done], axis=1)
    power = power + lax.ppermute(power, "tensor", swap)
    total = power
    for d in (1, 2, 3):
        total = total + lax.ppermute(power, "tensor", turn(d))
    norm = lax.rsqrt(total[0].reshape(rows, 1) / D + 1e-05)
    own_gain = lax.dynamic_slice_in_dim(gain, tensor_rank * cols, cols)
    normed = mixed * norm * own_gain.astype(jnp.float32)
    return (mixed.astype(jnp.bfloat16), normed.astype(jnp.bfloat16))


def solution(mesh):
    return jax.shard_map(
        body,
        mesh=mesh,
        in_specs=(
            P("dp", "tensor"),
            P("dp", "tensor"),
            P("dp", None, "tensor"),
            P(),
            P(),
            P(),
            P("tensor", None),
            P("dp", None),
            P(),
        ),
        out_specs=(P("dp", "tensor"), P("dp", "tensor")),
        check_vma=False,
    )
```

time: 188 us -> 177 us (0.941)
  other arithmetic: 13.8 us -> 4.31 us
  waiting for transfers between devices: 18.3 us -> 13.4 us
  local copies, waits for them, and re-layouts: 4.21 us -> 6.36 us
    ppermute x11 -> x12, waiting for transfers between devices: 13.6 us -> 8.15 us  [the longest x2 8.12 us: body(): ups.append(lax.ppermute(up, 'tensor', turn(1)))]
    concatenate x5 -> x1, other arithmetic: 3.89 us -> 0.09 us  [body(): power = jnp.concatenate([p for _, p in done], axis=1)]
    add x4 -> x1, other arithmetic: 3.72 us -> 0.67 us  [body(): other, same = (rest + 1 - core, rest + core)]
    ppermute x3, starting transfers between devices: 2.03 us -> 4.01 us  [body(): total = total + lax.ppermute(power, 'tensor', turn(d))]
    pallas_call x6 -> x9, Pallas kernels: 19.7 us -> 18.6 us  [the longest x3 9.53 us: project(): pl.pallas_call(project_kernel, out_shape=jax.ShapeDtypeStruct((count, row...]
    ppermute x11 -> x12, starting transfers between devices: 19 us -> 18.8 us  [the longest x2 5.74 us: body(): downs.append(lax.ppermute(down, 'tensor', turn(-1)))]
  transfers between devices with their start and end apart: 17 -> 17, of which waited for: 8 -> 5; matrix products, arithmetic and copies ran while one was open for 5% -> 3% of each run, Pallas kernels for 5% -> 6%
where the time goes in v4:
time: 177 us; the launch traced here: 175 us
  blocking collectives  102 us (58%)
  Pallas kernels  25.1 us (14%)
  starting transfers between devices  23.4 us (13%)
  waiting for transfers between devices  13.4 us (8%)
  local copies, waits for them, and re-layouts  6.36 us (4%)
  other arithmetic  4.31 us (2%)
    all_to_all x1, blocking collectives, body(): lax.all_to_all(send, 'dp', split_axis=0, concat_axis=0, tiled=True)  102 us
    pallas_call x3, Pallas kernels, project(): pl.pallas_call(project_kernel, out_shape=jax.ShapeDtypeStruct((count, row...  9.53 us
    ppermute x2, waiting for transfers between devices, body(): ups.append(lax.ppermute(up, 'tensor', turn(1)))  8.12 us
    pallas_call x1, Pallas kernels, attend(): pl.pallas_call(attend_kernel, out_shape=jax.ShapeDtypeStruct((rows, width...  6.54 us
    ppermute x2, starting transfers between devices, body(): downs.append(lax.ppermute(down, 'tensor', turn(-1)))  5.74 us
    ppermute x2, starting transfers between devices, body(): lax.ppermute(sent[2 * g + 1], 'tensor', turn(-1))  5.44 us
    pallas_call x5, Pallas kernels, local(): pl.pallas_call(kernel, out_shape=[jax.ShapeDtypeStruct(shape, dtype) for...  5.17 us
    ppermute x3, starting transfers between devices, body(): near = [roots] + [lax.ppermute(roots, 'dp', shift(0, d)) for d in (1, 2, 3)]  4.82 us
  transfers between devices with their start and end apart: 17, of which 5 were waited for; matrix products, arithmetic and copies ran while one was open for 3% of the time, Pallas kernels for 6%

profile of v4, /device:TPU:2, one launch (start us, length us, event | category | flops | bytes accessed | tf_op | source)
XLA Modules:
  0.0 175.3 jit_solution(7072467580769931535)
XLA Ops:
  0.6 0.9 slice.9.near0_ref
  1.5 0.5 collective-permute-start.2
  2.1 2.5 %collective-permute-start.1 = (bf16[192,256]{1,0:T(8,128)(2,1)S(1)}, bf16[192,256]{1,0:T(8,128)(2,1)S(1)}, u32[]{:S(2)}, u32[]{:S(2)}) collective-permute-start(bf16[192,256]{1,0:T(8,128)(2,1)S(1)} %slice.9.near0_ref), channel_id=1, source_target_pairs={{0,16},{8,24},{16,0},{24,8},{32,48},{40,56},{48,32},{56,40},{64,80... | collective-permute-start | bytes 294920 | tf_op jit(solution)/shard_map/ppermute | solution.py:316
  4.6 1.8 %collective-permute-start = (bf16[192,256]{1,0:T(8,128)(2,1)S(1)}, bf16[192,256]{1,0:T(8,128)(2,1)S(1)}, u32[]{:S(2)}, u32[]{:S(2)}) collective-permute-start(bf16[192,256]{1,0:T(8,128)(2,1)S(1)} %slice.9.near0_ref), channel_id=1, source_target_pairs={{0,8},{8,16},{16,24},{24,0},{32,40},{40,48},{48,56},{56,32},{64,72... | collective-permute-start | bytes 294920 | tf_op jit(solution)/shard_map/ppermute | solution.py:316
  6.4 0.8 constant_dynamic-slice_fusion.1
  7.2 0.1 copy.13
  7.3 0.1 reshape.75
  7.3 0.2 fusion
  7.6 0.8 dynamic_slice.16.len_ref
  8.3 0.8 and_select_fusion.5.above_ref
  9.1 0.7 broadcast_add_fusion
  9.8 0.3 convert_reduce_fusion
  10.1 0.1 pad_add_fusion.order_ref
  10.3 0.6 copy-done.5
  10.9 3.9 %pack.1 = bf16[16,16,64,256]{3,2,1,0:T(8,128)(2,1)S(1)} custom-call(s32[1]{0:T(128)} %bitcast.rank_ref, s32[384]{0:T(512)} %parent_hbm.1, s32[16,384]{1,0:T(8,128)} %bitcast.10, bf16[45,64,256]{2,1,0:T(8,128)(2,1)} %pool_hbm.1, bf16[192,256]{1,0:T(8,128)(2,1)} %copy-done.4, bf16[192,256]{1,0:T(8,128)(2,1)} %copy-done.7, bf16[192,256]{1,0:T(8,128)(2,1)} %copy-done.6, ...), custom_call_target="tpu_custom_call" | custom-call | tf_op jit(solution)/shard_map/pack/pallas_call | solution.py:107
  14.9 101.7 %all_to_all.5 = bf16[16,16,64,256]{3,2,1,0:T(8,128)(2,1)S(1)} all-to-all(bf16[16,16,64,256]{3,2,1,0:T(8,128)(2,1)S(1)} %pack.1), channel_id=1, replica_groups=mesh['dp'=16,'tensor'=8] {'dp'}, dimensions={0} | all-to-all | bytes 16777216 | tf_op jit(solution)/shard_map/all_to_all | solution.py:329
  116.6 6.5 %attend.1.attn_ref = bf16[384,1024]{1,0:T(8,128)(2,1)S(1)} custom-call(s32[384]{0:T(512)S(1)} %multiply_add_fusion.idx_ref, s32[24]{0:T(128)S(1)} %dynamic_slice.16.len_ref, s32[24]{0:T(128)S(1)} %and_select_fusion.5.above_ref, bf16[384,1024]{1,0:T(8,128)(2,1)S(1)} %copy-done.3, bf16[384,256]{1,0:T(8,128)(2,1)S(1)} %copy-done.2, ...), custom_call_target="tpu_custom_call" | custom-call | flops 6643777536 | bytes 9961472 | tf_op jit(solution)/shard_map/attend/pallas_call | solution.py:192
  123.2 2.5 %project.3.kept_ref = bf16[2,384,1024]{2,1,0:T(8,128)(2,1)S(1)} custom-call(s32[2]{0:T(128)S(1)} %pad_add_fusion.order_ref, bf16[384,1024]{1,0:T(8,128)(2,1)S(1)} %attend.1.attn_ref, bf16[1024,8192]{1,0:T(8,128)(2,1)S(1)} %bitcast.8), custom_call_target="tpu_custom_call" | custom-call | flops 1610612736 | bytes 1572864 | tf_op jit(solution)/shard_map/project/pallas_call | solution.py:220
  125.8 0.1 collective-permute-start.3
  125.9 3.5 %project.4 = bf16[3,384,1024]{2,1,0:T(8,128)(2,1)S(1)} custom-call(s32[3]{0:T(128)S(1)} %add_subtract_fusion.order_ref, bf16[384,1024]{1,0:T(8,128)(2,1)S(1)} %attend.1.attn_ref, bf16[1024,8192]{1,0:T(8,128)(2,1)S(1)} %bitcast.8), custom_call_target="tpu_custom_call" | custom-call | flops 2415919104 | bytes 2359296 | tf_op jit(solution)/shard_map/project/pallas_call | solution.py:220
  129.4 0.6 collective-permute-start.4
  130.0 0.2 far.1
  130.2 2.0 %collective-permute-start.5 = (bf16[96,1024]{1,0:T(8,128)(2,1)S(1)}, bf16[96,1024]{1,0:T(8,128)(2,1)S(1)}, u32[]{:S(2)}, u32[]{:S(2)}) collective-permute-start(bf16[96,1024]{1,0:T(8,128)(2,1)S(1)} %get-tuple-element.58), channel_id=1, source_target_pairs={{0,2},{1,3},{2,4},{3,5},{4,6},{5,7},{6,0},{7,1},{8,10},{9,11},{10,... | collective-permute-start | bytes 589832 | tf_op jit(solution)/shard_map/ppermute | solution.py:349
  132.2 2.2 %collective-permute-start.6 = (bf16[96,1024]{1,0:T(8,128)(2,1)S(1)}, bf16[96,1024]{1,0:T(8,128)(2,1)S(1)}, u32[]{:S(2)}, u32[]{:S(2)}) collective-permute-start(bf16[96,1024]{1,0:T(8,128)(2,1)S(1)} %get-tuple-element.59), channel_id=1, source_target_pairs={{0,6},{1,7},{2,0},{3,1},{4,2},{5,3},{6,4},{7,5},{8,14},{9,15},{10,... | collective-permute-start | bytes 589832 | tf_op jit(solution)/shard_map/ppermute | solution.py:350
  134.4 3.2 %collective-permute-start.10 = (bf16[96,1024]{1,0:T(8,128)(2,1)S(1)}, bf16[96,1024]{1,0:T(8,128)(2,1)S(1)}, u32[]{:S(2)}, u32[]{:S(2)}) collective-permute-start(bf16[96,1024]{1,0:T(8,128)(2,1)S(1)} %get-tuple-element.65), channel_id=1, source_target_pairs={{0,6},{1,7},{2,0},{3,1},{4,2},{5,3},{6,4},{7,5},{8,14},{9,15},{10,... | collective-permute-start | bytes 589832 | tf_op jit(solution)/shard_map/ppermute | solution.py:350
  137.6 3.5 %project.5.kept_ref = bf16[3,384,1024]{2,1,0:T(8,128)(2,1)S(1)} custom-call(s32[3]{0:T(128)S(1)} %get-tuple-element.37.order_ref, bf16[384,1024]{1,0:T(8,128)(2,1)S(1)} %attend.1.attn_ref, bf16[1024,8192]{1,0:T(8,128)(2,1)S(1)} %bitcast.8), custom_call_target="tpu_custom_call" | custom-call | flops 2415919104 | bytes 2359296 | tf_op jit(solution)/shard_map/project/pallas_call | solution.py:220
  141.2 1.2 near.2
  142.4 0.7 collective-permute-start.7
  143.1 2.5 %collective-permute-start.8 = (bf16[192,1024]{1,0:T(8,128)(2,1)}, bf16[192,1024]{1,0:T(8,128)(2,1)S(1)}, u32[]{:S(2)}, u32[]{:S(2)}) collective-permute-start(bf16[192,1024]{1,0:T(8,128)(2,1)} %get-tuple-element.61), channel_id=1, source_target_pairs={{0,6},{1,7},{2,0},{3,1},{4,2},{5,3},{6,4},{7,5},{8,14},{9,15},{10,... | collective-permute-start | bytes 1179656 | tf_op jit(solution)/shard_map/ppermute | solution.py:359
  145.6 1.0 near.3
  146.7 3.2 %collective-permute-start.12 = (bf16[192,1024]{1,0:T(8,128)(2,1)}, bf16[192,1024]{1,0:T(8,128)(2,1)}, u32[]{:S(2)}, u32[]{:S(2)}) collective-permute-start(bf16[192,1024]{1,0:T(8,128)(2,1)} %get-tuple-element.67), channel_id=1, source_target_pairs={{0,6},{1,7},{2,0},{3,1},{4,2},{5,3},{6,4},{7,5},{8,14},{9,15},{10,... | collective-permute-start | bytes 1179656 | tf_op jit(solution)/shard_map/ppermute | solution.py:359
  149.9 0.7 dynamic-slice_convert_fusion
  150.6 1.2 constant_dynamic-slice_fusion.residual_ref
  151.8 4.1 %collective-permute-done.7.up_ref = bf16[192,1024]{1,0:T(8,128)(2,1)S(1)} collective-permute-done((bf16[192,1024]{1,0:T(8,128)(2,1)}, bf16[192,1024]{1,0:T(8,128)(2,1)S(1)}, u32[]{:S(2)}, u32[]{:S(2)}) %collective-permute-start.7) | collective-permute-done | bytes 393248 | tf_op jit(solution)/shard_map/ppermute | solution.py:358
  155.9 1.7 copy-done.1
  157.5 0.9 last.2
  158.4 4.0 %collective-permute-done.11.up_ref = bf16[192,1024]{1,0:T(8,128)(2,1)S(1)} collective-permute-done((bf16[192,1024]{1,0:T(8,128)(2,1)}, bf16[192,1024]{1,0:T(8,128)(2,1)S(1)}, u32[]{:S(2)}, u32[]{:S(2)}) %collective-permute-start.11) | collective-permute-done | bytes 393248 | tf_op jit(solution)/shard_map/ppermute | solution.py:358
  162.4 1.9 %last.3 = (f32[192,1024]{1,0:T(8,128)S(1)}, f32[8,192]{1,0:T(8,128)S(1)}) custom-call(bf16[3,384,1024]{2,1,0:T(8,128)(2,1)S(1)} %project.5.kept_ref, bf16[3,384,1024]{2,1,0:T(8,128)(2,1)S(1)} %copy-done.1, bf16[192,1024]{1,0:T(8,128)(2,1)S(1)} %collective-permute-done.11.up_ref, bf16[192,1024]{1,0:T(8,128)(2,1)} %collective-permute-done.12.down_ref, ...), custom_call_target="tpu_custom_call" | custom-call | tf_op jit(solution)/shard_map/last/pallas_call | solution.py:298
  164.3 0.1 pad_maximum_fusion
  164.4 0.1 constant_dynamic-update-slice_fusion.1
  164.5 1.1 collective-permute-done.13
  165.6 0.1 fusion.12
  165.7 3.1 %collective-permute-start.16 = (f32[8,384]{1,0:T(8,128)S(1)}, f32[8,384]{1,0:T(8,128)S(1)}, u32[]{:S(2)}, u32[]{:S(2)}) collective-permute-start(f32[8,384]{1,0:T(8,128)S(1)} %fusion.12), channel_id=1, source_target_pairs={{0,6},{1,7},{2,0},{3,1},{4,2},{5,3},{6,4},{7,5},{8,14},{9,15},{10,... | collective-permute-start | bytes 36872 | tf_op jit(solution)/shard_map/ppermute | solution.py:371
  168.7 0.9 collective-permute-start.14
  169.7 0.1 constant_dynamic-update-slice_fusion
  169.8 0.4 collective-permute-done.16
  170.1 3.8 %collective-permute-done.15 = f32[8,384]{1,0:T(8,128)S(1)} collective-permute-done((f32[8,384]{1,0:T(8,128)S(1)}, f32[8,384]{1,0:T(8,128)S(1)}, u32[]{:S(2)}, u32[]{:S(2)}) %collective-permute-start.15) | collective-permute-done | bytes 12320 | tf_op jit(solution)/shard_map/ppermute | solution.py:371
  174.0 1.4 multiply_convert_fusion
  (45 shorter events, 0.3 us)
Async XLA Ops:
  1.5 8.7 %copy-start.4 = (bf16[192,256]{1,0:T(8,128)(2,1)}, bf16[192,256]{1,0:T(8,128)(2,1)S(1)}, u32[]{:S(2)}) copy-start(bf16[192,256]{1,0:T(8,128)(2,1)S(1)} %slice.9.near0_ref) | copy-start | bytes 294916
  1.5 8.7 %collective-permute-start.2 = (bf16[192,256]{1,0:T(8,128)(2,1)S(1)}, bf16[192,256]{1,0:T(8,128)(2,1)S(1)}, u32[]{:S(2)}, u32[]{:S(2)}) collective-permute-start(bf16[192,256]{1,0:T(8,128)(2,1)S(1)} %slice.9.near0_ref), channel_id=1, source_target_pairs={{0,24},{8,0},{16,8},{24,16},{32,56},{40,32},{48,40},{56,48},{64,88... | collective-permute-start | bytes 294920 | tf_op jit(solution)/shard_map/ppermute | solution.py:316
  2.1 8.2 %collective-permute-start.1 = (bf16[192,256]{1,0:T(8,128)(2,1)S(1)}, bf16[192,256]{1,0:T(8,128)(2,1)S(1)}, u32[]{:S(2)}, u32[]{:S(2)}) collective-permute-start(bf16[192,256]{1,0:T(8,128)(2,1)S(1)} %slice.9.near0_ref), channel_id=1, source_target_pairs={{0,16},{8,24},{16,0},{24,8},{32,48},{40,56},{48,32},{56,40},{64,80... | collective-permute-start | bytes 294920 | tf_op jit(solution)/shard_map/ppermute | solution.py:316
  4.6 5.7 %collective-permute-start = (bf16[192,256]{1,0:T(8,128)(2,1)S(1)}, bf16[192,256]{1,0:T(8,128)(2,1)S(1)}, u32[]{:S(2)}, u32[]{:S(2)}) collective-permute-start(bf16[192,256]{1,0:T(8,128)(2,1)S(1)} %slice.9.near0_ref), channel_id=1, source_target_pairs={{0,8},{8,16},{16,24},{24,0},{32,40},{40,48},{48,56},{56,32},{64,72... | collective-permute-start | bytes 294920 | tf_op jit(solution)/shard_map/ppermute | solution.py:316
  10.2 0.6 copy-start.5
  10.2 0.7 copy-start.6
  10.2 0.7 copy-start.7
  14.8 101.8 %copy-start.2 = (bf16[384,256]{1,0:T(8,128)(2,1)S(1)}, bf16[384,256]{1,0:T(8,128)(2,1)}, u32[]{:S(2)}) copy-start(bf16[384,256]{1,0:T(8,128)(2,1)} %fresh_ref) | copy-start | bytes 589828
  14.8 101.8 %copy-start.3 = (bf16[384,1024]{1,0:T(8,128)(2,1)S(1)}, bf16[384,1024]{1,0:T(8,128)(2,1)}, u32[]{:S(2)}) copy-start(bf16[384,1024]{1,0:T(8,128)(2,1)} %q_ref) | copy-start | bytes 2359300
  14.8 108.3 %slice-start = ((s8[16777216]{0:T(1024)(128)(4,1)}), s8[4194304]{0:T(1024)(128)(4,1)S(1)}, s32[]{:S(2)}) async-start(s8[16777216]{0:T(1024)(128)(4,1)} %bitcast.7), calls=%async_computation.1 | async-start | bytes 8388608
  14.8 108.3 %slice-start.1 = ((s8[16777216]{0:T(1024)(128)(4,1)}), s8[4194304]{0:T(1024)(128)(4,1)S(1)}, s32[]{:S(2)}) async-start(s8[16777216]{0:T(1024)(128)(4,1)} %bitcast.7), calls=%async_computation.2 | async-start | bytes 8388608
  116.6 6.6 %slice-start.2 = ((s8[16777216]{0:T(1024)(128)(4,1)}), s8[4194304]{0:T(1024)(128)(4,1)S(1)}, s32[]{:S(2)}) async-start(s8[16777216]{0:T(1024)(128)(4,1)} %bitcast.7), calls=%async_computation.3 | async-start | bytes 8388608
  116.6 6.6 %slice-start.3 = ((s8[16777216]{0:T(1024)(128)(4,1)}), s8[4194304]{0:T(1024)(128)(4,1)S(1)}, s32[]{:S(2)}) async-start(s8[16777216]{0:T(1024)(128)(4,1)} %bitcast.7), calls=%async_computation.4 | async-start | bytes 8388608
  125.8 3.6 %collective-permute-start.3 = (bf16[384,1024]{1,0:T(8,128)(2,1)S(1)}, bf16[384,1024]{1,0:T(8,128)(2,1)S(1)}, u32[]{:S(2)}, u32[]{:S(2)}) collective-permute-start(bf16[384,1024]{1,0:T(8,128)(2,1)S(1)} %slice_bitcast_fusion), channel_id=1, source_target_pairs={{0,1},{1,0},{2,3},{3,2},{4,5},{5,4},{6,7},{7,6},{8,9},{9,8},{10,11... | collective-permute-start | bytes 2359304 | tf_op jit(solution)/shard_map/ppermute | solution.py:342
  129.4 11.7 %collective-permute-start.4 = (bf16[3,384,1024]{2,1,0:T(8,128)(2,1)S(1)}, bf16[3,384,1024]{2,1,0:T(8,128)(2,1)S(1)}, u32[]{:S(2)}, u32[]{:S(2)}) collective-permute-start(bf16[3,384,1024]{2,1,0:T(8,128)(2,1)S(1)} %project.4), channel_id=1, source_target_pairs={{0,1},{1,0},{2,3},{3,2},{4,5},{5,4},{6,7},{7,6},{8,9},{9,8},{10,11... | collective-permute-start | bytes 7077896 | tf_op jit(solution)/shard_map/ppermute | solution.py:345
  130.2 10.9 %collective-permute-start.5 = (bf16[96,1024]{1,0:T(8,128)(2,1)S(1)}, bf16[96,1024]{1,0:T(8,128)(2,1)S(1)}, u32[]{:S(2)}, u32[]{:S(2)}) collective-permute-start(bf16[96,1024]{1,0:T(8,128)(2,1)S(1)} %get-tuple-element.58), channel_id=1, source_target_pairs={{0,2},{1,3},{2,4},{3,5},{4,6},{5,7},{6,0},{7,1},{8,10},{9,11},{10,... | collective-permute-start | bytes 589832 | tf_op jit(solution)/shard_map/ppermute | solution.py:349
  132.2 9.0 %collective-permute-start.6 = (bf16[96,1024]{1,0:T(8,128)(2,1)S(1)}, bf16[96,1024]{1,0:T(8,128)(2,1)S(1)}, u32[]{:S(2)}, u32[]{:S(2)}) collective-permute-start(bf16[96,1024]{1,0:T(8,128)(2,1)S(1)} %get-tuple-element.59), channel_id=1, source_target_pairs={{0,6},{1,7},{2,0},{3,1},{4,2},{5,3},{6,4},{7,5},{8,14},{9,15},{10,... | collective-permute-start | bytes 589832 | tf_op jit(solution)/shard_map/ppermute | solution.py:350
  134.4 11.3 %collective-permute-start.9 = (bf16[96,1024]{1,0:T(8,128)(2,1)S(1)}, bf16[96,1024]{1,0:T(8,128)(2,1)S(1)}, u32[]{:S(2)}, u32[]{:S(2)}) collective-permute-start(bf16[96,1024]{1,0:T(8,128)(2,1)S(1)} %get-tuple-element.64), channel_id=1, source_target_pairs={{0,2},{1,3},{2,4},{3,5},{4,6},{5,7},{6,0},{7,1},{8,10},{9,11},{10,... | collective-permute-start | bytes 589832 | tf_op jit(solution)/shard_map/ppermute | solution.py:349
  134.4 11.3 %collective-permute-start.10 = (bf16[96,1024]{1,0:T(8,128)(2,1)S(1)}, bf16[96,1024]{1,0:T(8,128)(2,1)S(1)}, u32[]{:S(2)}, u32[]{:S(2)}) collective-permute-start(bf16[96,1024]{1,0:T(8,128)(2,1)S(1)} %get-tuple-element.65), channel_id=1, source_target_pairs={{0,6},{1,7},{2,0},{3,1},{4,2},{5,3},{6,4},{7,5},{8,14},{9,15},{10,... | collective-permute-start | bytes 589832 | tf_op jit(solution)/shard_map/ppermute | solution.py:350
  141.2 4.5 %copy-start = (bf16[3,384,1024]{2,1,0:T(8,128)(2,1)}, bf16[3,384,1024]{2,1,0:T(8,128)(2,1)S(1)}, u32[]{:S(2)}) copy-start(bf16[3,384,1024]{2,1,0:T(8,128)(2,1)S(1)} %collective-permute-done.4.back_ref) | copy-start | bytes 7077892
  142.4 13.5 %collective-permute-start.7 = (bf16[192,1024]{1,0:T(8,128)(2,1)}, bf16[192,1024]{1,0:T(8,128)(2,1)S(1)}, u32[]{:S(2)}, u32[]{:S(2)}) collective-permute-start(bf16[192,1024]{1,0:T(8,128)(2,1)} %get-tuple-element.60), channel_id=1, source_target_pairs={{0,2},{1,3},{2,4},{3,5},{4,6},{5,7},{6,0},{7,1},{8,10},{9,11},{10,... | collective-permute-start | bytes 1179656 | tf_op jit(solution)/shard_map/ppermute | solution.py:358
  143.1 12.7 %collective-permute-start.8 = (bf16[192,1024]{1,0:T(8,128)(2,1)}, bf16[192,1024]{1,0:T(8,128)(2,1)S(1)}, u32[]{:S(2)}, u32[]{:S(2)}) collective-permute-start(bf16[192,1024]{1,0:T(8,128)(2,1)} %get-tuple-element.61), channel_id=1, source_target_pairs={{0,6},{1,7},{2,0},{3,1},{4,2},{5,3},{6,4},{7,5},{8,14},{9,15},{10,... | collective-permute-start | bytes 1179656 | tf_op jit(solution)/shard_map/ppermute | solution.py:359
  146.7 15.8 %collective-permute-start.11 = (bf16[192,1024]{1,0:T(8,128)(2,1)}, bf16[192,1024]{1,0:T(8,128)(2,1)S(1)}, u32[]{:S(2)}, u32[]{:S(2)}) collective-permute-start(bf16[192,1024]{1,0:T(8,128)(2,1)} %get-tuple-element.66), channel_id=1, source_target_pairs={{0,2},{1,3},{2,4},{3,5},{4,6},{5,7},{6,0},{7,1},{8,10},{9,11},{10,... | collective-permute-start | bytes 1179656 | tf_op jit(solution)/shard_map/ppermute | solution.py:358
  146.7 15.8 %collective-permute-start.12 = (bf16[192,1024]{1,0:T(8,128)(2,1)}, bf16[192,1024]{1,0:T(8,128)(2,1)}, u32[]{:S(2)}, u32[]{:S(2)}) collective-permute-start(bf16[192,1024]{1,0:T(8,128)(2,1)} %get-tuple-element.67), channel_id=1, source_target_pairs={{0,6},{1,7},{2,0},{3,1},{4,2},{5,3},{6,4},{7,5},{8,14},{9,15},{10,... | collective-permute-start | bytes 1179656 | tf_op jit(solution)/shard_map/ppermute | solution.py:359
  155.9 1.7 copy-start.1
  164.4 1.2 collective-permute-start.13
  165.7 4.5 %collective-permute-start.16 = (f32[8,384]{1,0:T(8,128)S(1)}, f32[8,384]{1,0:T(8,128)S(1)}, u32[]{:S(2)}, u32[]{:S(2)}) collective-permute-start(f32[8,384]{1,0:T(8,128)S(1)} %fusion.12), channel_id=1, source_target_pairs={{0,6},{1,7},{2,0},{3,1},{4,2},{5,3},{6,4},{7,5},{8,14},{9,15},{10,... | collective-permute-start | bytes 36872 | tf_op jit(solution)/shard_map/ppermute | solution.py:371
  168.7 5.2 %collective-permute-start.15 = (f32[8,384]{1,0:T(8,128)S(1)}, f32[8,384]{1,0:T(8,128)S(1)}, u32[]{:S(2)}, u32[]{:S(2)}) collective-permute-start(f32[8,384]{1,0:T(8,128)S(1)} %fusion.12), channel_id=1, source_target_pairs={{0,4},{1,5},{2,6},{3,7},{4,0},{5,1},{6,2},{7,3},{8,12},{9,13},{10,... | collective-permute-start | bytes 36872 | tf_op jit(solution)/shard_map/ppermute | solution.py:371
  168.7 5.2 %collective-permute-start.14 = (f32[8,384]{1,0:T(8,128)S(1)}, f32[8,384]{1,0:T(8,128)S(1)}, u32[]{:S(2)}, u32[]{:S(2)}) collective-permute-start(f32[8,384]{1,0:T(8,128)S(1)} %fusion.12), channel_id=1, source_target_pairs={{0,2},{1,3},{2,4},{3,5},{4,6},{5,7},{6,0},{7,1},{8,10},{9,11},{10,... | collective-permute-start | bytes 36872 | tf_op jit(solution)/shard_map/ppermute | solution.py:371

commit v5 on v4

v5 whole, which is shorter than its diff:
```python
import functools

import jax
import jax.numpy as jnp
from jax import lax
from jax.experimental import pallas as pl
from jax.experimental.pallas import tpu as pltpu
from jax.sharding import PartitionSpec as P

D = 8192
HD = 128
NEW = 16
PAGE = 64
PATH_PAGES = 16
SHARED = 8
FAM = 4
RANKS = 16
PAIR = 15
ROOTS = 12
EXTRA = 3
NEAR = (0, 1, 3)
GROUPS = 2
LOG2E = 1.4426950408889634
MIB = 1024 * 1024


def split_kernel(pool_ref, fresh_ref, *refs):
    outs, sem = refs[:-1], refs[-1]
    pages_dev = pool_ref.shape[0]
    for i, out in enumerate(outs):
        lanes = pl.ds(i * HD, HD)
        pltpu.make_async_copy(pool_ref.at[:, :, lanes], out.at[pl.ds(0, pages_dev)], sem.at[i]).start()
        for p in range(EXTRA):
            rows = pl.ds(p * PAGE, PAGE)
            pltpu.make_async_copy(fresh_ref.at[rows, lanes], out.at[pages_dev + p], sem.at[i]).start()
    for i, out in enumerate(outs):
        pltpu.make_async_copy(out, out, sem.at[i]).wait()


def split(pool, fresh):
    hbm = pl.BlockSpec(memory_space=pltpu.HBM)
    vmem = pl.BlockSpec(memory_space=pltpu.VMEM)
    part = jax.ShapeDtypeStruct((pool.shape[0] + EXTRA, PAGE, HD), pool.dtype)
    return pl.pallas_call(
        split_kernel,
        out_shape=[part, part],
        in_specs=[hbm, hbm],
        out_specs=[vmem, vmem],
        scratch_shapes=[pltpu.SemaphoreType.DMA((2,))],
        compiler_params=pltpu.CompilerParams(vmem_limit_bytes=55 * MIB),
        name="split",
    )(pool, fresh)


def plan_kernel(pages_dev, rank_ref, table_ref, wanted_ref):
    rank = rank_ref[0]
    y, x = rank // 4, rank % 4
    slots, nodes = table_ref.shape
    table = table_ref[...]
    height = -(-pages_dev // 16) * 16
    per_rank = nodes // RANKS
    row = lax.broadcasted_iota(jnp.int32, (height, nodes), 0)
    node = lax.broadcasted_iota(jnp.int32, (nodes, 128), 0)
    column = lax.broadcasted_iota(jnp.int32, (nodes, 128), 1)
    step = column & 3
    begin = jnp.where(column < 16, ((y + step) & 3) * 4 + x, y * 4 + ((x + step) & 3)) * per_rank
    belongs = (node >= begin) & (node < begin + per_rank)
    low = lax.broadcasted_iota(jnp.int32, (height, height), 0)
    high = lax.broadcasted_iota(jnp.int32, (height, height), 1)
    earlier = (high < low).astype(jnp.bfloat16)
    page_id = lax.broadcasted_iota(jnp.int32, (height, 128), 0).astype(jnp.float32)
    line = lax.broadcasted_iota(jnp.int32, (16, 128), 0)
    wanted_ref[...] = jnp.zeros((16, 128), jnp.int32)

    @pl.loop(0, 8)
    def _(part):
        back = part % 4
        owner = jnp.where(part < 4, y * 4 + (x + 4 - back) % 4, (y + 4 - back) % 4 * 4 + x)
        base = owner * pages_dev
        hits = jnp.zeros((height, nodes), jnp.float32)
        for page in range(pages_dev):
            hit = jnp.max((table == base + page).astype(jnp.float32), axis=0, keepdims=True)
            hits = jnp.where(row == page, hit, hits)
        mine = (belongs & (column // 4 == part)).astype(jnp.bfloat16)
        present = jnp.dot(hits.astype(jnp.bfloat16), mine, preferred_element_type=jnp.float32) > 0
        before = jnp.dot(earlier, present.astype(jnp.bfloat16), preferred_element_type=jnp.float32)
        place = jnp.where(present, before, -1.0)
        wanted = jnp.zeros((16, 128), jnp.float32)
        for slot in range(PAIR):
            page = jnp.sum(jnp.where(place == slot, page_id, 0.0), axis=0, keepdims=True)
            wanted = jnp.where(line == slot, page, wanted)
        wanted_ref[...] += wanted.astype(jnp.int32)


def plan(rank, table, pages_dev):
    vmem = pl.BlockSpec(memory_space=pltpu.VMEM)
    return pl.pallas_call(
        functools.partial(plan_kernel, pages_dev),
        out_shape=jax.ShapeDtypeStruct((16, 128), jnp.int32),
        in_specs=[pl.BlockSpec(memory_space=pltpu.SMEM), vmem],
        out_specs=vmem,
        name="plan",
    )(rank, table)


def copy_pages(out, first, ref, wanted_ref, column, pages_dev):
    for slot in range(PAIR):
        page = jnp.clip(wanted_ref[slot, column], 0, pages_dev - 1)
        out[first + slot] = ref[page]


def pack_first_kernel(pages_dev, wanted_ref, *refs):
    for i in range(2):
        parts, outs = refs[3 * i : 3 * i + 3], refs[6 + 4 * i : 10 + 4 * i]
        for e, out in enumerate(outs):
            for j, d in enumerate(NEAR):
                copy_pages(out, j * PAIR, parts[j], wanted_ref, 16 * i + 4 * d + e, pages_dev)


def pack_first(wanted, pages_dev, keys, values):
    outs = [((len(NEAR) * PAIR, PAGE, HD), jnp.bfloat16)] * 8
    args = [keys[d] for d in NEAR] + [values[d] for d in NEAR]
    return local(functools.partial(pack_first_kernel, pages_dev), "pack_first", outs, wanted, *args, scalars=1, limit=62)


def pack_second_kernel(pages_dev, rank_ref, parent_ref, wanted_ref, *refs):
    y, x = rank_ref[0] // 4, rank_ref[0] % 4
    per_rank = parent_ref.shape[0] // RANKS
    for i in range(2):
        parts, outs = refs[4 * i : 4 * i + 4], refs[8 + 4 * i : 12 + 4 * i]
        for e, out in enumerate(outs):
            copy_pages(out, 0, parts[2], wanted_ref, 16 * i + 8 + e, pages_dev)
            dest = (y + e) % 4 * 4 + x if i == 0 else y * 4 + (x + e) % 4
            for child in range(per_rank - ROOTS):
                named = jnp.maximum(parent_ref[dest * per_rank + ROOTS + child], 0)
                up = named // per_rank
                away = (x + 4 - up % 4) % 4 if i == 0 else (y + 4 - up // 4) % 4
                root = jnp.minimum(named % per_rank, ROOTS - 1)
                page, rows = pages_dev + root // 4, pl.ds(pl.multiple_of(root % 4 * NEW, NEW), NEW)
                picked = parts[0][page, rows, :]
                for d in (1, 2, 3):
                    picked = jnp.where(away == d, parts[d][page, rows, :], picked)
                out[PAIR + child // 4, child % 4 * NEW : (child % 4 + 1) * NEW, :] = picked


def pack_second(rank, parent, wanted, pages_dev, keys, values):
    outs = [((PAIR + EXTRA, PAGE, HD), jnp.bfloat16)] * 8
    kernel = functools.partial(pack_second_kernel, pages_dev)
    return local(kernel, "pack_second", outs, rank, parent, wanted, *keys, *values, scalars=3, limit=62)


def attend_family(first, node, at_refs, len_ref, above_refs, q_ref, fresh_ref, page_refs, attn_ref):
    scale = HD ** (-0.5) * LOG2E
    nt = (((1,), (1,)), ((), ()))

    def pages(i, n, slot):
        return [page_refs[i][at_refs[i][n * PATH_PAGES + slot + s]] for s in range(SHARED)]

    heads = q_ref.shape[1] // HD
    span = heads * NEW
    shared_key, shared_value = [jnp.concatenate(pages(i, node, 0), axis=0) for i in range(2)]
    queries = []
    for i in range(FAM):
        rows = q_ref[first + i * NEW : first + (i + 1) * NEW, :]
        queries.append(jnp.concatenate([rows[:, h * HD : (h + 1) * HD] for h in range(heads)], axis=0))
    s_shared = lax.dot_general(
        jnp.concatenate(queries, axis=0), shared_key, nt, preferred_element_type=jnp.float32
    )
    half = SHARED * PAGE // 2
    values, s_own = [], []
    for i in range(FAM):
        both = []
        for j in range(2):
            spot = jnp.maximum(above_refs[j][node + i], 0)
            upper = page_refs[j][spot // PAGE, pl.ds(pl.multiple_of(spot % PAGE, NEW), NEW), :]
            fresh = fresh_ref[first + i * NEW : first + (i + 1) * NEW, j * HD : (j + 1) * HD]
            both.append(jnp.concatenate(pages(j, node + i, SHARED) + [fresh, upper], axis=0))
        s = lax.dot_general(queries[i], both[0], nt, preferred_element_type=jnp.float32)
        late = s[:, half:]
        spot = lax.broadcasted_iota(jnp.int32, late.shape, 1) + SHARED * PAGE + half
        token = lax.broadcasted_iota(jnp.int32, late.shape, 0) % NEW
        key = spot - PATH_PAGES * PAGE
        limit = jnp.where(above_refs[0][node + i] >= 0, 2 * NEW, NEW)
        allowed = (spot < len_ref[node + i]) | ((key >= 0) & (key <= token)) | ((key >= NEW) & (key < limit))
        values.append(both[1])
        s_own.append(jnp.concatenate([s[:, :half], jnp.where(allowed, late, -jnp.inf)], axis=1))
    tops = [
        jnp.maximum(
            jnp.max(s_shared[i * span : (i + 1) * span], axis=1, keepdims=True),
            jnp.max(s_own[i], axis=1, keepdims=True),
        )
        for i in range(FAM)
    ]
    w_own = [jnp.exp2((s_own[i] - tops[i]) * scale).astype(jnp.bfloat16) for i in range(FAM)]
    w_shared = jnp.exp2((s_shared - jnp.concatenate(tops, axis=0)) * scale).astype(jnp.bfloat16)
    ones = jnp.ones((values[0].shape[0], HD), jnp.bfloat16)
    accum = [
        jnp.dot(w_own[i], jnp.concatenate([values[i], ones], axis=1), preferred_element_type=jnp.float32)
        for i in range(FAM)
    ]
    accum = jnp.concatenate(accum, axis=0) + jnp.dot(
        w_shared, jnp.concatenate([shared_value, ones[: SHARED * PAGE]], axis=1), preferred_element_type=jnp.float32
    )
    attn = (accum[:, :HD] / accum[:, HD:]).astype(jnp.bfloat16)
    for i in range(FAM):
        for h in range(heads):
            block = attn[i * span + h * NEW : i * span + (h + 1) * NEW, :]
            attn_ref[first + i * NEW : first + (i + 1) * NEW, h * HD : (h + 1) * HD] = block


def attend_kernel(*refs):
    at_refs, len_ref, above_refs, (q_ref, fresh_ref) = refs[:2], refs[2], refs[3:5], refs[5:7]
    sources, w_hbm, (attn_ref, w_ref), page_refs, sems = (refs[7:15], refs[15:23]), refs[23], refs[24:26], refs[26:28], refs[28]
    for i in range(2):
        start = 0
        for ref in sources[i]:
            count = ref.shape[0]
            pltpu.make_async_copy(ref, page_refs[i].at[pl.ds(start, count)], sems.at[i]).start()
            start += count
    weights = []
    for part in range(8):
        rows = pl.ds(part * (w_ref.shape[0] // 8), w_ref.shape[0] // 8)
        weights.append(pltpu.make_async_copy(w_hbm.at[rows], w_ref.at[rows], sems.at[2 + part]))
        weights[-1].start()
    for i in range(2):
        pltpu.make_async_copy(page_refs[i], page_refs[i], sems.at[i]).wait()
    for f in range(q_ref.shape[0] // (FAM * NEW)):
        attend_family(f * FAM * NEW, f * FAM, at_refs, len_ref, above_refs, q_ref, fresh_ref, page_refs, attn_ref)
    for copy in weights:
        copy.wait()


def attend(at, lengths, above, queries, fresh, keys, values, w_out):
    rows, width = queries.shape
    smem = pl.BlockSpec(memory_space=pltpu.SMEM)
    vmem = pl.BlockSpec(memory_space=pltpu.VMEM)
    hbm = pl.BlockSpec(memory_space=pltpu.HBM)
    pages = pltpu.VMEM((sum(k.shape[0] for k in keys), PAGE, HD), jnp.bfloat16)
    return pl.pallas_call(
        attend_kernel,
        out_shape=[jax.ShapeDtypeStruct((rows, width), jnp.bfloat16), pltpu.VMEM(w_out.shape, w_out.dtype)],
        in_specs=[smem] * 5 + [vmem] * 2 + [hbm] * 17,
        out_specs=[vmem, vmem],
        scratch_shapes=[pages, pages, pltpu.SemaphoreType.DMA((10,))],
        compiler_params=pltpu.CompilerParams(vmem_limit_bytes=45 * MIB),
        cost_estimate=pl.CostEstimate(
            flops=4 * rows * width * 1056 * 4, bytes_accessed=4 * rows * width, transcendentals=rows * 8 * 1056
        ),
        name="attend",
    )(*at, lengths, *above, queries, fresh, *keys, *values, w_out)


def project_kernel(order_ref, attn_ref, w_ref, out_ref):
    count, rows, cols = out_ref.shape

    @pl.loop(0, count)
    def _(b):
        w = w_ref[:, pl.ds(pl.multiple_of(order_ref[b] * cols, cols), cols)]
        out_ref[b] = jnp.dot(attn_ref[...], w, preferred_element_type=jnp.float32).astype(jnp.bfloat16)


def project(order, attn, w_out):
    rows, depth = attn.shape
    cols = w_out.shape[1] // 8
    count = order.shape[0]
    smem = pl.BlockSpec(memory_space=pltpu.SMEM)
    vmem = pl.BlockSpec(memory_space=pltpu.VMEM)
    return pl.pallas_call(
        project_kernel,
        out_shape=jax.ShapeDtypeStruct((count, rows, cols), jnp.bfloat16),
        in_specs=[smem, vmem, vmem],
        out_specs=vmem,
        compiler_params=pltpu.CompilerParams(vmem_limit_bytes=12 * MIB),
        cost_estimate=pl.CostEstimate(
            flops=2 * rows * depth * cols * count, bytes_accessed=rows * cols * count * 2, transcendentals=0
        ),
        name="project",
    )(order, attn, w_out)


def shift(dy, dx):
    return [(s, (s // 4 + dy) % 4 * 4 + (s % 4 + dx) % 4) for s in range(RANKS)]


def turn(d):
    return [(t, (t + 2 * d) % 8) for t in range(8)]


def places_of(table, path_parent, rank, pages_dev, nodes):
    owner = table // pages_dev
    other, mine = table[None, :], table[:, None]
    slot = jnp.arange(table.shape[0], dtype=jnp.int32)
    first = (slot % PATH_PAGES >= SHARED) | (slot // PATH_PAGES % FAM == 0)
    before = (other < mine) & (other >= (owner * pages_dev)[:, None]) & first[None, :]
    place = jnp.sum(before.astype(jnp.int32), axis=1)
    child = jnp.arange(nodes, dtype=jnp.int32) - ROOTS
    up = jnp.maximum(path_parent, 0) // nodes
    many, few = len(NEAR) * PAIR, PAIR + EXTRA

    def turns(r):
        return (rank // 4 - r // 4) % 4, (rank % 4 - r % 4) % 4

    at, above = [], []
    for i in range(2):
        e, d = turns(owner)[:: 1 - 2 * i]
        at.append(jnp.where(d == 2, 4 * many + e * few, e * many + jnp.minimum(d, 2) * PAIR) + place)
        row = (4 * many + turns(up)[i] * few + PAIR) * PAGE + child * NEW
        above.append(jnp.where((path_parent >= 0) & (child >= 0), row, -1))
    return at, above


def far_kernel(kept_ref, back_ref, *out_refs):
    rows = out_refs[0].shape[0]
    for i, ref in enumerate(out_refs):
        part = pl.ds(i * rows, rows)
        ref[...] = (kept_ref[1, part].astype(jnp.float32) + back_ref[part].astype(jnp.float32)).astype(jnp.bfloat16)


def near_kernel(first, kept_ref, back_ref, from_low_ref, from_high_ref, up_ref, down_ref):
    half = from_low_ref.shape[0]
    low, high = pl.ds(0, half), pl.ds(half, half)

    def pair(i, start):
        part = pl.ds(first + start, half)
        return kept_ref[i, part].astype(jnp.float32) + back_ref[i, part].astype(jnp.float32)

    up_ref[low] = (pair(0, 0) + from_low_ref[...].astype(jnp.float32)).astype(jnp.bfloat16)
    up_ref[high] = pair(0, half).astype(jnp.bfloat16)
    down_ref[low] = pair(1, 0).astype(jnp.bfloat16)
    down_ref[high] = (pair(1, half) + from_high_ref[...].astype(jnp.float32)).astype(jnp.bfloat16)


def last_kernel(first, kept_ref, back_ref, up_ref, down_ref, residual_ref, mixed_ref, power_ref):
    part = pl.ds(first, up_ref.shape[0])
    mixed = residual_ref[part].astype(jnp.float32)
    for term in (kept_ref[2, part], back_ref[2, part], up_ref[...], down_ref[...]):
        mixed = mixed + term.astype(jnp.float32)
    mixed_ref[...] = mixed
    power_ref[...] = lax.dot_general(
        jnp.ones((8, mixed.shape[1]), jnp.float32),
        mixed * mixed,
        (((1,), (1,)), ((), ())),
        precision=lax.Precision.HIGHEST,
        preferred_element_type=jnp.float32,
    )


def local(kernel, name, outs, *args, scalars=0, limit=12):
    vmem = pl.BlockSpec(memory_space=pltpu.VMEM)
    smem = pl.BlockSpec(memory_space=pltpu.SMEM)
    return pl.pallas_call(
        kernel,
        out_shape=[jax.ShapeDtypeStruct(shape, dtype) for shape, dtype in outs],
        in_specs=[smem] * scalars + [vmem] * (len(args) - scalars),
        out_specs=[vmem] * len(outs),
        compiler_params=pltpu.CompilerParams(vmem_limit_bytes=limit * MIB),
        name=name,
    )(*args)


def body(queries, fresh_kv, kv_pool, page_table, path_len, parent, w_out, residual, gain):
    rank = lax.axis_index("dp")
    tensor_rank = lax.axis_index("tensor")
    tensors = lax.axis_size("tensor")
    rows = queries.shape[0]
    nodes = rows // NEW
    pages_dev = kv_pool.shape[0]
    key, value = split(kv_pool, fresh_kv)
    place = rank.reshape(1)
    wanted = plan(place, page_table.T, pages_dev)
    far_key, far_value, wanted = lax.optimization_barrier((key, value, wanted))
    keys = [key] + [lax.ppermute(far_key if d == 2 else key, "dp", shift(0, d)) for d in (1, 2, 3)]
    values = [value] + [lax.ppermute(far_value if d == 2 else value, "dp", shift(d, 0)) for d in (1, 2, 3)]
    first = pack_first(wanted, pages_dev, keys, values)

    def deliver(parts):
        order = [(e, i) for e in (1, 3, 2) for i in range(2)]
        return {(i, e): lax.ppermute(parts[4 * i + e], "dp", shift(0, e) if i else shift(e, 0)) for e, i in order}

    got = deliver(first)
    got[0, 1], wanted = lax.optimization_barrier((got[0, 1], wanted))
    second = list(pack_second(place, parent, wanted, pages_dev, keys, values))
    for i, e in got:
        if (i, e) != (0, 1):
            got[i, e], second[4 * i + e] = lax.optimization_barrier((got[i, e], second[4 * i + e]))
    more = deliver(second)
    keys, values = (
        [first[4 * i]] + [got[i, e] for e in (1, 2, 3)] + [second[4 * i]] + [more[i, e] for e in (1, 2, 3)]
        for i in range(2)
    )
    keys, values, w_out, residual, gain = lax.optimization_barrier((keys, values, w_out, residual, gain))

    own_table = lax.dynamic_slice_in_dim(page_table, rank * nodes, nodes).reshape(-1)
    lengths = lax.dynamic_slice_in_dim(path_len, rank * nodes, nodes)
    at, above = places_of(own_table, lax.dynamic_slice_in_dim(parent, rank * nodes, nodes), rank, pages_dev, nodes)
    z, core = tensor_rank // 2, tensor_rank % 2
    far, rest = (z + 2) % 4 * 2, (z + jnp.array([1, 3, 0], jnp.int32)) % 4 * 2
    far = jnp.stack([far + 1 - core, far + core])
    other, same = rest + 1 - core, rest + core

    attn, w_held = attend(at, lengths, above, queries, fresh_kv, keys, values, w_out)

    swap = [(t, t ^ 1) for t in range(tensors)]
    cols = D // tensors
    mine = lax.dynamic_slice_in_dim(residual, tensor_rank * cols, cols, 1)
    group = rows // GROUPS
    both = project(far, attn, w_held)
    both, attn = lax.optimization_barrier((both, attn))
    far_back = lax.ppermute(both[0], "tensor", swap)
    away = project(other, attn, w_held)
    far_back, away, attn = lax.optimization_barrier((far_back, away, attn))
    back = lax.ppermute(away, "tensor", swap)
    halves = [((group // 2, cols), jnp.bfloat16)] * (2 * GROUPS)
    sent = local(far_kernel, "far", halves, both, far_back)
    *sent, attn = lax.optimization_barrier((*sent, attn))
    low = [lax.ppermute(sent[2 * g], "tensor", turn(1)) for g in range(GROUPS)]
    high = [lax.ppermute(sent[2 * g + 1], "tensor", turn(-1)) for g in range(GROUPS)]
    kept = project(same, attn, w_held)
    whole = ((group, cols), jnp.bfloat16)
    ups, downs = [], []
    for g in range(GROUPS):
        up, down = local(
            functools.partial(near_kernel, g * group), "near", [whole, whole], kept, back, low[g], high[g]
        )
        ups.append(lax.ppermute(up, "tensor", turn(1)))
        downs.append(lax.ppermute(down, "tensor", turn(-1)))
    outs = [((group, cols), jnp.float32), ((8, group), jnp.float32)]
    done = [
        local(functools.partial(last_kernel, g * group), "last", outs, kept, back, ups[g], downs[g], mine)
        for g in range(GROUPS)
    ]

    mixed = jnp.concatenate([m for m, _ in done], axis=0)
    power = jnp.concatenate([p for _, p in done], axis=1)
    power = power + lax.ppermute(power, "tensor", swap)
    total = power
    for d in (1, 2, 3):
        total = total + lax.ppermute(power, "tensor", turn(d))
    norm = lax.rsqrt(total[0].reshape(rows, 1) / D + 1e-05)
    own_gain = lax.dynamic_slice_in_dim(gain, tensor_rank * cols, cols)
    normed = mixed * norm * own_gain.astype(jnp.float32)
    return (mixed.astype(jnp.bfloat16), normed.astype(jnp.bfloat16))


def solution(mesh):
    return jax.shard_map(
        body,
        mesh=mesh,
        in_specs=(
            P("dp", "tensor"),
            P("dp", "tensor"),
            P("dp", None, "tensor"),
            P(),
            P(),
            P(),
            P("tensor", None),
            P("dp", None),
            P(),
        ),
        out_specs=(P("dp", "tensor"), P("dp", "tensor")),
        check_vma=False,
    )
```

time: 177 us -> 163 us (0.921)
  blocking collectives: 102 us -> 0 us
  starting transfers between devices: 23.4 us -> 70.1 us
  Pallas kernels: 25.1 us -> 46.7 us
  waiting for transfers between devices: 13.4 us -> 31.9 us
  local copies, waits for them, and re-layouts: 6.36 us -> 8.93 us
    all_to_all x1 -> x0, blocking collectives: 102 us -> none  [body(): lax.all_to_all(send, 'dp', split_axis=0, concat_axis=0, tiled=True)]
    ppermute x3 -> x18, starting transfers between devices: 4.82 us -> 51.5 us  [the longest x12 40.9 us: deliver(): lax.ppermute(parts[4 * i + e], 'dp', shift(0, e) if i else shift(e, 0))]
    ppermute x3 -> x18, waiting for transfers between devices: 0.01 us -> 18.4 us  [the longest x12 11.1 us: deliver(): lax.ppermute(parts[4 * i + e], 'dp', shift(0, e) if i else shift(e, 0))]
    pallas_call x5 -> x7, Pallas kernels: 5.17 us -> 17.5 us  [local(): pl.pallas_call(kernel, out_shape=[jax.ShapeDtypeStruct(shape, dtype) for...]
    pallas_call x2 -> x3, Pallas kernels: 10.4 us -> 19.7 us  [the longest x1 11.2 us: attend(): pl.pallas_call(attend_kernel, out_shape=[jax.ShapeDtypeStruct((rows, widt...]
    unnamed x25 -> x33, local copies, waits for them, and re-layouts: 2.44 us -> 5.41 us
  transfers between devices with their start and end apart: 17 -> 32, of which waited for: 5 -> 11; matrix products, arithmetic and copies ran while one was open for 3% -> 4% of each run, Pallas kernels for 6% -> 17%
where the time goes in v5:
time: 163 us
  starting transfers between devices  70.1 us (43%)
  Pallas kernels  46.7 us (29%)
  waiting for transfers between devices  31.9 us (20%)
  local copies, waits for them, and re-layouts  8.93 us (5%)
  other arithmetic  4.42 us (3%)
    ppermute x12, starting transfers between devices, deliver(): lax.ppermute(parts[4 * i + e], 'dp', shift(0, e) if i else shift(e, 0))  40.9 us
    pallas_call x7, Pallas kernels, local(): pl.pallas_call(kernel, out_shape=[jax.ShapeDtypeStruct(shape, dtype) for...  17.5 us
    pallas_call x1, Pallas kernels, attend(): pl.pallas_call(attend_kernel, out_shape=[jax.ShapeDtypeStruct((rows, widt...  11.2 us
    ppermute x12, waiting for transfers between devices, deliver(): lax.ppermute(parts[4 * i + e], 'dp', shift(0, e) if i else shift(e, 0))  11.1 us
    pallas_call x3, Pallas kernels, project(): pl.pallas_call(project_kernel, out_shape=jax.ShapeDtypeStruct((count, row...  9.47 us
    ppermute x2, waiting for transfers between devices, body(): ups.append(lax.ppermute(up, 'tensor', turn(1)))  8.69 us
    ppermute x3, waiting for transfers between devices, body(): lax.ppermute(far_key if d == 2 else key, 'dp', shift(0, d))  7.35 us
    ppermute x3, starting transfers between devices, body(): lax.ppermute(far_value if d == 2 else value, 'dp', shift(d, 0))  6.43 us
  transfers between devices with their start and end apart: 32, of which 11 were waited for; matrix products, arithmetic and copies ran while one was open for 4% of the time, Pallas kernels for 17%

profile of v5, /device:TPU:2, one launch (start us, length us, event | category | flops | bytes accessed | tf_op | source)
XLA Modules:
  0.0 162.9 jit_solution(5399303922362288593)
XLA Ops:
  0.6 2.5 %split.1 = (bf16[48,64,128]{2,1,0:T(8,128)(2,1)}, bf16[48,64,128]{2,1,0:T(8,128)(2,1)}) custom-call(bf16[45,64,256]{2,1,0:T(8,128)(2,1)} %pool_ref.1, bf16[384,256]{1,0:T(8,128)(2,1)} %refs_6_.1), custom_call_target="tpu_custom_call" | custom-call | tf_op jit(solution)/shard_map/split/pallas_call | solution.py:44
  3.2 1.6 collective-permute-start
  5.3 1.6 collective-permute-start.2
  6.9 1.7 %collective-permute-start.3 = (bf16[48,64,128]{2,1,0:T(8,128)(2,1)}, bf16[48,64,128]{2,1,0:T(8,128)(2,1)}, u32[]{:S(2)}, u32[]{:S(2)}) collective-permute-start(bf16[48,64,128]{2,1,0:T(8,128)(2,1)} %get-tuple-element.87.refs_3_.refs_4_), channel_id=1, source_target_pairs={{0,96},{8,104},{16,112},{24,120},{32,0},{40,8},{48,16},{56,24},{64... | collective-permute-start | bytes 2359304 | tf_op jit(solution)/shard_map/ppermute | solution.py:373
  8.5 5.9 %plan.1.wanted_ref = s32[16,128]{1,0:T(8,128)} custom-call(s32[1]{0:T(128)} %bitcast.2.rank_ref, s32[16,384]{1,0:T(8,128)} %bitcast.6), custom_call_target="tpu_custom_call" | custom-call | tf_op jit(solution)/shard_map/plan/pallas_call | solution.py:97
  14.4 2.1 %collective-permute-start.6 = (bf16[48,64,128]{2,1,0:T(8,128)(2,1)}, bf16[48,64,128]{2,1,0:T(8,128)(2,1)}, u32[]{:S(2)}, u32[]{:S(2)}) collective-permute-start(bf16[48,64,128]{2,1,0:T(8,128)(2,1)} %get-tuple-element.86.refs_0_), channel_id=1, source_target_pairs={{0,16},{8,24},{16,0},{24,8},{32,48},{40,56},{48,32},{56,40},{64,80... | collective-permute-start | bytes 2359304 | tf_op jit(solution)/shard_map/ppermute | solution.py:372
  16.5 7.3 %collective-permute-done.refs_1_ = bf16[48,64,128]{2,1,0:T(8,128)(2,1)S(1)} collective-permute-done((bf16[48,64,128]{2,1,0:T(8,128)(2,1)}, bf16[48,64,128]{2,1,0:T(8,128)(2,1)S(1)}, u32[]{:S(2)}, u32[]{:S(2)}) %collective-permute-start) | collective-permute-done | bytes 786464 | tf_op jit(solution)/shard_map/ppermute | solution.py:372
  23.9 3.2 %collective-permute-start.7 = (bf16[48,64,128]{2,1,0:T(8,128)(2,1)}, bf16[48,64,128]{2,1,0:T(8,128)(2,1)}, u32[]{:S(2)}, u32[]{:S(2)}) collective-permute-start(bf16[48,64,128]{2,1,0:T(8,128)(2,1)} %get-tuple-element.87.refs_3_.refs_4_), channel_id=1, source_target_pairs={{0,64},{8,72},{16,80},{24,88},{32,96},{40,104},{48,112},{56,120},{... | collective-permute-start | bytes 2359304 | tf_op jit(solution)/shard_map/ppermute | solution.py:373
  27.1 0.9 copy-done.5
  28.0 5.6 %pack_first.1 = (bf16[45,64,128]{2,1,0:T(8,128)(2,1)}, bf16[45,64,128]{2,1,0:T(8,128)(2,1)}, bf16[45,64,128]{2,1,0:T(8,128)(2,1)}, bf16[45,64,128]{2,1,0:T(8,128...) custom-call(s32[16,128]{1,0:T(8,128)} %plan.1.wanted_ref, ...), custom_call_target="tpu_custom_call" | custom-call | tf_op jit(solution)/shard_map/pack_first/pallas_call | solution.py:351
  34.3 13.1 %collective-permute-start.14 = (bf16[45,64,128]{2,1,0:T(8,128)(2,1)}, bf16[45,64,128]{2,1,0:T(8,128)(2,1)S(1)}, u32[]{:S(2)}, u32[]{:S(2)}) collective-permute-start(bf16[45,64,128]{2,1,0:T(8,128)(2,1)} %get-tuple-element.104), channel_id=1, source_target_pairs={{0,24},{8,0},{16,8},{24,16},{32,56},{40,32},{48,40},{56,48},{64,88... | collective-permute-start | bytes 2211848 | tf_op jit(solution)/shard_map/ppermute | solution.py:378
  48.2 2.9 %collective-permute-start.13 = (bf16[45,64,128]{2,1,0:T(8,128)(2,1)}, bf16[45,64,128]{2,1,0:T(8,128)(2,1)}, u32[]{:S(2)}, u32[]{:S(2)}) collective-permute-start(bf16[45,64,128]{2,1,0:T(8,128)(2,1)} %get-tuple-element.101), channel_id=1, source_target_pairs={{0,16},{8,24},{16,0},{24,8},{32,48},{40,56},{48,32},{56,40},{64,80... | collective-permute-start | bytes 2211848 | tf_op jit(solution)/shard_map/ppermute | solution.py:378
  51.0 2.6 %collective-permute-start.12 = (bf16[45,64,128]{2,1,0:T(8,128)(2,1)}, bf16[45,64,128]{2,1,0:T(8,128)(2,1)}, u32[]{:S(2)}, u32[]{:S(2)}) collective-permute-start(bf16[45,64,128]{2,1,0:T(8,128)(2,1)} %get-tuple-element.98), channel_id=1, source_target_pairs={{0,8},{8,16},{16,24},{24,0},{32,40},{40,48},{48,56},{56,32},{64,72... | collective-permute-start | bytes 2211848 | tf_op jit(solution)/shard_map/ppermute | solution.py:378
  53.6 1.5 collective-permute-start.8
  55.1 4.2 %collective-permute-done.4.refs_8_ = bf16[45,64,128]{2,1,0:T(8,128)(2,1)S(1)} collective-permute-done((bf16[45,64,128]{2,1,0:T(8,128)(2,1)}, bf16[45,64,128]{2,1,0:T(8,128)(2,1)S(1)}, u32[]{:S(2)}, u32[]{:S(2)}) %collective-permute-start.4) | collective-permute-done | bytes 737312 | tf_op jit(solution)/shard_map/ppermute | solution.py:378
  59.3 2.7 %collective-permute-start.5 = (bf16[45,64,128]{2,1,0:T(8,128)(2,1)}, bf16[45,64,128]{2,1,0:T(8,128)(2,1)}, u32[]{:S(2)}, u32[]{:S(2)}) collective-permute-start(bf16[45,64,128]{2,1,0:T(8,128)(2,1)} %get-tuple-element.84), channel_id=1, source_target_pairs={{0,64},{8,72},{16,80},{24,88},{32,96},{40,104},{48,112},{56,120},{... | collective-permute-start | bytes 2211848 | tf_op jit(solution)/shard_map/ppermute | solution.py:378
  62.1 1.3 dynamic_slice.16.refs_2_
  63.7 6.6 %pack_second.1 = (bf16[18,64,128]{2,1,0:T(8,128)(2,1)}, bf16[18,64,128]{2,1,0:T(8,128)(2,1)}, bf16[18,64,128]{2,1,0:T(8,128)(2,1)}, bf16[18,64,128]{2,1,0:T(8,12...) custom-call(s32[1]{0:T(128)} %bitcast.2.rank_ref, ...), custom_call_target="tpu_custom_call" | custom-call | tf_op jit(solution)/shard_map/pack_second/pallas_call | solution.py:351
  70.4 4.1 %collective-permute-start.17 = (bf16[18,64,128]{2,1,0:T(8,128)(2,1)}, bf16[18,64,128]{2,1,0:T(8,128)(2,1)S(1)}, u32[]{:S(2)}, u32[]{:S(2)}) collective-permute-start(bf16[18,64,128]{2,1,0:T(8,128)(2,1)} %get-tuple-element.110), channel_id=1, source_target_pairs={{0,24},{8,0},{16,8},{24,16},{32,56},{40,32},{48,40},{56,48},{64,88... | collective-permute-start | bytes 884744 | tf_op jit(solution)/shard_map/ppermute | solution.py:378
  75.6 2.5 %collective-permute-start.16 = (bf16[18,64,128]{2,1,0:T(8,128)(2,1)}, bf16[18,64,128]{2,1,0:T(8,128)(2,1)S(1)}, u32[]{:S(2)}, u32[]{:S(2)}) collective-permute-start(bf16[18,64,128]{2,1,0:T(8,128)(2,1)} %get-tuple-element.109), channel_id=1, source_target_pairs={{0,16},{8,24},{16,0},{24,8},{32,48},{40,56},{48,32},{56,40},{64,80... | collective-permute-start | bytes 884744 | tf_op jit(solution)/shard_map/ppermute | solution.py:378
  78.1 2.5 %collective-permute-start.15 = (bf16[18,64,128]{2,1,0:T(8,128)(2,1)}, bf16[18,64,128]{2,1,0:T(8,128)(2,1)S(1)}, u32[]{:S(2)}, u32[]{:S(2)}) collective-permute-start(bf16[18,64,128]{2,1,0:T(8,128)(2,1)} %get-tuple-element.108), channel_id=1, source_target_pairs={{0,8},{8,16},{16,24},{24,0},{32,40},{40,48},{48,56},{56,32},{64,72... | collective-permute-start | bytes 884744 | tf_op jit(solution)/shard_map/ppermute | solution.py:378
  80.7 3.0 %collective-permute-start.11 = (bf16[18,64,128]{2,1,0:T(8,128)(2,1)}, bf16[18,64,128]{2,1,0:T(8,128)(2,1)S(1)}, u32[]{:S(2)}, u32[]{:S(2)}) collective-permute-start(bf16[18,64,128]{2,1,0:T(8,128)(2,1)} %get-tuple-element.96), channel_id=1, source_target_pairs={{0,96},{8,104},{16,112},{24,120},{32,0},{40,8},{48,16},{56,24},{64... | collective-permute-start | bytes 884744 | tf_op jit(solution)/shard_map/ppermute | solution.py:378
  84.0 5.1 %collective-permute-start.9 = (bf16[18,64,128]{2,1,0:T(8,128)(2,1)}, bf16[18,64,128]{2,1,0:T(8,128)(2,1)S(1)}, u32[]{:S(2)}, u32[]{:S(2)}) collective-permute-start(bf16[18,64,128]{2,1,0:T(8,128)(2,1)} %get-tuple-element.94), channel_id=1, source_target_pairs={{0,32},{8,40},{16,48},{24,56},{32,64},{40,72},{48,80},{56,88},{64,... | collective-permute-start | bytes 884744 | tf_op jit(solution)/shard_map/ppermute | solution.py:378
  90.6 3.3 %collective-permute-done.10.refs_13_ = bf16[18,64,128]{2,1,0:T(8,128)(2,1)S(1)} collective-permute-done((bf16[18,64,128]{2,1,0:T(8,128)(2,1)}, bf16[18,64,128]{2,1,0:T(8,128)(2,1)S(1)}, u32[]{:S(2)}, u32[]{:S(2)}) %collective-permute-start.10) | collective-permute-done | bytes 294944 | tf_op jit(solution)/shard_map/ppermute | solution.py:378
  93.9 2.8 %collective-permute-done.9.refs_12_ = bf16[18,64,128]{2,1,0:T(8,128)(2,1)S(1)} collective-permute-done((bf16[18,64,128]{2,1,0:T(8,128)(2,1)}, bf16[18,64,128]{2,1,0:T(8,128)(2,1)S(1)}, u32[]{:S(2)}, u32[]{:S(2)}) %collective-permute-start.9) | collective-permute-done | bytes 294944 | tf_op jit(solution)/shard_map/ppermute | solution.py:378
  97.4 11.2 %attend.1 = (bf16[384,1024]{1,0:T(8,128)(2,1)}, bf16[1024,8192]{1,0:T(8,128)(2,1)S(1)}) custom-call(s32[384]{0:T(512)} %get-tuple-element.161.refs_0_, s32[384]{0:T(512)} %get-tuple-element.160.refs_1_, s32[24]{0:T(128)} %dynamic_slice.16.refs_2_, s32[24]{0:T(128)} %fusion.24.refs_3_, s32[24]{0:T(128)} %get-tuple-element.156.refs_4_, ...), custom_call_target="tpu_custom_call" | custom-call | flops 6643777536 | bytes 1572864 | tf_op jit(solution)/shard_map/attend/pallas_call | solution.py:239
  108.6 1.1 copy-done.2
  109.8 2.5 %project.3.kept_ref = bf16[2,384,1024]{2,1,0:T(8,128)(2,1)S(1)} custom-call(s32[2]{0:T(128)S(1)} %pad_add_fusion.order_ref, bf16[384,1024]{1,0:T(8,128)(2,1)S(1)} %copy-done.2, bf16[1024,8192]{1,0:T(8,128)(2,1)S(1)} %get-tuple-element.129.w_ref), custom_call_target="tpu_custom_call" | custom-call | flops 1610612736 | bytes 1572864 | tf_op jit(solution)/shard_map/project/pallas_call | solution.py:268
  113.4 3.5 %project.4 = bf16[3,384,1024]{2,1,0:T(8,128)(2,1)S(1)} custom-call(s32[3]{0:T(128)S(1)} %get-tuple-element.154.order_ref, bf16[384,1024]{1,0:T(8,128)(2,1)S(1)} %copy-done.3, bf16[1024,8192]{1,0:T(8,128)(2,1)S(1)} %get-tuple-element.129.w_ref), custom_call_target="tpu_custom_call" | custom-call | flops 2415919104 | bytes 2359296 | tf_op jit(solution)/shard_map/project/pallas_call | solution.py:268
  117.2 2.0 %collective-permute-start.24 = (bf16[96,1024]{1,0:T(8,128)(2,1)S(1)}, bf16[96,1024]{1,0:T(8,128)(2,1)S(1)}, u32[]{:S(2)}, u32[]{:S(2)}) collective-permute-start(bf16[96,1024]{1,0:T(8,128)(2,1)S(1)} %get-tuple-element.146), channel_id=1, source_target_pairs={{0,2},{1,3},{2,4},{3,5},{4,6},{5,7},{6,0},{7,1},{8,10},{9,11},{10,... | collective-permute-start | bytes 589832 | tf_op jit(solution)/shard_map/ppermute | solution.py:416
  119.2 2.2 %collective-permute-start.25 = (bf16[96,1024]{1,0:T(8,128)(2,1)S(1)}, bf16[96,1024]{1,0:T(8,128)(2,1)S(1)}, u32[]{:S(2)}, u32[]{:S(2)}) collective-permute-start(bf16[96,1024]{1,0:T(8,128)(2,1)S(1)} %get-tuple-element.147), channel_id=1, source_target_pairs={{0,6},{1,7},{2,0},{3,1},{4,2},{5,3},{6,4},{7,5},{8,14},{9,15},{10,... | collective-permute-start | bytes 589832 | tf_op jit(solution)/shard_map/ppermute | solution.py:417
  121.4 3.2 %collective-permute-start.21 = (bf16[96,1024]{1,0:T(8,128)(2,1)S(1)}, bf16[96,1024]{1,0:T(8,128)(2,1)S(1)}, u32[]{:S(2)}, u32[]{:S(2)}) collective-permute-start(bf16[96,1024]{1,0:T(8,128)(2,1)S(1)} %get-tuple-element.141), channel_id=1, source_target_pairs={{0,6},{1,7},{2,0},{3,1},{4,2},{5,3},{6,4},{7,5},{8,14},{9,15},{10,... | collective-permute-start | bytes 589832 | tf_op jit(solution)/shard_map/ppermute | solution.py:417
  124.7 3.5 %project.5.kept_ref = bf16[3,384,1024]{2,1,0:T(8,128)(2,1)S(1)} custom-call(s32[3]{0:T(128)S(1)} %broadcast_add_fusion.order_ref, bf16[384,1024]{1,0:T(8,128)(2,1)S(1)} %copy-done.3, bf16[1024,8192]{1,0:T(8,128)(2,1)S(1)} %get-tuple-element.129.w_ref), custom_call_target="tpu_custom_call" | custom-call | flops 2415919104 | bytes 2359296 | tf_op jit(solution)/shard_map/project/pallas_call | solution.py:268
  128.2 1.3 near.3
  130.1 2.6 %collective-permute-start.27 = (bf16[192,1024]{1,0:T(8,128)(2,1)}, bf16[192,1024]{1,0:T(8,128)(2,1)S(1)}, u32[]{:S(2)}, u32[]{:S(2)}) collective-permute-start(bf16[192,1024]{1,0:T(8,128)(2,1)} %get-tuple-element.149), channel_id=1, source_target_pairs={{0,6},{1,7},{2,0},{3,1},{4,2},{5,3},{6,4},{7,5},{8,14},{9,15},{10,... | collective-permute-start | bytes 1179656 | tf_op jit(solution)/shard_map/ppermute | solution.py:426
  132.7 1.0 near.2
  133.7 3.2 %collective-permute-start.23 = (bf16[192,1024]{1,0:T(8,128)(2,1)}, bf16[192,1024]{1,0:T(8,128)(2,1)}, u32[]{:S(2)}, u32[]{:S(2)}) collective-permute-start(bf16[192,1024]{1,0:T(8,128)(2,1)} %get-tuple-element.143), channel_id=1, source_target_pairs={{0,6},{1,7},{2,0},{3,1},{4,2},{5,3},{6,4},{7,5},{8,14},{9,15},{10,... | collective-permute-start | bytes 1179656 | tf_op jit(solution)/shard_map/ppermute | solution.py:426
  137.6 1.2 constant_dynamic-slice_fusion.residual_ref
  138.8 4.1 %collective-permute-done.26.up_ref = bf16[192,1024]{1,0:T(8,128)(2,1)S(1)} collective-permute-done((bf16[192,1024]{1,0:T(8,128)(2,1)}, bf16[192,1024]{1,0:T(8,128)(2,1)S(1)}, u32[]{:S(2)}, u32[]{:S(2)}) %collective-permute-start.26) | collective-permute-done | bytes 393248 | tf_op jit(solution)/shard_map/ppermute | solution.py:425
  142.9 1.7 %copy-done.1 = bf16[3,384,1024]{2,1,0:T(8,128)(2,1)S(1)} copy-done((bf16[3,384,1024]{2,1,0:T(8,128)(2,1)S(1)}, bf16[3,384,1024]{2,1,0:T(8,128)(2,1)}, u32[]{:S(2)}) %copy-start.1) | copy-done | bytes 2359320
  144.6 0.9 last.3
  145.4 4.6 %collective-permute-done.22.up_ref = bf16[192,1024]{1,0:T(8,128)(2,1)} collective-permute-done((bf16[192,1024]{1,0:T(8,128)(2,1)}, bf16[192,1024]{1,0:T(8,128)(2,1)}, u32[]{:S(2)}, u32[]{:S(2)}) %collective-permute-start.22) | collective-permute-done | bytes 393248 | tf_op jit(solution)/shard_map/ppermute | solution.py:425
  150.1 2.0 %last.2 = (f32[192,1024]{1,0:T(8,128)S(1)}, f32[8,192]{1,0:T(8,128)S(1)}) custom-call(bf16[3,384,1024]{2,1,0:T(8,128)(2,1)S(1)} %project.5.kept_ref, bf16[3,384,1024]{2,1,0:T(8,128)(2,1)S(1)} %copy-done.1, bf16[192,1024]{1,0:T(8,128)(2,1)} %collective-permute-done.22.up_ref, bf16[192,1024]{1,0:T(8,128)(2,1)} %collective-permute-done.23.down_ref, ...), custom_call_target="tpu_custom_call" | custom-call | tf_op jit(solution)/shard_map/last/pallas_call | solution.py:351
  152.2 1.1 collective-permute-done.28
  153.4 4.4 %collective-permute-start.30 = (f32[8,384]{1,0:T(8,128)S(1)}, f32[8,384]{1,0:T(8,128)S(1)}, u32[]{:S(2)}, u32[]{:S(2)}) collective-permute-start(f32[8,384]{1,0:T(8,128)S(1)} %fusion.35), channel_id=1, source_target_pairs={{0,4},{1,5},{2,6},{3,7},{4,0},{5,1},{6,2},{7,3},{8,12},{9,13},{10,... | collective-permute-start | bytes 36872 | tf_op jit(solution)/shard_map/ppermute | solution.py:438
  158.3 1.3 collective-permute-done.30
  159.6 1.9 %collective-permute-done.31 = f32[8,384]{1,0:T(8,128)S(1)} collective-permute-done((f32[8,384]{1,0:T(8,128)S(1)}, f32[8,384]{1,0:T(8,128)S(1)}, u32[]{:S(2)}, u32[]{:S(2)}) %collective-permute-start.31) | collective-permute-done | bytes 12320 | tf_op jit(solution)/shard_map/ppermute | solution.py:438
  161.5 1.4 multiply_convert_fusion
  (83 shorter events, 9.8 us)
Async XLA Ops:
  3.2 20.7 %collective-permute-start = (bf16[48,64,128]{2,1,0:T(8,128)(2,1)}, bf16[48,64,128]{2,1,0:T(8,128)(2,1)S(1)}, u32[]{:S(2)}, u32[]{:S(2)}) collective-permute-start(bf16[48,64,128]{2,1,0:T(8,128)(2,1)} %get-tuple-element.86.refs_0_), channel_id=1, source_target_pairs={{0,8},{8,16},{16,24},{24,0},{32,40},{40,48},{48,56},{56,32},{64,72... | collective-permute-start | bytes 2359304 | tf_op jit(solution)/shard_map/ppermute | solution.py:372
  4.7 22.3 %collective-permute-start.1 = (bf16[48,64,128]{2,1,0:T(8,128)(2,1)}, bf16[48,64,128]{2,1,0:T(8,128)(2,1)S(1)}, u32[]{:S(2)}, u32[]{:S(2)}) collective-permute-start(bf16[48,64,128]{2,1,0:T(8,128)(2,1)} %get-tuple-element.86.refs_0_), channel_id=1, source_target_pairs={{0,24},{8,0},{16,8},{24,16},{32,56},{40,32},{48,40},{56,48},{64,88... | collective-permute-start | bytes 2359304 | tf_op jit(solution)/shard_map/ppermute | solution.py:372
  5.3 21.8 %collective-permute-start.2 = (bf16[48,64,128]{2,1,0:T(8,128)(2,1)}, bf16[48,64,128]{2,1,0:T(8,128)(2,1)}, u32[]{:S(2)}, u32[]{:S(2)}) collective-permute-start(bf16[48,64,128]{2,1,0:T(8,128)(2,1)} %get-tuple-element.87.refs_3_.refs_4_), channel_id=1, source_target_pairs={{0,32},{8,40},{16,48},{24,56},{32,64},{40,72},{48,80},{56,88},{64,... | collective-permute-start | bytes 2359304 | tf_op jit(solution)/shard_map/ppermute | solution.py:373
  6.9 20.2 %collective-permute-start.3 = (bf16[48,64,128]{2,1,0:T(8,128)(2,1)}, bf16[48,64,128]{2,1,0:T(8,128)(2,1)}, u32[]{:S(2)}, u32[]{:S(2)}) collective-permute-start(bf16[48,64,128]{2,1,0:T(8,128)(2,1)} %get-tuple-element.87.refs_3_.refs_4_), channel_id=1, source_target_pairs={{0,96},{8,104},{16,112},{24,120},{32,0},{40,8},{48,16},{56,24},{64... | collective-permute-start | bytes 2359304 | tf_op jit(solution)/shard_map/ppermute | solution.py:373
  14.4 36.6 %collective-permute-start.6 = (bf16[48,64,128]{2,1,0:T(8,128)(2,1)}, bf16[48,64,128]{2,1,0:T(8,128)(2,1)}, u32[]{:S(2)}, u32[]{:S(2)}) collective-permute-start(bf16[48,64,128]{2,1,0:T(8,128)(2,1)} %get-tuple-element.86.refs_0_), channel_id=1, source_target_pairs={{0,16},{8,24},{16,0},{24,8},{32,48},{40,56},{48,32},{56,40},{64,80... | collective-permute-start | bytes 2359304 | tf_op jit(solution)/shard_map/ppermute | solution.py:372
  23.9 3.2 %copy-start.4 = (bf16[48,64,128]{2,1,0:T(8,128)(2,1)}, bf16[48,64,128]{2,1,0:T(8,128)(2,1)S(1)}, u32[]{:S(2)}) copy-start(bf16[48,64,128]{2,1,0:T(8,128)(2,1)S(1)} %collective-permute-done.refs_1_) | copy-start | bytes 2359300
  23.9 29.8 %collective-permute-start.7 = (bf16[48,64,128]{2,1,0:T(8,128)(2,1)}, bf16[48,64,128]{2,1,0:T(8,128)(2,1)}, u32[]{:S(2)}, u32[]{:S(2)}) collective-permute-start(bf16[48,64,128]{2,1,0:T(8,128)(2,1)} %get-tuple-element.87.refs_3_.refs_4_), channel_id=1, source_target_pairs={{0,64},{8,72},{16,80},{24,88},{32,96},{40,104},{48,112},{56,120},{... | collective-permute-start | bytes 2359304 | tf_op jit(solution)/shard_map/ppermute | solution.py:373
  27.1 0.9 copy-start.5
  33.6 25.7 %collective-permute-start.4 = (bf16[45,64,128]{2,1,0:T(8,128)(2,1)}, bf16[45,64,128]{2,1,0:T(8,128)(2,1)S(1)}, u32[]{:S(2)}, u32[]{:S(2)}) collective-permute-start(bf16[45,64,128]{2,1,0:T(8,128)(2,1)} %get-tuple-element.82), channel_id=1, source_target_pairs={{0,32},{8,40},{16,48},{24,56},{32,64},{40,72},{48,80},{56,88},{64,... | collective-permute-start | bytes 2211848 | tf_op jit(solution)/shard_map/ppermute | solution.py:378
  34.3 36.1 %collective-permute-start.14 = (bf16[45,64,128]{2,1,0:T(8,128)(2,1)}, bf16[45,64,128]{2,1,0:T(8,128)(2,1)S(1)}, u32[]{:S(2)}, u32[]{:S(2)}) collective-permute-start(bf16[45,64,128]{2,1,0:T(8,128)(2,1)} %get-tuple-element.104), channel_id=1, source_target_pairs={{0,24},{8,0},{16,8},{24,16},{32,56},{40,32},{48,40},{56,48},{64,88... | collective-permute-start | bytes 2211848 | tf_op jit(solution)/shard_map/ppermute | solution.py:378
  48.2 27.5 %collective-permute-start.13 = (bf16[45,64,128]{2,1,0:T(8,128)(2,1)}, bf16[45,64,128]{2,1,0:T(8,128)(2,1)}, u32[]{:S(2)}, u32[]{:S(2)}) collective-permute-start(bf16[45,64,128]{2,1,0:T(8,128)(2,1)} %get-tuple-element.101), channel_id=1, source_target_pairs={{0,16},{8,24},{16,0},{24,8},{32,48},{40,56},{48,32},{56,40},{64,80... | collective-permute-start | bytes 2211848 | tf_op jit(solution)/shard_map/ppermute | solution.py:378
  51.0 27.1 %collective-permute-start.12 = (bf16[45,64,128]{2,1,0:T(8,128)(2,1)}, bf16[45,64,128]{2,1,0:T(8,128)(2,1)}, u32[]{:S(2)}, u32[]{:S(2)}) collective-permute-start(bf16[45,64,128]{2,1,0:T(8,128)(2,1)} %get-tuple-element.98), channel_id=1, source_target_pairs={{0,8},{8,16},{16,24},{24,0},{32,40},{40,48},{48,56},{56,32},{64,72... | collective-permute-start | bytes 2211848 | tf_op jit(solution)/shard_map/ppermute | solution.py:378
  53.6 27.0 %collective-permute-start.8 = (bf16[45,64,128]{2,1,0:T(8,128)(2,1)}, bf16[45,64,128]{2,1,0:T(8,128)(2,1)}, u32[]{:S(2)}, u32[]{:S(2)}) collective-permute-start(bf16[45,64,128]{2,1,0:T(8,128)(2,1)} %get-tuple-element.90), channel_id=1, source_target_pairs={{0,96},{8,104},{16,112},{24,120},{32,0},{40,8},{48,16},{56,24},{64... | collective-permute-start | bytes 2211848 | tf_op jit(solution)/shard_map/ppermute | solution.py:378
  59.3 11.0 %copy-start.6 = (bf16[45,64,128]{2,1,0:T(8,128)(2,1)}, bf16[45,64,128]{2,1,0:T(8,128)(2,1)S(1)}, u32[]{:S(2)}) copy-start(bf16[45,64,128]{2,1,0:T(8,128)(2,1)S(1)} %collective-permute-done.4.refs_8_) | copy-start | bytes 2211844
  59.3 24.3 %collective-permute-start.5 = (bf16[45,64,128]{2,1,0:T(8,128)(2,1)}, bf16[45,64,128]{2,1,0:T(8,128)(2,1)}, u32[]{:S(2)}, u32[]{:S(2)}) collective-permute-start(bf16[45,64,128]{2,1,0:T(8,128)(2,1)} %get-tuple-element.84), channel_id=1, source_target_pairs={{0,64},{8,72},{16,80},{24,88},{32,96},{40,104},{48,112},{56,120},{... | collective-permute-start | bytes 2211848 | tf_op jit(solution)/shard_map/ppermute | solution.py:378
  63.7 10.7 %copy-start.14 = (s32[384]{0:T(512)S(1)}, s32[384]{0:T(512)}, u32[]{:S(2)}) copy-start(s32[384]{0:T(512)} %parent_ref.1) | copy-start | bytes 4612
  70.3 26.3 %copy-start.7 = (bf16[45,64,128]{2,1,0:T(8,128)(2,1)}, bf16[45,64,128]{2,1,0:T(8,128)(2,1)S(1)}, u32[]{:S(2)}) copy-start(bf16[45,64,128]{2,1,0:T(8,128)(2,1)S(1)} %collective-permute-done.14.refs_18_) | copy-start | bytes 2211844
  70.4 13.6 %collective-permute-start.17 = (bf16[18,64,128]{2,1,0:T(8,128)(2,1)}, bf16[18,64,128]{2,1,0:T(8,128)(2,1)S(1)}, u32[]{:S(2)}, u32[]{:S(2)}) collective-permute-start(bf16[18,64,128]{2,1,0:T(8,128)(2,1)} %get-tuple-element.110), channel_id=1, source_target_pairs={{0,24},{8,0},{16,8},{24,16},{32,56},{40,32},{48,40},{56,48},{64,88... | collective-permute-start | bytes 884744 | tf_op jit(solution)/shard_map/ppermute | solution.py:378
  75.6 14.2 %collective-permute-start.16 = (bf16[18,64,128]{2,1,0:T(8,128)(2,1)}, bf16[18,64,128]{2,1,0:T(8,128)(2,1)S(1)}, u32[]{:S(2)}, u32[]{:S(2)}) collective-permute-start(bf16[18,64,128]{2,1,0:T(8,128)(2,1)} %get-tuple-element.109), channel_id=1, source_target_pairs={{0,16},{8,24},{16,0},{24,8},{32,48},{40,56},{48,32},{56,40},{64,80... | collective-permute-start | bytes 884744 | tf_op jit(solution)/shard_map/ppermute | solution.py:378
  78.1 11.6 %collective-permute-start.15 = (bf16[18,64,128]{2,1,0:T(8,128)(2,1)}, bf16[18,64,128]{2,1,0:T(8,128)(2,1)S(1)}, u32[]{:S(2)}, u32[]{:S(2)}) collective-permute-start(bf16[18,64,128]{2,1,0:T(8,128)(2,1)} %get-tuple-element.108), channel_id=1, source_target_pairs={{0,8},{8,16},{16,24},{24,0},{32,40},{40,48},{48,56},{56,32},{64,72... | collective-permute-start | bytes 884744 | tf_op jit(solution)/shard_map/ppermute | solution.py:378
  80.7 9.9 %collective-permute-start.11 = (bf16[18,64,128]{2,1,0:T(8,128)(2,1)}, bf16[18,64,128]{2,1,0:T(8,128)(2,1)S(1)}, u32[]{:S(2)}, u32[]{:S(2)}) collective-permute-start(bf16[18,64,128]{2,1,0:T(8,128)(2,1)} %get-tuple-element.96), channel_id=1, source_target_pairs={{0,96},{8,104},{16,112},{24,120},{32,0},{40,8},{48,16},{56,24},{64... | collective-permute-start | bytes 884744 | tf_op jit(solution)/shard_map/ppermute | solution.py:378
  83.6 10.2 %collective-permute-start.10 = (bf16[18,64,128]{2,1,0:T(8,128)(2,1)}, bf16[18,64,128]{2,1,0:T(8,128)(2,1)S(1)}, u32[]{:S(2)}, u32[]{:S(2)}) collective-permute-start(bf16[18,64,128]{2,1,0:T(8,128)(2,1)} %get-tuple-element.95), channel_id=1, source_target_pairs={{0,64},{8,72},{16,80},{24,88},{32,96},{40,104},{48,112},{56,120},{... | collective-permute-start | bytes 884744 | tf_op jit(solution)/shard_map/ppermute | solution.py:378
  84.0 12.7 %copy-start.8 = (bf16[18,64,128]{2,1,0:T(8,128)(2,1)}, bf16[18,64,128]{2,1,0:T(8,128)(2,1)S(1)}, u32[]{:S(2)}) copy-start(bf16[18,64,128]{2,1,0:T(8,128)(2,1)S(1)} %collective-permute-done.17.refs_22_) | copy-start | bytes 884740
  84.0 12.7 %collective-permute-start.9 = (bf16[18,64,128]{2,1,0:T(8,128)(2,1)}, bf16[18,64,128]{2,1,0:T(8,128)(2,1)S(1)}, u32[]{:S(2)}, u32[]{:S(2)}) collective-permute-start(bf16[18,64,128]{2,1,0:T(8,128)(2,1)} %get-tuple-element.94), channel_id=1, source_target_pairs={{0,32},{8,40},{16,48},{24,56},{32,64},{40,72},{48,80},{56,88},{64,... | collective-permute-start | bytes 884744 | tf_op jit(solution)/shard_map/ppermute | solution.py:378
  89.8 6.9 %copy-start.9 = (bf16[18,64,128]{2,1,0:T(8,128)(2,1)}, bf16[18,64,128]{2,1,0:T(8,128)(2,1)S(1)}, u32[]{:S(2)}) copy-start(bf16[18,64,128]{2,1,0:T(8,128)(2,1)S(1)} %collective-permute-done.16.refs_21_) | copy-start | bytes 884740
  89.8 6.9 %copy-start.10 = (bf16[18,64,128]{2,1,0:T(8,128)(2,1)}, bf16[18,64,128]{2,1,0:T(8,128)(2,1)S(1)}, u32[]{:S(2)}) copy-start(bf16[18,64,128]{2,1,0:T(8,128)(2,1)S(1)} %collective-permute-done.15.refs_20_) | copy-start | bytes 884740
  90.6 6.1 %copy-start.11 = (bf16[18,64,128]{2,1,0:T(8,128)(2,1)}, bf16[18,64,128]{2,1,0:T(8,128)(2,1)S(1)}, u32[]{:S(2)}) copy-start(bf16[18,64,128]{2,1,0:T(8,128)(2,1)S(1)} %collective-permute-done.11.refs_14_) | copy-start | bytes 884740
  93.9 2.8 %copy-start.12 = (bf16[18,64,128]{2,1,0:T(8,128)(2,1)}, bf16[18,64,128]{2,1,0:T(8,128)(2,1)S(1)}, u32[]{:S(2)}) copy-start(bf16[18,64,128]{2,1,0:T(8,128)(2,1)S(1)} %collective-permute-done.10.refs_13_) | copy-start | bytes 884740
  96.7 0.7 copy-start.13
  108.6 1.1 copy-start.2
  112.3 0.7 copy-start.15
  112.3 1.1 copy-start.3
  112.4 4.6 %collective-permute-start.18 = (bf16[384,1024]{1,0:T(8,128)(2,1)S(1)}, bf16[384,1024]{1,0:T(8,128)(2,1)S(1)}, u32[]{:S(2)}, u32[]{:S(2)}) collective-permute-start(bf16[384,1024]{1,0:T(8,128)(2,1)S(1)} %slice_bitcast_fusion), channel_id=1, source_target_pairs={{0,1},{1,0},{2,3},{3,2},{4,5},{5,4},{6,7},{7,6},{8,9},{9,8},{10,11... | collective-permute-start | bytes 2359304 | tf_op jit(solution)/shard_map/ppermute | solution.py:409
  116.9 11.2 %collective-permute-start.19 = (bf16[3,384,1024]{2,1,0:T(8,128)(2,1)S(1)}, bf16[3,384,1024]{2,1,0:T(8,128)(2,1)S(1)}, u32[]{:S(2)}, u32[]{:S(2)}) collective-permute-start(bf16[3,384,1024]{2,1,0:T(8,128)(2,1)S(1)} %project.4), channel_id=1, source_target_pairs={{0,1},{1,0},{2,3},{3,2},{4,5},{5,4},{6,7},{7,6},{8,9},{9,8},{10,11... | collective-permute-start | bytes 7077896 | tf_op jit(solution)/shard_map/ppermute | solution.py:412
  117.2 10.9 %collective-permute-start.24 = (bf16[96,1024]{1,0:T(8,128)(2,1)S(1)}, bf16[96,1024]{1,0:T(8,128)(2,1)S(1)}, u32[]{:S(2)}, u32[]{:S(2)}) collective-permute-start(bf16[96,1024]{1,0:T(8,128)(2,1)S(1)} %get-tuple-element.146), channel_id=1, source_target_pairs={{0,2},{1,3},{2,4},{3,5},{4,6},{5,7},{6,0},{7,1},{8,10},{9,11},{10,... | collective-permute-start | bytes 589832 | tf_op jit(solution)/shard_map/ppermute | solution.py:416
  119.2 8.9 %collective-permute-start.25 = (bf16[96,1024]{1,0:T(8,128)(2,1)S(1)}, bf16[96,1024]{1,0:T(8,128)(2,1)S(1)}, u32[]{:S(2)}, u32[]{:S(2)}) collective-permute-start(bf16[96,1024]{1,0:T(8,128)(2,1)S(1)} %get-tuple-element.147), channel_id=1, source_target_pairs={{0,6},{1,7},{2,0},{3,1},{4,2},{5,3},{6,4},{7,5},{8,14},{9,15},{10,... | collective-permute-start | bytes 589832 | tf_op jit(solution)/shard_map/ppermute | solution.py:417
  121.4 11.3 %collective-permute-start.20 = (bf16[96,1024]{1,0:T(8,128)(2,1)S(1)}, bf16[96,1024]{1,0:T(8,128)(2,1)S(1)}, u32[]{:S(2)}, u32[]{:S(2)}) collective-permute-start(bf16[96,1024]{1,0:T(8,128)(2,1)S(1)} %get-tuple-element.140), channel_id=1, source_target_pairs={{0,2},{1,3},{2,4},{3,5},{4,6},{5,7},{6,0},{7,1},{8,10},{9,11},{10,... | collective-permute-start | bytes 589832 | tf_op jit(solution)/shard_map/ppermute | solution.py:416
  121.4 11.3 %collective-permute-start.21 = (bf16[96,1024]{1,0:T(8,128)(2,1)S(1)}, bf16[96,1024]{1,0:T(8,128)(2,1)S(1)}, u32[]{:S(2)}, u32[]{:S(2)}) collective-permute-start(bf16[96,1024]{1,0:T(8,128)(2,1)S(1)} %get-tuple-element.141), channel_id=1, source_target_pairs={{0,6},{1,7},{2,0},{3,1},{4,2},{5,3},{6,4},{7,5},{8,14},{9,15},{10,... | collective-permute-start | bytes 589832 | tf_op jit(solution)/shard_map/ppermute | solution.py:417
  128.2 4.5 %copy-start = (bf16[3,384,1024]{2,1,0:T(8,128)(2,1)}, bf16[3,384,1024]{2,1,0:T(8,128)(2,1)S(1)}, u32[]{:S(2)}) copy-start(bf16[3,384,1024]{2,1,0:T(8,128)(2,1)S(1)} %collective-permute-done.19.back_ref) | copy-start | bytes 7077892
  129.4 13.5 %collective-permute-start.26 = (bf16[192,1024]{1,0:T(8,128)(2,1)}, bf16[192,1024]{1,0:T(8,128)(2,1)S(1)}, u32[]{:S(2)}, u32[]{:S(2)}) collective-permute-start(bf16[192,1024]{1,0:T(8,128)(2,1)} %get-tuple-element.148), channel_id=1, source_target_pairs={{0,2},{1,3},{2,4},{3,5},{4,6},{5,7},{6,0},{7,1},{8,10},{9,11},{10,... | collective-permute-start | bytes 1179656 | tf_op jit(solution)/shard_map/ppermute | solution.py:425
  130.1 12.8 %collective-permute-start.27 = (bf16[192,1024]{1,0:T(8,128)(2,1)}, bf16[192,1024]{1,0:T(8,128)(2,1)S(1)}, u32[]{:S(2)}, u32[]{:S(2)}) collective-permute-start(bf16[192,1024]{1,0:T(8,128)(2,1)} %get-tuple-element.149), channel_id=1, source_target_pairs={{0,6},{1,7},{2,0},{3,1},{4,2},{5,3},{6,4},{7,5},{8,14},{9,15},{10,... | collective-permute-start | bytes 1179656 | tf_op jit(solution)/shard_map/ppermute | solution.py:426
  133.7 16.3 %collective-permute-start.22 = (bf16[192,1024]{1,0:T(8,128)(2,1)}, bf16[192,1024]{1,0:T(8,128)(2,1)}, u32[]{:S(2)}, u32[]{:S(2)}) collective-permute-start(bf16[192,1024]{1,0:T(8,128)(2,1)} %get-tuple-element.142), channel_id=1, source_target_pairs={{0,2},{1,3},{2,4},{3,5},{4,6},{5,7},{6,0},{7,1},{8,10},{9,11},{10,... | collective-permute-start | bytes 1179656 | tf_op jit(solution)/shard_map/ppermute | solution.py:425
  133.7 16.3 %collective-permute-start.23 = (bf16[192,1024]{1,0:T(8,128)(2,1)}, bf16[192,1024]{1,0:T(8,128)(2,1)}, u32[]{:S(2)}, u32[]{:S(2)}) collective-permute-start(bf16[192,1024]{1,0:T(8,128)(2,1)} %get-tuple-element.143), channel_id=1, source_target_pairs={{0,6},{1,7},{2,0},{3,1},{4,2},{5,3},{6,4},{7,5},{8,14},{9,15},{10,... | collective-permute-start | bytes 1179656 | tf_op jit(solution)/shard_map/ppermute | solution.py:426
  142.9 1.7 %copy-start.1 = (bf16[3,384,1024]{2,1,0:T(8,128)(2,1)S(1)}, bf16[3,384,1024]{2,1,0:T(8,128)(2,1)}, u32[]{:S(2)}) copy-start(bf16[3,384,1024]{2,1,0:T(8,128)(2,1)} %copy-done) | copy-start | bytes 7077892
  152.1 1.2 collective-permute-start.28
  153.4 4.9 %collective-permute-start.29 = (f32[8,384]{1,0:T(8,128)S(1)}, f32[8,384]{1,0:T(8,128)S(1)}, u32[]{:S(2)}, u32[]{:S(2)}) collective-permute-start(f32[8,384]{1,0:T(8,128)S(1)} %fusion.35), channel_id=1, source_target_pairs={{0,2},{1,3},{2,4},{3,5},{4,6},{5,7},{6,0},{7,1},{8,10},{9,11},{10,... | collective-permute-start | bytes 36872 | tf_op jit(solution)/shard_map/ppermute | solution.py:438
  153.4 6.2 %collective-permute-start.30 = (f32[8,384]{1,0:T(8,128)S(1)}, f32[8,384]{1,0:T(8,128)S(1)}, u32[]{:S(2)}, u32[]{:S(2)}) collective-permute-start(f32[8,384]{1,0:T(8,128)S(1)} %fusion.35), channel_id=1, source_target_pairs={{0,4},{1,5},{2,6},{3,7},{4,0},{5,1},{6,2},{7,3},{8,12},{9,13},{10,... | collective-permute-start | bytes 36872 | tf_op jit(solution)/shard_map/ppermute | solution.py:438
  157.8 3.7 %collective-permute-start.31 = (f32[8,384]{1,0:T(8,128)S(1)}, f32[8,384]{1,0:T(8,128)S(1)}, u32[]{:S(2)}, u32[]{:S(2)}) collective-permute-start(f32[8,384]{1,0:T(8,128)S(1)} %fusion.35), channel_id=1, source_target_pairs={{0,6},{1,7},{2,0},{3,1},{4,2},{5,3},{6,4},{7,5},{8,14},{9,15},{10,... | collective-permute-start | bytes 36872 | tf_op jit(solution)/shard_map/ppermute | solution.py:438

commit v6 on v5

--- a/solution.py
+++ b/solution.py
@@ -110,43 +110,84 @@
 
 
 def pack_first_kernel(pages_dev, wanted_ref, *refs):
+    sources, outs, (held, stage, in_sems, out_sem) = refs[:6], refs[6:14], refs[14:]
+    near = len(NEAR)
+    copies = [pltpu.make_async_copy(ref, held.at[k], in_sems.at[k]) for k, ref in enumerate(sources)]
+    for copy in copies:
+        copy.start()
     for i in range(2):
-        parts, outs = refs[3 * i : 3 * i + 3], refs[6 + 4 * i : 10 + 4 * i]
-        for e, out in enumerate(outs):
+        for copy in copies[i * near : (i + 1) * near]:
+            copy.wait()
+        for e in (1, 3, 2, 0):
+            part = stage.at[4 * i + e]
             for j, d in enumerate(NEAR):
-                copy_pages(out, j * PAIR, parts[j], wanted_ref, 16 * i + 4 * d + e, pages_dev)
+                copy_pages(part, j * PAIR, held.at[i * near + j], wanted_ref, 16 * i + 4 * d + e, pages_dev)
+            pltpu.make_async_copy(part, outs[4 * i + e], out_sem.at[4 * i + e]).start()
+    for k, out in enumerate(outs):
+        pltpu.make_async_copy(stage.at[k], out, out_sem.at[k]).wait()
 
 
 def pack_first(wanted, pages_dev, keys, values):
-    outs = [((len(NEAR) * PAIR, PAGE, HD), jnp.bfloat16)] * 8
     args = [keys[d] for d in NEAR] + [values[d] for d in NEAR]
-    return local(functools.partial(pack_first_kernel, pages_dev), "pack_first", outs, wanted, *args, scalars=1, limit=62)
+    part = (len(NEAR) * PAIR, PAGE, HD)
+    scratch = [pltpu.VMEM((len(args),) + keys[0].shape, jnp.bfloat16), pltpu.VMEM((8,) + part, jnp.bfloat16)]
+    scratch += [pltpu.SemaphoreType.DMA((len(args),)), pltpu.SemaphoreType.DMA((8,))]
+    return packing(functools.partial(pack_first_kernel, pages_dev), "pack_first", part, scratch, [wanted], args)
+
+
+def packing(kernel, name, part, scratch, scalars, args):
+    hbm = pl.BlockSpec(memory_space=pltpu.HBM)
+    return pl.pallas_call(
+        kernel,
+        out_shape=[jax.ShapeDtypeStruct(part, jnp.bfloat16)] * 8,
+        in_specs=[pl.BlockSpec(memory_space=pltpu.SMEM)] * len(scalars) + [hbm] * len(args),
+        out_specs=[hbm] * 8,
+        scratch_shapes=scratch,
+        compiler_params=pltpu.CompilerParams(vmem_limit_bytes=62 * MIB),
+        name=name,
+    )(*scalars, *args)
 
 
 def pack_second_kernel(pages_dev, rank_ref, parent_ref, wanted_ref, *refs):
+    sources, outs, (far, roots, stage, in_sems, out_sem) = refs[:8], refs[8:16], refs[16:]
     y, x = rank_ref[0] // 4, rank_ref[0] % 4
     per_rank = parent_ref.shape[0] // RANKS
+    copies = [
+        pltpu.make_async_copy(ref.at[pl.ds(pages_dev, EXTRA)], roots.at[k], in_sems.at[k]) for k, ref in enumerate(sources)
+    ]
+    copies += [pltpu.make_async_copy(sources[4 * i + 2], far.at[i], in_sems.at[8 + i]) for i in range(2)]
+    for copy in copies:
+        copy.start()
+    for copy in copies:
+        copy.wait()
     for i in range(2):
-        parts, outs = refs[4 * i : 4 * i + 4], refs[8 + 4 * i : 12 + 4 * i]
-        for e, out in enumerate(outs):
-            copy_pages(out, 0, parts[2], wanted_ref, 16 * i + 8 + e, pages_dev)
+        for e in (1, 3, 2, 0):
+            part = stage.at[4 * i + e]
+            copy_pages(part, 0, far.at[i], wanted_ref, 16 * i + 8 + e, pages_dev)
             dest = (y + e) % 4 * 4 + x if i == 0 else y * 4 + (x + e) % 4
             for child in range(per_rank - ROOTS):
                 named = jnp.maximum(parent_ref[dest * per_rank + ROOTS + child], 0)
                 up = named // per_rank
                 away = (x + 4 - up % 4) % 4 if i == 0 else (y + 4 - up // 4) % 4
                 root = jnp.minimum(named % per_rank, ROOTS - 1)
-                page, rows = pages_dev + root // 4, pl.ds(pl.multiple_of(root % 4 * NEW, NEW), NEW)
-                picked = parts[0][page, rows, :]
-                for d in (1, 2, 3):
-                    picked = jnp.where(away == d, parts[d][page, rows, :], picked)
-                out[PAIR + child // 4, child % 4 * NEW : (child % 4 + 1) * NEW, :] = picked
+                rows = pl.ds(pl.multiple_of(root % 4 * NEW, NEW), NEW)
+                part[PAIR + child // 4, child % 4 * NEW : (child % 4 + 1) * NEW, :] = roots[4 * i + away, root // 4, rows, :]
+            pltpu.make_async_copy(part, outs[4 * i + e], out_sem.at[4 * i + e]).start()
+    for k, out in enumerate(outs):
+        pltpu.make_async_copy(stage.at[k], out, out_sem.at[k]).wait()
 
 
 def pack_second(rank, parent, wanted, pages_dev, keys, values):
-    outs = [((PAIR + EXTRA, PAGE, HD), jnp.bfloat16)] * 8
+    part = (PAIR + EXTRA, PAGE, HD)
+    scratch = [
+        pltpu.VMEM((2,) + keys[0].shape, jnp.bfloat16),
+        pltpu.VMEM((8, EXTRA, PAGE, HD), jnp.bfloat16),
+        pltpu.VMEM((8,) + part, jnp.bfloat16),
+        pltpu.SemaphoreType.DMA((10,)),
+        pltpu.SemaphoreType.DMA((8,)),
+    ]
     kernel = functools.partial(pack_second_kernel, pages_dev)
-    return local(kernel, "pack_second", outs, rank, parent, wanted, *keys, *values, scalars=3, limit=62)
+    return packing(kernel, "pack_second", part, scratch, [rank, parent, wanted], [*keys, *values])
 
 
 def attend_family(first, node, at_refs, len_ref, above_refs, q_ref, fresh_ref, page_refs, attn_ref):
@@ -238,11 +279,11 @@
     pages = pltpu.VMEM((sum(k.shape[0] for k in keys), PAGE, HD), jnp.bfloat16)
     return pl.pallas_call(
         attend_kernel,
-        out_shape=[jax.ShapeDtypeStruct((rows, width), jnp.bfloat16), pltpu.VMEM(w_out.shape, w_out.dtype)],
+        out_shape=[pltpu.VMEM((rows, width), jnp.bfloat16), pltpu.VMEM(w_out.shape, w_out.dtype)],
         in_specs=[smem] * 5 + [vmem] * 2 + [hbm] * 17,
         out_specs=[vmem, vmem],
         scratch_shapes=[pages, pages, pltpu.SemaphoreType.DMA((10,))],
-        compiler_params=pltpu.CompilerParams(vmem_limit_bytes=45 * MIB),
+        compiler_params=pltpu.CompilerParams(vmem_limit_bytes=44 * MIB),
         cost_estimate=pl.CostEstimate(
             flops=4 * rows * width * 1056 * 4, bytes_accessed=4 * rows * width, transcendentals=rows * 8 * 1056
         ),
@@ -371,7 +412,7 @@
     far_key, far_value, wanted = lax.optimization_barrier((key, value, wanted))
     keys = [key] + [lax.ppermute(far_key if d == 2 else key, "dp", shift(0, d)) for d in (1, 2, 3)]
     values = [value] + [lax.ppermute(far_value if d == 2 else value, "dp", shift(d, 0)) for d in (1, 2, 3)]
-    first = pack_first(wanted, pages_dev, keys, values)
+    first = list(pack_first(wanted, pages_dev, keys, values))
 
     def deliver(parts):
         order = [(e, i) for e in (1, 3, 2) for i in range(2)]

time: 163 us -> 160 us (0.982)
  Pallas kernels: 46.7 us -> 44.2 us
    pallas_call x7 -> x5, Pallas kernels: 17.5 us -> 5.3 us  [local(): pl.pallas_call(kernel, out_shape=[jax.ShapeDtypeStruct(shape, dtype) for...]
    pallas_call x1 -> x3, Pallas kernels: 11.2 us -> 21 us  [the longest x2 10.5 us: packing(): pl.pallas_call(kernel, out_shape=[jax.ShapeDtypeStruct(part, jnp.bfloat16...]
    unnamed x33 -> x29, local copies, waits for them, and re-layouts: 5.41 us -> 3.8 us
where the time goes in v6:
time: 160 us
  starting transfers between devices  70.8 us (44%)
  Pallas kernels  44.2 us (28%)
  waiting for transfers between devices  32.1 us (20%)
  local copies, waits for them, and re-layouts  7.33 us (5%)
  other arithmetic  4.54 us (3%)
    ppermute x12, starting transfers between devices, deliver(): lax.ppermute(parts[4 * i + e], 'dp', shift(0, e) if i else shift(e, 0))  41.6 us
    ppermute x12, waiting for transfers between devices, deliver(): lax.ppermute(parts[4 * i + e], 'dp', shift(0, e) if i else shift(e, 0))  11.3 us
    pallas_call x2, Pallas kernels, packing(): pl.pallas_call(kernel, out_shape=[jax.ShapeDtypeStruct(part, jnp.bfloat16...  10.5 us
    pallas_call x1, Pallas kernels, attend(): pl.pallas_call(attend_kernel, out_shape=[pltpu.VMEM((rows, width), jnp.bf...  10.4 us
    pallas_call x3, Pallas kernels, project(): pl.pallas_call(project_kernel, out_shape=jax.ShapeDtypeStruct((count, row...  9.47 us
    ppermute x2, waiting for transfers between devices, body(): ups.append(lax.ppermute(up, 'tensor', turn(1)))  8.69 us
    ppermute x3, waiting for transfers between devices, body(): lax.ppermute(far_key if d == 2 else key, 'dp', shift(0, d))  7.35 us
    ppermute x3, starting transfers between devices, body(): lax.ppermute(far_value if d == 2 else value, 'dp', shift(d, 0))  6.43 us
  transfers between devices with their start and end apart: 32, of which 11 were waited for; matrix products, arithmetic and copies ran while one was open for 4% of the time, Pallas kernels for 17%

profile of v6, /device:TPU:2, one launch (start us, length us, event | category | flops | bytes accessed | tf_op | source)
XLA Modules:
  0.0 159.9 jit_solution(17212009247737679372)
XLA Ops:
  0.6 2.5 %split.1 = (bf16[48,64,128]{2,1,0:T(8,128)(2,1)}, bf16[48,64,128]{2,1,0:T(8,128)(2,1)}) custom-call(bf16[45,64,256]{2,1,0:T(8,128)(2,1)} %pool_ref.1, bf16[384,256]{1,0:T(8,128)(2,1)} %refs_6_.1), custom_call_target="tpu_custom_call" | custom-call | tf_op jit(solution)/shard_map/split/pallas_call | solution.py:44
  3.2 1.6 collective-permute-start
  5.3 1.6 collective-permute-start.2
  6.9 1.7 %collective-permute-start.3 = (bf16[48,64,128]{2,1,0:T(8,128)(2,1)}, bf16[48,64,128]{2,1,0:T(8,128)(2,1)}, u32[]{:S(2)}, u32[]{:S(2)}) collective-permute-start(bf16[48,64,128]{2,1,0:T(8,128)(2,1)} %get-tuple-element.87.refs_3_.refs_4_), channel_id=1, source_target_pairs={{0,96},{8,104},{16,112},{24,120},{32,0},{40,8},{48,16},{56,24},{64... | collective-permute-start | bytes 2359304 | tf_op jit(solution)/shard_map/ppermute | solution.py:414
  8.5 5.9 %plan.1.wanted_ref = s32[16,128]{1,0:T(8,128)} custom-call(s32[1]{0:T(128)} %bitcast.2.rank_ref, s32[16,384]{1,0:T(8,128)} %bitcast.6), custom_call_target="tpu_custom_call" | custom-call | tf_op jit(solution)/shard_map/plan/pallas_call | solution.py:97
  14.4 2.1 %collective-permute-start.6 = (bf16[48,64,128]{2,1,0:T(8,128)(2,1)}, bf16[48,64,128]{2,1,0:T(8,128)(2,1)}, u32[]{:S(2)}, u32[]{:S(2)}) collective-permute-start(bf16[48,64,128]{2,1,0:T(8,128)(2,1)} %get-tuple-element.86.refs_0_), channel_id=1, source_target_pairs={{0,16},{8,24},{16,0},{24,8},{32,48},{40,56},{48,32},{56,40},{64,80... | collective-permute-start | bytes 2359304 | tf_op jit(solution)/shard_map/ppermute | solution.py:413
  16.5 7.3 %collective-permute-done.refs_1_ = bf16[48,64,128]{2,1,0:T(8,128)(2,1)S(1)} collective-permute-done((bf16[48,64,128]{2,1,0:T(8,128)(2,1)}, bf16[48,64,128]{2,1,0:T(8,128)(2,1)S(1)}, u32[]{:S(2)}, u32[]{:S(2)}) %collective-permute-start) | collective-permute-done | bytes 786464 | tf_op jit(solution)/shard_map/ppermute | solution.py:413
  23.9 3.2 %collective-permute-start.7 = (bf16[48,64,128]{2,1,0:T(8,128)(2,1)}, bf16[48,64,128]{2,1,0:T(8,128)(2,1)}, u32[]{:S(2)}, u32[]{:S(2)}) collective-permute-start(bf16[48,64,128]{2,1,0:T(8,128)(2,1)} %get-tuple-element.87.refs_3_.refs_4_), channel_id=1, source_target_pairs={{0,64},{8,72},{16,80},{24,88},{32,96},{40,104},{48,112},{56,120},{... | collective-permute-start | bytes 2359304 | tf_op jit(solution)/shard_map/ppermute | solution.py:414
  27.1 0.9 copy-done.3
  28.0 5.1 %pack_first.1 = (bf16[45,64,128]{2,1,0:T(8,128)(2,1)}, bf16[45,64,128]{2,1,0:T(8,128)(2,1)}, bf16[45,64,128]{2,1,0:T(8,128)(2,1)}, bf16[45,64,128]{2,1,0:T(8,128...) custom-call(s32[16,128]{1,0:T(8,128)} %plan.1.wanted_ref, ...), custom_call_target="tpu_custom_call" | custom-call | tf_op jit(solution)/shard_map/pack_first/pallas_call | solution.py:140
  33.9 13.1 %collective-permute-start.14 = (bf16[45,64,128]{2,1,0:T(8,128)(2,1)}, bf16[45,64,128]{2,1,0:T(8,128)(2,1)S(1)}, u32[]{:S(2)}, u32[]{:S(2)}) collective-permute-start(bf16[45,64,128]{2,1,0:T(8,128)(2,1)} %get-tuple-element.104), channel_id=1, source_target_pairs={{0,24},{8,0},{16,8},{24,16},{32,56},{40,32},{48,40},{56,48},{64,88... | collective-permute-start | bytes 2211848 | tf_op jit(solution)/shard_map/ppermute | solution.py:419
  47.8 2.9 %collective-permute-start.13 = (bf16[45,64,128]{2,1,0:T(8,128)(2,1)}, bf16[45,64,128]{2,1,0:T(8,128)(2,1)}, u32[]{:S(2)}, u32[]{:S(2)}) collective-permute-start(bf16[45,64,128]{2,1,0:T(8,128)(2,1)} %get-tuple-element.101), channel_id=1, source_target_pairs={{0,16},{8,24},{16,0},{24,8},{32,48},{40,56},{48,32},{56,40},{64,80... | collective-permute-start | bytes 2211848 | tf_op jit(solution)/shard_map/ppermute | solution.py:419
  50.6 2.6 %collective-permute-start.12 = (bf16[45,64,128]{2,1,0:T(8,128)(2,1)}, bf16[45,64,128]{2,1,0:T(8,128)(2,1)}, u32[]{:S(2)}, u32[]{:S(2)}) collective-permute-start(bf16[45,64,128]{2,1,0:T(8,128)(2,1)} %get-tuple-element.98), channel_id=1, source_target_pairs={{0,8},{8,16},{16,24},{24,0},{32,40},{40,48},{48,56},{56,32},{64,72... | collective-permute-start | bytes 2211848 | tf_op jit(solution)/shard_map/ppermute | solution.py:419
  53.2 1.5 collective-permute-start.8
  54.7 4.6 %collective-permute-done.4.refs_8_ = bf16[45,64,128]{2,1,0:T(8,128)(2,1)S(1)} collective-permute-done((bf16[45,64,128]{2,1,0:T(8,128)(2,1)}, bf16[45,64,128]{2,1,0:T(8,128)(2,1)S(1)}, u32[]{:S(2)}, u32[]{:S(2)}) %collective-permute-start.4) | collective-permute-done | bytes 737312 | tf_op jit(solution)/shard_map/ppermute | solution.py:419
  59.3 2.7 %collective-permute-start.5 = (bf16[45,64,128]{2,1,0:T(8,128)(2,1)}, bf16[45,64,128]{2,1,0:T(8,128)(2,1)}, u32[]{:S(2)}, u32[]{:S(2)}) collective-permute-start(bf16[45,64,128]{2,1,0:T(8,128)(2,1)} %get-tuple-element.84), channel_id=1, source_target_pairs={{0,64},{8,72},{16,80},{24,88},{32,96},{40,104},{48,112},{56,120},{... | collective-permute-start | bytes 2211848 | tf_op jit(solution)/shard_map/ppermute | solution.py:419
  62.1 1.3 dynamic_slice.16.refs_2_
  63.7 5.4 %pack_second.1 = (bf16[18,64,128]{2,1,0:T(8,128)(2,1)}, bf16[18,64,128]{2,1,0:T(8,128)(2,1)}, bf16[18,64,128]{2,1,0:T(8,128)(2,1)}, bf16[18,64,128]{2,1,0:T(8,12...) custom-call(s32[1]{0:T(128)} %bitcast.2.rank_ref, ...), custom_call_target="tpu_custom_call" | custom-call | tf_op jit(solution)/shard_map/pack_second/pallas_call | solution.py:140
  69.2 5.3 %collective-permute-start.17 = (bf16[18,64,128]{2,1,0:T(8,128)(2,1)}, bf16[18,64,128]{2,1,0:T(8,128)(2,1)S(1)}, u32[]{:S(2)}, u32[]{:S(2)}) collective-permute-start(bf16[18,64,128]{2,1,0:T(8,128)(2,1)} %get-tuple-element.110), channel_id=1, source_target_pairs={{0,24},{8,0},{16,8},{24,16},{32,56},{40,32},{48,40},{56,48},{64,88... | collective-permute-start | bytes 884744 | tf_op jit(solution)/shard_map/ppermute | solution.py:419
  75.7 2.5 %collective-permute-start.16 = (bf16[18,64,128]{2,1,0:T(8,128)(2,1)}, bf16[18,64,128]{2,1,0:T(8,128)(2,1)S(1)}, u32[]{:S(2)}, u32[]{:S(2)}) collective-permute-start(bf16[18,64,128]{2,1,0:T(8,128)(2,1)} %get-tuple-element.109), channel_id=1, source_target_pairs={{0,16},{8,24},{16,0},{24,8},{32,48},{40,56},{48,32},{56,40},{64,80... | collective-permute-start | bytes 884744 | tf_op jit(solution)/shard_map/ppermute | solution.py:419
  78.3 2.5 %collective-permute-start.15 = (bf16[18,64,128]{2,1,0:T(8,128)(2,1)}, bf16[18,64,128]{2,1,0:T(8,128)(2,1)S(1)}, u32[]{:S(2)}, u32[]{:S(2)}) collective-permute-start(bf16[18,64,128]{2,1,0:T(8,128)(2,1)} %get-tuple-element.108), channel_id=1, source_target_pairs={{0,8},{8,16},{16,24},{24,0},{32,40},{40,48},{48,56},{56,32},{64,72... | collective-permute-start | bytes 884744 | tf_op jit(solution)/shard_map/ppermute | solution.py:419
  80.8 1.8 %collective-permute-start.11 = (bf16[18,64,128]{2,1,0:T(8,128)(2,1)}, bf16[18,64,128]{2,1,0:T(8,128)(2,1)S(1)}, u32[]{:S(2)}, u32[]{:S(2)}) collective-permute-start(bf16[18,64,128]{2,1,0:T(8,128)(2,1)} %get-tuple-element.96), channel_id=1, source_target_pairs={{0,96},{8,104},{16,112},{24,120},{32,0},{40,8},{48,16},{56,24},{64... | collective-permute-start | bytes 884744 | tf_op jit(solution)/shard_map/ppermute | solution.py:419
  83.3 5.4 %collective-permute-start.9 = (bf16[18,64,128]{2,1,0:T(8,128)(2,1)}, bf16[18,64,128]{2,1,0:T(8,128)(2,1)S(1)}, u32[]{:S(2)}, u32[]{:S(2)}) collective-permute-start(bf16[18,64,128]{2,1,0:T(8,128)(2,1)} %get-tuple-element.94), channel_id=1, source_target_pairs={{0,32},{8,40},{16,48},{24,56},{32,64},{40,72},{48,80},{56,88},{64,... | collective-permute-start | bytes 884744 | tf_op jit(solution)/shard_map/ppermute | solution.py:419
  89.4 0.9 collective-permute-done.11.refs_14_
  90.3 3.5 %collective-permute-done.10.refs_13_ = bf16[18,64,128]{2,1,0:T(8,128)(2,1)S(1)} collective-permute-done((bf16[18,64,128]{2,1,0:T(8,128)(2,1)}, bf16[18,64,128]{2,1,0:T(8,128)(2,1)S(1)}, u32[]{:S(2)}, u32[]{:S(2)}) %collective-permute-start.10) | collective-permute-done | bytes 294944 | tf_op jit(solution)/shard_map/ppermute | solution.py:419
  93.8 2.4 %collective-permute-done.9.refs_12_ = bf16[18,64,128]{2,1,0:T(8,128)(2,1)S(1)} collective-permute-done((bf16[18,64,128]{2,1,0:T(8,128)(2,1)}, bf16[18,64,128]{2,1,0:T(8,128)(2,1)S(1)}, u32[]{:S(2)}, u32[]{:S(2)}) %collective-permute-start.9) | collective-permute-done | bytes 294944 | tf_op jit(solution)/shard_map/ppermute | solution.py:419
  96.8 10.4 %attend.1 = (bf16[384,1024]{1,0:T(8,128)(2,1)S(1)}, bf16[1024,8192]{1,0:T(8,128)(2,1)S(1)}) custom-call(s32[384]{0:T(512)} %get-tuple-element.161.refs_0_, s32[384]{0:T(512)} %get-tuple-element.160.refs_1_, s32[24]{0:T(128)} %dynamic_slice.16.refs_2_, s32[24]{0:T(128)} %fusion.24.refs_3_, s32[24]{0:T(128)} %get-tuple-element.156.refs_4_, ...), custom_call_target="tpu_custom_call" | custom-call | flops 6643777536 | bytes 1572864 | tf_op jit(solution)/shard_map/attend/pallas_call | solution.py:280
  107.3 2.5 %project.3.kept_ref = bf16[2,384,1024]{2,1,0:T(8,128)(2,1)S(1)} custom-call(s32[2]{0:T(128)S(1)} %pad_add_fusion.order_ref, bf16[384,1024]{1,0:T(8,128)(2,1)S(1)} %get-tuple-element.138.attn_ref, bf16[1024,8192]{1,0:T(8,128)(2,1)S(1)} %get-tuple-element.129.w_ref), custom_call_target="tpu_custom_call" | custom-call | flops 1610612736 | bytes 1572864 | tf_op jit(solution)/shard_map/project/pallas_call | solution.py:309
  110.5 3.5 %project.4 = bf16[3,384,1024]{2,1,0:T(8,128)(2,1)S(1)} custom-call(s32[3]{0:T(128)S(1)} %get-tuple-element.154.order_ref, bf16[384,1024]{1,0:T(8,128)(2,1)S(1)} %get-tuple-element.138.attn_ref, bf16[1024,8192]{1,0:T(8,128)(2,1)S(1)} %get-tuple-element.129.w_ref), custom_call_target="tpu_custom_call" | custom-call | flops 2415919104 | bytes 2359296 | tf_op jit(solution)/shard_map/project/pallas_call | solution.py:309
  114.3 2.0 %collective-permute-start.24 = (bf16[96,1024]{1,0:T(8,128)(2,1)S(1)}, bf16[96,1024]{1,0:T(8,128)(2,1)S(1)}, u32[]{:S(2)}, u32[]{:S(2)}) collective-permute-start(bf16[96,1024]{1,0:T(8,128)(2,1)S(1)} %get-tuple-element.146), channel_id=1, source_target_pairs={{0,2},{1,3},{2,4},{3,5},{4,6},{5,7},{6,0},{7,1},{8,10},{9,11},{10,... | collective-permute-start | bytes 589832 | tf_op jit(solution)/shard_map/ppermute | solution.py:457
  116.2 2.2 %collective-permute-start.25 = (bf16[96,1024]{1,0:T(8,128)(2,1)S(1)}, bf16[96,1024]{1,0:T(8,128)(2,1)S(1)}, u32[]{:S(2)}, u32[]{:S(2)}) collective-permute-start(bf16[96,1024]{1,0:T(8,128)(2,1)S(1)} %get-tuple-element.147), channel_id=1, source_target_pairs={{0,6},{1,7},{2,0},{3,1},{4,2},{5,3},{6,4},{7,5},{8,14},{9,15},{10,... | collective-permute-start | bytes 589832 | tf_op jit(solution)/shard_map/ppermute | solution.py:458
  118.4 3.2 %collective-permute-start.21 = (bf16[96,1024]{1,0:T(8,128)(2,1)S(1)}, bf16[96,1024]{1,0:T(8,128)(2,1)S(1)}, u32[]{:S(2)}, u32[]{:S(2)}) collective-permute-start(bf16[96,1024]{1,0:T(8,128)(2,1)S(1)} %get-tuple-element.141), channel_id=1, source_target_pairs={{0,6},{1,7},{2,0},{3,1},{4,2},{5,3},{6,4},{7,5},{8,14},{9,15},{10,... | collective-permute-start | bytes 589832 | tf_op jit(solution)/shard_map/ppermute | solution.py:458
  121.7 3.5 %project.5.kept_ref = bf16[3,384,1024]{2,1,0:T(8,128)(2,1)S(1)} custom-call(s32[3]{0:T(128)S(1)} %broadcast_add_fusion.order_ref, bf16[384,1024]{1,0:T(8,128)(2,1)S(1)} %get-tuple-element.138.attn_ref, bf16[1024,8192]{1,0:T(8,128)(2,1)S(1)} %get-tuple-element.129.w_ref), custom_call_target="tpu_custom_call" | custom-call | flops 2415919104 | bytes 2359296 | tf_op jit(solution)/shard_map/project/pallas_call | solution.py:309
  125.2 1.2 near.3
  127.2 2.5 %collective-permute-start.27 = (bf16[192,1024]{1,0:T(8,128)(2,1)}, bf16[192,1024]{1,0:T(8,128)(2,1)S(1)}, u32[]{:S(2)}, u32[]{:S(2)}) collective-permute-start(bf16[192,1024]{1,0:T(8,128)(2,1)} %get-tuple-element.149), channel_id=1, source_target_pairs={{0,6},{1,7},{2,0},{3,1},{4,2},{5,3},{6,4},{7,5},{8,14},{9,15},{10,... | collective-permute-start | bytes 1179656 | tf_op jit(solution)/shard_map/ppermute | solution.py:467
  129.7 1.0 near.2
  130.7 3.2 %collective-permute-start.23 = (bf16[192,1024]{1,0:T(8,128)(2,1)}, bf16[192,1024]{1,0:T(8,128)(2,1)}, u32[]{:S(2)}, u32[]{:S(2)}) collective-permute-start(bf16[192,1024]{1,0:T(8,128)(2,1)} %get-tuple-element.143), channel_id=1, source_target_pairs={{0,6},{1,7},{2,0},{3,1},{4,2},{5,3},{6,4},{7,5},{8,14},{9,15},{10,... | collective-permute-start | bytes 1179656 | tf_op jit(solution)/shard_map/ppermute | solution.py:467
  134.7 1.2 constant_dynamic-slice_fusion.residual_ref
  135.9 4.1 %collective-permute-done.26.up_ref = bf16[192,1024]{1,0:T(8,128)(2,1)S(1)} collective-permute-done((bf16[192,1024]{1,0:T(8,128)(2,1)}, bf16[192,1024]{1,0:T(8,128)(2,1)S(1)}, u32[]{:S(2)}, u32[]{:S(2)}) %collective-permute-start.26) | collective-permute-done | bytes 393248 | tf_op jit(solution)/shard_map/ppermute | solution.py:466
  139.9 1.7 %copy-done.1 = bf16[3,384,1024]{2,1,0:T(8,128)(2,1)S(1)} copy-done((bf16[3,384,1024]{2,1,0:T(8,128)(2,1)S(1)}, bf16[3,384,1024]{2,1,0:T(8,128)(2,1)}, u32[]{:S(2)}) %copy-start.1) | copy-done | bytes 2359320
  141.6 0.9 last.3
  142.4 4.6 %collective-permute-done.22.up_ref = bf16[192,1024]{1,0:T(8,128)(2,1)} collective-permute-done((bf16[192,1024]{1,0:T(8,128)(2,1)}, bf16[192,1024]{1,0:T(8,128)(2,1)}, u32[]{:S(2)}, u32[]{:S(2)}) %collective-permute-start.22) | collective-permute-done | bytes 393248 | tf_op jit(solution)/shard_map/ppermute | solution.py:466
  147.1 2.0 %last.2 = (f32[192,1024]{1,0:T(8,128)S(1)}, f32[8,192]{1,0:T(8,128)S(1)}) custom-call(bf16[3,384,1024]{2,1,0:T(8,128)(2,1)S(1)} %project.5.kept_ref, bf16[3,384,1024]{2,1,0:T(8,128)(2,1)S(1)} %copy-done.1, bf16[192,1024]{1,0:T(8,128)(2,1)} %collective-permute-done.22.up_ref, bf16[192,1024]{1,0:T(8,128)(2,1)} %collective-permute-done.23.down_ref, ...), custom_call_target="tpu_custom_call" | custom-call | tf_op jit(solution)/shard_map/last/pallas_call | solution.py:392
  149.2 1.1 collective-permute-done.28
  150.4 4.4 %collective-permute-start.30 = (f32[8,384]{1,0:T(8,128)S(1)}, f32[8,384]{1,0:T(8,128)S(1)}, u32[]{:S(2)}, u32[]{:S(2)}) collective-permute-start(f32[8,384]{1,0:T(8,128)S(1)} %fusion.35), channel_id=1, source_target_pairs={{0,4},{1,5},{2,6},{3,7},{4,0},{5,1},{6,2},{7,3},{8,12},{9,13},{10,... | collective-permute-start | bytes 36872 | tf_op jit(solution)/shard_map/ppermute | solution.py:479
  155.3 1.3 collective-permute-done.30
  156.6 1.9 %collective-permute-done.31 = f32[8,384]{1,0:T(8,128)S(1)} collective-permute-done((f32[8,384]{1,0:T(8,128)S(1)}, f32[8,384]{1,0:T(8,128)S(1)}, u32[]{:S(2)}, u32[]{:S(2)}) %collective-permute-start.31) | collective-permute-done | bytes 12320 | tf_op jit(solution)/shard_map/ppermute | solution.py:479
  158.6 1.4 multiply_convert_fusion
  (79 shorter events, 9.1 us)
Async XLA Ops:
  3.2 20.7 %collective-permute-start = (bf16[48,64,128]{2,1,0:T(8,128)(2,1)}, bf16[48,64,128]{2,1,0:T(8,128)(2,1)S(1)}, u32[]{:S(2)}, u32[]{:S(2)}) collective-permute-start(bf16[48,64,128]{2,1,0:T(8,128)(2,1)} %get-tuple-element.86.refs_0_), channel_id=1, source_target_pairs={{0,8},{8,16},{16,24},{24,0},{32,40},{40,48},{48,56},{56,32},{64,72... | collective-permute-start | bytes 2359304 | tf_op jit(solution)/shard_map/ppermute | solution.py:413
  4.7 22.3 %collective-permute-start.1 = (bf16[48,64,128]{2,1,0:T(8,128)(2,1)}, bf16[48,64,128]{2,1,0:T(8,128)(2,1)S(1)}, u32[]{:S(2)}, u32[]{:S(2)}) collective-permute-start(bf16[48,64,128]{2,1,0:T(8,128)(2,1)} %get-tuple-element.86.refs_0_), channel_id=1, source_target_pairs={{0,24},{8,0},{16,8},{24,16},{32,56},{40,32},{48,40},{56,48},{64,88... | collective-permute-start | bytes 2359304 | tf_op jit(solution)/shard_map/ppermute | solution.py:413
  5.3 21.8 %collective-permute-start.2 = (bf16[48,64,128]{2,1,0:T(8,128)(2,1)}, bf16[48,64,128]{2,1,0:T(8,128)(2,1)}, u32[]{:S(2)}, u32[]{:S(2)}) collective-permute-start(bf16[48,64,128]{2,1,0:T(8,128)(2,1)} %get-tuple-element.87.refs_3_.refs_4_), channel_id=1, source_target_pairs={{0,32},{8,40},{16,48},{24,56},{32,64},{40,72},{48,80},{56,88},{64,... | collective-permute-start | bytes 2359304 | tf_op jit(solution)/shard_map/ppermute | solution.py:414
  6.9 20.2 %collective-permute-start.3 = (bf16[48,64,128]{2,1,0:T(8,128)(2,1)}, bf16[48,64,128]{2,1,0:T(8,128)(2,1)}, u32[]{:S(2)}, u32[]{:S(2)}) collective-permute-start(bf16[48,64,128]{2,1,0:T(8,128)(2,1)} %get-tuple-element.87.refs_3_.refs_4_), channel_id=1, source_target_pairs={{0,96},{8,104},{16,112},{24,120},{32,0},{40,8},{48,16},{56,24},{64... | collective-permute-start | bytes 2359304 | tf_op jit(solution)/shard_map/ppermute | solution.py:414
  14.4 36.2 %collective-permute-start.6 = (bf16[48,64,128]{2,1,0:T(8,128)(2,1)}, bf16[48,64,128]{2,1,0:T(8,128)(2,1)}, u32[]{:S(2)}, u32[]{:S(2)}) collective-permute-start(bf16[48,64,128]{2,1,0:T(8,128)(2,1)} %get-tuple-element.86.refs_0_), channel_id=1, source_target_pairs={{0,16},{8,24},{16,0},{24,8},{32,48},{40,56},{48,32},{56,40},{64,80... | collective-permute-start | bytes 2359304 | tf_op jit(solution)/shard_map/ppermute | solution.py:413
  23.9 3.2 %copy-start.2 = (bf16[48,64,128]{2,1,0:T(8,128)(2,1)}, bf16[48,64,128]{2,1,0:T(8,128)(2,1)S(1)}, u32[]{:S(2)}) copy-start(bf16[48,64,128]{2,1,0:T(8,128)(2,1)S(1)} %collective-permute-done.refs_1_) | copy-start | bytes 2359300
  23.9 29.4 %collective-permute-start.7 = (bf16[48,64,128]{2,1,0:T(8,128)(2,1)}, bf16[48,64,128]{2,1,0:T(8,128)(2,1)}, u32[]{:S(2)}, u32[]{:S(2)}) collective-permute-start(bf16[48,64,128]{2,1,0:T(8,128)(2,1)} %get-tuple-element.87.refs_3_.refs_4_), channel_id=1, source_target_pairs={{0,64},{8,72},{16,80},{24,88},{32,96},{40,104},{48,112},{56,120},{... | collective-permute-start | bytes 2359304 | tf_op jit(solution)/shard_map/ppermute | solution.py:414
  27.1 0.9 copy-start.3
  33.1 26.2 %collective-permute-start.4 = (bf16[45,64,128]{2,1,0:T(8,128)(2,1)}, bf16[45,64,128]{2,1,0:T(8,128)(2,1)S(1)}, u32[]{:S(2)}, u32[]{:S(2)}) collective-permute-start(bf16[45,64,128]{2,1,0:T(8,128)(2,1)} %get-tuple-element.82), channel_id=1, source_target_pairs={{0,32},{8,40},{16,48},{24,56},{32,64},{40,72},{48,80},{56,88},{64,... | collective-permute-start | bytes 2211848 | tf_op jit(solution)/shard_map/ppermute | solution.py:419
  33.9 35.2 %collective-permute-start.14 = (bf16[45,64,128]{2,1,0:T(8,128)(2,1)}, bf16[45,64,128]{2,1,0:T(8,128)(2,1)S(1)}, u32[]{:S(2)}, u32[]{:S(2)}) collective-permute-start(bf16[45,64,128]{2,1,0:T(8,128)(2,1)} %get-tuple-element.104), channel_id=1, source_target_pairs={{0,24},{8,0},{16,8},{24,16},{32,56},{40,32},{48,40},{56,48},{64,88... | collective-permute-start | bytes 2211848 | tf_op jit(solution)/shard_map/ppermute | solution.py:419
  47.8 28.0 %collective-permute-start.13 = (bf16[45,64,128]{2,1,0:T(8,128)(2,1)}, bf16[45,64,128]{2,1,0:T(8,128)(2,1)}, u32[]{:S(2)}, u32[]{:S(2)}) collective-permute-start(bf16[45,64,128]{2,1,0:T(8,128)(2,1)} %get-tuple-element.101), channel_id=1, source_target_pairs={{0,16},{8,24},{16,0},{24,8},{32,48},{40,56},{48,32},{56,40},{64,80... | collective-permute-start | bytes 2211848 | tf_op jit(solution)/shard_map/ppermute | solution.py:419
  50.6 27.7 %collective-permute-start.12 = (bf16[45,64,128]{2,1,0:T(8,128)(2,1)}, bf16[45,64,128]{2,1,0:T(8,128)(2,1)}, u32[]{:S(2)}, u32[]{:S(2)}) collective-permute-start(bf16[45,64,128]{2,1,0:T(8,128)(2,1)} %get-tuple-element.98), channel_id=1, source_target_pairs={{0,8},{8,16},{16,24},{24,0},{32,40},{40,48},{48,56},{56,32},{64,72... | collective-permute-start | bytes 2211848 | tf_op jit(solution)/shard_map/ppermute | solution.py:419
  53.2 27.5 %collective-permute-start.8 = (bf16[45,64,128]{2,1,0:T(8,128)(2,1)}, bf16[45,64,128]{2,1,0:T(8,128)(2,1)}, u32[]{:S(2)}, u32[]{:S(2)}) collective-permute-start(bf16[45,64,128]{2,1,0:T(8,128)(2,1)} %get-tuple-element.90), channel_id=1, source_target_pairs={{0,96},{8,104},{16,112},{24,120},{32,0},{40,8},{48,16},{56,24},{64... | collective-permute-start | bytes 2211848 | tf_op jit(solution)/shard_map/ppermute | solution.py:419
  59.3 9.8 %copy-start.4 = (bf16[45,64,128]{2,1,0:T(8,128)(2,1)}, bf16[45,64,128]{2,1,0:T(8,128)(2,1)S(1)}, u32[]{:S(2)}) copy-start(bf16[45,64,128]{2,1,0:T(8,128)(2,1)S(1)} %collective-permute-done.4.refs_8_) | copy-start | bytes 2211844
  59.3 23.2 %collective-permute-start.5 = (bf16[45,64,128]{2,1,0:T(8,128)(2,1)}, bf16[45,64,128]{2,1,0:T(8,128)(2,1)}, u32[]{:S(2)}, u32[]{:S(2)}) collective-permute-start(bf16[45,64,128]{2,1,0:T(8,128)(2,1)} %get-tuple-element.84), channel_id=1, source_target_pairs={{0,64},{8,72},{16,80},{24,88},{32,96},{40,104},{48,112},{56,120},{... | collective-permute-start | bytes 2211848 | tf_op jit(solution)/shard_map/ppermute | solution.py:419
  63.7 10.7 %copy-start.12 = (s32[384]{0:T(512)S(1)}, s32[384]{0:T(512)}, u32[]{:S(2)}) copy-start(s32[384]{0:T(512)} %parent_ref.1) | copy-start | bytes 4612
  69.1 27.0 %copy-start.5 = (bf16[45,64,128]{2,1,0:T(8,128)(2,1)}, bf16[45,64,128]{2,1,0:T(8,128)(2,1)S(1)}, u32[]{:S(2)}) copy-start(bf16[45,64,128]{2,1,0:T(8,128)(2,1)S(1)} %collective-permute-done.14.refs_18_) | copy-start | bytes 2211844
  69.2 14.1 %collective-permute-start.17 = (bf16[18,64,128]{2,1,0:T(8,128)(2,1)}, bf16[18,64,128]{2,1,0:T(8,128)(2,1)S(1)}, u32[]{:S(2)}, u32[]{:S(2)}) collective-permute-start(bf16[18,64,128]{2,1,0:T(8,128)(2,1)} %get-tuple-element.110), channel_id=1, source_target_pairs={{0,24},{8,0},{16,8},{24,16},{32,56},{40,32},{48,40},{56,48},{64,88... | collective-permute-start | bytes 884744 | tf_op jit(solution)/shard_map/ppermute | solution.py:419
  75.7 13.6 %collective-permute-start.16 = (bf16[18,64,128]{2,1,0:T(8,128)(2,1)}, bf16[18,64,128]{2,1,0:T(8,128)(2,1)S(1)}, u32[]{:S(2)}, u32[]{:S(2)}) collective-permute-start(bf16[18,64,128]{2,1,0:T(8,128)(2,1)} %get-tuple-element.109), channel_id=1, source_target_pairs={{0,16},{8,24},{16,0},{24,8},{32,48},{40,56},{48,32},{56,40},{64,80... | collective-permute-start | bytes 884744 | tf_op jit(solution)/shard_map/ppermute | solution.py:419
  78.3 11.1 %collective-permute-start.15 = (bf16[18,64,128]{2,1,0:T(8,128)(2,1)}, bf16[18,64,128]{2,1,0:T(8,128)(2,1)S(1)}, u32[]{:S(2)}, u32[]{:S(2)}) collective-permute-start(bf16[18,64,128]{2,1,0:T(8,128)(2,1)} %get-tuple-element.108), channel_id=1, source_target_pairs={{0,8},{8,16},{16,24},{24,0},{32,40},{40,48},{48,56},{56,32},{64,72... | collective-permute-start | bytes 884744 | tf_op jit(solution)/shard_map/ppermute | solution.py:419
  80.8 9.5 %collective-permute-start.11 = (bf16[18,64,128]{2,1,0:T(8,128)(2,1)}, bf16[18,64,128]{2,1,0:T(8,128)(2,1)S(1)}, u32[]{:S(2)}, u32[]{:S(2)}) collective-permute-start(bf16[18,64,128]{2,1,0:T(8,128)(2,1)} %get-tuple-element.96), channel_id=1, source_target_pairs={{0,96},{8,104},{16,112},{24,120},{32,0},{40,8},{48,16},{56,24},{64... | collective-permute-start | bytes 884744 | tf_op jit(solution)/shard_map/ppermute | solution.py:419
  82.6 11.2 %collective-permute-start.10 = (bf16[18,64,128]{2,1,0:T(8,128)(2,1)}, bf16[18,64,128]{2,1,0:T(8,128)(2,1)S(1)}, u32[]{:S(2)}, u32[]{:S(2)}) collective-permute-start(bf16[18,64,128]{2,1,0:T(8,128)(2,1)} %get-tuple-element.95), channel_id=1, source_target_pairs={{0,64},{8,72},{16,80},{24,88},{32,96},{40,104},{48,112},{56,120},{... | collective-permute-start | bytes 884744 | tf_op jit(solution)/shard_map/ppermute | solution.py:419
  83.3 12.8 %copy-start.6 = (bf16[18,64,128]{2,1,0:T(8,128)(2,1)}, bf16[18,64,128]{2,1,0:T(8,128)(2,1)S(1)}, u32[]{:S(2)}) copy-start(bf16[18,64,128]{2,1,0:T(8,128)(2,1)S(1)} %collective-permute-done.17.refs_22_) | copy-start | bytes 884740
  83.3 12.8 %collective-permute-start.9 = (bf16[18,64,128]{2,1,0:T(8,128)(2,1)}, bf16[18,64,128]{2,1,0:T(8,128)(2,1)S(1)}, u32[]{:S(2)}, u32[]{:S(2)}) collective-permute-start(bf16[18,64,128]{2,1,0:T(8,128)(2,1)} %get-tuple-element.94), channel_id=1, source_target_pairs={{0,32},{8,40},{16,48},{24,56},{32,64},{40,72},{48,80},{56,88},{64,... | collective-permute-start | bytes 884744 | tf_op jit(solution)/shard_map/ppermute | solution.py:419
  89.4 6.8 %copy-start.7 = (bf16[18,64,128]{2,1,0:T(8,128)(2,1)}, bf16[18,64,128]{2,1,0:T(8,128)(2,1)S(1)}, u32[]{:S(2)}) copy-start(bf16[18,64,128]{2,1,0:T(8,128)(2,1)S(1)} %collective-permute-done.16.refs_21_) | copy-start | bytes 884740
  89.4 6.8 %copy-start.8 = (bf16[18,64,128]{2,1,0:T(8,128)(2,1)}, bf16[18,64,128]{2,1,0:T(8,128)(2,1)S(1)}, u32[]{:S(2)}) copy-start(bf16[18,64,128]{2,1,0:T(8,128)(2,1)S(1)} %collective-permute-done.15.refs_20_) | copy-start | bytes 884740
  90.3 5.9 %copy-start.9 = (bf16[18,64,128]{2,1,0:T(8,128)(2,1)}, bf16[18,64,128]{2,1,0:T(8,128)(2,1)S(1)}, u32[]{:S(2)}) copy-start(bf16[18,64,128]{2,1,0:T(8,128)(2,1)S(1)} %collective-permute-done.11.refs_14_) | copy-start | bytes 884740
  93.7 2.4 %copy-start.10 = (bf16[18,64,128]{2,1,0:T(8,128)(2,1)}, bf16[18,64,128]{2,1,0:T(8,128)(2,1)S(1)}, u32[]{:S(2)}) copy-start(bf16[18,64,128]{2,1,0:T(8,128)(2,1)S(1)} %collective-permute-done.10.refs_13_) | copy-start | bytes 884740
  96.1 0.7 copy-start.11
  109.8 0.7 copy-start.13
  109.9 4.1 %collective-permute-start.18 = (bf16[384,1024]{1,0:T(8,128)(2,1)S(1)}, bf16[384,1024]{1,0:T(8,128)(2,1)S(1)}, u32[]{:S(2)}, u32[]{:S(2)}) collective-permute-start(bf16[384,1024]{1,0:T(8,128)(2,1)S(1)} %slice_bitcast_fusion), channel_id=1, source_target_pairs={{0,1},{1,0},{2,3},{3,2},{4,5},{5,4},{6,7},{7,6},{8,9},{9,8},{10,11... | collective-permute-start | bytes 2359304 | tf_op jit(solution)/shard_map/ppermute | solution.py:450
  114.0 11.2 %collective-permute-start.19 = (bf16[3,384,1024]{2,1,0:T(8,128)(2,1)S(1)}, bf16[3,384,1024]{2,1,0:T(8,128)(2,1)S(1)}, u32[]{:S(2)}, u32[]{:S(2)}) collective-permute-start(bf16[3,384,1024]{2,1,0:T(8,128)(2,1)S(1)} %project.4), channel_id=1, source_target_pairs={{0,1},{1,0},{2,3},{3,2},{4,5},{5,4},{6,7},{7,6},{8,9},{9,8},{10,11... | collective-permute-start | bytes 7077896 | tf_op jit(solution)/shard_map/ppermute | solution.py:453
  114.3 10.9 %collective-permute-start.24 = (bf16[96,1024]{1,0:T(8,128)(2,1)S(1)}, bf16[96,1024]{1,0:T(8,128)(2,1)S(1)}, u32[]{:S(2)}, u32[]{:S(2)}) collective-permute-start(bf16[96,1024]{1,0:T(8,128)(2,1)S(1)} %get-tuple-element.146), channel_id=1, source_target_pairs={{0,2},{1,3},{2,4},{3,5},{4,6},{5,7},{6,0},{7,1},{8,10},{9,11},{10,... | collective-permute-start | bytes 589832 | tf_op jit(solution)/shard_map/ppermute | solution.py:457
  116.2 8.9 %collective-permute-start.25 = (bf16[96,1024]{1,0:T(8,128)(2,1)S(1)}, bf16[96,1024]{1,0:T(8,128)(2,1)S(1)}, u32[]{:S(2)}, u32[]{:S(2)}) collective-permute-start(bf16[96,1024]{1,0:T(8,128)(2,1)S(1)} %get-tuple-element.147), channel_id=1, source_target_pairs={{0,6},{1,7},{2,0},{3,1},{4,2},{5,3},{6,4},{7,5},{8,14},{9,15},{10,... | collective-permute-start | bytes 589832 | tf_op jit(solution)/shard_map/ppermute | solution.py:458
  118.4 11.3 %collective-permute-start.20 = (bf16[96,1024]{1,0:T(8,128)(2,1)S(1)}, bf16[96,1024]{1,0:T(8,128)(2,1)S(1)}, u32[]{:S(2)}, u32[]{:S(2)}) collective-permute-start(bf16[96,1024]{1,0:T(8,128)(2,1)S(1)} %get-tuple-element.140), channel_id=1, source_target_pairs={{0,2},{1,3},{2,4},{3,5},{4,6},{5,7},{6,0},{7,1},{8,10},{9,11},{10,... | collective-permute-start | bytes 589832 | tf_op jit(solution)/shard_map/ppermute | solution.py:457
  118.4 11.3 %collective-permute-start.21 = (bf16[96,1024]{1,0:T(8,128)(2,1)S(1)}, bf16[96,1024]{1,0:T(8,128)(2,1)S(1)}, u32[]{:S(2)}, u32[]{:S(2)}) collective-permute-start(bf16[96,1024]{1,0:T(8,128)(2,1)S(1)} %get-tuple-element.141), channel_id=1, source_target_pairs={{0,6},{1,7},{2,0},{3,1},{4,2},{5,3},{6,4},{7,5},{8,14},{9,15},{10,... | collective-permute-start | bytes 589832 | tf_op jit(solution)/shard_map/ppermute | solution.py:458
  125.2 4.5 %copy-start = (bf16[3,384,1024]{2,1,0:T(8,128)(2,1)}, bf16[3,384,1024]{2,1,0:T(8,128)(2,1)S(1)}, u32[]{:S(2)}) copy-start(bf16[3,384,1024]{2,1,0:T(8,128)(2,1)S(1)} %collective-permute-done.19.back_ref) | copy-start | bytes 7077892
  126.5 13.5 %collective-permute-start.26 = (bf16[192,1024]{1,0:T(8,128)(2,1)}, bf16[192,1024]{1,0:T(8,128)(2,1)S(1)}, u32[]{:S(2)}, u32[]{:S(2)}) collective-permute-start(bf16[192,1024]{1,0:T(8,128)(2,1)} %get-tuple-element.148), channel_id=1, source_target_pairs={{0,2},{1,3},{2,4},{3,5},{4,6},{5,7},{6,0},{7,1},{8,10},{9,11},{10,... | collective-permute-start | bytes 1179656 | tf_op jit(solution)/shard_map/ppermute | solution.py:466
  127.2 12.8 %collective-permute-start.27 = (bf16[192,1024]{1,0:T(8,128)(2,1)}, bf16[192,1024]{1,0:T(8,128)(2,1)S(1)}, u32[]{:S(2)}, u32[]{:S(2)}) collective-permute-start(bf16[192,1024]{1,0:T(8,128)(2,1)} %get-tuple-element.149), channel_id=1, source_target_pairs={{0,6},{1,7},{2,0},{3,1},{4,2},{5,3},{6,4},{7,5},{8,14},{9,15},{10,... | collective-permute-start | bytes 1179656 | tf_op jit(solution)/shard_map/ppermute | solution.py:467
  130.7 16.3 %collective-permute-start.22 = (bf16[192,1024]{1,0:T(8,128)(2,1)}, bf16[192,1024]{1,0:T(8,128)(2,1)}, u32[]{:S(2)}, u32[]{:S(2)}) collective-permute-start(bf16[192,1024]{1,0:T(8,128)(2,1)} %get-tuple-element.142), channel_id=1, source_target_pairs={{0,2},{1,3},{2,4},{3,5},{4,6},{5,7},{6,0},{7,1},{8,10},{9,11},{10,... | collective-permute-start | bytes 1179656 | tf_op jit(solution)/shard_map/ppermute | solution.py:466
  130.7 16.3 %collective-permute-start.23 = (bf16[192,1024]{1,0:T(8,128)(2,1)}, bf16[192,1024]{1,0:T(8,128)(2,1)}, u32[]{:S(2)}, u32[]{:S(2)}) collective-permute-start(bf16[192,1024]{1,0:T(8,128)(2,1)} %get-tuple-element.143), channel_id=1, source_target_pairs={{0,6},{1,7},{2,0},{3,1},{4,2},{5,3},{6,4},{7,5},{8,14},{9,15},{10,... | collective-permute-start | bytes 1179656 | tf_op jit(solution)/shard_map/ppermute | solution.py:467
  139.9 1.7 %copy-start.1 = (bf16[3,384,1024]{2,1,0:T(8,128)(2,1)S(1)}, bf16[3,384,1024]{2,1,0:T(8,128)(2,1)}, u32[]{:S(2)}) copy-start(bf16[3,384,1024]{2,1,0:T(8,128)(2,1)} %copy-done) | copy-start | bytes 7077892
  149.1 1.2 collective-permute-start.28
  150.4 4.9 %collective-permute-start.29 = (f32[8,384]{1,0:T(8,128)S(1)}, f32[8,384]{1,0:T(8,128)S(1)}, u32[]{:S(2)}, u32[]{:S(2)}) collective-permute-start(f32[8,384]{1,0:T(8,128)S(1)} %fusion.35), channel_id=1, source_target_pairs={{0,2},{1,3},{2,4},{3,5},{4,6},{5,7},{6,0},{7,1},{8,10},{9,11},{10,... | collective-permute-start | bytes 36872 | tf_op jit(solution)/shard_map/ppermute | solution.py:479
  150.4 6.2 %collective-permute-start.30 = (f32[8,384]{1,0:T(8,128)S(1)}, f32[8,384]{1,0:T(8,128)S(1)}, u32[]{:S(2)}, u32[]{:S(2)}) collective-permute-start(f32[8,384]{1,0:T(8,128)S(1)} %fusion.35), channel_id=1, source_target_pairs={{0,4},{1,5},{2,6},{3,7},{4,0},{5,1},{6,2},{7,3},{8,12},{9,13},{10,... | collective-permute-start | bytes 36872 | tf_op jit(solution)/shard_map/ppermute | solution.py:479
  154.8 3.7 %collective-permute-start.31 = (f32[8,384]{1,0:T(8,128)S(1)}, f32[8,384]{1,0:T(8,128)S(1)}, u32[]{:S(2)}, u32[]{:S(2)}) collective-permute-start(f32[8,384]{1,0:T(8,128)S(1)} %fusion.35), channel_id=1, source_target_pairs={{0,6},{1,7},{2,0},{3,1},{4,2},{5,3},{6,4},{7,5},{8,14},{9,15},{10,... | collective-permute-start | bytes 36872 | tf_op jit(solution)/shard_map/ppermute | solution.py:479

commit v7 on v6

--- a/solution.py
+++ b/solution.py
@@ -18,6 +18,7 @@
 PAIR = 15
 ROOTS = 12
 EXTRA = 3
+CHUNK = 6
 NEAR = (0, 1, 3)
 GROUPS = 2
 LOG2E = 1.4426950408889634
@@ -29,7 +30,9 @@
     pages_dev = pool_ref.shape[0]
     for i, out in enumerate(outs):
         lanes = pl.ds(i * HD, HD)
-        pltpu.make_async_copy(pool_ref.at[:, :, lanes], out.at[pl.ds(0, pages_dev)], sem.at[i]).start()
+        for start in range(0, pages_dev, CHUNK):
+            some = pl.ds(start, min(CHUNK, pages_dev - start))
+            pltpu.make_async_copy(pool_ref.at[some, :, lanes], out.at[some], sem.at[i]).start()
         for p in range(EXTRA):
             rows = pl.ds(p * PAGE, PAGE)
             pltpu.make_async_copy(fresh_ref.at[rows, lanes], out.at[pages_dev + p], sem.at[i]).start()
@@ -40,14 +43,14 @@
 def split(pool, fresh):
     hbm = pl.BlockSpec(memory_space=pltpu.HBM)
     vmem = pl.BlockSpec(memory_space=pltpu.VMEM)
-    part = jax.ShapeDtypeStruct((pool.shape[0] + EXTRA, PAGE, HD), pool.dtype)
+    part = pltpu.VMEM((pool.shape[0] + EXTRA, PAGE, HD), pool.dtype)
     return pl.pallas_call(
         split_kernel,
         out_shape=[part, part],
         in_specs=[hbm, hbm],
         out_specs=[vmem, vmem],
         scratch_shapes=[pltpu.SemaphoreType.DMA((2,))],
-        compiler_params=pltpu.CompilerParams(vmem_limit_bytes=55 * MIB),
+        compiler_params=pltpu.CompilerParams(vmem_limit_bytes=61 * MIB),
         name="split",
     )(pool, fresh)
 
@@ -190,7 +193,7 @@
     return packing(kernel, "pack_second", part, scratch, [rank, parent, wanted], [*keys, *values])
 
 
-def attend_family(first, node, at_refs, len_ref, above_refs, q_ref, fresh_ref, page_refs, attn_ref):
+def attend_family(wait_values, first, node, at_refs, len_ref, above_refs, q_ref, fresh_ref, page_refs, attn_ref):
     scale = HD ** (-0.5) * LOG2E
     nt = (((1,), (1,)), ((), ()))
 
@@ -199,7 +202,7 @@
 
     heads = q_ref.shape[1] // HD
     span = heads * NEW
-    shared_key, shared_value = [jnp.concatenate(pages(i, node, 0), axis=0) for i in range(2)]
+    shared_key = jnp.concatenate(pages(0, node, 0), axis=0)
     queries = []
     for i in range(FAM):
         rows = q_ref[first + i * NEW : first + (i + 1) * NEW, :]
@@ -208,22 +211,21 @@
         jnp.concatenate(queries, axis=0), shared_key, nt, preferred_element_type=jnp.float32
     )
     half = SHARED * PAGE // 2
-    values, s_own = [], []
+    def near(j, i):
+        spot = jnp.maximum(above_refs[j][node + i], 0)
+        upper = page_refs[j][spot // PAGE, pl.ds(pl.multiple_of(spot % PAGE, NEW), NEW), :]
+        fresh = fresh_ref[first + i * NEW : first + (i + 1) * NEW, j * HD : (j + 1) * HD]
+        return jnp.concatenate(pages(j, node + i, SHARED) + [fresh, upper], axis=0)
+
+    s_own = []
     for i in range(FAM):
-        both = []
-        for j in range(2):
-            spot = jnp.maximum(above_refs[j][node + i], 0)
-            upper = page_refs[j][spot // PAGE, pl.ds(pl.multiple_of(spot % PAGE, NEW), NEW), :]
-            fresh = fresh_ref[first + i * NEW : first + (i + 1) * NEW, j * HD : (j + 1) * HD]
-            both.append(jnp.concatenate(pages(j, node + i, SHARED) + [fresh, upper], axis=0))
-        s = lax.dot_general(queries[i], both[0], nt, preferred_element_type=jnp.float32)
+        s = lax.dot_general(queries[i], near(0, i), nt, preferred_element_type=jnp.float32)
         late = s[:, half:]
         spot = lax.broadcasted_iota(jnp.int32, late.shape, 1) + SHARED * PAGE + half
         token = lax.broadcasted_iota(jnp.int32, late.shape, 0) % NEW
         key = spot - PATH_PAGES * PAGE
         limit = jnp.where(above_refs[0][node + i] >= 0, 2 * NEW, NEW)
         allowed = (spot < len_ref[node + i]) | ((key >= 0) & (key <= token)) | ((key >= NEW) & (key < limit))
-        values.append(both[1])
         s_own.append(jnp.concatenate([s[:, :half], jnp.where(allowed, late, -jnp.inf)], axis=1))
     tops = [
         jnp.maximum(
@@ -234,6 +236,9 @@
     ]
     w_own = [jnp.exp2((s_own[i] - tops[i]) * scale).astype(jnp.bfloat16) for i in range(FAM)]
     w_shared = jnp.exp2((s_shared - jnp.concatenate(tops, axis=0)) * scale).astype(jnp.bfloat16)
+    wait_values()
+    values = [near(1, i) for i in range(FAM)]
+    shared_value = jnp.concatenate(pages(1, node, 0), axis=0)
     ones = jnp.ones((values[0].shape[0], HD), jnp.bfloat16)
     accum = [
         jnp.dot(w_own[i], jnp.concatenate([values[i], ones], axis=1), preferred_element_type=jnp.float32)
@@ -263,10 +268,13 @@
         rows = pl.ds(part * (w_ref.shape[0] // 8), w_ref.shape[0] // 8)
         weights.append(pltpu.make_async_copy(w_hbm.at[rows], w_ref.at[rows], sems.at[2 + part]))
         weights[-1].start()
-    for i in range(2):
-        pltpu.make_async_copy(page_refs[i], page_refs[i], sems.at[i]).wait()
+    all_pages = [pltpu.make_async_copy(page_refs[i], page_refs[i], sems.at[i]) for i in range(2)]
+    all_pages[0].wait()
     for f in range(q_ref.shape[0] // (FAM * NEW)):
-        attend_family(f * FAM * NEW, f * FAM, at_refs, len_ref, above_refs, q_ref, fresh_ref, page_refs, attn_ref)
+        wait_values = all_pages[1].wait if f == 0 else lambda: None
+        attend_family(
+            wait_values, f * FAM * NEW, f * FAM, at_refs, len_ref, above_refs, q_ref, fresh_ref, page_refs, attn_ref
+        )
     for copy in weights:
         copy.wait()
 
@@ -371,27 +379,42 @@
     down_ref[high] = (pair(1, half) + from_high_ref[...].astype(jnp.float32)).astype(jnp.bfloat16)
 
 
-def last_kernel(first, kept_ref, back_ref, up_ref, down_ref, residual_ref, mixed_ref, power_ref):
-    part = pl.ds(first, up_ref.shape[0])
-    mixed = residual_ref[part].astype(jnp.float32)
-    for term in (kept_ref[2, part], back_ref[2, part], up_ref[...], down_ref[...]):
+def last_kernel(kept_ref, back_ref, up_ref, down_ref, residual_ref, mixed_ref, power_ref):
+    mixed = residual_ref[...].astype(jnp.float32)
+    for term in (kept_ref[0], back_ref[0], up_ref[...], down_ref[...]):
         mixed = mixed + term.astype(jnp.float32)
     mixed_ref[...] = mixed
+    squares = mixed * mixed
     power_ref[...] = lax.dot_general(
-        jnp.ones((8, mixed.shape[1]), jnp.float32),
-        mixed * mixed,
+        jnp.ones((8, 128), jnp.float32),
+        sum(squares[:, start : start + 128] for start in range(0, mixed.shape[1], 128)),
         (((1,), (1,)), ((), ())),
         precision=lax.Precision.HIGHEST,
         preferred_element_type=jnp.float32,
     )
 
 
+def last(g, kept, back, up, down, residual):
+    group, cols = up.shape
+    own = pl.BlockSpec((1, group, cols), lambda i: (2, g, 0))
+    whole = pl.BlockSpec((group, cols), lambda i: (0, 0))
+    return pl.pallas_call(
+        last_kernel,
+        out_shape=[jax.ShapeDtypeStruct((group, cols), jnp.float32), jax.ShapeDtypeStruct((8, group), jnp.float32)],
+        grid=(1,),
+        in_specs=[own, own, whole, whole, pl.BlockSpec((group, cols), lambda i: (g, 0))],
+        out_specs=[whole, pl.BlockSpec((8, group), lambda i: (0, 0))],
+        compiler_params=pltpu.CompilerParams(vmem_limit_bytes=12 * MIB),
+        name="last",
+    )(kept, back, up, down, residual)
+
+
 def local(kernel, name, outs, *args, scalars=0, limit=12):
     vmem = pl.BlockSpec(memory_space=pltpu.VMEM)
     smem = pl.BlockSpec(memory_space=pltpu.SMEM)
     return pl.pallas_call(
         kernel,
-        out_shape=[jax.ShapeDtypeStruct(shape, dtype) for shape, dtype in outs],
+        out_shape=[jax.ShapeDtypeStruct(*out) if isinstance(out, tuple) else out for out in outs],
         in_specs=[smem] * scalars + [vmem] * (len(args) - scalars),
         out_specs=[vmem] * len(outs),
         compiler_params=pltpu.CompilerParams(vmem_limit_bytes=limit * MIB),
@@ -435,7 +458,7 @@
     lengths = lax.dynamic_slice_in_dim(path_len, rank * nodes, nodes)
     at, above = places_of(own_table, lax.dynamic_slice_in_dim(parent, rank * nodes, nodes), rank, pages_dev, nodes)
     z, core = tensor_rank // 2, tensor_rank % 2
-    far, rest = (z + 2) % 4 * 2, (z + jnp.array([1, 3, 0], jnp.int32)) % 4 * 2
+    far, rest = (z + 2) % 4 * 2, (z + (1 + 2 * jnp.arange(3, dtype=jnp.int32)) % 5) % 4 * 2
     far = jnp.stack([far + 1 - core, far + core])
     other, same = rest + 1 - core, rest + core
 
@@ -457,7 +480,7 @@
     low = [lax.ppermute(sent[2 * g], "tensor", turn(1)) for g in range(GROUPS)]
     high = [lax.ppermute(sent[2 * g + 1], "tensor", turn(-1)) for g in range(GROUPS)]
     kept = project(same, attn, w_held)
-    whole = ((group, cols), jnp.bfloat16)
+    whole = pltpu.VMEM((group, cols), jnp.bfloat16)
     ups, downs = [], []
     for g in range(GROUPS):
         up, down = local(
@@ -465,19 +488,13 @@
         )
         ups.append(lax.ppermute(up, "tensor", turn(1)))
         downs.append(lax.ppermute(down, "tensor", turn(-1)))
-    outs = [((group, cols), jnp.float32), ((8, group), jnp.float32)]
-    done = [
-        local(functools.partial(last_kernel, g * group), "last", outs, kept, back, ups[g], downs[g], mine)
-        for g in range(GROUPS)
-    ]
+    done = [last(g, kept, back, ups[g], downs[g], mine) for g in range(GROUPS)]
 
     mixed = jnp.concatenate([m for m, _ in done], axis=0)
     power = jnp.concatenate([p for _, p in done], axis=1)
-    power = power + lax.ppermute(power, "tensor", swap)
-    total = power
-    for d in (1, 2, 3):
-        total = total + lax.ppermute(power, "tensor", turn(d))
-    norm = lax.rsqrt(total[0].reshape(rows, 1) / D + 1e-05)
+    for flip in (1, 2, 6):
+        power = power + lax.ppermute(power, "tensor", [(t, t ^ flip) for t in range(tensors)])
+    norm = lax.rsqrt(power[0].reshape(rows, 1) / D + 1e-05)
     own_gain = lax.dynamic_slice_in_dim(gain, tensor_rank * cols, cols)
     normed = mixed * norm * own_gain.astype(jnp.float32)
     return (mixed.astype(jnp.bfloat16), normed.astype(jnp.bfloat16))

time: 160 us -> 159 us (level)
  waiting for transfers between devices: 32.1 us -> 34.1 us
  Pallas kernels: 44.2 us -> 42.5 us
    ppermute x4 -> x3, starting transfers between devices: 4.44 us -> 3.03 us  [body(): lax.ppermute(power, 'tensor', [(t, t ^ flip) for t in range(tensors)])]
    ppermute x4 -> x3, waiting for transfers between devices: 4.73 us -> 5.99 us  [body(): lax.ppermute(power, 'tensor', [(t, t ^ flip) for t in range(tensors)])]
  transfers between devices with their start and end apart: 32 -> 31, of which waited for: 11 -> 10; matrix products, arithmetic and copies ran while one was open for 4% -> 4% of each run, Pallas kernels for 17% -> 17%
where the time goes in v7:
time: 159 us
  starting transfers between devices  69.5 us (44%)
  Pallas kernels  42.5 us (27%)
  waiting for transfers between devices  34.1 us (21%)
  local copies, waits for them, and re-layouts  6.94 us (4%)
  other arithmetic  4.54 us (3%)
    ppermute x12, starting transfers between devices, deliver(): lax.ppermute(parts[4 * i + e], 'dp', shift(0, e) if i else shift(e, 0))  41.3 us
    ppermute x12, waiting for transfers between devices, deliver(): lax.ppermute(parts[4 * i + e], 'dp', shift(0, e) if i else shift(e, 0))  11.7 us
    pallas_call x2, Pallas kernels, packing(): pl.pallas_call(kernel, out_shape=[jax.ShapeDtypeStruct(part, jnp.bfloat16...  10.5 us
    pallas_call x1, Pallas kernels, attend(): pl.pallas_call(attend_kernel, out_shape=[pltpu.VMEM((rows, width), jnp.bf...  9.75 us
    pallas_call x3, Pallas kernels, project(): pl.pallas_call(project_kernel, out_shape=jax.ShapeDtypeStruct((count, row...  9.47 us
    ppermute x2, waiting for transfers between devices, body(): ups.append(lax.ppermute(up, 'tensor', turn(1)))  9.3 us
    ppermute x3, waiting for transfers between devices, body(): lax.ppermute(far_key if d == 2 else key, 'dp', shift(0, d))  7.15 us
    ppermute x3, starting transfers between devices, body(): lax.ppermute(far_value if d == 2 else value, 'dp', shift(d, 0))  6.43 us
  transfers between devices with their start and end apart: 31, of which 10 were waited for; matrix products, arithmetic and copies ran while one was open for 4% of the time, Pallas kernels for 17%

profile of v7, /device:TPU:2, one launch (start us, length us, event | category | flops | bytes accessed | tf_op | source)
XLA Modules:
  0.0 158.5 jit_solution(6622043070333411907)
XLA Ops:
  0.6 2.3 %split.1 = (bf16[48,64,128]{2,1,0:T(8,128)(2,1)S(1)}, bf16[48,64,128]{2,1,0:T(8,128)(2,1)}) custom-call(bf16[45,64,256]{2,1,0:T(8,128)(2,1)} %pool_ref.1, bf16[384,256]{1,0:T(8,128)(2,1)} %refs_6_.1), custom_call_target="tpu_custom_call" | custom-call | tf_op jit(solution)/shard_map/split/pallas_call | solution.py:47
  3.0 1.6 collective-permute-start
  5.1 1.6 collective-permute-start.2
  6.6 1.7 %collective-permute-start.3 = (bf16[48,64,128]{2,1,0:T(8,128)(2,1)}, bf16[48,64,128]{2,1,0:T(8,128)(2,1)}, u32[]{:S(2)}, u32[]{:S(2)}) collective-permute-start(bf16[48,64,128]{2,1,0:T(8,128)(2,1)} %get-tuple-element.87.refs_3_.refs_4_), channel_id=1, source_target_pairs={{0,96},{8,104},{16,112},{24,120},{32,0},{40,8},{48,16},{56,24},{64... | collective-permute-start | bytes 2359304 | tf_op jit(solution)/shard_map/ppermute | solution.py:437
  8.3 5.9 %plan.1.wanted_ref = s32[16,128]{1,0:T(8,128)} custom-call(s32[1]{0:T(128)} %bitcast.2.rank_ref, s32[16,384]{1,0:T(8,128)} %bitcast.6), custom_call_target="tpu_custom_call" | custom-call | tf_op jit(solution)/shard_map/plan/pallas_call | solution.py:100
  14.2 2.1 %collective-permute-start.6 = (bf16[48,64,128]{2,1,0:T(8,128)(2,1)S(1)}, bf16[48,64,128]{2,1,0:T(8,128)(2,1)}, u32[]{:S(2)}, u32[]{:S(2)}) collective-permute-start(bf16[48,64,128]{2,1,0:T(8,128)(2,1)S(1)} %get-tuple-element.86.refs_0_), channel_id=1, source_target_pairs={{0,16},{8,24},{16,0},{24,8},{32,48},{40,56},{48,32},{56,40},{64,80... | collective-permute-start | bytes 2359304 | tf_op jit(solution)/shard_map/ppermute | solution.py:436
  16.3 7.1 %collective-permute-done.refs_1_ = bf16[48,64,128]{2,1,0:T(8,128)(2,1)S(1)} collective-permute-done((bf16[48,64,128]{2,1,0:T(8,128)(2,1)S(1)}, bf16[48,64,128]{2,1,0:T(8,128)(2,1)S(1)}, u32[]{:S(2)}, u32[]{:S(2)}) %collective-permute-start) | collective-permute-done | bytes 786464 | tf_op jit(solution)/shard_map/ppermute | solution.py:436
  23.5 3.2 %collective-permute-start.7 = (bf16[48,64,128]{2,1,0:T(8,128)(2,1)}, bf16[48,64,128]{2,1,0:T(8,128)(2,1)}, u32[]{:S(2)}, u32[]{:S(2)}) collective-permute-start(bf16[48,64,128]{2,1,0:T(8,128)(2,1)} %get-tuple-element.87.refs_3_.refs_4_), channel_id=1, source_target_pairs={{0,64},{8,72},{16,80},{24,88},{32,96},{40,104},{48,112},{56,120},{... | collective-permute-start | bytes 2359304 | tf_op jit(solution)/shard_map/ppermute | solution.py:437
  26.7 0.9 copy-done.4
  27.6 5.2 %pack_first.1 = (bf16[45,64,128]{2,1,0:T(8,128)(2,1)}, bf16[45,64,128]{2,1,0:T(8,128)(2,1)}, bf16[45,64,128]{2,1,0:T(8,128)(2,1)}, bf16[45,64,128]{2,1,0:T(8,128...) custom-call(s32[16,128]{1,0:T(8,128)} %plan.1.wanted_ref, ...), custom_call_target="tpu_custom_call" | custom-call | tf_op jit(solution)/shard_map/pack_first/pallas_call | solution.py:143
  33.5 13.0 %collective-permute-start.14 = (bf16[45,64,128]{2,1,0:T(8,128)(2,1)}, bf16[45,64,128]{2,1,0:T(8,128)(2,1)}, u32[]{:S(2)}, u32[]{:S(2)}) collective-permute-start(bf16[45,64,128]{2,1,0:T(8,128)(2,1)} %get-tuple-element.104), channel_id=1, source_target_pairs={{0,24},{8,0},{16,8},{24,16},{32,56},{40,32},{48,40},{56,48},{64,88... | collective-permute-start | bytes 2211848 | tf_op jit(solution)/shard_map/ppermute | solution.py:442
  46.5 0.8 constant_dynamic-slice_fusion.1
  47.3 3.0 %collective-permute-start.13 = (bf16[45,64,128]{2,1,0:T(8,128)(2,1)}, bf16[45,64,128]{2,1,0:T(8,128)(2,1)}, u32[]{:S(2)}, u32[]{:S(2)}) collective-permute-start(bf16[45,64,128]{2,1,0:T(8,128)(2,1)} %get-tuple-element.101), channel_id=1, source_target_pairs={{0,16},{8,24},{16,0},{24,8},{32,48},{40,56},{48,32},{56,40},{64,80... | collective-permute-start | bytes 2211848 | tf_op jit(solution)/shard_map/ppermute | solution.py:442
  50.2 2.6 %collective-permute-start.12 = (bf16[45,64,128]{2,1,0:T(8,128)(2,1)}, bf16[45,64,128]{2,1,0:T(8,128)(2,1)S(1)}, u32[]{:S(2)}, u32[]{:S(2)}) collective-permute-start(bf16[45,64,128]{2,1,0:T(8,128)(2,1)} %get-tuple-element.98), channel_id=1, source_target_pairs={{0,8},{8,16},{16,24},{24,0},{32,40},{40,48},{48,56},{56,32},{64,72... | collective-permute-start | bytes 2211848 | tf_op jit(solution)/shard_map/ppermute | solution.py:442
  52.9 1.5 collective-permute-start.8
  54.4 4.8 %collective-permute-done.4.refs_8_ = bf16[45,64,128]{2,1,0:T(8,128)(2,1)} collective-permute-done((bf16[45,64,128]{2,1,0:T(8,128)(2,1)}, bf16[45,64,128]{2,1,0:T(8,128)(2,1)}, u32[]{:S(2)}, u32[]{:S(2)}) %collective-permute-start.4) | collective-permute-done | bytes 737312 | tf_op jit(solution)/shard_map/ppermute | solution.py:442
  59.2 2.4 %collective-permute-start.5 = (bf16[45,64,128]{2,1,0:T(8,128)(2,1)}, bf16[45,64,128]{2,1,0:T(8,128)(2,1)}, u32[]{:S(2)}, u32[]{:S(2)}) collective-permute-start(bf16[45,64,128]{2,1,0:T(8,128)(2,1)} %get-tuple-element.84), channel_id=1, source_target_pairs={{0,64},{8,72},{16,80},{24,88},{32,96},{40,104},{48,112},{56,120},{... | collective-permute-start | bytes 2211848 | tf_op jit(solution)/shard_map/ppermute | solution.py:442
  61.8 1.3 dynamic_slice.16.refs_2_
  63.4 5.4 %pack_second.1 = (bf16[18,64,128]{2,1,0:T(8,128)(2,1)}, bf16[18,64,128]{2,1,0:T(8,128)(2,1)}, bf16[18,64,128]{2,1,0:T(8,128)(2,1)}, bf16[18,64,128]{2,1,0:T(8,12...) custom-call(s32[1]{0:T(128)} %bitcast.2.rank_ref, ...), custom_call_target="tpu_custom_call" | custom-call | tf_op jit(solution)/shard_map/pack_second/pallas_call | solution.py:143
  68.8 5.3 %collective-permute-start.17 = (bf16[18,64,128]{2,1,0:T(8,128)(2,1)}, bf16[18,64,128]{2,1,0:T(8,128)(2,1)S(1)}, u32[]{:S(2)}, u32[]{:S(2)}) collective-permute-start(bf16[18,64,128]{2,1,0:T(8,128)(2,1)} %get-tuple-element.110), channel_id=1, source_target_pairs={{0,24},{8,0},{16,8},{24,16},{32,56},{40,32},{48,40},{56,48},{64,88... | collective-permute-start | bytes 884744 | tf_op jit(solution)/shard_map/ppermute | solution.py:442
  75.4 2.5 %collective-permute-start.16 = (bf16[18,64,128]{2,1,0:T(8,128)(2,1)}, bf16[18,64,128]{2,1,0:T(8,128)(2,1)S(1)}, u32[]{:S(2)}, u32[]{:S(2)}) collective-permute-start(bf16[18,64,128]{2,1,0:T(8,128)(2,1)} %get-tuple-element.109), channel_id=1, source_target_pairs={{0,16},{8,24},{16,0},{24,8},{32,48},{40,56},{48,32},{56,40},{64,80... | collective-permute-start | bytes 884744 | tf_op jit(solution)/shard_map/ppermute | solution.py:442
  77.9 2.6 %collective-permute-start.15 = (bf16[18,64,128]{2,1,0:T(8,128)(2,1)}, bf16[18,64,128]{2,1,0:T(8,128)(2,1)S(1)}, u32[]{:S(2)}, u32[]{:S(2)}) collective-permute-start(bf16[18,64,128]{2,1,0:T(8,128)(2,1)} %get-tuple-element.108), channel_id=1, source_target_pairs={{0,8},{8,16},{16,24},{24,0},{32,40},{40,48},{48,56},{56,32},{64,72... | collective-permute-start | bytes 884744 | tf_op jit(solution)/shard_map/ppermute | solution.py:442
  80.6 1.7 %collective-permute-start.11 = (bf16[18,64,128]{2,1,0:T(8,128)(2,1)}, bf16[18,64,128]{2,1,0:T(8,128)(2,1)S(1)}, u32[]{:S(2)}, u32[]{:S(2)}) collective-permute-start(bf16[18,64,128]{2,1,0:T(8,128)(2,1)} %get-tuple-element.96), channel_id=1, source_target_pairs={{0,96},{8,104},{16,112},{24,120},{32,0},{40,8},{48,16},{56,24},{64... | collective-permute-start | bytes 884744 | tf_op jit(solution)/shard_map/ppermute | solution.py:442
  82.2 1.0 collective-permute-start.10
  83.3 4.9 %collective-permute-start.9 = (bf16[18,64,128]{2,1,0:T(8,128)(2,1)}, bf16[18,64,128]{2,1,0:T(8,128)(2,1)S(1)}, u32[]{:S(2)}, u32[]{:S(2)}) collective-permute-start(bf16[18,64,128]{2,1,0:T(8,128)(2,1)} %get-tuple-element.94), channel_id=1, source_target_pairs={{0,32},{8,40},{16,48},{24,56},{32,64},{40,72},{48,80},{56,88},{64,... | collective-permute-start | bytes 884744 | tf_op jit(solution)/shard_map/ppermute | solution.py:442
  88.8 1.0 collective-permute-done.11.refs_14_
  89.9 3.4 %collective-permute-done.10.refs_13_ = bf16[18,64,128]{2,1,0:T(8,128)(2,1)S(1)} collective-permute-done((bf16[18,64,128]{2,1,0:T(8,128)(2,1)}, bf16[18,64,128]{2,1,0:T(8,128)(2,1)S(1)}, u32[]{:S(2)}, u32[]{:S(2)}) %collective-permute-start.10) | collective-permute-done | bytes 294944 | tf_op jit(solution)/shard_map/ppermute | solution.py:442
  93.3 2.4 %collective-permute-done.9.refs_12_ = bf16[18,64,128]{2,1,0:T(8,128)(2,1)S(1)} collective-permute-done((bf16[18,64,128]{2,1,0:T(8,128)(2,1)}, bf16[18,64,128]{2,1,0:T(8,128)(2,1)S(1)}, u32[]{:S(2)}, u32[]{:S(2)}) %collective-permute-start.9) | collective-permute-done | bytes 294944 | tf_op jit(solution)/shard_map/ppermute | solution.py:442
  96.4 9.7 %attend.1 = (bf16[384,1024]{1,0:T(8,128)(2,1)S(1)}, bf16[1024,8192]{1,0:T(8,128)(2,1)S(1)}) custom-call(s32[384]{0:T(512)} %get-tuple-element.159.refs_0_, s32[384]{0:T(512)} %get-tuple-element.158.refs_1_, s32[24]{0:T(128)} %dynamic_slice.16.refs_2_, s32[24]{0:T(128)} %fusion.24.refs_3_, s32[24]{0:T(128)} %get-tuple-element.154.refs_4_, ...), custom_call_target="tpu_custom_call" | custom-call | flops 6643777536 | bytes 1572864 | tf_op jit(solution)/shard_map/attend/pallas_call | solution.py:288
  106.2 2.5 %project.3.kept_ref = bf16[2,384,1024]{2,1,0:T(8,128)(2,1)S(1)} custom-call(s32[2]{0:T(128)S(1)} %pad_add_fusion.order_ref, bf16[384,1024]{1,0:T(8,128)(2,1)S(1)} %get-tuple-element.138.attn_ref, bf16[1024,8192]{1,0:T(8,128)(2,1)S(1)} %get-tuple-element.129.w_ref), custom_call_target="tpu_custom_call" | custom-call | flops 1610612736 | bytes 1572864 | tf_op jit(solution)/shard_map/project/pallas_call | solution.py:317
  108.9 3.5 %project.4 = bf16[3,384,1024]{2,1,0:T(8,128)(2,1)S(1)} custom-call(s32[3]{0:T(128)S(1)} %add_subtract_fusion.order_ref, bf16[384,1024]{1,0:T(8,128)(2,1)S(1)} %get-tuple-element.138.attn_ref, bf16[1024,8192]{1,0:T(8,128)(2,1)S(1)} %get-tuple-element.129.w_ref), custom_call_target="tpu_custom_call" | custom-call | flops 2415919104 | bytes 2359296 | tf_op jit(solution)/shard_map/project/pallas_call | solution.py:317
  113.2 2.0 %collective-permute-start.24 = (bf16[96,1024]{1,0:T(8,128)(2,1)S(1)}, bf16[96,1024]{1,0:T(8,128)(2,1)S(1)}, u32[]{:S(2)}, u32[]{:S(2)}) collective-permute-start(bf16[96,1024]{1,0:T(8,128)(2,1)S(1)} %get-tuple-element.146), channel_id=1, source_target_pairs={{0,2},{1,3},{2,4},{3,5},{4,6},{5,7},{6,0},{7,1},{8,10},{9,11},{10,... | collective-permute-start | bytes 589832 | tf_op jit(solution)/shard_map/ppermute | solution.py:480
  115.2 2.2 %collective-permute-start.25 = (bf16[96,1024]{1,0:T(8,128)(2,1)S(1)}, bf16[96,1024]{1,0:T(8,128)(2,1)S(1)}, u32[]{:S(2)}, u32[]{:S(2)}) collective-permute-start(bf16[96,1024]{1,0:T(8,128)(2,1)S(1)} %get-tuple-element.147), channel_id=1, source_target_pairs={{0,6},{1,7},{2,0},{3,1},{4,2},{5,3},{6,4},{7,5},{8,14},{9,15},{10,... | collective-permute-start | bytes 589832 | tf_op jit(solution)/shard_map/ppermute | solution.py:481
  117.4 3.2 %collective-permute-start.21 = (bf16[96,1024]{1,0:T(8,128)(2,1)S(1)}, bf16[96,1024]{1,0:T(8,128)(2,1)S(1)}, u32[]{:S(2)}, u32[]{:S(2)}) collective-permute-start(bf16[96,1024]{1,0:T(8,128)(2,1)S(1)} %get-tuple-element.141), channel_id=1, source_target_pairs={{0,6},{1,7},{2,0},{3,1},{4,2},{5,3},{6,4},{7,5},{8,14},{9,15},{10,... | collective-permute-start | bytes 589832 | tf_op jit(solution)/shard_map/ppermute | solution.py:481
  120.6 3.5 %project.5.kept_ref = bf16[3,384,1024]{2,1,0:T(8,128)(2,1)S(1)} custom-call(s32[3]{0:T(128)S(1)} %broadcast_add_fusion.order_ref, bf16[384,1024]{1,0:T(8,128)(2,1)S(1)} %get-tuple-element.138.attn_ref, bf16[1024,8192]{1,0:T(8,128)(2,1)S(1)} %get-tuple-element.129.w_ref), custom_call_target="tpu_custom_call" | custom-call | flops 2415919104 | bytes 2359296 | tf_op jit(solution)/shard_map/project/pallas_call | solution.py:317
  124.1 1.2 near.3
  126.1 2.5 %collective-permute-start.27 = (bf16[192,1024]{1,0:T(8,128)(2,1)}, bf16[192,1024]{1,0:T(8,128)(2,1)S(1)}, u32[]{:S(2)}, u32[]{:S(2)}) collective-permute-start(bf16[192,1024]{1,0:T(8,128)(2,1)} %get-tuple-element.149), channel_id=1, source_target_pairs={{0,6},{1,7},{2,0},{3,1},{4,2},{5,3},{6,4},{7,5},{8,14},{9,15},{10,... | collective-permute-start | bytes 1179656 | tf_op jit(solution)/shard_map/ppermute | solution.py:490
  128.6 1.0 near.2
  129.7 3.2 %collective-permute-start.23 = (bf16[192,1024]{1,0:T(8,128)(2,1)}, bf16[192,1024]{1,0:T(8,128)(2,1)}, u32[]{:S(2)}, u32[]{:S(2)}) collective-permute-start(bf16[192,1024]{1,0:T(8,128)(2,1)} %get-tuple-element.143), channel_id=1, source_target_pairs={{0,6},{1,7},{2,0},{3,1},{4,2},{5,3},{6,4},{7,5},{8,14},{9,15},{10,... | collective-permute-start | bytes 1179656 | tf_op jit(solution)/shard_map/ppermute | solution.py:490
  132.9 1.2 constant_dynamic-slice_fusion.residual_ref
  134.1 4.8 %collective-permute-done.26.up_ref = bf16[192,1024]{1,0:T(8,128)(2,1)S(1)} collective-permute-done((bf16[192,1024]{1,0:T(8,128)(2,1)}, bf16[192,1024]{1,0:T(8,128)(2,1)S(1)}, u32[]{:S(2)}, u32[]{:S(2)}) %collective-permute-start.26) | collective-permute-done | bytes 393248 | tf_op jit(solution)/shard_map/ppermute | solution.py:489
  138.9 1.7 %copy-done.1 = bf16[3,384,1024]{2,1,0:T(8,128)(2,1)S(1)} copy-done((bf16[3,384,1024]{2,1,0:T(8,128)(2,1)S(1)}, bf16[3,384,1024]{2,1,0:T(8,128)(2,1)}, u32[]{:S(2)}) %copy-start.1) | copy-done | bytes 2359320
  141.0 4.5 %collective-permute-done.22.up_ref = bf16[192,1024]{1,0:T(8,128)(2,1)} collective-permute-done((bf16[192,1024]{1,0:T(8,128)(2,1)}, bf16[192,1024]{1,0:T(8,128)(2,1)}, u32[]{:S(2)}, u32[]{:S(2)}) %collective-permute-start.22) | collective-permute-done | bytes 393248 | tf_op jit(solution)/shard_map/ppermute | solution.py:489
  145.5 1.6 %last.2 = (f32[192,1024]{1,0:T(8,128)S(1)}, f32[8,192]{1,0:T(8,128)S(1)}) custom-call(bf16[3,384,1024]{2,1,0:T(8,128)(2,1)S(1)} %project.5.kept_ref, bf16[3,384,1024]{2,1,0:T(8,128)(2,1)S(1)} %copy-done.1, bf16[192,1024]{1,0:T(8,128)(2,1)} %collective-permute-done.22.up_ref, bf16[192,1024]{1,0:T(8,128)(2,1)} %collective-permute-done.23.down_ref, ...), custom_call_target="tpu_custom_call" | custom-call | tf_op jit(solution)/shard_map/last/pallas_call | solution.py:401
  148.6 3.6 %collective-permute-done.29 = f32[8,384]{1,0:T(8,128)S(1)} collective-permute-done((f32[8,384]{1,0:T(8,128)S(1)}, f32[8,384]{1,0:T(8,128)S(1)}, u32[]{:S(2)}, u32[]{:S(2)}) %collective-permute-start.29) | collective-permute-done | bytes 12320 | tf_op jit(solution)/shard_map/ppermute | solution.py:496
  152.2 3.0 %collective-permute-start.30 = (f32[8,384]{1,0:T(8,128)S(1)}, f32[8,384]{1,0:T(8,128)S(1)}, u32[]{:S(2)}, u32[]{:S(2)}) collective-permute-start(f32[8,384]{1,0:T(8,128)S(1)} %add.219), channel_id=1, source_target_pairs={{0,6},{1,7},{2,4},{3,5},{4,2},{5,3},{6,0},{7,1},{8,14},{9,15},{10,... | collective-permute-start | bytes 36872 | tf_op jit(solution)/shard_map/ppermute | solution.py:496
  155.2 1.9 %collective-permute-done.30 = f32[8,384]{1,0:T(8,128)S(1)} collective-permute-done((f32[8,384]{1,0:T(8,128)S(1)}, f32[8,384]{1,0:T(8,128)S(1)}, u32[]{:S(2)}, u32[]{:S(2)}) %collective-permute-start.30) | collective-permute-done | bytes 12320 | tf_op jit(solution)/shard_map/ppermute | solution.py:496
  157.2 1.4 multiply_convert_fusion
  (78 shorter events, 8.2 us)
Async XLA Ops:
  3.0 24.6 %copy-start.2 = (bf16[48,64,128]{2,1,0:T(8,128)(2,1)}, bf16[48,64,128]{2,1,0:T(8,128)(2,1)S(1)}, u32[]{:S(2)}) copy-start(bf16[48,64,128]{2,1,0:T(8,128)(2,1)S(1)} %get-tuple-element.86.refs_0_) | copy-start | bytes 2359300
  3.0 20.5 %collective-permute-start = (bf16[48,64,128]{2,1,0:T(8,128)(2,1)S(1)}, bf16[48,64,128]{2,1,0:T(8,128)(2,1)S(1)}, u32[]{:S(2)}, u32[]{:S(2)}) collective-permute-start(bf16[48,64,128]{2,1,0:T(8,128)(2,1)S(1)} %get-tuple-element.86.refs_0_), channel_id=1, source_target_pairs={{0,8},{8,16},{16,24},{24,0},{32,40},{40,48},{48,56},{56,32},{64,72... | collective-permute-start | bytes 2359304 | tf_op jit(solution)/shard_map/ppermute | solution.py:436
  4.5 22.1 %collective-permute-start.1 = (bf16[48,64,128]{2,1,0:T(8,128)(2,1)S(1)}, bf16[48,64,128]{2,1,0:T(8,128)(2,1)S(1)}, u32[]{:S(2)}, u32[]{:S(2)}) collective-permute-start(bf16[48,64,128]{2,1,0:T(8,128)(2,1)S(1)} %get-tuple-element.86.refs_0_), channel_id=1, source_target_pairs={{0,24},{8,0},{16,8},{24,16},{32,56},{40,32},{48,40},{56,48},{64,88... | collective-permute-start | bytes 2359304 | tf_op jit(solution)/shard_map/ppermute | solution.py:436
  5.1 21.6 %collective-permute-start.2 = (bf16[48,64,128]{2,1,0:T(8,128)(2,1)}, bf16[48,64,128]{2,1,0:T(8,128)(2,1)}, u32[]{:S(2)}, u32[]{:S(2)}) collective-permute-start(bf16[48,64,128]{2,1,0:T(8,128)(2,1)} %get-tuple-element.87.refs_3_.refs_4_), channel_id=1, source_target_pairs={{0,32},{8,40},{16,48},{24,56},{32,64},{40,72},{48,80},{56,88},{64,... | collective-permute-start | bytes 2359304 | tf_op jit(solution)/shard_map/ppermute | solution.py:437
  6.6 20.9 %collective-permute-start.3 = (bf16[48,64,128]{2,1,0:T(8,128)(2,1)}, bf16[48,64,128]{2,1,0:T(8,128)(2,1)}, u32[]{:S(2)}, u32[]{:S(2)}) collective-permute-start(bf16[48,64,128]{2,1,0:T(8,128)(2,1)} %get-tuple-element.87.refs_3_.refs_4_), channel_id=1, source_target_pairs={{0,96},{8,104},{16,112},{24,120},{32,0},{40,8},{48,16},{56,24},{64... | collective-permute-start | bytes 2359304 | tf_op jit(solution)/shard_map/ppermute | solution.py:437
  14.2 36.1 %collective-permute-start.6 = (bf16[48,64,128]{2,1,0:T(8,128)(2,1)S(1)}, bf16[48,64,128]{2,1,0:T(8,128)(2,1)}, u32[]{:S(2)}, u32[]{:S(2)}) collective-permute-start(bf16[48,64,128]{2,1,0:T(8,128)(2,1)S(1)} %get-tuple-element.86.refs_0_), channel_id=1, source_target_pairs={{0,16},{8,24},{16,0},{24,8},{32,48},{40,56},{48,32},{56,40},{64,80... | collective-permute-start | bytes 2359304 | tf_op jit(solution)/shard_map/ppermute | solution.py:436
  23.5 3.2 %copy-start.3 = (bf16[48,64,128]{2,1,0:T(8,128)(2,1)}, bf16[48,64,128]{2,1,0:T(8,128)(2,1)S(1)}, u32[]{:S(2)}) copy-start(bf16[48,64,128]{2,1,0:T(8,128)(2,1)S(1)} %collective-permute-done.refs_1_) | copy-start | bytes 2359300
  23.5 29.4 %collective-permute-start.7 = (bf16[48,64,128]{2,1,0:T(8,128)(2,1)}, bf16[48,64,128]{2,1,0:T(8,128)(2,1)}, u32[]{:S(2)}, u32[]{:S(2)}) collective-permute-start(bf16[48,64,128]{2,1,0:T(8,128)(2,1)} %get-tuple-element.87.refs_3_.refs_4_), channel_id=1, source_target_pairs={{0,64},{8,72},{16,80},{24,88},{32,96},{40,104},{48,112},{56,120},{... | collective-permute-start | bytes 2359304 | tf_op jit(solution)/shard_map/ppermute | solution.py:437
  26.7 0.9 copy-start.4
  32.8 26.4 %collective-permute-start.4 = (bf16[45,64,128]{2,1,0:T(8,128)(2,1)}, bf16[45,64,128]{2,1,0:T(8,128)(2,1)}, u32[]{:S(2)}, u32[]{:S(2)}) collective-permute-start(bf16[45,64,128]{2,1,0:T(8,128)(2,1)} %get-tuple-element.82), channel_id=1, source_target_pairs={{0,32},{8,40},{16,48},{24,56},{32,64},{40,72},{48,80},{56,88},{64,... | collective-permute-start | bytes 2211848 | tf_op jit(solution)/shard_map/ppermute | solution.py:442
  33.5 35.3 %collective-permute-start.14 = (bf16[45,64,128]{2,1,0:T(8,128)(2,1)}, bf16[45,64,128]{2,1,0:T(8,128)(2,1)}, u32[]{:S(2)}, u32[]{:S(2)}) collective-permute-start(bf16[45,64,128]{2,1,0:T(8,128)(2,1)} %get-tuple-element.104), channel_id=1, source_target_pairs={{0,24},{8,0},{16,8},{24,16},{32,56},{40,32},{48,40},{56,48},{64,88... | collective-permute-start | bytes 2211848 | tf_op jit(solution)/shard_map/ppermute | solution.py:442
  47.3 28.1 %collective-permute-start.13 = (bf16[45,64,128]{2,1,0:T(8,128)(2,1)}, bf16[45,64,128]{2,1,0:T(8,128)(2,1)}, u32[]{:S(2)}, u32[]{:S(2)}) collective-permute-start(bf16[45,64,128]{2,1,0:T(8,128)(2,1)} %get-tuple-element.101), channel_id=1, source_target_pairs={{0,16},{8,24},{16,0},{24,8},{32,48},{40,56},{48,32},{56,40},{64,80... | collective-permute-start | bytes 2211848 | tf_op jit(solution)/shard_map/ppermute | solution.py:442
  50.2 27.7 %collective-permute-start.12 = (bf16[45,64,128]{2,1,0:T(8,128)(2,1)}, bf16[45,64,128]{2,1,0:T(8,128)(2,1)S(1)}, u32[]{:S(2)}, u32[]{:S(2)}) collective-permute-start(bf16[45,64,128]{2,1,0:T(8,128)(2,1)} %get-tuple-element.98), channel_id=1, source_target_pairs={{0,8},{8,16},{16,24},{24,0},{32,40},{40,48},{48,56},{56,32},{64,72... | collective-permute-start | bytes 2211848 | tf_op jit(solution)/shard_map/ppermute | solution.py:442
  52.9 27.7 %collective-permute-start.8 = (bf16[45,64,128]{2,1,0:T(8,128)(2,1)}, bf16[45,64,128]{2,1,0:T(8,128)(2,1)S(1)}, u32[]{:S(2)}, u32[]{:S(2)}) collective-permute-start(bf16[45,64,128]{2,1,0:T(8,128)(2,1)} %get-tuple-element.90), channel_id=1, source_target_pairs={{0,96},{8,104},{16,112},{24,120},{32,0},{40,8},{48,16},{56,24},{64... | collective-permute-start | bytes 2211848 | tf_op jit(solution)/shard_map/ppermute | solution.py:442
  59.2 23.0 %collective-permute-start.5 = (bf16[45,64,128]{2,1,0:T(8,128)(2,1)}, bf16[45,64,128]{2,1,0:T(8,128)(2,1)}, u32[]{:S(2)}, u32[]{:S(2)}) collective-permute-start(bf16[45,64,128]{2,1,0:T(8,128)(2,1)} %get-tuple-element.84), channel_id=1, source_target_pairs={{0,64},{8,72},{16,80},{24,88},{32,96},{40,104},{48,112},{56,120},{... | collective-permute-start | bytes 2211848 | tf_op jit(solution)/shard_map/ppermute | solution.py:442
  63.4 10.7 %copy-start.13 = (s32[384]{0:T(512)S(1)}, s32[384]{0:T(512)}, u32[]{:S(2)}) copy-start(s32[384]{0:T(512)} %parent_ref.1) | copy-start | bytes 4612
  68.8 14.4 %collective-permute-start.17 = (bf16[18,64,128]{2,1,0:T(8,128)(2,1)}, bf16[18,64,128]{2,1,0:T(8,128)(2,1)S(1)}, u32[]{:S(2)}, u32[]{:S(2)}) collective-permute-start(bf16[18,64,128]{2,1,0:T(8,128)(2,1)} %get-tuple-element.110), channel_id=1, source_target_pairs={{0,24},{8,0},{16,8},{24,16},{32,56},{40,32},{48,40},{56,48},{64,88... | collective-permute-start | bytes 884744 | tf_op jit(solution)/shard_map/ppermute | solution.py:442
  75.4 13.4 %collective-permute-start.16 = (bf16[18,64,128]{2,1,0:T(8,128)(2,1)}, bf16[18,64,128]{2,1,0:T(8,128)(2,1)S(1)}, u32[]{:S(2)}, u32[]{:S(2)}) collective-permute-start(bf16[18,64,128]{2,1,0:T(8,128)(2,1)} %get-tuple-element.109), channel_id=1, source_target_pairs={{0,16},{8,24},{16,0},{24,8},{32,48},{40,56},{48,32},{56,40},{64,80... | collective-permute-start | bytes 884744 | tf_op jit(solution)/shard_map/ppermute | solution.py:442
  77.9 18.5 %copy-start.5 = (bf16[45,64,128]{2,1,0:T(8,128)(2,1)}, bf16[45,64,128]{2,1,0:T(8,128)(2,1)S(1)}, u32[]{:S(2)}) copy-start(bf16[45,64,128]{2,1,0:T(8,128)(2,1)S(1)} %collective-permute-done.12.refs_16_) | copy-start | bytes 2211844
  77.9 10.9 %collective-permute-start.15 = (bf16[18,64,128]{2,1,0:T(8,128)(2,1)}, bf16[18,64,128]{2,1,0:T(8,128)(2,1)S(1)}, u32[]{:S(2)}, u32[]{:S(2)}) collective-permute-start(bf16[18,64,128]{2,1,0:T(8,128)(2,1)} %get-tuple-element.108), channel_id=1, source_target_pairs={{0,8},{8,16},{16,24},{24,0},{32,40},{40,48},{48,56},{56,32},{64,72... | collective-permute-start | bytes 884744 | tf_op jit(solution)/shard_map/ppermute | solution.py:442
  80.6 15.8 %copy-start.6 = (bf16[45,64,128]{2,1,0:T(8,128)(2,1)}, bf16[45,64,128]{2,1,0:T(8,128)(2,1)S(1)}, u32[]{:S(2)}) copy-start(bf16[45,64,128]{2,1,0:T(8,128)(2,1)S(1)} %collective-permute-done.8.refs_10_) | copy-start | bytes 2211844
  80.6 9.3 %collective-permute-start.11 = (bf16[18,64,128]{2,1,0:T(8,128)(2,1)}, bf16[18,64,128]{2,1,0:T(8,128)(2,1)S(1)}, u32[]{:S(2)}, u32[]{:S(2)}) collective-permute-start(bf16[18,64,128]{2,1,0:T(8,128)(2,1)} %get-tuple-element.96), channel_id=1, source_target_pairs={{0,96},{8,104},{16,112},{24,120},{32,0},{40,8},{48,16},{56,24},{64... | collective-permute-start | bytes 884744 | tf_op jit(solution)/shard_map/ppermute | solution.py:442
  82.2 11.1 %collective-permute-start.10 = (bf16[18,64,128]{2,1,0:T(8,128)(2,1)}, bf16[18,64,128]{2,1,0:T(8,128)(2,1)S(1)}, u32[]{:S(2)}, u32[]{:S(2)}) collective-permute-start(bf16[18,64,128]{2,1,0:T(8,128)(2,1)} %get-tuple-element.95), channel_id=1, source_target_pairs={{0,64},{8,72},{16,80},{24,88},{32,96},{40,104},{48,112},{56,120},{... | collective-permute-start | bytes 884744 | tf_op jit(solution)/shard_map/ppermute | solution.py:442
  83.3 13.1 %copy-start.7 = (bf16[18,64,128]{2,1,0:T(8,128)(2,1)}, bf16[18,64,128]{2,1,0:T(8,128)(2,1)S(1)}, u32[]{:S(2)}) copy-start(bf16[18,64,128]{2,1,0:T(8,128)(2,1)S(1)} %collective-permute-done.17.refs_22_) | copy-start | bytes 884740
  83.3 12.4 %collective-permute-start.9 = (bf16[18,64,128]{2,1,0:T(8,128)(2,1)}, bf16[18,64,128]{2,1,0:T(8,128)(2,1)S(1)}, u32[]{:S(2)}, u32[]{:S(2)}) collective-permute-start(bf16[18,64,128]{2,1,0:T(8,128)(2,1)} %get-tuple-element.94), channel_id=1, source_target_pairs={{0,32},{8,40},{16,48},{24,56},{32,64},{40,72},{48,80},{56,88},{64,... | collective-permute-start | bytes 884744 | tf_op jit(solution)/shard_map/ppermute | solution.py:442
  88.8 7.6 %copy-start.8 = (bf16[18,64,128]{2,1,0:T(8,128)(2,1)}, bf16[18,64,128]{2,1,0:T(8,128)(2,1)S(1)}, u32[]{:S(2)}) copy-start(bf16[18,64,128]{2,1,0:T(8,128)(2,1)S(1)} %collective-permute-done.16.refs_21_) | copy-start | bytes 884740
  88.8 7.6 %copy-start.9 = (bf16[18,64,128]{2,1,0:T(8,128)(2,1)}, bf16[18,64,128]{2,1,0:T(8,128)(2,1)S(1)}, u32[]{:S(2)}) copy-start(bf16[18,64,128]{2,1,0:T(8,128)(2,1)S(1)} %collective-permute-done.15.refs_20_) | copy-start | bytes 884740
  89.9 6.5 %copy-start.10 = (bf16[18,64,128]{2,1,0:T(8,128)(2,1)}, bf16[18,64,128]{2,1,0:T(8,128)(2,1)S(1)}, u32[]{:S(2)}) copy-start(bf16[18,64,128]{2,1,0:T(8,128)(2,1)S(1)} %collective-permute-done.11.refs_14_) | copy-start | bytes 884740
  93.3 3.1 %copy-start.11 = (bf16[18,64,128]{2,1,0:T(8,128)(2,1)}, bf16[18,64,128]{2,1,0:T(8,128)(2,1)S(1)}, u32[]{:S(2)}) copy-start(bf16[18,64,128]{2,1,0:T(8,128)(2,1)S(1)} %collective-permute-done.10.refs_13_) | copy-start | bytes 884740
  95.7 0.7 copy-start.12
  108.8 3.6 %collective-permute-start.18 = (bf16[384,1024]{1,0:T(8,128)(2,1)S(1)}, bf16[384,1024]{1,0:T(8,128)(2,1)S(1)}, u32[]{:S(2)}, u32[]{:S(2)}) collective-permute-start(bf16[384,1024]{1,0:T(8,128)(2,1)S(1)} %slice_bitcast_fusion), channel_id=1, source_target_pairs={{0,1},{1,0},{2,3},{3,2},{4,5},{5,4},{6,7},{7,6},{8,9},{9,8},{10,11... | collective-permute-start | bytes 2359304 | tf_op jit(solution)/shard_map/ppermute | solution.py:473
  112.4 11.7 %collective-permute-start.19 = (bf16[3,384,1024]{2,1,0:T(8,128)(2,1)S(1)}, bf16[3,384,1024]{2,1,0:T(8,128)(2,1)S(1)}, u32[]{:S(2)}, u32[]{:S(2)}) collective-permute-start(bf16[3,384,1024]{2,1,0:T(8,128)(2,1)S(1)} %project.4), channel_id=1, source_target_pairs={{0,1},{1,0},{2,3},{3,2},{4,5},{5,4},{6,7},{7,6},{8,9},{9,8},{10,11... | collective-permute-start | bytes 7077896 | tf_op jit(solution)/shard_map/ppermute | solution.py:476
  113.2 10.9 %collective-permute-start.24 = (bf16[96,1024]{1,0:T(8,128)(2,1)S(1)}, bf16[96,1024]{1,0:T(8,128)(2,1)S(1)}, u32[]{:S(2)}, u32[]{:S(2)}) collective-permute-start(bf16[96,1024]{1,0:T(8,128)(2,1)S(1)} %get-tuple-element.146), channel_id=1, source_target_pairs={{0,2},{1,3},{2,4},{3,5},{4,6},{5,7},{6,0},{7,1},{8,10},{9,11},{10,... | collective-permute-start | bytes 589832 | tf_op jit(solution)/shard_map/ppermute | solution.py:480
  115.2 8.9 %collective-permute-start.25 = (bf16[96,1024]{1,0:T(8,128)(2,1)S(1)}, bf16[96,1024]{1,0:T(8,128)(2,1)S(1)}, u32[]{:S(2)}, u32[]{:S(2)}) collective-permute-start(bf16[96,1024]{1,0:T(8,128)(2,1)S(1)} %get-tuple-element.147), channel_id=1, source_target_pairs={{0,6},{1,7},{2,0},{3,1},{4,2},{5,3},{6,4},{7,5},{8,14},{9,15},{10,... | collective-permute-start | bytes 589832 | tf_op jit(solution)/shard_map/ppermute | solution.py:481
  117.4 11.3 %collective-permute-start.20 = (bf16[96,1024]{1,0:T(8,128)(2,1)S(1)}, bf16[96,1024]{1,0:T(8,128)(2,1)S(1)}, u32[]{:S(2)}, u32[]{:S(2)}) collective-permute-start(bf16[96,1024]{1,0:T(8,128)(2,1)S(1)} %get-tuple-element.140), channel_id=1, source_target_pairs={{0,2},{1,3},{2,4},{3,5},{4,6},{5,7},{6,0},{7,1},{8,10},{9,11},{10,... | collective-permute-start | bytes 589832 | tf_op jit(solution)/shard_map/ppermute | solution.py:480
  117.4 11.3 %collective-permute-start.21 = (bf16[96,1024]{1,0:T(8,128)(2,1)S(1)}, bf16[96,1024]{1,0:T(8,128)(2,1)S(1)}, u32[]{:S(2)}, u32[]{:S(2)}) collective-permute-start(bf16[96,1024]{1,0:T(8,128)(2,1)S(1)} %get-tuple-element.141), channel_id=1, source_target_pairs={{0,6},{1,7},{2,0},{3,1},{4,2},{5,3},{6,4},{7,5},{8,14},{9,15},{10,... | collective-permute-start | bytes 589832 | tf_op jit(solution)/shard_map/ppermute | solution.py:481
  124.1 4.5 %copy-start = (bf16[3,384,1024]{2,1,0:T(8,128)(2,1)}, bf16[3,384,1024]{2,1,0:T(8,128)(2,1)S(1)}, u32[]{:S(2)}) copy-start(bf16[3,384,1024]{2,1,0:T(8,128)(2,1)S(1)} %collective-permute-done.19.back_ref) | copy-start | bytes 7077892
  125.4 13.5 %collective-permute-start.26 = (bf16[192,1024]{1,0:T(8,128)(2,1)}, bf16[192,1024]{1,0:T(8,128)(2,1)S(1)}, u32[]{:S(2)}, u32[]{:S(2)}) collective-permute-start(bf16[192,1024]{1,0:T(8,128)(2,1)} %get-tuple-element.148), channel_id=1, source_target_pairs={{0,2},{1,3},{2,4},{3,5},{4,6},{5,7},{6,0},{7,1},{8,10},{9,11},{10,... | collective-permute-start | bytes 1179656 | tf_op jit(solution)/shard_map/ppermute | solution.py:489
  126.1 12.7 %collective-permute-start.27 = (bf16[192,1024]{1,0:T(8,128)(2,1)}, bf16[192,1024]{1,0:T(8,128)(2,1)S(1)}, u32[]{:S(2)}, u32[]{:S(2)}) collective-permute-start(bf16[192,1024]{1,0:T(8,128)(2,1)} %get-tuple-element.149), channel_id=1, source_target_pairs={{0,6},{1,7},{2,0},{3,1},{4,2},{5,3},{6,4},{7,5},{8,14},{9,15},{10,... | collective-permute-start | bytes 1179656 | tf_op jit(solution)/shard_map/ppermute | solution.py:490
  129.7 15.9 %collective-permute-start.22 = (bf16[192,1024]{1,0:T(8,128)(2,1)}, bf16[192,1024]{1,0:T(8,128)(2,1)}, u32[]{:S(2)}, u32[]{:S(2)}) collective-permute-start(bf16[192,1024]{1,0:T(8,128)(2,1)} %get-tuple-element.142), channel_id=1, source_target_pairs={{0,2},{1,3},{2,4},{3,5},{4,6},{5,7},{6,0},{7,1},{8,10},{9,11},{10,... | collective-permute-start | bytes 1179656 | tf_op jit(solution)/shard_map/ppermute | solution.py:489
  129.7 15.9 %collective-permute-start.23 = (bf16[192,1024]{1,0:T(8,128)(2,1)}, bf16[192,1024]{1,0:T(8,128)(2,1)}, u32[]{:S(2)}, u32[]{:S(2)}) collective-permute-start(bf16[192,1024]{1,0:T(8,128)(2,1)} %get-tuple-element.143), channel_id=1, source_target_pairs={{0,6},{1,7},{2,0},{3,1},{4,2},{5,3},{6,4},{7,5},{8,14},{9,15},{10,... | collective-permute-start | bytes 1179656 | tf_op jit(solution)/shard_map/ppermute | solution.py:490
  138.9 1.7 %copy-start.1 = (bf16[3,384,1024]{2,1,0:T(8,128)(2,1)S(1)}, bf16[3,384,1024]{2,1,0:T(8,128)(2,1)}, u32[]{:S(2)}) copy-start(bf16[3,384,1024]{2,1,0:T(8,128)(2,1)} %copy-done) | copy-start | bytes 7077892
  147.2 1.2 collective-permute-start.28
  148.5 3.7 %collective-permute-start.29 = (f32[8,384]{1,0:T(8,128)S(1)}, f32[8,384]{1,0:T(8,128)S(1)}, u32[]{:S(2)}, u32[]{:S(2)}) collective-permute-start(f32[8,384]{1,0:T(8,128)S(1)} %fusion.35), channel_id=1, source_target_pairs={{0,2},{1,3},{2,0},{3,1},{4,6},{5,7},{6,4},{7,5},{8,10},{9,11},{10,... | collective-permute-start | bytes 36872 | tf_op jit(solution)/shard_map/ppermute | solution.py:496
  152.2 4.9 %collective-permute-start.30 = (f32[8,384]{1,0:T(8,128)S(1)}, f32[8,384]{1,0:T(8,128)S(1)}, u32[]{:S(2)}, u32[]{:S(2)}) collective-permute-start(f32[8,384]{1,0:T(8,128)S(1)} %add.219), channel_id=1, source_target_pairs={{0,6},{1,7},{2,4},{3,5},{4,2},{5,3},{6,0},{7,1},{8,14},{9,15},{10,... | collective-permute-start | bytes 36872 | tf_op jit(solution)/shard_map/ppermute | solution.py:496

commit v8 on v7

--- a/solution.py
+++ b/solution.py
@@ -146,7 +146,7 @@
         in_specs=[pl.BlockSpec(memory_space=pltpu.SMEM)] * len(scalars) + [hbm] * len(args),
         out_specs=[hbm] * 8,
         scratch_shapes=scratch,
-        compiler_params=pltpu.CompilerParams(vmem_limit_bytes=62 * MIB),
+        compiler_params=pltpu.CompilerParams(vmem_limit_bytes=59 * MIB),
         name=name,
     )(*scalars, *args)
 

time: 159 us -> 158 us (level)
  waiting for transfers between devices: 34.1 us -> 36 us
    ppermute x12, waiting for transfers between devices: 11.7 us -> 13.6 us  [deliver(): lax.ppermute(parts[4 * i + e], 'dp', shift(0, e) if i else shift(e, 0))]
    unnamed x29 -> x33, local copies, waits for them, and re-layouts: 3.37 us -> 2.5 us
where the time goes in v8:
time: 158 us
  starting transfers between devices  68.5 us (43%)
  Pallas kernels  41.6 us (26%)
  waiting for transfers between devices  36 us (23%)
  local copies, waits for them, and re-layouts  6.03 us (4%)
  other arithmetic  4.52 us (3%)
    ppermute x12, starting transfers between devices, deliver(): lax.ppermute(parts[4 * i + e], 'dp', shift(0, e) if i else shift(e, 0))  40.3 us
    ppermute x12, waiting for transfers between devices, deliver(): lax.ppermute(parts[4 * i + e], 'dp', shift(0, e) if i else shift(e, 0))  13.6 us
    pallas_call x2, Pallas kernels, packing(): pl.pallas_call(kernel, out_shape=[jax.ShapeDtypeStruct(part, jnp.bfloat16...  10.5 us
    pallas_call x1, Pallas kernels, attend(): pl.pallas_call(attend_kernel, out_shape=[pltpu.VMEM((rows, width), jnp.bf...  9.74 us
    pallas_call x3, Pallas kernels, project(): pl.pallas_call(project_kernel, out_shape=jax.ShapeDtypeStruct((count, row...  9.47 us
    ppermute x2, waiting for transfers between devices, body(): ups.append(lax.ppermute(up, 'tensor', turn(1)))  9.3 us
    ppermute x3, waiting for transfers between devices, body(): lax.ppermute(far_key if d == 2 else key, 'dp', shift(0, d))  7.14 us
    ppermute x3, starting transfers between devices, body(): lax.ppermute(far_value if d == 2 else value, 'dp', shift(d, 0))  6.43 us
  transfers between devices with their start and end apart: 31, of which 10 were waited for; matrix products, arithmetic and copies ran while one was open for 4% of the time, Pallas kernels for 17%

profile of v8, /device:TPU:2, one launch (start us, length us, event | category | flops | bytes accessed | tf_op | source)
XLA Modules:
  0.0 157.7 jit_solution(11556843225285085137)
XLA Ops:
  0.6 1.4 split.1
  2.1 1.6 collective-permute-start
  4.2 1.6 collective-permute-start.2
  5.8 1.7 %collective-permute-start.3 = (bf16[48,64,128]{2,1,0:T(8,128)(2,1)S(1)}, bf16[48,64,128]{2,1,0:T(8,128)(2,1)}, u32[]{:S(2)}, u32[]{:S(2)}) collective-permute-start(bf16[48,64,128]{2,1,0:T(8,128)(2,1)S(1)} %get-tuple-element.87.refs_3_.refs_4_), channel_id=1, source_target_pairs={{0,96},{8,104},{16,112},{24,120},{32,0},{40,8},{48,16},{56,24},{64... | collective-permute-start | bytes 2359304 | tf_op jit(solution)/shard_map/ppermute | solution.py:437
  7.4 5.9 %plan.1.wanted_ref = s32[16,128]{1,0:T(8,128)} custom-call(s32[1]{0:T(128)} %bitcast.2.rank_ref, s32[16,384]{1,0:T(8,128)} %bitcast.6), custom_call_target="tpu_custom_call" | custom-call | tf_op jit(solution)/shard_map/plan/pallas_call | solution.py:100
  13.3 2.1 %collective-permute-start.6 = (bf16[48,64,128]{2,1,0:T(8,128)(2,1)S(1)}, bf16[48,64,128]{2,1,0:T(8,128)(2,1)}, u32[]{:S(2)}, u32[]{:S(2)}) collective-permute-start(bf16[48,64,128]{2,1,0:T(8,128)(2,1)S(1)} %get-tuple-element.86.refs_0_), channel_id=1, source_target_pairs={{0,16},{8,24},{16,0},{24,8},{32,48},{40,56},{48,32},{56,40},{64,80... | collective-permute-start | bytes 2359304 | tf_op jit(solution)/shard_map/ppermute | solution.py:436
  15.5 7.1 %collective-permute-done.refs_1_ = bf16[48,64,128]{2,1,0:T(8,128)(2,1)S(1)} collective-permute-done((bf16[48,64,128]{2,1,0:T(8,128)(2,1)S(1)}, bf16[48,64,128]{2,1,0:T(8,128)(2,1)S(1)}, u32[]{:S(2)}, u32[]{:S(2)}) %collective-permute-start) | collective-permute-done | bytes 786464 | tf_op jit(solution)/shard_map/ppermute | solution.py:436
  22.6 3.2 %collective-permute-start.7 = (bf16[48,64,128]{2,1,0:T(8,128)(2,1)S(1)}, bf16[48,64,128]{2,1,0:T(8,128)(2,1)}, u32[]{:S(2)}, u32[]{:S(2)}) collective-permute-start(bf16[48,64,128]{2,1,0:T(8,128)(2,1)S(1)} %get-tuple-element.87.refs_3_.refs_4_), channel_id=1, source_target_pairs={{0,64},{8,72},{16,80},{24,88},{32,96},{40,104},{48,112},{56,120},{... | collective-permute-start | bytes 2359304 | tf_op jit(solution)/shard_map/ppermute | solution.py:437
  25.8 5.2 %pack_first.1 = (bf16[45,64,128]{2,1,0:T(8,128)(2,1)}, bf16[45,64,128]{2,1,0:T(8,128)(2,1)}, bf16[45,64,128]{2,1,0:T(8,128)(2,1)}, bf16[45,64,128]{2,1,0:T(8,128...) custom-call(s32[16,128]{1,0:T(8,128)} %plan.1.wanted_ref, ...), custom_call_target="tpu_custom_call" | custom-call | tf_op jit(solution)/shard_map/pack_first/pallas_call | solution.py:143
  31.7 13.0 %collective-permute-start.14 = (bf16[45,64,128]{2,1,0:T(8,128)(2,1)}, bf16[45,64,128]{2,1,0:T(8,128)(2,1)S(1)}, u32[]{:S(2)}, u32[]{:S(2)}) collective-permute-start(bf16[45,64,128]{2,1,0:T(8,128)(2,1)} %get-tuple-element.104), channel_id=1, source_target_pairs={{0,24},{8,0},{16,8},{24,16},{32,56},{40,32},{48,40},{56,48},{64,88... | collective-permute-start | bytes 2211848 | tf_op jit(solution)/shard_map/ppermute | solution.py:442
  44.7 0.8 constant_dynamic-slice_fusion.1
  45.5 3.1 %collective-permute-start.13 = (bf16[45,64,128]{2,1,0:T(8,128)(2,1)}, bf16[45,64,128]{2,1,0:T(8,128)(2,1)}, u32[]{:S(2)}, u32[]{:S(2)}) collective-permute-start(bf16[45,64,128]{2,1,0:T(8,128)(2,1)} %get-tuple-element.101), channel_id=1, source_target_pairs={{0,16},{8,24},{16,0},{24,8},{32,48},{40,56},{48,32},{56,40},{64,80... | collective-permute-start | bytes 2211848 | tf_op jit(solution)/shard_map/ppermute | solution.py:442
  48.6 2.6 %collective-permute-start.12 = (bf16[45,64,128]{2,1,0:T(8,128)(2,1)}, bf16[45,64,128]{2,1,0:T(8,128)(2,1)S(1)}, u32[]{:S(2)}, u32[]{:S(2)}) collective-permute-start(bf16[45,64,128]{2,1,0:T(8,128)(2,1)} %get-tuple-element.98), channel_id=1, source_target_pairs={{0,8},{8,16},{16,24},{24,0},{32,40},{40,48},{48,56},{56,32},{64,72... | collective-permute-start | bytes 2211848 | tf_op jit(solution)/shard_map/ppermute | solution.py:442
  51.2 1.5 collective-permute-start.8
  52.7 5.3 %collective-permute-done.4.refs_8_ = bf16[45,64,128]{2,1,0:T(8,128)(2,1)S(1)} collective-permute-done((bf16[45,64,128]{2,1,0:T(8,128)(2,1)}, bf16[45,64,128]{2,1,0:T(8,128)(2,1)S(1)}, u32[]{:S(2)}, u32[]{:S(2)}) %collective-permute-start.4) | collective-permute-done | bytes 737312 | tf_op jit(solution)/shard_map/ppermute | solution.py:442
  58.0 2.4 %collective-permute-start.5 = (bf16[45,64,128]{2,1,0:T(8,128)(2,1)}, bf16[45,64,128]{2,1,0:T(8,128)(2,1)}, u32[]{:S(2)}, u32[]{:S(2)}) collective-permute-start(bf16[45,64,128]{2,1,0:T(8,128)(2,1)} %get-tuple-element.84), channel_id=1, source_target_pairs={{0,64},{8,72},{16,80},{24,88},{32,96},{40,104},{48,112},{56,120},{... | collective-permute-start | bytes 2211848 | tf_op jit(solution)/shard_map/ppermute | solution.py:442
  60.6 1.3 dynamic_slice.16.refs_2_
  62.2 5.4 %pack_second.1 = (bf16[18,64,128]{2,1,0:T(8,128)(2,1)}, bf16[18,64,128]{2,1,0:T(8,128)(2,1)}, bf16[18,64,128]{2,1,0:T(8,128)(2,1)}, bf16[18,64,128]{2,1,0:T(8,12...) custom-call(s32[1]{0:T(128)} %bitcast.2.rank_ref, ...), custom_call_target="tpu_custom_call" | custom-call | tf_op jit(solution)/shard_map/pack_second/pallas_call | solution.py:143
  67.6 5.7 %collective-permute-start.17 = (bf16[18,64,128]{2,1,0:T(8,128)(2,1)}, bf16[18,64,128]{2,1,0:T(8,128)(2,1)S(1)}, u32[]{:S(2)}, u32[]{:S(2)}) collective-permute-start(bf16[18,64,128]{2,1,0:T(8,128)(2,1)} %get-tuple-element.110), channel_id=1, source_target_pairs={{0,24},{8,0},{16,8},{24,16},{32,56},{40,32},{48,40},{56,48},{64,88... | collective-permute-start | bytes 884744 | tf_op jit(solution)/shard_map/ppermute | solution.py:442
  74.6 2.6 %collective-permute-start.16 = (bf16[18,64,128]{2,1,0:T(8,128)(2,1)}, bf16[18,64,128]{2,1,0:T(8,128)(2,1)S(1)}, u32[]{:S(2)}, u32[]{:S(2)}) collective-permute-start(bf16[18,64,128]{2,1,0:T(8,128)(2,1)} %get-tuple-element.109), channel_id=1, source_target_pairs={{0,16},{8,24},{16,0},{24,8},{32,48},{40,56},{48,32},{56,40},{64,80... | collective-permute-start | bytes 884744 | tf_op jit(solution)/shard_map/ppermute | solution.py:442
  77.2 2.5 %collective-permute-start.15 = (bf16[18,64,128]{2,1,0:T(8,128)(2,1)}, bf16[18,64,128]{2,1,0:T(8,128)(2,1)S(1)}, u32[]{:S(2)}, u32[]{:S(2)}) collective-permute-start(bf16[18,64,128]{2,1,0:T(8,128)(2,1)} %get-tuple-element.108), channel_id=1, source_target_pairs={{0,8},{8,16},{16,24},{24,0},{32,40},{40,48},{48,56},{56,32},{64,72... | collective-permute-start | bytes 884744 | tf_op jit(solution)/shard_map/ppermute | solution.py:442
  79.7 1.6 collective-permute-start.11
  81.2 1.1 collective-permute-start.10
  82.3 3.5 %collective-permute-start.9 = (bf16[18,64,128]{2,1,0:T(8,128)(2,1)}, bf16[18,64,128]{2,1,0:T(8,128)(2,1)S(1)}, u32[]{:S(2)}, u32[]{:S(2)}) collective-permute-start(bf16[18,64,128]{2,1,0:T(8,128)(2,1)} %get-tuple-element.94), channel_id=1, source_target_pairs={{0,32},{8,40},{16,48},{24,56},{32,64},{40,72},{48,80},{56,88},{64,... | collective-permute-start | bytes 884744 | tf_op jit(solution)/shard_map/ppermute | solution.py:442
  86.6 1.6 %collective-permute-done.11.refs_14_ = bf16[18,64,128]{2,1,0:T(8,128)(2,1)S(1)} collective-permute-done((bf16[18,64,128]{2,1,0:T(8,128)(2,1)}, bf16[18,64,128]{2,1,0:T(8,128)(2,1)S(1)}, u32[]{:S(2)}, u32[]{:S(2)}) %collective-permute-start.11) | collective-permute-done | bytes 294944 | tf_op jit(solution)/shard_map/ppermute | solution.py:442
  88.2 4.2 %collective-permute-done.10.refs_13_ = bf16[18,64,128]{2,1,0:T(8,128)(2,1)S(1)} collective-permute-done((bf16[18,64,128]{2,1,0:T(8,128)(2,1)}, bf16[18,64,128]{2,1,0:T(8,128)(2,1)S(1)}, u32[]{:S(2)}, u32[]{:S(2)}) %collective-permute-start.10) | collective-permute-done | bytes 294944 | tf_op jit(solution)/shard_map/ppermute | solution.py:442
  92.5 2.4 %collective-permute-done.9.refs_12_ = bf16[18,64,128]{2,1,0:T(8,128)(2,1)S(1)} collective-permute-done((bf16[18,64,128]{2,1,0:T(8,128)(2,1)}, bf16[18,64,128]{2,1,0:T(8,128)(2,1)S(1)}, u32[]{:S(2)}, u32[]{:S(2)}) %collective-permute-start.9) | collective-permute-done | bytes 294944 | tf_op jit(solution)/shard_map/ppermute | solution.py:442
  95.6 9.7 %attend.1 = (bf16[384,1024]{1,0:T(8,128)(2,1)S(1)}, bf16[1024,8192]{1,0:T(8,128)(2,1)S(1)}) custom-call(s32[384]{0:T(512)} %get-tuple-element.159.refs_0_, s32[384]{0:T(512)} %get-tuple-element.158.refs_1_, s32[24]{0:T(128)} %dynamic_slice.16.refs_2_, s32[24]{0:T(128)} %fusion.24.refs_3_, s32[24]{0:T(128)} %get-tuple-element.154.refs_4_, ...), custom_call_target="tpu_custom_call" | custom-call | flops 6643777536 | bytes 1572864 | tf_op jit(solution)/shard_map/attend/pallas_call | solution.py:288
  105.3 2.5 %project.3.kept_ref = bf16[2,384,1024]{2,1,0:T(8,128)(2,1)S(1)} custom-call(s32[2]{0:T(128)S(1)} %pad_add_fusion.order_ref, bf16[384,1024]{1,0:T(8,128)(2,1)S(1)} %get-tuple-element.138.attn_ref, bf16[1024,8192]{1,0:T(8,128)(2,1)S(1)} %get-tuple-element.129.w_ref), custom_call_target="tpu_custom_call" | custom-call | flops 1610612736 | bytes 1572864 | tf_op jit(solution)/shard_map/project/pallas_call | solution.py:317
  108.0 3.5 %project.4 = bf16[3,384,1024]{2,1,0:T(8,128)(2,1)S(1)} custom-call(s32[3]{0:T(128)S(1)} %add_subtract_fusion.order_ref, bf16[384,1024]{1,0:T(8,128)(2,1)S(1)} %get-tuple-element.138.attn_ref, bf16[1024,8192]{1,0:T(8,128)(2,1)S(1)} %get-tuple-element.129.w_ref), custom_call_target="tpu_custom_call" | custom-call | flops 2415919104 | bytes 2359296 | tf_op jit(solution)/shard_map/project/pallas_call | solution.py:317
  112.3 2.0 %collective-permute-start.24 = (bf16[96,1024]{1,0:T(8,128)(2,1)S(1)}, bf16[96,1024]{1,0:T(8,128)(2,1)S(1)}, u32[]{:S(2)}, u32[]{:S(2)}) collective-permute-start(bf16[96,1024]{1,0:T(8,128)(2,1)S(1)} %get-tuple-element.146), channel_id=1, source_target_pairs={{0,2},{1,3},{2,4},{3,5},{4,6},{5,7},{6,0},{7,1},{8,10},{9,11},{10,... | collective-permute-start | bytes 589832 | tf_op jit(solution)/shard_map/ppermute | solution.py:480
  114.3 2.2 %collective-permute-start.25 = (bf16[96,1024]{1,0:T(8,128)(2,1)S(1)}, bf16[96,1024]{1,0:T(8,128)(2,1)S(1)}, u32[]{:S(2)}, u32[]{:S(2)}) collective-permute-start(bf16[96,1024]{1,0:T(8,128)(2,1)S(1)} %get-tuple-element.147), channel_id=1, source_target_pairs={{0,6},{1,7},{2,0},{3,1},{4,2},{5,3},{6,4},{7,5},{8,14},{9,15},{10,... | collective-permute-start | bytes 589832 | tf_op jit(solution)/shard_map/ppermute | solution.py:481
  116.5 3.2 %collective-permute-start.21 = (bf16[96,1024]{1,0:T(8,128)(2,1)S(1)}, bf16[96,1024]{1,0:T(8,128)(2,1)S(1)}, u32[]{:S(2)}, u32[]{:S(2)}) collective-permute-start(bf16[96,1024]{1,0:T(8,128)(2,1)S(1)} %get-tuple-element.141), channel_id=1, source_target_pairs={{0,6},{1,7},{2,0},{3,1},{4,2},{5,3},{6,4},{7,5},{8,14},{9,15},{10,... | collective-permute-start | bytes 589832 | tf_op jit(solution)/shard_map/ppermute | solution.py:481
  119.7 3.5 %project.5.kept_ref = bf16[3,384,1024]{2,1,0:T(8,128)(2,1)S(1)} custom-call(s32[3]{0:T(128)S(1)} %broadcast_add_fusion.order_ref, bf16[384,1024]{1,0:T(8,128)(2,1)S(1)} %get-tuple-element.138.attn_ref, bf16[1024,8192]{1,0:T(8,128)(2,1)S(1)} %get-tuple-element.129.w_ref), custom_call_target="tpu_custom_call" | custom-call | flops 2415919104 | bytes 2359296 | tf_op jit(solution)/shard_map/project/pallas_call | solution.py:317
  123.3 1.2 near.3
  124.5 0.8 collective-permute-start.26
  125.3 2.5 %collective-permute-start.27 = (bf16[192,1024]{1,0:T(8,128)(2,1)}, bf16[192,1024]{1,0:T(8,128)(2,1)S(1)}, u32[]{:S(2)}, u32[]{:S(2)}) collective-permute-start(bf16[192,1024]{1,0:T(8,128)(2,1)} %get-tuple-element.149), channel_id=1, source_target_pairs={{0,6},{1,7},{2,0},{3,1},{4,2},{5,3},{6,4},{7,5},{8,14},{9,15},{10,... | collective-permute-start | bytes 1179656 | tf_op jit(solution)/shard_map/ppermute | solution.py:490
  127.8 1.0 near.2
  128.8 3.2 %collective-permute-start.23 = (bf16[192,1024]{1,0:T(8,128)(2,1)}, bf16[192,1024]{1,0:T(8,128)(2,1)}, u32[]{:S(2)}, u32[]{:S(2)}) collective-permute-start(bf16[192,1024]{1,0:T(8,128)(2,1)} %get-tuple-element.143), channel_id=1, source_target_pairs={{0,6},{1,7},{2,0},{3,1},{4,2},{5,3},{6,4},{7,5},{8,14},{9,15},{10,... | collective-permute-start | bytes 1179656 | tf_op jit(solution)/shard_map/ppermute | solution.py:490
  132.0 1.2 constant_dynamic-slice_fusion.residual_ref
  133.2 4.8 %collective-permute-done.26.up_ref = bf16[192,1024]{1,0:T(8,128)(2,1)S(1)} collective-permute-done((bf16[192,1024]{1,0:T(8,128)(2,1)}, bf16[192,1024]{1,0:T(8,128)(2,1)S(1)}, u32[]{:S(2)}, u32[]{:S(2)}) %collective-permute-start.26) | collective-permute-done | bytes 393248 | tf_op jit(solution)/shard_map/ppermute | solution.py:489
  138.0 1.7 %copy-done.1 = bf16[3,384,1024]{2,1,0:T(8,128)(2,1)S(1)} copy-done((bf16[3,384,1024]{2,1,0:T(8,128)(2,1)S(1)}, bf16[3,384,1024]{2,1,0:T(8,128)(2,1)}, u32[]{:S(2)}) %copy-start.1) | copy-done | bytes 2359320
  140.1 4.5 %collective-permute-done.22.up_ref = bf16[192,1024]{1,0:T(8,128)(2,1)} collective-permute-done((bf16[192,1024]{1,0:T(8,128)(2,1)}, bf16[192,1024]{1,0:T(8,128)(2,1)}, u32[]{:S(2)}, u32[]{:S(2)}) %collective-permute-start.22) | collective-permute-done | bytes 393248 | tf_op jit(solution)/shard_map/ppermute | solution.py:489
  144.7 1.6 %last.2 = (f32[192,1024]{1,0:T(8,128)S(1)}, f32[8,192]{1,0:T(8,128)S(1)}) custom-call(bf16[3,384,1024]{2,1,0:T(8,128)(2,1)S(1)} %project.5.kept_ref, bf16[3,384,1024]{2,1,0:T(8,128)(2,1)S(1)} %copy-done.1, bf16[192,1024]{1,0:T(8,128)(2,1)} %collective-permute-done.22.up_ref, bf16[192,1024]{1,0:T(8,128)(2,1)} %collective-permute-done.23.down_ref, ...), custom_call_target="tpu_custom_call" | custom-call | tf_op jit(solution)/shard_map/last/pallas_call | solution.py:401
  147.7 3.6 %collective-permute-done.29 = f32[8,384]{1,0:T(8,128)S(1)} collective-permute-done((f32[8,384]{1,0:T(8,128)S(1)}, f32[8,384]{1,0:T(8,128)S(1)}, u32[]{:S(2)}, u32[]{:S(2)}) %collective-permute-start.29) | collective-permute-done | bytes 12320 | tf_op jit(solution)/shard_map/ppermute | solution.py:496
  151.4 3.0 %collective-permute-start.30 = (f32[8,384]{1,0:T(8,128)S(1)}, f32[8,384]{1,0:T(8,128)S(1)}, u32[]{:S(2)}, u32[]{:S(2)}) collective-permute-start(f32[8,384]{1,0:T(8,128)S(1)} %add.219), channel_id=1, source_target_pairs={{0,6},{1,7},{2,4},{3,5},{4,2},{5,3},{6,0},{7,1},{8,14},{9,15},{10,... | collective-permute-start | bytes 36872 | tf_op jit(solution)/shard_map/ppermute | solution.py:496
  154.4 1.9 %collective-permute-done.30 = f32[8,384]{1,0:T(8,128)S(1)} collective-permute-done((f32[8,384]{1,0:T(8,128)S(1)}, f32[8,384]{1,0:T(8,128)S(1)}, u32[]{:S(2)}, u32[]{:S(2)}) %collective-permute-start.30) | collective-permute-done | bytes 12320 | tf_op jit(solution)/shard_map/ppermute | solution.py:496
  156.3 1.4 multiply_convert_fusion
  (82 shorter events, 7.5 us)
Async XLA Ops:
  2.1 23.7 %copy-start.2 = (bf16[48,64,128]{2,1,0:T(8,128)(2,1)}, bf16[48,64,128]{2,1,0:T(8,128)(2,1)S(1)}, u32[]{:S(2)}) copy-start(bf16[48,64,128]{2,1,0:T(8,128)(2,1)S(1)} %get-tuple-element.86.refs_0_) | copy-start | bytes 2359300
  2.1 23.7 %copy-start.3 = (bf16[48,64,128]{2,1,0:T(8,128)(2,1)}, bf16[48,64,128]{2,1,0:T(8,128)(2,1)S(1)}, u32[]{:S(2)}) copy-start(bf16[48,64,128]{2,1,0:T(8,128)(2,1)S(1)} %get-tuple-element.87.refs_3_.refs_4_) | copy-start | bytes 2359300
  2.1 20.5 %collective-permute-start = (bf16[48,64,128]{2,1,0:T(8,128)(2,1)S(1)}, bf16[48,64,128]{2,1,0:T(8,128)(2,1)S(1)}, u32[]{:S(2)}, u32[]{:S(2)}) collective-permute-start(bf16[48,64,128]{2,1,0:T(8,128)(2,1)S(1)} %get-tuple-element.86.refs_0_), channel_id=1, source_target_pairs={{0,8},{8,16},{16,24},{24,0},{32,40},{40,48},{48,56},{56,32},{64,72... | collective-permute-start | bytes 2359304 | tf_op jit(solution)/shard_map/ppermute | solution.py:436
  3.7 22.1 %collective-permute-start.1 = (bf16[48,64,128]{2,1,0:T(8,128)(2,1)S(1)}, bf16[48,64,128]{2,1,0:T(8,128)(2,1)}, u32[]{:S(2)}, u32[]{:S(2)}) collective-permute-start(bf16[48,64,128]{2,1,0:T(8,128)(2,1)S(1)} %get-tuple-element.86.refs_0_), channel_id=1, source_target_pairs={{0,24},{8,0},{16,8},{24,16},{32,56},{40,32},{48,40},{56,48},{64,88... | collective-permute-start | bytes 2359304 | tf_op jit(solution)/shard_map/ppermute | solution.py:436
  4.2 21.6 %collective-permute-start.2 = (bf16[48,64,128]{2,1,0:T(8,128)(2,1)S(1)}, bf16[48,64,128]{2,1,0:T(8,128)(2,1)}, u32[]{:S(2)}, u32[]{:S(2)}) collective-permute-start(bf16[48,64,128]{2,1,0:T(8,128)(2,1)S(1)} %get-tuple-element.87.refs_3_.refs_4_), channel_id=1, source_target_pairs={{0,32},{8,40},{16,48},{24,56},{32,64},{40,72},{48,80},{56,88},{64,... | collective-permute-start | bytes 2359304 | tf_op jit(solution)/shard_map/ppermute | solution.py:437
  5.8 20.0 %collective-permute-start.3 = (bf16[48,64,128]{2,1,0:T(8,128)(2,1)S(1)}, bf16[48,64,128]{2,1,0:T(8,128)(2,1)}, u32[]{:S(2)}, u32[]{:S(2)}) collective-permute-start(bf16[48,64,128]{2,1,0:T(8,128)(2,1)S(1)} %get-tuple-element.87.refs_3_.refs_4_), channel_id=1, source_target_pairs={{0,96},{8,104},{16,112},{24,120},{32,0},{40,8},{48,16},{56,24},{64... | collective-permute-start | bytes 2359304 | tf_op jit(solution)/shard_map/ppermute | solution.py:437
  13.3 35.2 %collective-permute-start.6 = (bf16[48,64,128]{2,1,0:T(8,128)(2,1)S(1)}, bf16[48,64,128]{2,1,0:T(8,128)(2,1)}, u32[]{:S(2)}, u32[]{:S(2)}) collective-permute-start(bf16[48,64,128]{2,1,0:T(8,128)(2,1)S(1)} %get-tuple-element.86.refs_0_), channel_id=1, source_target_pairs={{0,16},{8,24},{16,0},{24,8},{32,48},{40,56},{48,32},{56,40},{64,80... | collective-permute-start | bytes 2359304 | tf_op jit(solution)/shard_map/ppermute | solution.py:436
  22.6 3.2 %copy-start.4 = (bf16[48,64,128]{2,1,0:T(8,128)(2,1)}, bf16[48,64,128]{2,1,0:T(8,128)(2,1)S(1)}, u32[]{:S(2)}) copy-start(bf16[48,64,128]{2,1,0:T(8,128)(2,1)S(1)} %collective-permute-done.refs_1_) | copy-start | bytes 2359300
  22.6 28.6 %collective-permute-start.7 = (bf16[48,64,128]{2,1,0:T(8,128)(2,1)S(1)}, bf16[48,64,128]{2,1,0:T(8,128)(2,1)}, u32[]{:S(2)}, u32[]{:S(2)}) collective-permute-start(bf16[48,64,128]{2,1,0:T(8,128)(2,1)S(1)} %get-tuple-element.87.refs_3_.refs_4_), channel_id=1, source_target_pairs={{0,64},{8,72},{16,80},{24,88},{32,96},{40,104},{48,112},{56,120},{... | collective-permute-start | bytes 2359304 | tf_op jit(solution)/shard_map/ppermute | solution.py:437
  31.0 27.0 %collective-permute-start.4 = (bf16[45,64,128]{2,1,0:T(8,128)(2,1)}, bf16[45,64,128]{2,1,0:T(8,128)(2,1)S(1)}, u32[]{:S(2)}, u32[]{:S(2)}) collective-permute-start(bf16[45,64,128]{2,1,0:T(8,128)(2,1)} %get-tuple-element.82), channel_id=1, source_target_pairs={{0,32},{8,40},{16,48},{24,56},{32,64},{40,72},{48,80},{56,88},{64,... | collective-permute-start | bytes 2211848 | tf_op jit(solution)/shard_map/ppermute | solution.py:442
  31.7 35.9 %collective-permute-start.14 = (bf16[45,64,128]{2,1,0:T(8,128)(2,1)}, bf16[45,64,128]{2,1,0:T(8,128)(2,1)S(1)}, u32[]{:S(2)}, u32[]{:S(2)}) collective-permute-start(bf16[45,64,128]{2,1,0:T(8,128)(2,1)} %get-tuple-element.104), channel_id=1, source_target_pairs={{0,24},{8,0},{16,8},{24,16},{32,56},{40,32},{48,40},{56,48},{64,88... | collective-permute-start | bytes 2211848 | tf_op jit(solution)/shard_map/ppermute | solution.py:442
  45.5 29.1 %collective-permute-start.13 = (bf16[45,64,128]{2,1,0:T(8,128)(2,1)}, bf16[45,64,128]{2,1,0:T(8,128)(2,1)}, u32[]{:S(2)}, u32[]{:S(2)}) collective-permute-start(bf16[45,64,128]{2,1,0:T(8,128)(2,1)} %get-tuple-element.101), channel_id=1, source_target_pairs={{0,16},{8,24},{16,0},{24,8},{32,48},{40,56},{48,32},{56,40},{64,80... | collective-permute-start | bytes 2211848 | tf_op jit(solution)/shard_map/ppermute | solution.py:442
  48.6 28.6 %collective-permute-start.12 = (bf16[45,64,128]{2,1,0:T(8,128)(2,1)}, bf16[45,64,128]{2,1,0:T(8,128)(2,1)S(1)}, u32[]{:S(2)}, u32[]{:S(2)}) collective-permute-start(bf16[45,64,128]{2,1,0:T(8,128)(2,1)} %get-tuple-element.98), channel_id=1, source_target_pairs={{0,8},{8,16},{16,24},{24,0},{32,40},{40,48},{48,56},{56,32},{64,72... | collective-permute-start | bytes 2211848 | tf_op jit(solution)/shard_map/ppermute | solution.py:442
  51.2 28.5 %collective-permute-start.8 = (bf16[45,64,128]{2,1,0:T(8,128)(2,1)}, bf16[45,64,128]{2,1,0:T(8,128)(2,1)S(1)}, u32[]{:S(2)}, u32[]{:S(2)}) collective-permute-start(bf16[45,64,128]{2,1,0:T(8,128)(2,1)} %get-tuple-element.90), channel_id=1, source_target_pairs={{0,96},{8,104},{16,112},{24,120},{32,0},{40,8},{48,16},{56,24},{64... | collective-permute-start | bytes 2211848 | tf_op jit(solution)/shard_map/ppermute | solution.py:442
  58.0 9.6 %copy-start.5 = (bf16[45,64,128]{2,1,0:T(8,128)(2,1)}, bf16[45,64,128]{2,1,0:T(8,128)(2,1)S(1)}, u32[]{:S(2)}) copy-start(bf16[45,64,128]{2,1,0:T(8,128)(2,1)S(1)} %collective-permute-done.4.refs_8_) | copy-start | bytes 2211844
  58.0 23.2 %collective-permute-start.5 = (bf16[45,64,128]{2,1,0:T(8,128)(2,1)}, bf16[45,64,128]{2,1,0:T(8,128)(2,1)}, u32[]{:S(2)}, u32[]{:S(2)}) collective-permute-start(bf16[45,64,128]{2,1,0:T(8,128)(2,1)} %get-tuple-element.84), channel_id=1, source_target_pairs={{0,64},{8,72},{16,80},{24,88},{32,96},{40,104},{48,112},{56,120},{... | collective-permute-start | bytes 2211848 | tf_op jit(solution)/shard_map/ppermute | solution.py:442
  62.2 11.2 %copy-start.15 = (s32[384]{0:T(512)S(1)}, s32[384]{0:T(512)}, u32[]{:S(2)}) copy-start(s32[384]{0:T(512)} %parent_ref.1) | copy-start | bytes 4612
  67.6 27.9 %copy-start.6 = (bf16[45,64,128]{2,1,0:T(8,128)(2,1)}, bf16[45,64,128]{2,1,0:T(8,128)(2,1)S(1)}, u32[]{:S(2)}) copy-start(bf16[45,64,128]{2,1,0:T(8,128)(2,1)S(1)} %collective-permute-done.14.refs_18_) | copy-start | bytes 2211844
  67.6 14.7 %collective-permute-start.17 = (bf16[18,64,128]{2,1,0:T(8,128)(2,1)}, bf16[18,64,128]{2,1,0:T(8,128)(2,1)S(1)}, u32[]{:S(2)}, u32[]{:S(2)}) collective-permute-start(bf16[18,64,128]{2,1,0:T(8,128)(2,1)} %get-tuple-element.110), channel_id=1, source_target_pairs={{0,24},{8,0},{16,8},{24,16},{32,56},{40,32},{48,40},{56,48},{64,88... | collective-permute-start | bytes 884744 | tf_op jit(solution)/shard_map/ppermute | solution.py:442
  74.6 11.9 %collective-permute-start.16 = (bf16[18,64,128]{2,1,0:T(8,128)(2,1)}, bf16[18,64,128]{2,1,0:T(8,128)(2,1)S(1)}, u32[]{:S(2)}, u32[]{:S(2)}) collective-permute-start(bf16[18,64,128]{2,1,0:T(8,128)(2,1)} %get-tuple-element.109), channel_id=1, source_target_pairs={{0,16},{8,24},{16,0},{24,8},{32,48},{40,56},{48,32},{56,40},{64,80... | collective-permute-start | bytes 884744 | tf_op jit(solution)/shard_map/ppermute | solution.py:442
  77.2 18.4 %copy-start.7 = (bf16[45,64,128]{2,1,0:T(8,128)(2,1)}, bf16[45,64,128]{2,1,0:T(8,128)(2,1)S(1)}, u32[]{:S(2)}) copy-start(bf16[45,64,128]{2,1,0:T(8,128)(2,1)S(1)} %collective-permute-done.12.refs_16_) | copy-start | bytes 2211844
  77.2 9.4 %collective-permute-start.15 = (bf16[18,64,128]{2,1,0:T(8,128)(2,1)}, bf16[18,64,128]{2,1,0:T(8,128)(2,1)S(1)}, u32[]{:S(2)}, u32[]{:S(2)}) collective-permute-start(bf16[18,64,128]{2,1,0:T(8,128)(2,1)} %get-tuple-element.108), channel_id=1, source_target_pairs={{0,8},{8,16},{16,24},{24,0},{32,40},{40,48},{48,56},{56,32},{64,72... | collective-permute-start | bytes 884744 | tf_op jit(solution)/shard_map/ppermute | solution.py:442
  79.7 15.9 %copy-start.8 = (bf16[45,64,128]{2,1,0:T(8,128)(2,1)}, bf16[45,64,128]{2,1,0:T(8,128)(2,1)S(1)}, u32[]{:S(2)}) copy-start(bf16[45,64,128]{2,1,0:T(8,128)(2,1)S(1)} %collective-permute-done.8.refs_10_) | copy-start | bytes 2211844
  79.7 8.5 %collective-permute-start.11 = (bf16[18,64,128]{2,1,0:T(8,128)(2,1)}, bf16[18,64,128]{2,1,0:T(8,128)(2,1)S(1)}, u32[]{:S(2)}, u32[]{:S(2)}) collective-permute-start(bf16[18,64,128]{2,1,0:T(8,128)(2,1)} %get-tuple-element.96), channel_id=1, source_target_pairs={{0,96},{8,104},{16,112},{24,120},{32,0},{40,8},{48,16},{56,24},{64... | collective-permute-start | bytes 884744 | tf_op jit(solution)/shard_map/ppermute | solution.py:442
  81.2 11.2 %collective-permute-start.10 = (bf16[18,64,128]{2,1,0:T(8,128)(2,1)}, bf16[18,64,128]{2,1,0:T(8,128)(2,1)S(1)}, u32[]{:S(2)}, u32[]{:S(2)}) collective-permute-start(bf16[18,64,128]{2,1,0:T(8,128)(2,1)} %get-tuple-element.95), channel_id=1, source_target_pairs={{0,64},{8,72},{16,80},{24,88},{32,96},{40,104},{48,112},{56,120},{... | collective-permute-start | bytes 884744 | tf_op jit(solution)/shard_map/ppermute | solution.py:442
  82.3 13.2 %copy-start.9 = (bf16[18,64,128]{2,1,0:T(8,128)(2,1)}, bf16[18,64,128]{2,1,0:T(8,128)(2,1)S(1)}, u32[]{:S(2)}) copy-start(bf16[18,64,128]{2,1,0:T(8,128)(2,1)S(1)} %collective-permute-done.17.refs_22_) | copy-start | bytes 884740
  82.3 12.5 %collective-permute-start.9 = (bf16[18,64,128]{2,1,0:T(8,128)(2,1)}, bf16[18,64,128]{2,1,0:T(8,128)(2,1)S(1)}, u32[]{:S(2)}, u32[]{:S(2)}) collective-permute-start(bf16[18,64,128]{2,1,0:T(8,128)(2,1)} %get-tuple-element.94), channel_id=1, source_target_pairs={{0,32},{8,40},{16,48},{24,56},{32,64},{40,72},{48,80},{56,88},{64,... | collective-permute-start | bytes 884744 | tf_op jit(solution)/shard_map/ppermute | solution.py:442
  86.6 9.0 %copy-start.10 = (bf16[18,64,128]{2,1,0:T(8,128)(2,1)}, bf16[18,64,128]{2,1,0:T(8,128)(2,1)S(1)}, u32[]{:S(2)}) copy-start(bf16[18,64,128]{2,1,0:T(8,128)(2,1)S(1)} %collective-permute-done.16.refs_21_) | copy-start | bytes 884740
  86.6 9.0 %copy-start.11 = (bf16[18,64,128]{2,1,0:T(8,128)(2,1)}, bf16[18,64,128]{2,1,0:T(8,128)(2,1)S(1)}, u32[]{:S(2)}) copy-start(bf16[18,64,128]{2,1,0:T(8,128)(2,1)S(1)} %collective-permute-done.15.refs_20_) | copy-start | bytes 884740
  88.2 6.6 %copy-start.12 = (bf16[18,64,128]{2,1,0:T(8,128)(2,1)}, bf16[18,64,128]{2,1,0:T(8,128)(2,1)S(1)}, u32[]{:S(2)}) copy-start(bf16[18,64,128]{2,1,0:T(8,128)(2,1)S(1)} %collective-permute-done.11.refs_14_) | copy-start | bytes 884740
  92.5 2.4 %copy-start.13 = (bf16[18,64,128]{2,1,0:T(8,128)(2,1)}, bf16[18,64,128]{2,1,0:T(8,128)(2,1)S(1)}, u32[]{:S(2)}) copy-start(bf16[18,64,128]{2,1,0:T(8,128)(2,1)S(1)} %collective-permute-done.10.refs_13_) | copy-start | bytes 884740
  94.8 0.7 copy-start.14
  107.9 3.6 %collective-permute-start.18 = (bf16[384,1024]{1,0:T(8,128)(2,1)S(1)}, bf16[384,1024]{1,0:T(8,128)(2,1)S(1)}, u32[]{:S(2)}, u32[]{:S(2)}) collective-permute-start(bf16[384,1024]{1,0:T(8,128)(2,1)S(1)} %slice_bitcast_fusion), channel_id=1, source_target_pairs={{0,1},{1,0},{2,3},{3,2},{4,5},{5,4},{6,7},{7,6},{8,9},{9,8},{10,11... | collective-permute-start | bytes 2359304 | tf_op jit(solution)/shard_map/ppermute | solution.py:473
  111.5 11.7 %collective-permute-start.19 = (bf16[3,384,1024]{2,1,0:T(8,128)(2,1)S(1)}, bf16[3,384,1024]{2,1,0:T(8,128)(2,1)S(1)}, u32[]{:S(2)}, u32[]{:S(2)}) collective-permute-start(bf16[3,384,1024]{2,1,0:T(8,128)(2,1)S(1)} %project.4), channel_id=1, source_target_pairs={{0,1},{1,0},{2,3},{3,2},{4,5},{5,4},{6,7},{7,6},{8,9},{9,8},{10,11... | collective-permute-start | bytes 7077896 | tf_op jit(solution)/shard_map/ppermute | solution.py:476
  112.3 10.9 %collective-permute-start.24 = (bf16[96,1024]{1,0:T(8,128)(2,1)S(1)}, bf16[96,1024]{1,0:T(8,128)(2,1)S(1)}, u32[]{:S(2)}, u32[]{:S(2)}) collective-permute-start(bf16[96,1024]{1,0:T(8,128)(2,1)S(1)} %get-tuple-element.146), channel_id=1, source_target_pairs={{0,2},{1,3},{2,4},{3,5},{4,6},{5,7},{6,0},{7,1},{8,10},{9,11},{10,... | collective-permute-start | bytes 589832 | tf_op jit(solution)/shard_map/ppermute | solution.py:480
  114.3 8.9 %collective-permute-start.25 = (bf16[96,1024]{1,0:T(8,128)(2,1)S(1)}, bf16[96,1024]{1,0:T(8,128)(2,1)S(1)}, u32[]{:S(2)}, u32[]{:S(2)}) collective-permute-start(bf16[96,1024]{1,0:T(8,128)(2,1)S(1)} %get-tuple-element.147), channel_id=1, source_target_pairs={{0,6},{1,7},{2,0},{3,1},{4,2},{5,3},{6,4},{7,5},{8,14},{9,15},{10,... | collective-permute-start | bytes 589832 | tf_op jit(solution)/shard_map/ppermute | solution.py:481
  116.5 11.3 %collective-permute-start.20 = (bf16[96,1024]{1,0:T(8,128)(2,1)S(1)}, bf16[96,1024]{1,0:T(8,128)(2,1)S(1)}, u32[]{:S(2)}, u32[]{:S(2)}) collective-permute-start(bf16[96,1024]{1,0:T(8,128)(2,1)S(1)} %get-tuple-element.140), channel_id=1, source_target_pairs={{0,2},{1,3},{2,4},{3,5},{4,6},{5,7},{6,0},{7,1},{8,10},{9,11},{10,... | collective-permute-start | bytes 589832 | tf_op jit(solution)/shard_map/ppermute | solution.py:480
  116.5 11.3 %collective-permute-start.21 = (bf16[96,1024]{1,0:T(8,128)(2,1)S(1)}, bf16[96,1024]{1,0:T(8,128)(2,1)S(1)}, u32[]{:S(2)}, u32[]{:S(2)}) collective-permute-start(bf16[96,1024]{1,0:T(8,128)(2,1)S(1)} %get-tuple-element.141), channel_id=1, source_target_pairs={{0,6},{1,7},{2,0},{3,1},{4,2},{5,3},{6,4},{7,5},{8,14},{9,15},{10,... | collective-permute-start | bytes 589832 | tf_op jit(solution)/shard_map/ppermute | solution.py:481
  123.3 4.5 %copy-start = (bf16[3,384,1024]{2,1,0:T(8,128)(2,1)}, bf16[3,384,1024]{2,1,0:T(8,128)(2,1)S(1)}, u32[]{:S(2)}) copy-start(bf16[3,384,1024]{2,1,0:T(8,128)(2,1)S(1)} %collective-permute-done.19.back_ref) | copy-start | bytes 7077892
  124.5 13.5 %collective-permute-start.26 = (bf16[192,1024]{1,0:T(8,128)(2,1)}, bf16[192,1024]{1,0:T(8,128)(2,1)S(1)}, u32[]{:S(2)}, u32[]{:S(2)}) collective-permute-start(bf16[192,1024]{1,0:T(8,128)(2,1)} %get-tuple-element.148), channel_id=1, source_target_pairs={{0,2},{1,3},{2,4},{3,5},{4,6},{5,7},{6,0},{7,1},{8,10},{9,11},{10,... | collective-permute-start | bytes 1179656 | tf_op jit(solution)/shard_map/ppermute | solution.py:489
  125.3 12.7 %collective-permute-start.27 = (bf16[192,1024]{1,0:T(8,128)(2,1)}, bf16[192,1024]{1,0:T(8,128)(2,1)S(1)}, u32[]{:S(2)}, u32[]{:S(2)}) collective-permute-start(bf16[192,1024]{1,0:T(8,128)(2,1)} %get-tuple-element.149), channel_id=1, source_target_pairs={{0,6},{1,7},{2,0},{3,1},{4,2},{5,3},{6,4},{7,5},{8,14},{9,15},{10,... | collective-permute-start | bytes 1179656 | tf_op jit(solution)/shard_map/ppermute | solution.py:490
  128.8 15.9 %collective-permute-start.22 = (bf16[192,1024]{1,0:T(8,128)(2,1)}, bf16[192,1024]{1,0:T(8,128)(2,1)}, u32[]{:S(2)}, u32[]{:S(2)}) collective-permute-start(bf16[192,1024]{1,0:T(8,128)(2,1)} %get-tuple-element.142), channel_id=1, source_target_pairs={{0,2},{1,3},{2,4},{3,5},{4,6},{5,7},{6,0},{7,1},{8,10},{9,11},{10,... | collective-permute-start | bytes 1179656 | tf_op jit(solution)/shard_map/ppermute | solution.py:489
  128.8 15.9 %collective-permute-start.23 = (bf16[192,1024]{1,0:T(8,128)(2,1)}, bf16[192,1024]{1,0:T(8,128)(2,1)}, u32[]{:S(2)}, u32[]{:S(2)}) collective-permute-start(bf16[192,1024]{1,0:T(8,128)(2,1)} %get-tuple-element.143), channel_id=1, source_target_pairs={{0,6},{1,7},{2,0},{3,1},{4,2},{5,3},{6,4},{7,5},{8,14},{9,15},{10,... | collective-permute-start | bytes 1179656 | tf_op jit(solution)/shard_map/ppermute | solution.py:490
  138.0 1.7 %copy-start.1 = (bf16[3,384,1024]{2,1,0:T(8,128)(2,1)S(1)}, bf16[3,384,1024]{2,1,0:T(8,128)(2,1)}, u32[]{:S(2)}) copy-start(bf16[3,384,1024]{2,1,0:T(8,128)(2,1)} %copy-done) | copy-start | bytes 7077892
  146.3 1.2 collective-permute-start.28
  147.7 3.7 %collective-permute-start.29 = (f32[8,384]{1,0:T(8,128)S(1)}, f32[8,384]{1,0:T(8,128)S(1)}, u32[]{:S(2)}, u32[]{:S(2)}) collective-permute-start(f32[8,384]{1,0:T(8,128)S(1)} %fusion.35), channel_id=1, source_target_pairs={{0,2},{1,3},{2,0},{3,1},{4,6},{5,7},{6,4},{7,5},{8,10},{9,11},{10,... | collective-permute-start | bytes 36872 | tf_op jit(solution)/shard_map/ppermute | solution.py:496
  151.4 4.9 %collective-permute-start.30 = (f32[8,384]{1,0:T(8,128)S(1)}, f32[8,384]{1,0:T(8,128)S(1)}, u32[]{:S(2)}, u32[]{:S(2)}) collective-permute-start(f32[8,384]{1,0:T(8,128)S(1)} %add.219), channel_id=1, source_target_pairs={{0,6},{1,7},{2,4},{3,5},{4,2},{5,3},{6,0},{7,1},{8,14},{9,15},{10,... | collective-permute-start | bytes 36872 | tf_op jit(solution)/shard_map/ppermute | solution.py:496
